TPU v7x, 32 devices: a whole 2x2x4 slice. The times are simulated.
32 devices in a mesh: dp: 16 (over z, y, core), chan: 2 (over x).
Axes of the slice: x: 2, y: 2, z: 4, core: 2. Of those that a mesh axis runs over, the one named last changes fastest.
Arguments:
- features: bfloat16 [16, 512, 4096], P('dp', 'chan'), may hold values from -6 to 6
- crop_ids: int32 [16, 64, 64], P('dp'), may hold values from 0 to 15, as said below
- cotangent: bfloat16 [16, 512, 4096], P('dp', 'chan'), may hold values from -6 to 6
- norm1_gain: float32 [512], P('chan'), may hold values from 0.5 to 1.5
- norm1_bias: float32 [512], P('chan'), may hold values from -3 to 3
- conv1_weight: bfloat16 [9, 512, 512], P(None, 'chan'), may hold values from -0.09375 to 0.09375
- conv1_bias: float32 [512], P('chan'), may hold values from -3 to 3
- norm2_gain: float32 [512], P('chan'), may hold values from 0.5 to 1.5
- norm2_bias: float32 [512], P('chan'), may hold values from -3 to 3
- conv2_weight: bfloat16 [9, 512, 512], P(None, 'chan'), may hold values from -0.09375 to 0.09375
- conv2_bias: float32 [512], P('chan'), may hold values from -3 to 3
- norm3_gain: float32 [512], P('chan'), may hold values from 0.5 to 1.5
- norm3_bias: float32 [512], P('chan'), may hold values from -3 to 3
- query_weight: bfloat16 [512, 512], P('chan'), may hold values from -0.25 to 0.25
- query_bias: float32 [512], P('chan'), may hold values from -3 to 3
- key_weight: bfloat16 [512, 512], P('chan'), may hold values from -0.25 to 0.25
- value_weight: bfloat16 [512, 512], P('chan'), may hold values from -0.25 to 0.25
- value_bias: float32 [512], P('chan'), may hold values from -3 to 3
- proj_weight: bfloat16 [512, 512], P('chan'), may hold values from -1 to 1
- proj_bias: float32 [512], P('chan'), may hold values from -3 to 3
Outputs:
- output: bfloat16 [16, 512, 4096], P('dp', 'chan')
- input_grad: float32 [16, 512, 4096], P('dp', 'chan')
- norm1_gain_grad: float32 [512], P('chan')
- norm1_bias_grad: float32 [512], P('chan')
- conv1_weight_grad: float32 [9, 512, 512], P(None, 'chan')
- conv1_bias_grad: float32 [512], P('chan')
- norm2_gain_grad: float32 [512], P('chan')
- norm2_bias_grad: float32 [512], P('chan')
- conv2_weight_grad: float32 [9, 512, 512], P(None, 'chan')
- conv2_bias_grad: float32 [512], P('chan')
- norm3_gain_grad: float32 [512], P('chan')
- norm3_bias_grad: float32 [512], P('chan')
- query_weight_grad: float32 [512, 512], P('chan')
- query_bias_grad: float32 [512], P('chan')
- key_weight_grad: float32 [512, 512], P('chan')
- value_weight_grad: float32 [512, 512], P('chan')
- value_bias_grad: float32 [512], P('chan')
- proj_weight_grad: float32 [512, 512], P('chan')
- proj_bias_grad: float32 [512], P('chan')
Inputs may be any that keep to these rules, and one draw needn't show every extreme that they name: `crop_ids`: in each canvas the 16 crops are rectangles laid out as 4 bands of rows by 4 bands of columns, numbered 4 * row band + column band; every band spans a whole multiple of 8 rows or columns, at least 8.
All inputs are finite; a program needn't handle non-finite values.
Results may differ from a plain program's by a relative error of at most 0.023.
Values may be sent and summed in bfloat16 or wider, within the bound.
No kernel may reach another device: no remote copies, remote signals or barrier semaphores. Data moves between devices by JAX's collectives and lax.ppermute only.
A program may use at most 320 MiB of HBM per device.

v0:
```python
import jax
import jax.numpy as jnp
from jax import lax
from jax.sharding import PartitionSpec as P

CH = 512
GROUPS = 32
CROPS = 16


epsilon = 1e-06
highest = lax.Precision.HIGHEST


def crop_onehot(crop_ids):
    flat_crops = crop_ids.reshape(crop_ids.shape[0], -1)
    return (flat_crops[:, :, None] == jnp.arange(CROPS)[None, None, :]).astype(jnp.float32)


def crop_mean(crop_table, signal):
    group_width = CH // GROUPS
    summed = jnp.einsum("bpr,bcp->bcr", crop_table, signal, precision=highest)
    grouped = jnp.sum(summed.reshape(summed.shape[0], -1, group_width, summed.shape[2]), axis=2)
    counted = jnp.sum(crop_table, axis=1)[:, None, :] * group_width
    spread = jnp.repeat(grouped / counted, group_width, axis=1)
    return jnp.einsum("bpr,bcr->bcp", crop_table, spread, precision=highest)


def norm_forward(signal, crop_table, norm_gain, norm_bias):
    centred = signal - crop_mean(crop_table, signal)
    inverse = lax.rsqrt(crop_mean(crop_table, centred * centred) + epsilon)
    normed = centred * inverse
    return (normed * norm_gain[None, :, None] + norm_bias[None, :, None], normed, inverse)


def norm_backward(upstream, normed, inverse, crop_table, norm_gain):
    gain_grad = jnp.sum(upstream * normed, axis=(0, 2))
    bias_grad = jnp.sum(upstream, axis=(0, 2))
    scaled = upstream * norm_gain[None, :, None]
    centred = (
        scaled - crop_mean(crop_table, scaled) - normed * crop_mean(crop_table, scaled * normed)
    )
    return (inverse * centred, gain_grad, bias_grad)


def swish(before):
    return before * jax.nn.sigmoid(before)


def swish_backward(upstream, before):
    gating = jax.nn.sigmoid(before)
    return upstream * (gating + before * gating * (1.0 - gating))


def tap_steps(tap_index):
    return (tap_index // 3 - 1, tap_index % 3 - 1)


def tap_masks(crop_ids):
    canvases, canvas_side = (crop_ids.shape[0], crop_ids.shape[1])
    padded = jnp.pad(crop_ids, ((0, 0), (1, 1), (1, 1)), constant_values=-1)
    masks_list = []
    for tap_index in range(9):
        row_step, col_step = tap_steps(tap_index)
        nearby = padded[
            :, 1 + row_step : 1 + row_step + canvas_side, 1 + col_step : 1 + col_step + canvas_side
        ]
        masks_list.append((nearby == crop_ids).reshape(canvases, 1, canvas_side * canvas_side))
    return masks_list


def tap_start(tap_index, canvas_side):
    row_step, col_step = tap_steps(tap_index)
    return canvas_side + 1 + row_step * canvas_side + col_step


def neighbours(padded, tap_index, tap_mask, canvas_side):
    pixels = canvas_side * canvas_side
    start = tap_start(tap_index, canvas_side)
    nearby = padded[:, :, start : start + pixels]
    return jnp.where(tap_mask, nearby, jnp.zeros_like(nearby))


def pad_pixels(signal, canvas_side):
    return jnp.pad(signal, ((0, 0), (0, 0), (canvas_side + 1, canvas_side + 1)))


def place_back(term_list, tap_list, canvas_side):
    shape_now = term_list[0].shape
    pixels = shape_now[2]
    result = jnp.zeros((shape_now[0], shape_now[1], pixels + 2 * canvas_side + 2), jnp.float32)
    for tap_index in range(9):
        start = tap_start(tap_index, canvas_side)
        masked = jnp.where(tap_list[tap_index], term_list[tap_index], 0.0)
        result = result.at[:, :, start : start + pixels].add(masked)
    return result[:, :, canvas_side + 1 : canvas_side + 1 + pixels]


def gather_channels(signal):
    return lax.all_gather(signal, "chan", axis=1, tiled=True)


def conv_forward(gathered, conv_weight, conv_bias, tap_list, canvas_side):
    padded = pad_pixels(gathered, canvas_side)
    result = conv_bias[None, :, None]
    for tap_index in range(9):
        result = result + jnp.einsum(
            "bcp,oc->bop",
            neighbours(padded, tap_index, tap_list[tap_index], canvas_side),
            conv_weight[tap_index],
            preferred_element_type=jnp.float32,
        )
    return result


def conv_backward(branch_grad, gathered, conv_weight, tap_list, canvas_side):
    padded = pad_pixels(gathered, canvas_side)
    weight_grad = jnp.stack(
        [
            jnp.einsum(
                "bcp,bop->oc",
                neighbours(padded, tap_index, tap_list[tap_index], canvas_side),
                branch_grad,
                preferred_element_type=jnp.float32,
            )
            for tap_index in range(9)
        ]
    )
    bias_grad = jnp.sum(branch_grad.astype(jnp.float32), axis=(0, 2))
    local_width = branch_grad.shape[1]
    grad_full, weight_full = (
        lax.all_gather(branch_grad, "chan", axis=1, tiled=True),
        lax.all_gather(conv_weight, "chan", axis=1, tiled=True),
    )
    own_weight = lax.dynamic_slice_in_dim(
        weight_full, lax.axis_index("chan") * local_width, local_width, 2
    )
    term_list = [
        jnp.einsum(
            "bop,oc->bcp", grad_full, own_weight[tap_index], preferred_element_type=jnp.float32
        )
        for tap_index in range(9)
    ]
    input_grad = place_back(term_list, tap_list, canvas_side)
    return (weight_grad, bias_grad, input_grad)


def attend(sliced):
    query_rows, key_rows, value_rows, row_crops, key_crops = sliced
    scores = jnp.einsum(
        "cq,ck->qk", query_rows, key_rows, preferred_element_type=jnp.float32
    ) * CH ** (-0.5)
    scores = jnp.where(row_crops[:, None] == key_crops[None, :], scores, -1e30)
    highest_score = jnp.max(scores, axis=1, keepdims=True)
    exponent = jnp.exp(scores - highest_score)
    normaliser = jnp.sum(exponent, axis=1, keepdims=True)
    weights = (exponent / normaliser).astype(jnp.bfloat16)
    mixed_rows = jnp.einsum("qk,ck->cq", weights, value_rows, preferred_element_type=jnp.float32)
    return (mixed_rows.astype(jnp.bfloat16), (highest_score + jnp.log(normaliser))[:, 0])


def attend_back(sliced):
    query_rows, key_rows, value_rows, row_crops, key_crops, log_total, mixed_grad = sliced
    scale_factor = CH ** (-0.5)
    scores = (
        jnp.einsum("cq,ck->qk", query_rows, key_rows, preferred_element_type=jnp.float32)
        * scale_factor
    )
    scores = jnp.where(row_crops[:, None] == key_crops[None, :], scores, -1e30)
    weights = jnp.exp(scores - log_total[:, None])
    prob_grad = jnp.einsum("cq,ck->qk", mixed_grad, value_rows, preferred_element_type=jnp.float32)
    inner = jnp.sum(weights * prob_grad, axis=1, keepdims=True)
    score_grad = (weights * (prob_grad - inner)).astype(jnp.bfloat16)
    query_grad = (
        jnp.einsum("qk,ck->cq", score_grad, key_rows, preferred_element_type=jnp.float32)
        * scale_factor
    ).astype(jnp.bfloat16)
    key_grad = (
        jnp.einsum("qk,cq->ck", score_grad, query_rows, preferred_element_type=jnp.float32)
        * scale_factor
    )
    value_grad = jnp.einsum(
        "qk,cq->ck", weights.astype(jnp.bfloat16), mixed_grad, preferred_element_type=jnp.float32
    )
    return (query_grad, key_grad, value_grad)


def body(
    features,
    crop_ids,
    cotangent,
    norm1_gain,
    norm1_bias,
    conv1_weight,
    conv1_bias,
    norm2_gain,
    norm2_bias,
    conv2_weight,
    conv2_bias,
    norm3_gain,
    norm3_bias,
    query_weight,
    query_bias,
    key_weight,
    value_weight,
    value_bias,
    proj_weight,
    proj_bias,
):
    canvases, local_width, pixels = features.shape
    canvas_side = crop_ids.shape[1]
    crop_table = crop_onehot(crop_ids)
    tap_list = tap_masks(crop_ids)
    flat_crops = crop_ids.reshape(canvases, pixels)
    own_rows = pixels // lax.axis_size("chan")
    row_crops = lax.dynamic_slice_in_dim(flat_crops, lax.axis_index("chan") * own_rows, own_rows, 1)
    inputs = features.astype(jnp.float32)
    before1, normed1, inverse1 = norm_forward(inputs, crop_table, norm1_gain, norm1_bias)
    full1 = gather_channels(swish(before1).astype(jnp.bfloat16))
    hidden1 = conv_forward(full1, conv1_weight, conv1_bias, tap_list, canvas_side)
    before2, normed2, inverse2 = norm_forward(hidden1, crop_table, norm2_gain, norm2_bias)
    full2 = gather_channels(swish(before2).astype(jnp.bfloat16))
    hidden2 = conv_forward(full2, conv2_weight, conv2_bias, tap_list, canvas_side)
    residual = inputs + hidden2
    before3, normed3, inverse3 = norm_forward(residual, crop_table, norm3_gain, norm3_bias)
    normed_full = gather_channels(before3.astype(jnp.bfloat16))
    query_local = (
        jnp.einsum("oc,bcp->bop", query_weight, normed_full, preferred_element_type=jnp.float32)
        + query_bias[None, :, None]
    ).astype(jnp.bfloat16)
    key_local = jnp.einsum(
        "oc,bcp->bop", key_weight, normed_full, preferred_element_type=jnp.float32
    ).astype(jnp.bfloat16)
    value_local = (
        jnp.einsum("oc,bcp->bop", value_weight, normed_full, preferred_element_type=jnp.float32)
        + value_bias[None, :, None]
    ).astype(jnp.bfloat16)
    query_mine = lax.all_to_all(query_local, "chan", split_axis=2, concat_axis=1, tiled=True)
    key_full, value_full = (
        lax.all_gather(key_local, "chan", axis=1, tiled=True),
        lax.all_gather(value_local, "chan", axis=1, tiled=True),
    )
    mixed_mine, log_total = lax.map(
        attend, (query_mine, key_full, value_full, row_crops, flat_crops)
    )
    mixed_full = lax.all_gather(mixed_mine, "chan", axis=2, tiled=True)
    projected = (
        jnp.einsum("oc,bcp->bop", proj_weight, mixed_full, preferred_element_type=jnp.float32)
        + proj_bias[None, :, None]
    )
    output = (residual + projected).astype(jnp.bfloat16)
    proj_bias_grad = jnp.sum(cotangent.astype(jnp.float32), axis=(0, 2))
    proj_weight_grad = jnp.einsum(
        "bop,bcp->oc", cotangent, mixed_full, preferred_element_type=jnp.float32
    )
    mixed_part = jnp.einsum(
        "bop,oc->bcp", cotangent, proj_weight, preferred_element_type=jnp.float32
    )
    mixed_grad = lax.psum_scatter(mixed_part, "chan", scatter_dimension=2, tiled=True).astype(
        jnp.bfloat16
    )
    query_grad, key_part, value_part = lax.map(
        attend_back,
        (query_mine, key_full, value_full, row_crops, flat_crops, log_total, mixed_grad),
    )
    key_sum, value_sum = (
        lax.psum_scatter(
            key_part.astype(jnp.bfloat16), "chan", scatter_dimension=2, tiled=True
        ).astype(jnp.float32),
        lax.psum_scatter(
            value_part.astype(jnp.bfloat16), "chan", scatter_dimension=2, tiled=True
        ).astype(jnp.float32),
    )
    key_rows_grad = key_sum.astype(jnp.bfloat16)
    value_rows_grad = value_sum.astype(jnp.bfloat16)
    query_back, key_grad, value_grad = (
        lax.all_to_all(query_grad, "chan", split_axis=1, concat_axis=2, tiled=True),
        lax.all_to_all(key_rows_grad, "chan", split_axis=1, concat_axis=2, tiled=True),
        lax.all_to_all(value_rows_grad, "chan", split_axis=1, concat_axis=2, tiled=True),
    )
    query_weight_grad = jnp.einsum(
        "bop,bcp->oc", query_back, normed_full, preferred_element_type=jnp.float32
    )
    query_bias_grad = jnp.sum(query_back.astype(jnp.float32), axis=(0, 2))
    key_weight_grad = jnp.einsum(
        "bop,bcp->oc", key_grad, normed_full, preferred_element_type=jnp.float32
    )
    value_weight_grad = jnp.einsum(
        "bop,bcp->oc", value_grad, normed_full, preferred_element_type=jnp.float32
    )
    value_bias_grad = jnp.sum(value_grad.astype(jnp.float32), axis=(0, 2))
    normed_part = jnp.einsum(
        "bop,oc->bcp", query_back, query_weight, preferred_element_type=jnp.float32
    )
    normed_part = normed_part + jnp.einsum(
        "bop,oc->bcp", key_grad, key_weight, preferred_element_type=jnp.float32
    )
    normed_part = normed_part + jnp.einsum(
        "bop,oc->bcp", value_grad, value_weight, preferred_element_type=jnp.float32
    )
    normed_grad = lax.psum_scatter(normed_part, "chan", scatter_dimension=1, tiled=True)
    attention_part, norm3_gain_grad, norm3_bias_grad = norm_backward(
        normed_grad, normed3, inverse3, crop_table, norm3_gain
    )
    residual_grad = cotangent.astype(jnp.float32) + attention_part
    branch2_grad = residual_grad.astype(jnp.bfloat16)
    conv2_weight_grad, conv2_bias_grad, active2_grad = conv_backward(
        branch2_grad, full2, conv2_weight, tap_list, canvas_side
    )
    before2_grad = swish_backward(active2_grad, before2)
    hidden1_grad, norm2_gain_grad, norm2_bias_grad = norm_backward(
        before2_grad, normed2, inverse2, crop_table, norm2_gain
    )
    branch1_grad = hidden1_grad.astype(jnp.bfloat16)
    conv1_weight_grad, conv1_bias_grad, active1_grad = conv_backward(
        branch1_grad, full1, conv1_weight, tap_list, canvas_side
    )
    before1_grad = swish_backward(active1_grad, before1)
    input_part, norm1_gain_grad, norm1_bias_grad = norm_backward(
        before1_grad, normed1, inverse1, crop_table, norm1_gain
    )
    input_grad = residual_grad + input_part
    (
        norm1_gain_grad,
        norm1_bias_grad,
        conv1_weight_grad,
        conv1_bias_grad,
        norm2_gain_grad,
        norm2_bias_grad,
        conv2_weight_grad,
        conv2_bias_grad,
        norm3_gain_grad,
        norm3_bias_grad,
        query_weight_grad,
        query_bias_grad,
        key_weight_grad,
        value_weight_grad,
        value_bias_grad,
        proj_weight_grad,
        proj_bias_grad,
    ) = (
        lax.psum(norm1_gain_grad.astype(jnp.bfloat16), "dp").astype(jnp.float32),
        lax.psum(norm1_bias_grad.astype(jnp.bfloat16), "dp").astype(jnp.float32),
        lax.psum(conv1_weight_grad.astype(jnp.bfloat16), "dp").astype(jnp.float32),
        lax.psum(conv1_bias_grad.astype(jnp.bfloat16), "dp").astype(jnp.float32),
        lax.psum(norm2_gain_grad.astype(jnp.bfloat16), "dp").astype(jnp.float32),
        lax.psum(norm2_bias_grad.astype(jnp.bfloat16), "dp").astype(jnp.float32),
        lax.psum(conv2_weight_grad.astype(jnp.bfloat16), "dp").astype(jnp.float32),
        lax.psum(conv2_bias_grad.astype(jnp.bfloat16), "dp").astype(jnp.float32),
        lax.psum(norm3_gain_grad.astype(jnp.bfloat16), "dp").astype(jnp.float32),
        lax.psum(norm3_bias_grad.astype(jnp.bfloat16), "dp").astype(jnp.float32),
        lax.psum(query_weight_grad.astype(jnp.bfloat16), "dp").astype(jnp.float32),
        lax.psum(query_bias_grad.astype(jnp.bfloat16), "dp").astype(jnp.float32),
        lax.psum(key_weight_grad.astype(jnp.bfloat16), "dp").astype(jnp.float32),
        lax.psum(value_weight_grad.astype(jnp.bfloat16), "dp").astype(jnp.float32),
        lax.psum(value_bias_grad.astype(jnp.bfloat16), "dp").astype(jnp.float32),
        lax.psum(proj_weight_grad.astype(jnp.bfloat16), "dp").astype(jnp.float32),
        lax.psum(proj_bias_grad.astype(jnp.bfloat16), "dp").astype(jnp.float32),
    )
    return (
        output,
        input_grad,
        norm1_gain_grad,
        norm1_bias_grad,
        conv1_weight_grad,
        conv1_bias_grad,
        norm2_gain_grad,
        norm2_bias_grad,
        conv2_weight_grad,
        conv2_bias_grad,
        norm3_gain_grad,
        norm3_bias_grad,
        query_weight_grad,
        query_bias_grad,
        key_weight_grad,
        value_weight_grad,
        value_bias_grad,
        proj_weight_grad,
        proj_bias_grad,
    )


def solution(mesh):
    placed = (
        P("dp", "chan", None),
        P("dp", None, None),
        P("dp", "chan", None),
        P("chan"),
        P("chan"),
        P(None, "chan", None),
        P("chan"),
        P("chan"),
        P("chan"),
        P(None, "chan", None),
        P("chan"),
        P("chan"),
        P("chan"),
        P("chan", None),
        P("chan"),
        P("chan", None),
        P("chan", None),
        P("chan"),
        P("chan", None),
        P("chan"),
    )
    return jax.shard_map(
        body,
        mesh=mesh,
        in_specs=placed,
        out_specs=(
            P("dp", "chan", None),
            P("dp", "chan", None),
            P("chan"),
            P("chan"),
            P(None, "chan", None),
            P("chan"),
            P("chan"),
            P("chan"),
            P(None, "chan", None),
            P("chan"),
            P("chan"),
            P("chan"),
            P("chan", None),
            P("chan"),
            P("chan", None),
            P("chan", None),
            P("chan"),
            P("chan", None),
            P("chan"),
        ),
        check_vma=False,
    )
```

profile of v0, /device:TPU:0, one launch (start us, length us, event | category | flops | bytes accessed | tf_op | source)
XLA Modules:
  0.0 1833.2 jit_solution(10864730401548106291)
XLA Ops:
  21.7 58.5 %all-gather.13.cloned.1.call-done = bf16[1,512,4096]{2,1,0:T(8,128)(2,1)} async-done(((bf16[1,256,4096]{2,1,0:T(8,128)(2,1)}), bf16[1,512,4096]{2,1,0:T(8,128)(2,1)}) %all-gather.13.cloned.1.call-update) | async-done | bytes 4194320 | tf_op jit(solution)/shard_map/all_gather | solution.py:100
  110.2 56.7 %all-gather.29.cloned.1.call-done = bf16[512,4096]{1,0:T(8,128)(2,1)} async-done(((bf16[256,4096]{1,0:T(8,128)(2,1)}), bf16[512,4096]{1,0:T(8,128)(2,1)}) %all-gather.29.cloned.1.call-update) | async-done | bytes 4194320 | tf_op jit(solution)/shard_map/all_gather | solution.py:100
  199.4 56.4 %all-gather.15.cloned.1.call-done = bf16[1,512,4096]{2,1,0:T(8,128)(2,1)} async-done(((bf16[1,256,4096]{2,1,0:T(8,128)(2,1)}), bf16[1,512,4096]{2,1,0:T(8,128)(2,1)}) %all-gather.15.cloned.1.call-update) | async-done | bytes 4194320 | tf_op jit(solution)/shard_map/all_gather | solution.py:100
  275.3 25.0 %copy.105 = bf16[1,256,4096]{1,0,2:T(2,128)(2,1)} copy(bf16[1,256,4096]{1,2,0:T(8,128)(2,1)S(1)} %fusion.80) | data formatting | bytes 4194304 | tf_op jit(solution)/shard_map/convert_element_type | solution.py:230
  300.9 21.6 %reduce.75 = bf16[4096,256]{1,0:T(8,128)(2,1)S(1)} reduce(bf16[4096,1,256]{2,1,0:T(2,128)(2,1)} %bitcast.982, bf16[]{:T(256)} %broadcast.874), dimensions={1}, to_apply=%bitcast.955.reduce_sub_computation | reduce | bytes 4194306
  328.3 47.7 %all-to-all-done = bf16[2,2,262144]{2,1,0:T(2,128)(2,1)S(1)} async-done(((bf16[2,2,262144]{2,1,0:T(2,128)(2,1)}), bf16[2,2,262144]{2,1,0:T(2,128)(2,1)S(1)}, u32[]{:S(2)}, u32[]{:S(2)}) %all-to-all-start) | async-done | bytes 2097184 | tf_op jit(solution)/shard_map/all_to_all | solution.py:238
  384.1 22.9 %fusion.700 = (f32[2048]{0:T(1024)S(1)}, f32[2048,4096]{1,0:T(8,128)}) fusion(bf16[512,2048]{1,0:T(8,128)(2,1)} %bitcast.1004, bf16[1,512,4096]{1,2,0:T(8,128)(2,1)} %all-gather.19.cloned.1.call-done, s32[4096]{0:T(1024)S(1)} %eq.223, s32[2048]{0:T(1024)S(1)} %bitcast.1018), kind=kOutput, calls=%fused_computation.594 | convolution fusion | flops 8623486976 | bytes 39878656 | tf_op jit(solution)/shard_map/while/body/eval_jaxpr/cq,ck->qk/dot_general | solution.py:150
  407.0 13.8 fusion
  420.8 78.9 %reduce-scatter.5.cloned.1.call-done = f32[1,512,2048]{2,1,0:T(8,128)} async-done(((f32[1,512,4096]{2,1,0:T(8,128)}), f32[1,512,2048]{2,1,0:T(8,128)}) %reduce-scatter.5.cloned.1.call-update) | async-done | bytes 4194320 | tf_op jit(solution)/shard_map/reduce_scatter | solution.py:259
  499.7 32.4 %multiply_reduce_fusion = (f32[2048]{0:T(1024)S(1)}, f32[2048,4096]{1,0:T(8,128)}) fusion(f32[2048,4096]{1,0:T(8,128)} %get-tuple-element.452, f32[2048]{0:T(1024)S(1)} %log_add_fusion, bf16[1,512,4096]{1,2,0:T(8,128)(2,1)} %all-gather.17.cloned.1.call-done, f32[1,512,2048]{2,1,0:T(8,128)} %reduce-scatter.5.cloned.1.call-done), kind=kOutput, calls=%fused_computation.1 | convolution fusion | flops 8616146944 | bytes 75513856 | tf_op jit(solution)/shard_map/while/body/eval_jaxpr/cq,ck->qk/dot_general | solution.py:171
  532.1 27.6 %multiply_convert_fusion = bf16[2048,4096]{1,0:T(8,128)(2,1)} fusion(f32[2048,4096]{1,0:T(8,128)} %get-tuple-element.454, f32[2048,4096]{1,0:T(8,128)} %get-tuple-element.452, f32[2048]{0:T(1024)S(1)} %get-tuple-element.453, f32[2048]{0:T(1024)S(1)} %log_add_fusion), kind=kLoop, calls=%fused_computation | loop fusion | flops 33554432 | bytes 83902464 | tf_op jit(solution)/shard_map/while/body/eval_jaxpr/convert_element_type | solution.py:173
  559.8 13.7 fusion.28
  573.5 14.1 fusion.175
  592.9 13.2 reduce.76
  612.5 17.8 fusion.25
  630.4 18.0 fusion.172
  655.2 14.5 reduce.77
  678.7 30.8 %reduce-scatter.9.cloned.1.call-done = bf16[1,512,2048]{2,1,0:T(8,128)(2,1)} async-done(((bf16[1,512,4096]{2,1,0:T(8,128)(2,1)}), bf16[1,512,2048]{2,1,0:T(8,128)(2,1)}) %reduce-scatter.9.cloned.1.call-update) | async-done | bytes 2097168 | tf_op jit(solution)/shard_map/reduce_scatter | solution.py:270
  716.4 14.5 reduce.78
  767.1 20.7 %all-to-all-done.3 = bf16[2,2,262144]{2,1,0:T(2,128)(2,1)} async-done(((bf16[2,2,262144]{2,1,0:T(2,128)(2,1)}), bf16[2,2,262144]{2,1,0:T(2,128)(2,1)}, u32[]{:S(2)}, u32[]{:S(2)}) %all-to-all-start.3) | async-done | bytes 2097184 | tf_op jit(solution)/shard_map/all_to_all | solution.py:279
  824.3 84.8 %reduce-scatter.11.cloned.1.call-done = f32[1,256,4096]{2,1,0:T(8,128)} async-done(((f32[1,512,4096]{2,1,0:T(8,128)}), f32[1,256,4096]{2,1,0:T(8,128)}) %reduce-scatter.11.cloned.1.call-update) | async-done | bytes 4194320 | tf_op jit(solution)/shard_map/reduce_scatter | solution.py:301
  953.7 19.6 %all-gather.23.cloned.1.call-done = bf16[9,512,512]{2,1,0:T(8,128)(2,1)} async-done(((bf16[9,256,512]{2,1,0:T(8,128)(2,1)}), bf16[9,512,512]{2,1,0:T(8,128)(2,1)}) %all-gather.23.cloned.1.call-update) | async-done | bytes 4718608 | tf_op jit(solution)/shard_map/all_gather | solution.py:133
  973.3 58.8 %all-gather.25.cloned.1.call-done = bf16[1,512,4096]{2,1,0:T(8,128)(2,1)} async-done(((bf16[1,256,4096]{2,1,0:T(8,128)(2,1)}), bf16[1,512,4096]{2,1,0:T(8,128)(2,1)}) %all-gather.25.cloned.1.call-update) | async-done | bytes 4194320 | tf_op jit(solution)/shard_map/all_gather | solution.py:132
  1043.9 22.0 %scatter-add.61 = f32[1,256,4226]{2,1,0:T(8,128)} dynamic-update-slice(f32[1,256,4226]{2,1,0:T(8,128)} %scatter-add.60, f32[1,256,4096]{2,1,0:T(8,128)} %fusion.51, s32[]{:T(128)} %constant.500.clone.1, s32[]{:T(128)} %constant.500.clone.1, s32[]{:T(128)} %constant.509.clone.1) | dynamic-update-slice | bytes 8388612 | tf_op jit(solution)/shard_map/scatter-add | solution.py:95
  1073.0 22.0 %scatter-add.64 = f32[1,256,4226]{2,1,0:T(8,128)} dynamic-update-slice(f32[1,256,4226]{2,1,0:T(8,128)} %scatter-add.61, f32[1,256,4096]{2,1,0:T(8,128)} %fusion.52, s32[]{:T(128)} %constant.500.clone.1, s32[]{:T(128)} %constant.500.clone.1, s32[]{:T(128)} %constant.510.clone.1) | dynamic-update-slice | bytes 8388612 | tf_op jit(solution)/shard_map/scatter-add | solution.py:95
  1102.1 22.0 %scatter-add.65 = f32[1,256,4226]{2,1,0:T(8,128)} dynamic-update-slice(f32[1,256,4226]{2,1,0:T(8,128)} %scatter-add.64, f32[1,256,4096]{2,1,0:T(8,128)} %fusion.53, s32[]{:T(128)} %constant.500.clone.1, s32[]{:T(128)} %constant.500.clone.1, s32[]{:T(128)} %constant.511.clone.1) | dynamic-update-slice | bytes 8388612 | tf_op jit(solution)/shard_map/scatter-add | solution.py:95
  1131.2 22.0 %scatter-add.66 = f32[1,256,4226]{2,1,0:T(8,128)} dynamic-update-slice(f32[1,256,4226]{2,1,0:T(8,128)} %scatter-add.65, f32[1,256,4096]{2,1,0:T(8,128)} %fusion.69, s32[]{:T(128)} %constant.500.clone.1, s32[]{:T(128)} %constant.500.clone.1, s32[]{:T(128)} %constant.512.clone.1) | dynamic-update-slice | bytes 8388612 | tf_op jit(solution)/shard_map/scatter-add | solution.py:95
  1160.3 22.0 %scatter-add.69 = f32[1,256,4226]{2,1,0:T(8,128)} dynamic-update-slice(f32[1,256,4226]{2,1,0:T(8,128)} %scatter-add.66, f32[1,256,4096]{2,1,0:T(8,128)} %fusion.54, s32[]{:T(128)} %constant.500.clone.1, s32[]{:T(128)} %constant.500.clone.1, s32[]{:T(128)} %constant.513.clone.1) | dynamic-update-slice | bytes 8388612 | tf_op jit(solution)/shard_map/scatter-add | solution.py:95
  1195.3 22.0 %scatter-add.71 = f32[1,256,4226]{2,1,0:T(8,128)} dynamic-update-slice(f32[1,256,4226]{2,1,0:T(8,128)} %fusion.56, f32[1,256,4096]{2,1,0:T(8,128)} %fusion.57, s32[]{:T(128)} %constant.500.clone.1, s32[]{:T(128)} %constant.500.clone.1, s32[]{:T(128)} %constant.515.clone.1) | dynamic-update-slice | bytes 8388612 | tf_op jit(solution)/shard_map/scatter-add | solution.py:95
  1217.3 7.1 fusion.58
  1224.4 22.0 %scatter-add.74 = f32[1,256,4226]{2,1,0:T(8,128)} dynamic-update-slice(f32[1,256,4226]{2,1,0:T(8,128)} %scatter-add.71, f32[1,256,4096]{2,1,0:T(8,128)} %fusion.58, s32[]{:T(128)} %constant.500.clone.1, s32[]{:T(128)} %constant.500.clone.1, s32[]{:T(128)} %constant.516.clone.1) | dynamic-update-slice | bytes 8388612 | tf_op jit(solution)/shard_map/scatter-add | solution.py:95
  1307.8 116.4 %all-reduce.9.cloned.1.call-done = (bf16[256,512]{0,1:T(8,128)(2,1)}, bf16[9,256,512]{2,1,0:T(8,128)(2,1)}, bf16[9,256,512]{2,1,0:T(8,128)(2,1)}, bf16[256,512]{...) async-done(((bf16[256,512]{0,1:T(8,128)(2,1)}, bf16[9,256,512]{2,1,0:T(8,128)(2,1)}, bf16[9,256,512]{2,1,0:T(8,128)(2,1)}, ...) | async-done | bytes 5767184 | tf_op jit(solution)/shard_map/psum | solution.py:357
  1435.2 53.0 %all-gather.21.cloned.1.call-done = bf16[9,512,512]{2,1,0:T(8,128)(2,1)} async-done(((bf16[9,256,512]{2,1,0:T(8,128)(2,1)}), bf16[9,512,512]{2,1,0:T(8,128)(2,1)}) %all-gather.21.cloned.1.call-update) | async-done | bytes 4718608 | tf_op jit(solution)/shard_map/all_gather | solution.py:133
  1488.2 58.2 %all-gather.27.cloned.1.call-done = bf16[1,512,4096]{2,1,0:T(8,128)(2,1)} async-done(((bf16[1,256,4096]{2,1,0:T(8,128)(2,1)}), bf16[1,512,4096]{2,1,0:T(8,128)(2,1)}) %all-gather.27.cloned.1.call-update) | async-done | bytes 4194320 | tf_op jit(solution)/shard_map/all_gather | solution.py:132
  1558.3 22.0 %scatter-add.76 = f32[1,256,4226]{2,1,0:T(8,128)} dynamic-update-slice(f32[1,256,4226]{2,1,0:T(8,128)} %scatter-add.75, f32[1,256,4096]{2,1,0:T(8,128)} %fusion.59, s32[]{:T(128)} %constant.500.clone.1, s32[]{:T(128)} %constant.500.clone.1, s32[]{:T(128)} %constant.509.clone.1) | dynamic-update-slice | bytes 8388612 | tf_op jit(solution)/shard_map/scatter-add | solution.py:95
  1580.3 7.2 fusion.60
  1587.5 22.0 %scatter-add.79 = f32[1,256,4226]{2,1,0:T(8,128)} dynamic-update-slice(f32[1,256,4226]{2,1,0:T(8,128)} %scatter-add.76, f32[1,256,4096]{2,1,0:T(8,128)} %fusion.60, s32[]{:T(128)} %constant.500.clone.1, s32[]{:T(128)} %constant.500.clone.1, s32[]{:T(128)} %constant.510.clone.1) | dynamic-update-slice | bytes 8388612 | tf_op jit(solution)/shard_map/scatter-add | solution.py:95
  1609.5 7.2 fusion.61
  1616.7 22.0 %scatter-add.80 = f32[1,256,4226]{2,1,0:T(8,128)} dynamic-update-slice(f32[1,256,4226]{2,1,0:T(8,128)} %scatter-add.79, f32[1,256,4096]{2,1,0:T(8,128)} %fusion.61, s32[]{:T(128)} %constant.500.clone.1, s32[]{:T(128)} %constant.500.clone.1, s32[]{:T(128)} %constant.511.clone.1) | dynamic-update-slice | bytes 8388612 | tf_op jit(solution)/shard_map/scatter-add | solution.py:95
  1638.7 7.1 fusion.70
  1645.8 22.0 %scatter-add.81 = f32[1,256,4226]{2,1,0:T(8,128)} dynamic-update-slice(f32[1,256,4226]{2,1,0:T(8,128)} %scatter-add.80, f32[1,256,4096]{2,1,0:T(8,128)} %fusion.70, s32[]{:T(128)} %constant.500.clone.1, s32[]{:T(128)} %constant.500.clone.1, s32[]{:T(128)} %constant.512.clone.1) | dynamic-update-slice | bytes 8388612 | tf_op jit(solution)/shard_map/scatter-add | solution.py:95
  1667.8 7.2 fusion.62
  1675.0 22.0 %scatter-add.84 = f32[1,256,4226]{2,1,0:T(8,128)} dynamic-update-slice(f32[1,256,4226]{2,1,0:T(8,128)} %scatter-add.81, f32[1,256,4096]{2,1,0:T(8,128)} %fusion.62, s32[]{:T(128)} %constant.500.clone.1, s32[]{:T(128)} %constant.500.clone.1, s32[]{:T(128)} %constant.513.clone.1) | dynamic-update-slice | bytes 8388612 | tf_op jit(solution)/shard_map/scatter-add | solution.py:95
  1710.2 22.0 %scatter-add.86 = f32[1,256,4226]{2,1,0:T(8,128)} dynamic-update-slice(f32[1,256,4226]{2,1,0:T(8,128)} %fusion.64, f32[1,256,4096]{2,1,0:T(8,128)} %fusion.65, s32[]{:T(128)} %constant.500.clone.1, s32[]{:T(128)} %constant.500.clone.1, s32[]{:T(128)} %constant.515.clone.1) | dynamic-update-slice | bytes 8388612 | tf_op jit(solution)/shard_map/scatter-add | solution.py:95
  1732.1 7.2 fusion.66
  1739.3 22.0 %scatter-add.89 = f32[1,256,4226]{2,1,0:T(8,128)} dynamic-update-slice(f32[1,256,4226]{2,1,0:T(8,128)} %scatter-add.86, f32[1,256,4096]{2,1,0:T(8,128)} %fusion.66, s32[]{:T(128)} %constant.500.clone.1, s32[]{:T(128)} %constant.500.clone.1, s32[]{:T(128)} %constant.516.clone.1) | dynamic-update-slice | bytes 8388612 | tf_op jit(solution)/shard_map/scatter-add | solution.py:95
  1776.2 33.7 %all-reduce.5 = (bf16[256]{0:T(256)(128)(2,1)S(1)}, bf16[256]{0:T(256)(128)(2,1)S(1)}, bf16[256]{0:T(256)(128)(2,1)S(1)}, bf16[256]{0:T(256)(128)(2,1)S(1)}, bf1...) all-reduce(bf16[256]{0:T(256)(128)(2,1)S(1)} %get-tuple-element.392, ...), channel_id=1, replica_groups=mesh['dp'=16,'chan'=2] {'dp'}, use_global_device_ids=true, to_apply=%region_21.22 | all-reduce | flops 2816 | bytes 11264 | tf_op jit(solution)/shard_map/psum | solution.py:342
  1816.2 10.3 fusion.49
  (381 shorter events, 433.2 us)
Async XLA Ops:
  7.2 263.9 %copy-start = (bf16[256,512]{1,0:T(8,128)(2,1)S(1)}, bf16[256,512]{1,0:T(8,128)(2,1)}, u32[]{:S(2)}) copy-start(bf16[256,512]{1,0:T(8,128)(2,1)} %param.69) | copy-start | bytes 786436
  7.2 73.0 %all-gather.13.cloned.1.call-start = ((), (), s32[]{:S(2)}) async-start(), calls=%async_computation.8 | async-start | bytes 6291456 | tf_op jit(solution)/shard_map/all_gather | solution.py:100
  8.2 375.8 %copy-start.22 = (s32[4096]{0:T(1024)}, s32[4096]{0:T(1024)S(1)}, u32[]{:S(2)}) copy-start(s32[4096]{0:T(1024)S(1)} %eq.223) | copy-start | bytes 49156
  10.7 181.7 %copy-start.60 = (f32[16]{0:T(128)}, f32[16]{0:T(128)S(1)}, u32[]{:S(2)}) copy-start(f32[16]{0:T(128)S(1)} %broadcast_multiply_fusion.3) | copy-start | bytes 196
  14.9 65.3 %copy-start.79 = (f32[256]{0:T(256)S(1)}, f32[256]{0:T(256)}, u32[]{:S(2)}) copy-start(f32[256]{0:T(256)} %param.62) | copy-start | bytes 3076
  20.6 146.3 %all-gather.29.cloned.1.call-start = ((), (), s32[]{:S(2)}) async-start(), calls=%async_computation.20 | async-start | bytes 6291456 | tf_op jit(solution)/shard_map/all_gather | solution.py:100
  21.1 145.8 %copy-start.62 = (pred[4096]{0:T(1024)(128)(4,1)}, pred[4096]{0:T(1024)(128)(4,1)S(1)}, u32[]{:S(2)}) copy-start(pred[4096]{0:T(1024)(128)(4,1)S(1)} %broadcast_in_dim.363) | copy-start | bytes 12292
  21.2 149.9 %copy-start.56 = (pred[4096]{0:T(1024)(128)(4,1)}, pred[4096]{0:T(1024)(128)(4,1)S(1)}, u32[]{:S(2)}) copy-start(pred[4096]{0:T(1024)(128)(4,1)S(1)} %broadcast_in_dim.369) | copy-start | bytes 12292
  21.3 151.8 %copy-start.54 = (pred[4096]{0:T(1024)(128)(4,1)}, pred[4096]{0:T(1024)(128)(4,1)S(1)}, u32[]{:S(2)}) copy-start(pred[4096]{0:T(1024)(128)(4,1)S(1)} %broadcast_in_dim.371) | copy-start | bytes 12292
  21.4 153.6 %copy-start.52 = (pred[4096]{0:T(1024)(128)(4,1)}, pred[4096]{0:T(1024)(128)(4,1)S(1)}, u32[]{:S(2)}) copy-start(pred[4096]{0:T(1024)(128)(4,1)S(1)} %broadcast_in_dim.373) | copy-start | bytes 12292
  21.4 156.7 %copy-start.50 = (pred[4096]{0:T(1024)(128)(4,1)}, pred[4096]{0:T(1024)(128)(4,1)S(1)}, u32[]{:S(2)}) copy-start(pred[4096]{0:T(1024)(128)(4,1)S(1)} %broadcast_in_dim.375) | copy-start | bytes 12292
  21.5 158.4 %copy-start.48 = (pred[4096]{0:T(1024)(128)(4,1)}, pred[4096]{0:T(1024)(128)(4,1)S(1)}, u32[]{:S(2)}) copy-start(pred[4096]{0:T(1024)(128)(4,1)S(1)} %broadcast_in_dim.377) | copy-start | bytes 12292
  21.6 160.2 %copy-start.46 = (pred[4096]{0:T(1024)(128)(4,1)}, pred[4096]{0:T(1024)(128)(4,1)S(1)}, u32[]{:S(2)}) copy-start(pred[4096]{0:T(1024)(128)(4,1)S(1)} %broadcast_in_dim.379) | copy-start | bytes 12292
  21.7 162.2 %copy-start.58 = (pred[4096]{0:T(1024)(128)(4,1)}, pred[4096]{0:T(1024)(128)(4,1)S(1)}, u32[]{:S(2)}) copy-start(pred[4096]{0:T(1024)(128)(4,1)S(1)} %broadcast_in_dim.381) | copy-start | bytes 12292
  104.3 62.6 %copy-start.80 = (f32[256]{0:T(256)S(1)}, f32[256]{0:T(256)}, u32[]{:S(2)}) copy-start(f32[256]{0:T(256)} %param.66) | copy-start | bytes 3076
  110.0 145.9 %all-gather.15.cloned.1.call-start = ((), (), s32[]{:S(2)}) async-start(), calls=%async_computation.9 | async-start | bytes 6291456 | tf_op jit(solution)/shard_map/all_gather | solution.py:100
  192.4 63.4 %copy-start.37 = (bf16[256,512]{1,0:T(8,128)(2,1)S(1)}, bf16[256,512]{1,0:T(8,128)(2,1)}, u32[]{:S(2)}) copy-start(bf16[256,512]{1,0:T(8,128)(2,1)} %param.71) | copy-start | bytes 786436
  199.0 61.9 %copy-start.40 = (bf16[256,512]{1,0:T(8,128)(2,1)S(1)}, bf16[256,512]{1,0:T(8,128)(2,1)}, u32[]{:S(2)}) copy-start(bf16[256,512]{1,0:T(8,128)(2,1)} %param.72) | copy-start | bytes 786436
  199.0 61.9 %copy-start.81 = (f32[256]{0:T(256)S(1)}, f32[256]{0:T(256)}, u32[]{:S(2)}) copy-start(f32[256]{0:T(256)} %param.73) | copy-start | bytes 3076
  199.0 185.1 %all-gather.19.cloned.1.call-start = ((), (), s32[]{:S(2)}) async-start(), calls=%async_computation.11 | async-start | bytes 6291456 | tf_op jit(solution)/shard_map/all_gather | solution.py:240
  260.8 160.0 %all-gather.17.cloned.1.call-start = ((), (), s32[]{:S(2)}) async-start(), calls=%async_computation.10 | async-start | bytes 6291456 | tf_op jit(solution)/shard_map/all_gather | solution.py:241
  265.9 233.8 %reduce-scatter.5.cloned.1.call-start = ((), (), s32[]{:S(2)}) async-start(), calls=%async_computation.12 | async-start | bytes 12582912 | tf_op jit(solution)/shard_map/reduce_scatter | solution.py:259
  324.1 52.0 %all-to-all-start = ((bf16[2,2,262144]{2,1,0:T(2,128)(2,1)}), bf16[2,2,262144]{2,1,0:T(2,128)(2,1)S(1)}, u32[]{:S(2)}, u32[]{:S(2)}) async-start(bf16[2,2,262144]{2,1,0:T(2,128)(2,1)} %reshape.1983), calls=%async_computation | async-start | bytes 4194304 | tf_op jit(solution)/shard_map/all_to_all | solution.py:238
  328.0 320.4 %reduce-scatter.7.cloned.1.call-start = ((), (), s32[]{:S(2)}) async-start(), calls=%async_computation.13 | async-start | bytes 6291456 | tf_op jit(solution)/shard_map/reduce_scatter | solution.py:267
  532.1 27.6 %copy-start.34 = (bf16[1,2,256,2048]{3,2,1,0:T(8,128)(2,1)S(1)}, bf16[1,2,256,2048]{3,2,1,0:T(8,128)(2,1)}, u32[]{:S(2)}) copy-start(bf16[1,2,256,2048]{3,2,1,0:T(8,128)(2,1)} %copy.78) | copy-start | bytes 6291460
  608.7 64.9 %all-to-all-start.1 = ((bf16[2,2,262144]{2,1,0:T(2,128)(2,1)}), bf16[2,2,262144]{2,1,0:T(2,128)(2,1)S(1)}, u32[]{:S(2)}, u32[]{:S(2)}) async-start(bf16[2,2,262144]{2,1,0:T(2,128)(2,1)} %reshape.1985), calls=%async_computation.2 | async-start | bytes 4194304 | tf_op jit(solution)/shard_map/all_to_all | solution.py:277
  612.5 97.1 %reduce-scatter.9.cloned.1.call-start = ((), (), s32[]{:S(2)}) async-start(), calls=%async_computation.14 | async-start | bytes 6291456 | tf_op jit(solution)/shard_map/reduce_scatter | solution.py:270
  630.3 185.4 %all-gather.31.cloned.1.call-start = ((), (), s32[]{:S(2)}) async-start(), calls=%async_computation.21 | async-start | bytes 6291456 | tf_op jit(solution)/shard_map/all_gather | solution.py:246
  673.5 61.2 %all-to-all-start.2 = ((bf16[2,2,262144]{2,1,0:T(2,128)(2,1)}), bf16[2,2,262144]{2,1,0:T(2,128)(2,1)}, u32[]{:S(2)}, u32[]{:S(2)}) async-start(bf16[2,2,262144]{2,1,0:T(2,128)(2,1)} %reshape.1987), calls=%async_computation.4 | async-start | bytes 4194304 | tf_op jit(solution)/shard_map/all_to_all | solution.py:278
  734.7 53.0 %all-to-all-start.3 = ((bf16[2,2,262144]{2,1,0:T(2,128)(2,1)}), bf16[2,2,262144]{2,1,0:T(2,128)(2,1)}, u32[]{:S(2)}, u32[]{:S(2)}) async-start(bf16[2,2,262144]{2,1,0:T(2,128)(2,1)} %reshape.1989), calls=%async_computation.6 | async-start | bytes 4194304 | tf_op jit(solution)/shard_map/all_to_all | solution.py:279
  739.6 169.5 %reduce-scatter.11.cloned.1.call-start = ((), (), s32[]{:S(2)}) async-start(), calls=%async_computation.15 | async-start | bytes 12582912 | tf_op jit(solution)/shard_map/reduce_scatter | solution.py:301
  767.1 33.9 %copy-start.20 = (bf16[1,256,2,2048]{1,3,2,0:T(8,128)(2,1)}, bf16[1,256,2,2048]{1,3,2,0:T(8,128)(2,1)S(1)}, u32[]{:S(2)}) copy-start(bf16[1,256,2,2048]{1,3,2,0:T(8,128)(2,1)S(1)} %copy.83) | copy-start | bytes 6291460
  792.2 8.7 copy-start.38
  809.8 163.5 %all-gather.23.cloned.1.call-start = ((), (), s32[]{:S(2)}) async-start(), calls=%async_computation.17 | async-start | bytes 7077888 | tf_op jit(solution)/shard_map/all_gather | solution.py:133
  810.6 221.5 %all-gather.25.cloned.1.call-start = ((), (), s32[]{:S(2)}) async-start(), calls=%async_computation.18 | async-start | bytes 6291456 | tf_op jit(solution)/shard_map/all_gather | solution.py:132
  822.3 86.8 %copy-start.66 = (f32[256]{0:T(256)S(1)}, f32[256]{0:T(256)}, u32[]{:S(2)}) copy-start(f32[256]{0:T(256)} %param.67) | copy-start | bytes 3076
  927.8 496.4 %all-reduce.9.cloned.1.call-start = ((), (), s32[]{:S(2)}) async-start(), calls=%async_computation.22 | async-start | bytes 11534336 | tf_op jit(solution)/shard_map/psum | solution.py:357
  1182.3 7.0 copy-start.5
  1224.4 22.0 %copy-start.68 = (f32[256]{0:T(256)S(1)}, f32[256]{0:T(256)}, u32[]{:S(2)}) copy-start(f32[256]{0:T(256)} %param.63) | copy-start | bytes 3076
  1224.4 22.0 %copy-start.76 = (f32[256]{0:T(256)S(1)}, f32[256]{0:T(256)}, u32[]{:S(2)}) copy-start(f32[256]{0:T(256)} %param.64) | copy-start | bytes 3076
  1290.0 198.3 %all-gather.21.cloned.1.call-start = ((), (), s32[]{:S(2)}) async-start(), calls=%async_computation.16 | async-start | bytes 7077888 | tf_op jit(solution)/shard_map/all_gather | solution.py:133
  1290.6 7.1 copy-start.36
  1290.6 7.1 copy-start.64
  1290.6 255.8 %all-gather.27.cloned.1.call-start = ((), (), s32[]{:S(2)}) async-start(), calls=%async_computation.19 | async-start | bytes 6291456 | tf_op jit(solution)/shard_map/all_gather | solution.py:132
  1697.0 7.1 copy-start.3
  1739.3 22.0 %copy-start.70 = (f32[256]{0:T(256)S(1)}, f32[256]{0:T(256)}, u32[]{:S(2)}) copy-start(f32[256]{0:T(256)} %param.59) | copy-start | bytes 3076
  1739.3 22.0 %copy-start.78 = (f32[256]{0:T(256)S(1)}, f32[256]{0:T(256)}, u32[]{:S(2)}) copy-start(f32[256]{0:T(256)} %param.60) | copy-start | bytes 3076
  1816.1 10.3 copy-start.1
  (56 other events, 218.4 us)
Sparse Core Ops, SparseCore 0:
  20.7 59.4 all-gather.12
  110.1 56.7 all-gather.28
  199.1 56.7 all-gather.14
  260.9 56.7 all-gather.18
  319.0 79.1 all-gather.16
  400.4 99.2 reduce-scatter.4
  573.6 65.6 reduce-scatter.6
  641.6 67.9 reduce-scatter.8
  711.8 79.4 all-gather.30
  809.9 99.0 reduce-scatter.10
  910.6 62.6 all-gather.22
  975.3 56.7 all-gather.24
  1290.1 134.0 all-reduce.8
  1425.6 62.6 all-gather.20
  1489.6 56.7 all-gather.26
where the time goes:
time: 1850 us; the launch traced here: 1830 us
  waiting for transfers between devices  742 us (40%)
  matrix products  447 us (24%)
  local copies, waits for them, and re-layouts  424 us (23%)
  other arithmetic  151 us (8%)
  blocking collectives  33.7 us (2%)
  starting transfers between devices  19.5 us (1%)
    scatter-add x16, local copies, waits for them, and re-layouts, place_back(): result = result.at[:, :, start:start + pixels].add(masked)  313 us
    all_gather x3, waiting for transfers between devices, gather_channels(): return lax.all_gather(signal, 'chan', axis=1, tiled=True)  172 us
    all_gather x2, waiting for transfers between devices, conv_backward(): lax.all_gather(branch_grad, 'chan', axis=1, tiled=True)  117 us
    psum x1, waiting for transfers between devices, body(): lax.psum(proj_weight_grad.astype(jnp.bfloat16), 'dp').astype(jnp.float32)  116 us
    dot_general x18, matrix products, conv_backward(): jnp.einsum('bop,oc->bcp', grad_full, own_weight[tap_index], preferred_ele...  114 us
    reduce_scatter x1, waiting for transfers between devices, body(): lax.psum_scatter(normed_part, 'chan', scatter_dimension=1, tiled=True)  84.8 us
    reduce_scatter x1, waiting for transfers between devices, body(): lax.psum_scatter(mixed_part, 'chan', scatter_dimension=2, tiled=True)  78.9 us
    all_gather x2, waiting for transfers between devices, conv_backward(): lax.all_gather(conv_weight, 'chan', axis=1, tiled=True)  72.7 us
  transfers between devices with their start and end apart: 19, of which 13 were waited for; matrix products, arithmetic and copies ran while one was open for 20% of the time, Pallas kernels for 0%

commit v1 on v0

v1 whole, which is shorter than its diff:
```python
import functools
import itertools

import jax
import jax.numpy as jnp
import numpy as np
from jax import lax
from jax.experimental import pallas as pl
from jax.experimental.pallas import tpu as pltpu
from jax.sharding import PartitionSpec as P

CH = 512
GROUPS = 32
CROPS = 16
TILE = 8
BANDS = 4
EPS = 1e-06
F32 = jnp.float32
BF16 = jnp.bfloat16
HIGH = lax.Precision.HIGHEST
NN = (((1,), (0,)), ((), ()))
NT = (((1,), (1,)), ((), ()))
TN = (((0,), (0,)), ((), ()))
VMEM = pltpu.VMEM
ANY = pl.ANY
SCALE = CH ** (-0.5)


def band_layouts(units):
    return [
        tuple(np.diff((0,) + cuts + (units,)))
        for cuts in itertools.combinations(range(1, units), BANDS - 1)
    ]


@functools.lru_cache(maxsize=None)
def owner_tables(devices, units, slots):
    layouts = band_layouts(units)
    rank = np.zeros(1 << (units - 1), np.int32)
    for number, sizes in enumerate(layouts):
        cuts = np.cumsum(sizes)[:-1]
        rank[sum(1 << (int(c) - 1) for c in cuts)] = number
    sizes = np.array(
        [[r * c for r in rows for c in cols] for rows in layouts for cols in layouts], np.int32
    )
    owners = np.zeros(sizes.shape, np.int32)
    if devices == 2:
        masks = np.arange(1 << (CROPS - 1), dtype=np.int32)
        bits = ((masks[None, :] >> np.arange(CROPS)[:, None]) & 1).astype(np.float32)
        for at, row in enumerate(sizes.astype(np.float32)):
            filled = row @ bits
            squares = (row * row) @ bits
            cost = np.abs(squares - (row * row).sum() / 2) + 1e6 * np.abs(filled - slots)
            owners[at] = bits[:, int(np.argmin(cost))].astype(np.int32)
    else:
        for at, row in enumerate(sizes):
            loads = [0] * devices
            for crop in sorted(range(CROPS), key=lambda c: -row[c]):
                device = loads.index(min(loads))
                owners[at, crop] = device
                loads[device] += int(row[crop])
    for device in range(devices):
        assert (np.where(owners == device, sizes, 0).sum(axis=1) <= slots).all()
    return rank, owners


def packed_tables(devices, units, slots):
    rank, owners = owner_tables(devices, units, slots)
    shifts = np.arange(0, 32, 4, dtype=np.int64)
    words = (owners.reshape(-1, 2, 8).astype(np.int64) << shifts).sum(axis=2)
    words = np.where(words >= 1 << 31, words - (1 << 32), words)
    return np.concatenate([rank, words.reshape(-1).astype(np.int32)])


WINDOWS = (8, 16, 24, 32)


def write_plan(devices, slots, ids, table, slot_tile, slot_crop, starts, ends):
    units = ids.shape[0] // TILE
    count = units * units
    layouts = len(band_layouts(units))

    def code(at):
        bits = 0
        for step in range(units - 1):
            bits = bits + jnp.where(at(step) != at(step + 1), 1 << step, 0)
        return table[bits]

    def row_id(step):
        return ids[TILE * step, 0]

    def col_id(step):
        return ids[0, TILE * step]

    layout = code(row_id) * layouts + code(col_id)
    words = [table[(1 << (units - 1)) + 2 * layout + half] for half in range(2)]
    heights, widths = [], []
    for band in range(BANDS):
        heights.append(sum(jnp.where(row_id(k) // BANDS == band, 1, 0) for k in range(units)))
        widths.append(sum(jnp.where(col_id(k) % BANDS == band, 1, 0) for k in range(units)))
    if devices * slots > count:

        def clear(at, carry):
            slot_tile[at] = -1
            slot_crop[at] = -1
            return carry

        lax.fori_loop(0, devices * slots, clear, 0)
    filled = [jnp.int32(device * slots) for device in range(devices)]
    for crop in range(CROPS):
        owner = lax.shift_right_logical(words[crop // 8], jnp.int32(4 * (crop % 8))) & 15
        size = heights[crop // BANDS] * widths[crop % BANDS]
        start = filled[0]
        for device in range(1, devices):
            start = jnp.where(owner == device, filled[device], start)
        starts[crop] = start
        ends[crop] = start
        for device in range(devices):
            filled[device] = filled[device] + jnp.where(owner == device, size, 0)

    def place(row, carry):
        for col in range(units):
            crop = ids[row * TILE, col * TILE]
            at = ends[crop]
            slot_tile[at] = row * units + col
            slot_crop[at] = crop
            ends[crop] = at + 1
        return carry

    lax.fori_loop(0, units, place, 0)


class Plan:
    def __init__(self, me, slot_tile, slot_crop, slots):
        self.slots = slots
        base = me * slots
        lane = lax.broadcasted_iota(jnp.int32, (1, 128), 1) % slots
        down = lax.broadcasted_iota(jnp.int32, (slots, 1), 0)
        self.tile_row, self.crop_row = jnp.zeros_like(lane), jnp.zeros_like(lane)
        self.tile_col, self.crop_col = jnp.zeros_like(down), jnp.zeros_like(down)
        for slot in range(slots):
            tile, crop = slot_tile[base + slot], slot_crop[base + slot]
            self.tile_row = jnp.where(lane == slot, tile, self.tile_row)
            self.crop_row = jnp.where(lane == slot, crop, self.crop_row)
            self.tile_col = jnp.where(down == slot, tile, self.tile_col)
            self.crop_col = jnp.where(down == slot, crop, self.crop_col)
        self.same = (self.crop_col == self.crop_row[:, 0:slots]).astype(F32)


def place_of(position):
    return position[0], position[1], position[2], position[3]


def group_total(value):
    width = CH // GROUPS
    lane = lax.broadcasted_iota(jnp.int32, (value.shape[0], 128), 1)
    parts = []
    for at in range(0, CH, 128):
        part = value[:, at : at + 128]
        step = 1
        while step < width:
            up = pltpu.roll(part, 128 - step, 1)
            down = pltpu.roll(part, step, 1)
            part = part + jnp.where((lane & step) == 0, up, down)
            step *= 2
        parts.append(part)
    return jnp.concatenate(parts, axis=1)


def crop_mean(same, value):
    count = jnp.sum(same, axis=1, keepdims=True) * float(TILE * TILE * (CH // GROUPS))
    total = lax.dot_general(same, group_total(value), NN, precision=HIGH, preferred_element_type=F32)
    return total / count


def slab_sum(pixels, slots, term):
    def step(at, total):
        return total + term(at)

    return lax.fori_loop(0, pixels, step, jnp.zeros((slots, CH), F32), unroll=8)


def stats_slabs(ref, same):
    pixels, slots, _ = ref.shape
    mean = crop_mean(same, slab_sum(pixels, slots, lambda at: ref[at]))

    def square(at):
        centred = ref[at] - mean
        return centred * centred

    inverse = lax.rsqrt(crop_mean(same, slab_sum(pixels, slots, square)) + EPS)
    return mean, inverse


def fill_halo(pad, plan):
    slots = plan.slots
    wide = TILE * slots
    tile_c = jnp.concatenate([plan.tile_col] * TILE, axis=0)
    crop_c = jnp.concatenate([plan.crop_col] * TILE, axis=0)
    tile_r = jnp.concatenate([plan.tile_row] * (wide // 128), axis=1)
    crop_r = jnp.concatenate([plan.crop_row] * (wide // 128), axis=1)
    block_c = lax.broadcasted_iota(jnp.int32, (wide, wide), 0) // slots
    block_r = lax.broadcasted_iota(jnp.int32, (wide, wide), 1) // slots
    linked = (crop_c == crop_r) & (tile_c >= 0)

    def near(row_step, col_step):
        return linked & (tile_r == tile_c + (TILE * row_step + col_step))

    def edge(row_step, col_step, source):
        pick = (near(row_step, col_step) & (block_c == block_r)).astype(F32).astype(BF16)
        moved = jnp.dot(pick, source.reshape(wide, CH), preferred_element_type=F32).astype(BF16)
        return moved.reshape(TILE, slots, CH)

    def corner(row_step, col_step, source):
        pick = near(row_step, col_step)[0:slots, 0:slots].astype(F32).astype(BF16)
        return jnp.dot(pick, source, preferred_element_type=F32).astype(BF16)

    low, high, end = 1, TILE, TILE + 1
    pad[0, low:end] = edge(-1, 0, pad[high, low:end])
    pad[end, low:end] = edge(1, 0, pad[low, low:end])
    pad[low:end, 0] = edge(0, -1, pad[low:end, high])
    pad[low:end, end] = edge(0, 1, pad[low:end, low])
    pad[0, 0] = corner(-1, -1, pad[high, high])
    pad[0, end] = corner(-1, 1, pad[high, low])
    pad[end, 0] = corner(1, -1, pad[low, high])
    pad[end, end] = corner(1, 1, pad[low, low])


class WeightLoad:
    def __init__(self, position, pieces, target, sem):
        self.copies = []
        if len(pieces) == 1:
            self.copies.append(pltpu.make_async_copy(pieces[0], target, sem.at[0]))
        else:
            me = position[0]
            half = pieces[0].shape[1]
            width = pieces[1].shape[1]
            mine = position[1] if len(pieces) == 9 else position[2]
            spots = [me * half]
            for at in range(len(pieces) - 1):
                spots.append((1 - me) * half + (mine ^ at) * width)
            for at, (piece, spot) in enumerate(zip(pieces, spots)):
                rows = pl.ds(pl.multiple_of(spot, width), piece.shape[1])
                self.copies.append(
                    pltpu.make_async_copy(piece, target.at[:, rows, :], sem.at[at])
                )

    def start(self):
        for copy in self.copies:
            copy.start()

    def wait(self):
        for copy in self.copies:
            copy.wait()


def weight_sems(pieces):
    return pltpu.SemaphoreType.DMA((len(pieces),))


def store_grad(grad, outs, work, position, number):
    if len(outs) == 1:
        outs[0][number] = grad.astype(BF16)
    else:
        work[...] = grad
        mine = position[3]
        width = CH // 16
        for at in range(16):
            rows = pl.ds(pl.multiple_of((mine ^ at) * width, width), width)
            part = work[rows, :].astype(BF16)
            core, spot = (at // 4) % 2, (at // 8) * 4 + at % 4
            outs[core][number, spot * width : (spot + 1) * width, :] = part


def grad_shapes(count, paired):
    if paired:
        return [shape((count, CH // 2, CH), BF16)] * 2
    return [shape((count, CH, CH), BF16)]


def conv_rows(pad, weight, row, slots, dims, flipped, count=1):
    total = None
    for tap in range(9):
        down, right = tap // 3, tap % 3
        if flipped:
            down, right = 2 - down, 2 - right
        left = pad[pl.ds(row + down, count), right : right + TILE].reshape(count * TILE * slots, CH)
        part = lax.dot_general(left, weight[tap], dims, preferred_element_type=F32)
        total = part if total is None else total + part
    return total


def load_full(parts, me, dtype, store):
    if len(parts) == 1:
        store(slice(None), parts[0][...].astype(dtype))
    else:
        local = parts[0].shape[-1]
        own = pl.ds(pl.multiple_of(me * local, local), local)
        other = pl.ds(pl.multiple_of((1 - me) * local, local), local)
        store(own, parts[0][...].astype(dtype))
        store(other, parts[1][...].astype(dtype))


def vmem(shape, dtype):
    return pltpu.VMEM(shape, dtype)


def specs(kinds):
    table = {
        "v": pl.BlockSpec(memory_space=pltpu.VMEM),
        "s": pl.BlockSpec(memory_space=pltpu.SMEM),
        "h": pl.BlockSpec(memory_space=pl.ANY),
    }
    return [table[k] for k in kinds]


def call(body, ins, outs, shapes, scratch, name, flops, moved):
    return pl.pallas_call(
        body,
        in_specs=specs(ins),
        out_specs=tuple(specs(outs)),
        out_shape=tuple(shapes),
        scratch_shapes=list(scratch),
        compiler_params=pltpu.CompilerParams(vmem_limit_bytes=60 << 20),
        cost_estimate=pl.CostEstimate(
            flops=int(flops), bytes_accessed=int(moved), transcendentals=0
        ),
        name=name,
    )


def shape(dims, dtype):
    return jax.ShapeDtypeStruct(dims, dtype)


def pack_first_kernel(devices, slots, position, ids, table, signal, *rest):
    plan, rest = rest[:4], rest[4:]
    write_plan(devices, slots, ids, table, *plan)
    pack_kernel(True, slots, position, plan[0], signal, *rest)


def pack_kernel(by_pixel, slots, position, slot_tile, signal, *rest):
    outs, (raster, stage) = rest[:-2], rest[-2:]
    local, pixels = signal.shape
    side = int(pixels**0.5)
    chunk = 512
    cols = local // 128
    for at in range(0, pixels, chunk):
        flipped = signal[:, at : at + chunk].astype(F32).T
        for col in range(cols):
            raster[col, at : at + chunk, :] = flipped[:, col * 128 : (col + 1) * 128]
    for number, out in enumerate(outs):

        def step(slot, carry):
            tile = slot_tile[pack_base(position, number, len(outs), slots) + slot]
            keep = tile >= 0
            tile = jnp.maximum(tile, 0)
            start = (tile // TILE) * (TILE * side) + (tile % TILE) * TILE
            for row in range(TILE):
                for col in range(cols):
                    value = raster[col, pl.ds(pl.multiple_of(start + row * side, TILE), TILE), :]
                    value = jnp.where(keep, value, 0.0)
                    if by_pixel:
                        stage[col, pl.ds(row * TILE * slots + slot, TILE, stride=slots), :] = value
                    else:
                        at = pl.multiple_of(slot * (TILE * TILE) + row * TILE, TILE)
                        stage[col, pl.ds(at, TILE), :] = value
            return carry

        lax.fori_loop(0, slots, step, 0)
        for at in range(0, stage.shape[1], chunk):
            for col in range(cols):
                span = slice(col * 128, (col + 1) * 128)
                out[at : at + chunk, span] = stage[col, at : at + chunk, :].astype(BF16)


def pack_base(position, number, devices, slots):
    return (position[0] ^ number if devices == 2 else number) * slots


def pack_first(position, ids, signal, devices, slots, name):
    local, pixels = signal.shape
    rows = slots * TILE * TILE
    table = jnp.asarray(packed_tables(devices, ids.shape[0] // TILE, slots))
    result = call(
        functools.partial(pack_first_kernel, devices, slots),
        "sssv",
        "ssss" + "v" * devices,
        [shape((devices * slots,), jnp.int32)] * 2
        + [shape((CROPS,), jnp.int32)] * 2
        + [shape((rows, local), BF16)] * devices,
        [vmem((local // 128, pixels, 128), F32), vmem((local // 128, rows, 128), F32)],
        name,
        4 << 30,
        6 << 20,
    )(position, ids, table, signal)
    return result[:4], result[4:]


def pack(position, slot_tile, signal, by_pixel, devices, slots, name):
    local, pixels = signal.shape
    rows = slots * TILE * TILE
    return call(
        functools.partial(pack_kernel, by_pixel, slots),
        "ssv",
        "v" * devices,
        [shape((rows, local), BF16)] * devices,
        [vmem((local // 128, pixels, 128), F32), vmem((local // 128, rows, 128), F32)],
        name,
        4 << 30,
        6 << 20,
    )(position, slot_tile, signal)


def unpack_kernel(by_pixel, slots, position, slot_tile, *rest):
    ins, out, (raster, stage) = rest[:-3], rest[-3], rest[-2:]
    local, pixels = out.shape
    side = int(pixels**0.5)
    chunk = 512
    cols = local // 128
    for number, part in enumerate(ins):
        for at in range(0, stage.shape[1], chunk):
            for col in range(cols):
                span = slice(col * 128, (col + 1) * 128)
                stage[col, at : at + chunk, :] = part[at : at + chunk, span].astype(F32)

        def step(slot, carry):
            tile = slot_tile[pack_base(position, number, len(ins), slots) + slot]

            @pl.when(tile >= 0)
            def _():
                start = (tile // TILE) * (TILE * side) + (tile % TILE) * TILE
                for row in range(TILE):
                    to = pl.ds(pl.multiple_of(start + row * side, TILE), TILE)
                    for col in range(cols):
                        if by_pixel:
                            at = pl.ds(row * TILE * slots + slot, TILE, stride=slots)
                        else:
                            first = pl.multiple_of(slot * (TILE * TILE) + row * TILE, TILE)
                            at = pl.ds(first, TILE)
                        raster[col, to, :] = stage[col, at, :]

            return carry

        lax.fori_loop(0, slots, step, 0)
    for at in range(0, pixels, chunk):
        for col in range(cols):
            span = slice(col * 128, (col + 1) * 128)
            out[span, at : at + chunk] = raster[col, at : at + chunk, :].T.astype(out.dtype)


def unpack(position, slot_tile, parts, pixels, by_pixel, dtype, slots, name):
    rows, local = parts[0].shape
    return call(
        functools.partial(unpack_kernel, by_pixel, slots),
        "ss" + "v" * len(parts),
        "v",
        [shape((local, pixels), dtype)],
        [vmem((local // 128, pixels, 128), F32), vmem((local // 128, rows, 128), F32)],
        name,
        4 << 30,
        8 << 20,
    )(position, slot_tile, *parts)[0]


(G1, B1, C1, G2, B2, C2, G3, B3, QB, VB, PB) = range(11)


def norm_swish_pad(source, mean, inverse, gain, bias, pad, slots):
    scaled = inverse * gain

    def step(row, carry):
        for col in range(TILE):
            before = (source[row * TILE + col] - mean) * scaled + bias
            pad[row + 1, col + 1] = (before * jax.nn.sigmoid(before)).astype(BF16)
        return carry

    lax.fori_loop(0, TILE, step, 0)


def first_kernel(parts, count, position, slot_tile, slot_crop, *rest):
    feature_parts, rest = rest[:parts], rest[parts:]
    par_parts, rest = rest[:parts], rest[parts:]
    pieces, rest = rest[:count], rest[count:]
    (par, feats_hbm, pad1_hbm, hidden_hbm, pad2_hbm, stats1, stats2) = rest[:7]
    feats, wide, hidden, pad1, pad2, weight, weight_sem, sem = rest[7:]
    pixels, slots, _ = wide.shape
    load_weight = WeightLoad(position, pieces, weight, weight_sem)
    load_weight.start()

    def put_par(columns, value):
        par[:, columns] = value

    load_full(par_parts, position[0], F32, put_par)

    def put(columns, value):
        feats[:, columns] = value

    load_full(feature_parts, position[0], BF16, put)
    save_feats = pltpu.make_async_copy(feats, feats_hbm, sem.at[1])
    save_feats.start()

    def widen(at, carry):
        wide[at] = feats[pl.ds(pl.multiple_of(at * slots, slots), slots), :].astype(F32)
        return carry

    lax.fori_loop(0, pixels, widen, 0, unroll=4)
    plan = Plan(position[0], slot_tile, slot_crop, slots)
    mean, inverse = stats_slabs(wide, plan.same)
    stats1[0], stats1[1] = mean, inverse
    norm_swish_pad(
        wide, mean, inverse, par[G1 : G1 + 1, :], par[B1 : B1 + 1, :], pad1, slots
    )
    fill_halo(pad1, plan)
    save_pad1 = pltpu.make_async_copy(pad1, pad1_hbm, sem.at[2])
    save_pad1.start()
    load_weight.wait()

    def step(row, carry):
        total = conv_rows(pad1, weight, row, slots, NT, False) + par[C1 : C1 + 1, :]
        hidden[pl.ds(row * TILE, TILE)] = total.reshape(TILE, slots, CH)
        return carry

    lax.fori_loop(0, TILE, step, 0)
    save_hidden = pltpu.make_async_copy(hidden, hidden_hbm, sem.at[3])
    save_hidden.start()
    mean, inverse = stats_slabs(hidden, plan.same)
    stats2[0], stats2[1] = mean, inverse
    norm_swish_pad(
        hidden, mean, inverse, par[G2 : G2 + 1, :], par[B2 : B2 + 1, :], pad2, slots
    )
    fill_halo(pad2, plan)
    save_pad2 = pltpu.make_async_copy(pad2, pad2_hbm, sem.at[4])
    save_pad2.start()
    save_feats.wait()
    save_pad1.wait()
    save_hidden.wait()
    save_pad2.wait()


def first(position, tables, par_parts, parts, weight, slots):
    pixels = TILE * TILE
    rows = pixels * slots
    pad = (TILE + 2, TILE + 2, slots, CH)
    return call(
        functools.partial(first_kernel, len(parts), len(weight)),
        "sss" + "v" * len(parts) + "v" * len(parts) + "h" * len(weight),
        "vhhhhvv",
        [
            shape((16, CH), F32),
            shape((rows, CH), BF16),
            shape(pad, BF16),
            shape((pixels, slots, CH), F32),
            shape(pad, BF16),
            shape((2, slots, CH), F32),
            shape((2, slots, CH), F32),
        ],
        [
            vmem((rows, CH), BF16),
            vmem((pixels, slots, CH), F32),
            vmem((pixels, slots, CH), F32),
            vmem(pad, BF16),
            vmem(pad, BF16),
            vmem((9, CH, CH), BF16),
            weight_sems(weight),
            pltpu.SemaphoreType.DMA((5,)),
        ],
        "conv1_forward",
        2 * rows * CH * CH * 9,
        20 << 20,
    )(position, *tables[:2], *parts, *par_parts, *weight)


def second_kernel(count, position, slot_tile, slot_crop, par, feats, pad_hbm, *rest):
    pieces, rest = rest[:count], rest[count:]
    resid_hbm, normed_hbm, stats3 = rest[:3]
    resid, resid_tile, normed, pad, weight, rows_scr, weight_sem, sem = rest[3:]
    slots = pad.shape[2]
    pixels = TILE * TILE
    load_pad = pltpu.make_async_copy(pad_hbm, pad, sem.at[0])
    load_weight = WeightLoad(position, pieces, weight, weight_sem)
    load_pad.start()
    load_weight.start()
    plan = Plan(position[0], slot_tile, slot_crop, slots)
    same = plan.same
    load_pad.wait()
    load_weight.wait()
    wide = TILE * slots

    def step(row, carry):
        at = pl.ds(pl.multiple_of(row * wide, wide), wide)
        total = conv_rows(pad, weight, row, slots, NT, False) + par[C2 : C2 + 1, :]
        total = total + feats[at, :].astype(F32)
        for col in range(CH // 128):
            resid[col, at, :] = total[:, col * 128 : (col + 1) * 128]
        return carry

    lax.fori_loop(0, TILE, step, 0)

    def slab(at):
        span = pl.ds(pl.multiple_of(at * slots, slots), slots)
        return jnp.concatenate([resid[col, span, :] for col in range(CH // 128)], axis=1)

    mean = crop_mean(same, slab_sum(pixels, slots, slab))

    def square(at):
        centred = slab(at) - mean
        return centred * centred

    inverse = lax.rsqrt(crop_mean(same, slab_sum(pixels, slots, square)) + EPS)
    stats3[0], stats3[1] = mean, inverse
    rows_scr[0], rows_scr[1] = mean, inverse * par[G3 : G3 + 1, :]
    bias = par[B3 : B3 + 1, :]

    def tile_step(slot, carry):
        value = jnp.concatenate(
            [resid[col, pl.ds(slot, pixels, stride=slots), :] for col in range(CH // 128)],
            axis=1,
        )
        at = pl.ds(pl.multiple_of(slot * pixels, pixels), pixels)
        resid_tile[at, :] = value
        row = pl.ds(slot, 1)
        normed[at, :] = ((value - rows_scr[0, row]) * rows_scr[1, row] + bias).astype(BF16)
        return carry

    lax.fori_loop(0, slots, tile_step, 0)
    save_resid = pltpu.make_async_copy(resid_tile, resid_hbm, sem.at[2])
    save_normed = pltpu.make_async_copy(normed, normed_hbm, sem.at[3])
    save_resid.start()
    save_normed.start()
    save_resid.wait()
    save_normed.wait()


def second(position, tables, par, feats, pad, weight, slots):
    pixels = TILE * TILE
    rows = pixels * slots
    return call(
        functools.partial(second_kernel, len(weight)),
        "sssvvh" + "h" * len(weight),
        "hhv",
        [shape((rows, CH), F32), shape((rows, CH), BF16), shape((2, slots, CH), F32)],
        [
            vmem((CH // 128, rows, 128), F32),
            vmem((rows, CH), F32),
            vmem((rows, CH), BF16),
            vmem(pad.shape, BF16),
            vmem((9, CH, CH), BF16),
            vmem((2, slots, CH), F32),
            weight_sems(weight),
            pltpu.SemaphoreType.DMA((4,)),
        ],
        "conv2_forward",
        2 * rows * CH * CH * 9,
        16 << 20,
    )(position, *tables[:2], par, feats, pad, *weight)


def attention_kernel(parts, outs, count, position, slot_tile, slot_crop, starts, ends, *rest):
    par, normed, resid, stats3 = rest[:4]
    tangent_parts, rest = rest[4 : 4 + parts], rest[4 + parts :]
    pieces, rest = rest[:count], rest[count:]
    out_parts, rest = rest[:outs], rest[outs:]
    grad_outs, rest = rest[:outs], rest[outs:]
    vecs, resid_grad, pad = rest[:3]
    (tangent, query, key, value, mixed_grad, mixed, query_grad, key_grad, value_grad) = rest[3:12]
    normed_grad, by_tile, rows_scr, weight, key_crop, work, weight_sem = rest[12:]
    load_weight = WeightLoad(position, pieces, weight, weight_sem)
    load_weight.start()
    wq, wk, wv, wp = (weight.at[k] for k in range(4))
    rows = normed.shape[0]
    pixels = TILE * TILE
    slots = rows // pixels
    me = position[0]
    base = me * slots
    block = 256
    per_block = block // pixels
    plan = Plan(me, slot_tile, slot_crop, slots)
    lane_slot = lax.broadcasted_iota(jnp.int32, (1, rows), 1) // pixels
    crops = jnp.zeros((1, rows), jnp.int32)
    for slot in range(slots):
        crops = jnp.where(lane_slot == slot, slot_crop[base + slot], crops)
    key_crop[...] = crops

    def put(columns, part):
        tangent[:, columns] = part

    load_full(tangent_parts, me, BF16, put)
    load_weight.wait()

    def project(at, carry):
        span = pl.ds(pl.multiple_of(at * block, block), block)
        left = normed[span, :]
        total = lax.dot_general(left, wq[...], NT, preferred_element_type=F32)
        query[span, :] = (total + par[QB : QB + 1, :]).astype(BF16)
        key[span, :] = lax.dot_general(left, wk[...], NT, preferred_element_type=F32).astype(BF16)
        total = lax.dot_general(left, wv[...], NT, preferred_element_type=F32)
        value[span, :] = (total + par[VB : VB + 1, :]).astype(BF16)
        mixed_grad[span, :] = jnp.dot(
            tangent[span, :], wp[...], preferred_element_type=F32
        ).astype(BF16)
        key_grad[span, :] = jnp.zeros((block, CH), F32)
        value_grad[span, :] = jnp.zeros((block, CH), F32)
        return carry

    lax.fori_loop(0, rows // block, project, 0)

    def attend(at, begin, width):
        span = pl.ds(pl.multiple_of(at * block, block), block)
        keys = pl.ds(pl.multiple_of(begin, 128), width)
        q, g = query[span, :], mixed_grad[span, :]
        scores = lax.dot_general(q, key[keys, :], NT, preferred_element_type=F32) * SCALE
        down = lax.broadcasted_iota(jnp.int32, (block, 1), 0) // pixels
        own_crop = jnp.zeros((block, 1), jnp.int32)
        for slot in range(per_block):
            own_crop = jnp.where(down == slot, slot_crop[base + at * per_block + slot], own_crop)
        scores = jnp.where(own_crop == key_crop[:, keys], scores, -1e30)
        top = jnp.max(scores, axis=1, keepdims=True)
        exponent = jnp.exp(scores - top)
        total = jnp.sum(exponent, axis=1, keepdims=True)
        prob = exponent * (1.0 / total)
        rounded = prob.astype(BF16)
        mixed[span, :] = jnp.dot(
            rounded, value[keys, :], preferred_element_type=F32
        ).astype(BF16)
        prob_grad = lax.dot_general(g, value[keys, :], NT, preferred_element_type=F32)
        inner = jnp.sum(prob * prob_grad, axis=1, keepdims=True)
        score_grad = (prob * (prob_grad - inner)).astype(BF16)
        query_grad[span, :] = (
            jnp.dot(score_grad, key[keys, :], preferred_element_type=F32) * SCALE
        ).astype(BF16)
        key_grad[keys, :] += lax.dot_general(score_grad, q, TN, preferred_element_type=F32)
        value_grad[keys, :] += lax.dot_general(rounded, g, TN, preferred_element_type=F32)

    def attend_step(at, carry):
        low_crop = slot_crop[base + at * per_block]
        high_crop = slot_crop[base + at * per_block + per_block - 1]
        low = starts[jnp.maximum(low_crop, 0)] - base
        low = jnp.where(low_crop < 0, at * per_block, low) // 2 * 2
        high = jnp.where(high_crop < 0, slots, ends[jnp.maximum(high_crop, 0)] - base)
        kind = sum(jnp.where(high - low > width, 1, 0) for width in WINDOWS[:-1])
        span = jnp.int32(WINDOWS[0])
        for number, width in enumerate(WINDOWS):
            span = jnp.where(kind == number, width, span)
        begin = jnp.minimum(low, slots - span) * pixels
        for number, width in enumerate(WINDOWS):

            @pl.when(kind == number)
            def _():
                attend(at, begin, width * pixels)

        return carry

    lax.fori_loop(0, rows // block, attend_step, 0)

    def back(at, carry):
        query_bias, value_bias, tangent_sum = carry
        span = pl.ds(pl.multiple_of(at * block, block), block)
        dq = query_grad[span, :]
        dk = (key_grad[span, :] * SCALE).astype(BF16)
        dv = value_grad[span, :].astype(BF16)
        key[span, :] = dk
        value[span, :] = dv
        total = jnp.dot(dq, wq[...], preferred_element_type=F32)
        total += jnp.dot(dk, wk[...], preferred_element_type=F32)
        total += jnp.dot(dv, wv[...], preferred_element_type=F32)
        normed_grad[span, :] = total
        result = lax.dot_general(mixed[span, :], wp[...], NT, preferred_element_type=F32)
        result = (result + par[PB : PB + 1, :] + resid[span, :]).astype(BF16)
        if outs == 1:
            out_parts[0][span, :] = result
        else:
            mixed_scr = query
            mixed_scr[span, :] = result
        query_bias += jnp.sum(dq.astype(F32), axis=0, keepdims=True)
        value_bias += jnp.sum(dv.astype(F32), axis=0, keepdims=True)
        tangent_sum += jnp.sum(tangent[span, :].astype(F32), axis=0, keepdims=True)
        return query_bias, value_bias, tangent_sum

    zero = jnp.zeros((1, CH), F32)
    query_bias, value_bias, tangent_sum = lax.fori_loop(
        0, rows // block, back, (zero, zero, zero)
    )
    if outs == 2:
        local = out_parts[0].shape[1]
        own = pl.ds(pl.multiple_of(me * local, local), local)
        other = pl.ds(pl.multiple_of((1 - me) * local, local), local)
        out_parts[0][...] = query[:, own]
        out_parts[1][...] = query[:, other]
    left = normed[...]
    for number, grad in enumerate((query_grad, key, value)):
        total = lax.dot_general(grad[...], left, TN, preferred_element_type=F32)
        store_grad(total, grad_outs, work, position, number)
    total = lax.dot_general(tangent[...], mixed[...], TN, preferred_element_type=F32)
    store_grad(total, grad_outs, work, position, 3)

    def hat_of(slot, span):
        row = pl.ds(slot, 1)
        return (resid[span, :] - stats3[0, row]) * stats3[1, row]

    def sums(slot, carry):
        span = pl.ds(pl.multiple_of(slot * pixels, pixels), pixels)
        upstream = normed_grad[span, :]
        row = pl.ds(slot, 1)
        rows_scr[0, row] = jnp.sum(upstream, axis=0, keepdims=True)
        rows_scr[1, row] = jnp.sum(upstream * hat_of(slot, span), axis=0, keepdims=True)
        return carry

    lax.fori_loop(0, slots, sums, 0)
    same = plan.same
    gain = par[G3 : G3 + 1, :]
    plain, crossed = rows_scr[0], rows_scr[1]
    vecs[...] = jnp.zeros_like(vecs)
    vecs[G3 : G3 + 1, :] = jnp.sum(crossed, axis=0, keepdims=True)
    vecs[B3 : B3 + 1, :] = jnp.sum(plain, axis=0, keepdims=True)
    vecs[QB : QB + 1, :] = query_bias
    vecs[VB : VB + 1, :] = value_bias
    vecs[PB : PB + 1, :] = tangent_sum
    rows_scr[0] = crop_mean(same, plain * gain)
    rows_scr[1] = crop_mean(same, crossed * gain)

    def apply(slot, carry):
        span = pl.ds(pl.multiple_of(slot * pixels, pixels), pixels)
        row = pl.ds(slot, 1)
        scaled = normed_grad[span, :] * gain
        centred = scaled - rows_scr[0, row] - hat_of(slot, span) * rows_scr[1, row]
        result = tangent[span, :].astype(F32) + stats3[1, row] * centred
        for col in range(CH // 128):
            by_tile[col, span, :] = result[:, col * 128 : (col + 1) * 128]
        return carry

    lax.fori_loop(0, slots, apply, 0)

    def spread(row, carry):
        total = carry
        for col in range(TILE):
            at = row * TILE + col
            slab = jnp.concatenate(
                [
                    by_tile[c, pl.ds(at, slots, stride=pixels), :] for c in range(CH // 128)
                ],
                axis=1,
            )
            resid_grad[at] = slab
            rounded = slab.astype(BF16)
            pad[row + 1, col + 1] = rounded
            total += jnp.sum(rounded.astype(F32), axis=0, keepdims=True)
        return total

    vecs[C2 : C2 + 1, :] = lax.fori_loop(0, TILE, spread, zero)
    fill_halo(pad, plan)


def attention(position, tables, par, normed, resid, stats3, tangent_parts, weight, slots):
    pixels = TILE * TILE
    rows = pixels * slots
    parts = len(tangent_parts)
    pad = (TILE + 2, TILE + 2, slots, CH)
    if parts == 2:
        out_shapes = [shape((rows, CH // 2), BF16)] * 2
    else:
        out_shapes = [shape((rows, CH), BF16)]
    outs = len(out_shapes)
    result = call(
        functools.partial(attention_kernel, parts, outs, len(weight)),
        "sssss" + "v" * (4 + parts) + "h" * len(weight),
        "v" * (2 * outs + 3),
        out_shapes
        + grad_shapes(4, outs == 2)
        + [shape((16, CH), F32), shape((pixels, slots, CH), F32), shape(pad, BF16)],
        [vmem((rows, CH), BF16)] * 7
        + [vmem((rows, CH), F32)] * 3
        + [vmem((CH // 128, rows, 128), F32), vmem((2, slots, CH), F32)]
        + [vmem((4, CH, CH), BF16), vmem((1, rows), jnp.int32), vmem((CH, CH), F32)]
        + [weight_sems(weight)],
        "attention",
        30 << 30,
        24 << 20,
    )(
        position,
        *tables,
        par,
        normed,
        resid,
        stats3,
        *tangent_parts,
        *weight,
    )
    return result[:outs], result[outs : 2 * outs], result[2 * outs :]


def weight_grad_kernel(outs, begin, position, active, grad, *rest):
    out_parts, (flipped, work) = rest[:outs], rest[outs:]
    slots = active.shape[2]
    wide = TILE * slots
    for row in range(TILE):
        left = grad[row + 1, 1 : TILE + 1].reshape(wide, CH)
        flipped[:, row * wide : (row + 1) * wide] = left.T

    def step(number, carry):
        tap = begin + number
        right = active[pl.ds(tap // 3, TILE), pl.ds(tap % 3, TILE)].reshape(TILE * wide, CH)
        total = jnp.dot(flipped[...], right, preferred_element_type=F32)
        store_grad(total, out_parts, work, position, number)
        return carry

    lax.fori_loop(0, out_parts[0].shape[0], step, 0)


def weight_grad(position, active, grad, paired, slots, name, begin=0, count=9):
    rows = TILE * TILE * slots
    shapes = grad_shapes(count, paired)
    return call(
        functools.partial(weight_grad_kernel, len(shapes), begin),
        "svv",
        "v" * len(shapes),
        shapes,
        [vmem((CH, rows), BF16), vmem((CH, CH), F32)],
        name,
        2 * rows * CH * CH * count,
        12 << 20,
    )(position, active, grad)


def swish_back(upstream, before):
    gate = jax.nn.sigmoid(before)
    return upstream * (gate + before * gate * (1.0 - gate))


def norm_back_sums(source, upstream, mean, inverse, gain, bias, slots):
    def step(at, carry):
        plain, crossed = carry
        hat = (source(at) - mean) * inverse
        grad = swish_back(upstream[at], hat * gain + bias)
        upstream[at] = grad
        return plain + grad, crossed + grad * hat

    zero = jnp.zeros((slots, CH), F32)
    return lax.fori_loop(0, TILE * TILE, step, (zero, zero), unroll=2)


def middle_kernel(count, position, slot_tile, slot_crop, par, stats2, pad_hbm, hidden_hbm, *rest):
    pieces, rest = rest[:count], rest[count:]
    pad_out_hbm, vecs = rest[:2]
    pad, weight, hidden, upstream, pad_out, weight_sem, sem = rest[2:]
    slots = pad.shape[2]
    load_pad = pltpu.make_async_copy(pad_hbm, pad, sem.at[0])
    load_weight = WeightLoad(position, pieces, weight, weight_sem)
    load_hidden = pltpu.make_async_copy(hidden_hbm, hidden, sem.at[2])
    load_pad.start()
    load_weight.start()
    load_hidden.start()
    plan = Plan(position[0], slot_tile, slot_crop, slots)
    same = plan.same
    load_pad.wait()
    load_weight.wait()

    def step(row, carry):
        total = conv_rows(pad, weight, row, slots, NN, True)
        upstream[pl.ds(row * TILE, TILE)] = total.reshape(TILE, slots, CH)
        return carry

    lax.fori_loop(0, TILE, step, 0)
    load_hidden.wait()
    mean, inverse = stats2[0], stats2[1]
    gain, bias = par[G2 : G2 + 1, :], par[B2 : B2 + 1, :]
    plain, crossed = norm_back_sums(
        lambda at: hidden[at], upstream, mean, inverse, gain, bias, slots
    )
    vecs[...] = jnp.zeros_like(vecs)
    vecs[G2 : G2 + 1, :] = jnp.sum(crossed, axis=0, keepdims=True)
    vecs[B2 : B2 + 1, :] = jnp.sum(plain, axis=0, keepdims=True)
    plain = crop_mean(same, plain * gain)
    crossed = crop_mean(same, crossed * gain)

    def apply(row, carry):
        total = carry
        for col in range(TILE):
            at = row * TILE + col
            hat = (hidden[at] - mean) * inverse
            grad = inverse * (upstream[at] * gain - plain - hat * crossed)
            rounded = grad.astype(BF16)
            pad_out[row + 1, col + 1] = rounded
            total += rounded.astype(F32)
        return total

    total = lax.fori_loop(0, TILE, apply, jnp.zeros((slots, CH), F32))
    vecs[C1 : C1 + 1, :] = jnp.sum(total, axis=0, keepdims=True)
    fill_halo(pad_out, plan)
    save = pltpu.make_async_copy(pad_out, pad_out_hbm, sem.at[3])
    save.start()
    save.wait()


def middle(position, tables, par, stats2, pad, weight, hidden, slots):
    pixels = TILE * TILE
    rows = pixels * slots
    return call(
        functools.partial(middle_kernel, len(weight)),
        "sssvvhh" + "h" * len(weight),
        "hv",
        [shape(pad.shape, BF16), shape((16, CH), F32)],
        [
            vmem(pad.shape, BF16),
            vmem((9, CH, CH), BF16),
            vmem((pixels, slots, CH), F32),
            vmem((pixels, slots, CH), F32),
            vmem(pad.shape, BF16),
            weight_sems(weight),
            pltpu.SemaphoreType.DMA((4,)),
        ],
        "conv2_input_grad",
        2 * rows * CH * CH * 9,
        16 << 20,
    )(position, *tables[:2], par, stats2, pad, hidden, *weight)


def last_kernel(
    outs, count, position, slot_tile, slot_crop, par, stats1, feats, pad_hbm, resid_hbm, *rest
):
    pieces, rest = rest[:count], rest[count:]
    out_parts, (vecs, pad, weight, resid, upstream, weight_sem, sem) = rest[:outs], rest[outs:]
    slots = pad.shape[2]
    pixels = TILE * TILE
    me = position[0]
    load_pad = pltpu.make_async_copy(pad_hbm, pad, sem.at[0])
    load_weight = WeightLoad(position, pieces, weight, weight_sem)
    load_resid = pltpu.make_async_copy(resid_hbm, resid, sem.at[2])
    load_pad.start()
    load_weight.start()
    load_resid.start()
    plan = Plan(me, slot_tile, slot_crop, slots)
    same = plan.same
    load_pad.wait()
    load_weight.wait()

    def step(row, carry):
        total = conv_rows(pad, weight, row, slots, NN, True)
        upstream[pl.ds(row * TILE, TILE)] = total.reshape(TILE, slots, CH)
        return carry

    lax.fori_loop(0, TILE, step, 0)
    load_resid.wait()
    mean, inverse = stats1[0], stats1[1]
    gain, bias = par[G1 : G1 + 1, :], par[B1 : B1 + 1, :]

    def source(at):
        return feats[pl.ds(pl.multiple_of(at * slots, slots), slots), :].astype(F32)

    plain, crossed = norm_back_sums(source, upstream, mean, inverse, gain, bias, slots)
    vecs[...] = jnp.zeros_like(vecs)
    vecs[G1 : G1 + 1, :] = jnp.sum(crossed, axis=0, keepdims=True)
    vecs[B1 : B1 + 1, :] = jnp.sum(plain, axis=0, keepdims=True)
    plain = crop_mean(same, plain * gain)
    crossed = crop_mean(same, crossed * gain)

    def apply(at, carry):
        hat = (source(at) - mean) * inverse
        grad = resid[at] + inverse * (upstream[at] * gain - plain - hat * crossed)
        if outs == 1:
            span = pl.ds(pl.multiple_of(at * slots, slots), slots)
            out_parts[0][span, :] = grad.astype(BF16)
        else:
            upstream[at] = grad
        return carry

    lax.fori_loop(0, pixels, apply, 0, unroll=2)
    if outs == 2:
        local = out_parts[0].shape[1]
        own = pl.ds(pl.multiple_of(me * local, local), local)
        other = pl.ds(pl.multiple_of((1 - me) * local, local), local)
        out_parts[0][...] = upstream[:, :, own].reshape(pixels * slots, local)
        out_parts[1][...] = upstream[:, :, other].reshape(pixels * slots, local).astype(BF16)


def last(position, tables, par, stats1, feats, pad, weight, resid_grad, parts, slots):
    pixels = TILE * TILE
    rows = pixels * slots
    if parts == 2:
        out_shapes = [shape((rows, CH // 2), F32), shape((rows, CH // 2), BF16)]
    else:
        out_shapes = [shape((rows, CH), BF16)]
    outs = len(out_shapes)
    result = call(
        functools.partial(last_kernel, outs, len(weight)),
        "sssvvvhh" + "h" * len(weight),
        "v" * (outs + 1),
        out_shapes + [shape((16, CH), F32)],
        [
            vmem(pad.shape, BF16),
            vmem((9, CH, CH), BF16),
            vmem((pixels, slots, CH), F32),
            vmem((pixels, slots, CH), F32),
            weight_sems(weight),
            pltpu.SemaphoreType.DMA((3,)),
        ],
        "conv1_input_grad",
        2 * rows * CH * CH * 9,
        16 << 20,
    )(position, *tables[:2], par, stats1, feats, pad, resid_grad, *weight)
    return result[:outs], result[outs]


class Links:
    def flip(self, value, bit):
        return lax.ppermute(value, "dp", [(at, at ^ bit) for at in range(16)])

    def chan(self, value):
        return lax.ppermute(value, "chan", [(0, 1), (1, 0)])

    def core(self, value):
        return self.flip(value, 1)

    def down(self, value):
        return self.flip(value, 2)

    def near(self, value):
        return self.flip(value, 4)

    def far(self, value):
        return self.flip(value, 8)

    def spread(self, value):
        parts = [value, self.near(value), self.down(value)]
        parts.append(self.down(parts[1]))
        return parts + [self.core(part) for part in parts]

    def gather_eighths(self, weight, piece):
        width = weight.shape[1] // 8
        own = lax.dynamic_slice_in_dim(weight, piece * width, width, 1)
        return [weight] + self.spread(self.chan(own))

    def gather_halves(self, weight, core):
        width = weight.shape[1] // 2
        own = self.chan(lax.dynamic_slice_in_dim(weight, core * width, width, 1))
        return [weight, own, self.core(own)]

    def add(self, left, right):
        return (left.astype(F32) + right.astype(F32)).astype(BF16)

    def reduce(self, halves):
        count = halves[0].shape[0]
        value = self.add(halves[0], self.core(halves[1]))
        value = value.reshape(count, 2, 2, 2, CH // 16, CH)
        third = -(-count // 3)
        orders = (("chan", "down", "near"), ("down", "near", "chan"), ("near", "chan", "down"))
        done = []
        for number, order in enumerate(orders):
            part = value[number * third : (number + 1) * third]
            if part.shape[0] == 0:
                continue
            names = ["chan", "down", "near"]
            for name in order:
                at = 1 + names.index(name)
                names.remove(name)
                keep = lax.index_in_dim(part, 0, at, keepdims=False)
                send = lax.index_in_dim(part, 1, at, keepdims=False)
                part = self.add(keep, getattr(self, name)(send))
            done.append(part)
        value = jnp.concatenate(done, axis=0)
        return self.spread(self.add(value, self.far(value)))

    def total(self, value):
        for step in (self.core, self.chan, self.down, self.near, self.far):
            value = value + step(value)
        return value


def assemble_kernel(position, *rest):
    parts, out = rest[:-1], rest[-1]
    width = parts[0].shape[1]
    for at, part in enumerate(parts):
        rows = pl.ds(pl.multiple_of((position[1] ^ at) * width, width), width)
        out[:, rows, :] = part[...].astype(F32)


def assemble(position, parts, name):
    count, width, _ = parts[0].shape
    return call(
        assemble_kernel,
        "s" + "v" * len(parts),
        "v",
        [shape((count, width * len(parts), CH), F32)],
        [],
        name,
        1 << 20,
        6 << 20,
    )(position, *parts)[0]


def body(
    features,
    crop_ids,
    cotangent,
    norm1_gain,
    norm1_bias,
    conv1_weight,
    conv1_bias,
    norm2_gain,
    norm2_bias,
    conv2_weight,
    conv2_bias,
    norm3_gain,
    norm3_bias,
    query_weight,
    query_bias,
    key_weight,
    value_weight,
    value_bias,
    proj_weight,
    proj_bias,
):
    _, local, pixels = features.shape
    devices = lax.axis_size("chan")
    copies = lax.axis_size("dp")
    index = lax.axis_index("chan").astype(jnp.int32)
    tiles = pixels // (TILE * TILE)
    slots = tiles if devices == 1 else tiles // 2
    paired = devices == 2 and copies == 16
    links = Links()
    turn = lax.axis_index("dp").astype(jnp.int32)
    core, down, near = turn & 1, (turn >> 1) & 1, (turn >> 2) & 1
    piece = core * 4 + down * 2 + near
    position = jnp.stack([index, piece, core, index * 8 + piece])

    def exchange(parts):
        if paired:
            return [parts[0], links.chan(parts[1])]
        if devices == 2:
            parts = [jnp.where(index == 0, parts[k], parts[1 - k]) for k in range(2)]
        moved = lax.all_to_all(jnp.stack(parts), "chan", 0, 0)
        return [jnp.transpose(moved, (1, 0, 2)).reshape(moved.shape[1], CH)]

    def give_back(parts):
        if paired:
            return [parts[0], links.chan(parts[1])]
        whole = parts[0].reshape(parts[0].shape[0], devices, local)
        moved = lax.all_to_all(jnp.transpose(whole, (1, 0, 2)), "chan", 0, 0)
        parts = [moved[at] for at in range(devices)]
        if devices == 2:
            parts = [jnp.where(index == 0, parts[k], parts[1 - k]) for k in range(2)]
        return parts

    lanes = -(-local // 128) * 128

    def widened(signal):
        return jnp.pad(signal, ((0, lanes - local), (0, 0))) if lanes > local else signal

    def narrowed(parts):
        return [part[:, :local] for part in parts] if lanes > local else parts

    def unpack_lanes(parts, by_pixel, dtype, name):
        if lanes > local:
            parts = [jnp.pad(part, ((0, 0), (0, lanes - local))) for part in parts]
        whole = unpack(position, tables[0], parts, pixels, by_pixel, dtype, slots, name)
        return whole[:local]

    vectors = jnp.stack(
        [
            norm1_gain,
            norm1_bias,
            conv1_bias,
            norm2_gain,
            norm2_bias,
            conv2_bias,
            norm3_gain,
            norm3_bias,
            query_bias,
            value_bias,
            proj_bias,
        ]
        + [jnp.zeros_like(proj_bias)] * 5
    )
    small = jnp.stack([query_weight, key_weight, value_weight, proj_weight])
    if paired:
        weight1 = links.gather_eighths(conv1_weight, piece)
        weight2 = links.gather_eighths(conv2_weight, piece)
        par_parts = [vectors, links.chan(vectors)]
    else:
        par_parts = [lax.all_gather(vectors, "chan", axis=1, tiled=True)]
        weight1 = [lax.all_gather(conv1_weight, "chan", axis=1, tiled=True)]
        weight2 = [lax.all_gather(conv2_weight, "chan", axis=1, tiled=True)]
    tables, packed = pack_first(
        position, crop_ids[0], widened(features[0]), devices, slots, "pack_features"
    )
    feature_parts = exchange(narrowed(packed))
    packed = pack(
        position, tables[0], widened(cotangent[0]), False, devices, slots, "pack_cotangent"
    )
    packed = list(packed)
    if paired:
        small, packed[1], _ = lax.optimization_barrier((small, packed[1], feature_parts[1]))
        weight3 = links.gather_halves(small, core)
    else:
        weight3 = [lax.all_gather(small, "chan", axis=1, tiled=True)]
    tangent_parts = exchange(narrowed(packed))
    par, feats, pad1, hidden, pad2, stats1, stats2 = first(
        position, tables, par_parts, feature_parts, weight1, slots
    )
    resid, normed, stats3 = second(position, tables, par, feats, pad2, weight2, slots)
    out_parts, small_grads, (vecs3, resid_grad, grad2) = attention(
        position, tables, par, normed, resid, stats3, tangent_parts, weight3, slots
    )
    out_parts = give_back(out_parts)
    output = unpack_lanes(out_parts, False, BF16, "unpack_output")
    grads2 = weight_grad(position, pad2, grad2, paired, slots, "conv2_weight_grad")
    grad1, vecs2 = middle(position, tables, par, stats2, grad2, weight2, hidden, slots)
    grads1 = weight_grad(position, pad1, grad1, paired, slots, "conv1_weight_grad")
    in_parts, vecs1 = last(
        position, tables, par, stats1, feats, grad1, weight1, resid_grad, len(feature_parts), slots
    )
    in_parts = give_back(in_parts)
    input_grad = unpack_lanes(in_parts, True, F32, "unpack_input_grad")

    vecs = vecs1 + vecs2 + vecs3
    if paired:
        small_grads = assemble(position, links.reduce(small_grads), "small_grads")
        weight2_grad = assemble(position, links.reduce(grads2), "conv2_grads")
        weight1_grad = assemble(position, links.reduce(grads1), "conv1_grads")
        vecs = links.total(vecs)
        vecs = lax.dynamic_slice_in_dim(vecs, index * local, local, 1)
    else:

        def total(grad, axis):
            part = lax.psum_scatter(grad, "chan", scatter_dimension=axis, tiled=True)
            return lax.psum(part, "dp").astype(F32)

        small_grads, weight2_grad, weight1_grad = [
            total(g[0], 1) for g in (small_grads, grads2, grads1)
        ]
        vecs = total(vecs, 1)
    gq, gk, gv, gp = [small_grads[k] for k in range(4)]
    return (
        output[None],
        input_grad[None],
        vecs[G1],
        vecs[B1],
        weight1_grad,
        vecs[C1],
        vecs[G2],
        vecs[B2],
        weight2_grad,
        vecs[C2],
        vecs[G3],
        vecs[B3],
        gq,
        vecs[QB],
        gk,
        gv,
        vecs[VB],
        gp,
        vecs[PB],
    )


def solution(mesh):
    canvas = P("dp", "chan", None)
    vector = P("chan")
    conv = P(None, "chan", None)
    matrix = P("chan", None)
    placed = (
        (canvas, P("dp", None, None), canvas)
        + (vector, vector, conv, vector, vector, vector, conv, vector, vector, vector)
        + (matrix, vector, matrix, matrix, vector, matrix, vector)
    )
    results = (
        (canvas, canvas, vector, vector, conv, vector, vector, vector, conv, vector)
        + (vector, vector, matrix, vector, matrix, matrix, vector, matrix, vector)
    )
    return jax.shard_map(body, mesh=mesh, in_specs=placed, out_specs=results, check_vma=False)
```

time: 1850 us -> 549 us (0.30)
  waiting for transfers between devices: 742 us -> 225 us
  matrix products: 447 us -> 0 us
  local copies, waits for them, and re-layouts: 424 us -> 12.6 us
  Pallas kernels: 0 us -> 222 us
  other arithmetic: 151 us -> 4.86 us
  starting transfers between devices: 19.5 us -> 71.6 us
  blocking collectives: 33.7 us -> 0 us
    dot_general x96 -> x0, matrix products: 447 us -> none  [the longest x18 114 us: conv_backward(): jnp.einsum('bop,oc->bcp', grad_full, own_weight[tap_index], preferred_ele...]
    all_gather x10 -> x0, waiting for transfers between devices: 361 us -> none  [the longest x3 172 us: gather_channels(): return lax.all_gather(signal, 'chan', axis=1, tiled=True)]
    scatter-add x16 -> x0, local copies, waits for them, and re-layouts: 313 us -> none  [place_back(): result = result.at[:, :, start:start + pixels].add(masked)]
    ppermute x0 -> x79, waiting for transfers between devices: none -> 225 us  [the longest x62 113 us: flip(): return lax.ppermute(value, 'dp', [(at, at ^ bit) for at in range(16)])]
    pallas_call x0 -> x14, Pallas kernels: none -> 222 us  [the longest x1 50.6 us: attention(): call(functools.partial(attention_kernel, parts, outs, len(weight)), 'ssss...]
    reduce_scatter x4 -> x0, waiting for transfers between devices: 195 us -> none  [the longest x1 84.8 us: body(): lax.psum_scatter(normed_part, 'chan', scatter_dimension=1, tiled=True)]
    psum x1 -> x0, waiting for transfers between devices: 116 us -> none  [body(): lax.psum(proj_weight_grad.astype(jnp.bfloat16), 'dp').astype(jnp.float32)]
    ppermute x0 -> x79, starting transfers between devices: none -> 71.6 us  [the longest x62 53.2 us: flip(): return lax.ppermute(value, 'dp', [(at, at ^ bit) for at in range(16)])]
  transfers between devices with their start and end apart: 19 -> 79, of which waited for: 13 -> 39; matrix products, arithmetic and copies ran while one was open for 20% -> 2% of each run, Pallas kernels for 0% -> 29%
where the time goes in v1:
time: 549 us; the launch traced here: 538 us
  waiting for transfers between devices  225 us (41%)
  Pallas kernels  222 us (40%)
  starting transfers between devices  71.6 us (13%)
  local copies, waits for them, and re-layouts  12.6 us (2%)
    ppermute x62, waiting for transfers between devices, flip(): return lax.ppermute(value, 'dp', [(at, at ^ bit) for at in range(16)])  113 us
    ppermute x17, waiting for transfers between devices, chan(): return lax.ppermute(value, 'chan', [(0, 1), (1, 0)])  112 us
    ppermute x62, starting transfers between devices, flip(): return lax.ppermute(value, 'dp', [(at, at ^ bit) for at in range(16)])  53.2 us
    pallas_call x1, Pallas kernels, attention(): call(functools.partial(attention_kernel, parts, outs, len(weight)), 'ssss...  50.6 us
    pallas_call x2, Pallas kernels, weight_grad(): call(functools.partial(weight_grad_kernel, len(shapes), begin), 'svv', 'v...  35.4 us
    pallas_call x1, Pallas kernels, second(): call(functools.partial(second_kernel, len(weight)), 'sssvvh' + 'h' * len(...  26.2 us
    pallas_call x1, Pallas kernels, last(): call(functools.partial(last_kernel, outs, len(weight)), 'sssvvvhh' + 'h'...  22.9 us
    pallas_call x1, Pallas kernels, middle(): call(functools.partial(middle_kernel, len(weight)), 'sssvvhh' + 'h' * len...  22.8 us
  transfers between devices with their start and end apart: 79, of which 39 were waited for; matrix products, arithmetic and copies ran while one was open for 2% of the time, Pallas kernels for 29%

profile of v1, /device:TPU:0, one launch (start us, length us, event | category | flops | bytes accessed | tf_op | source)
XLA Modules:
  0.0 538.2 jit_solution(13636181811574884286)
XLA Ops:
  1.4 8.9 %pack_features.1 = (s32[64]{0:T(128)}, s32[64]{0:T(128)}, s32[16]{0:T(128)}, s32[16]{0:T(128)}, bf16[2048,256]{1,0:T(8,128)(2,1)}, /*index=5*/bf16[2048,256]{1,0:T(8,128)(2,1)}) custom-call(s32[4]{0:T(128)} %pad_add_fusion.position, s32[64,64]{1,0:T(8,128)} %bitcast.271, s32[2578]{0:T(1024)} %constant.31.clone.table, bf16[256,4096]{1,0:T(8,128)(2,1)} %bitcast.269), custom_call_target="tpu_custom_call" | custom-call | flops 4294967296 | bytes 6291456 | tf_op jit(solution)/shard_map/pack_features/pallas_call | solution.py:385
  10.3 3.0 collective-permute-start
  17.4 26.4 %collective-permute-done.10.rest_1_ = bf16[9,32,512]{2,1,0:T(8,128)(2,1)S(1)} collective-permute-done((bf16[9,32,512]{2,1,0:T(8,128)(2,1)S(1)}, bf16[9,32,512]{2,1,0:T(8,128)(2,1)S(1)}, u32[]{:S(2)}, u32[]{:S(2)}) %collective-permute-start.10) | collective-permute-done | bytes 294944 | tf_op jit(solution)/shard_map/ppermute | solution.py:1109
  43.8 5.5 %collective-permute-done.2.rest_5_.rest_1_ = bf16[9,32,512]{2,1,0:T(8,128)(2,1)S(1)} collective-permute-done((bf16[9,32,512]{2,1,0:T(8,128)(2,1)S(1)}, bf16[9,32,512]{2,1,0:T(8,128)(2,1)S(1)}, u32[]{:S(2)}, u32[]{:S(2)}) %collective-permute-start.2) | collective-permute-done | bytes 294944 | tf_op jit(solution)/shard_map/ppermute | solution.py:1109
  63.9 5.3 collective-permute-done.4.rest_7_.rest_3_
  70.7 4.8 collective-permute-done.5.rest_8_.rest_4_
  76.1 5.2 pack_cotangent.1
  84.8 22.2 %conv1_forward.1 = (f32[16,512]{1,0:T(8,128)}, bf16[2048,512]{1,0:T(8,128)(2,1)}, bf16[10,10,32,512]{3,2,1,0:T(8,128)(2,1)}, f32[64,32,512]{2,1,0:T(8,128)}, bf1...) custom-call(s32[4]{0:T(128)} %pad_add_fusion.position, ...), custom_call_target="tpu_custom_call" | custom-call | flops 9663676416 | bytes 20971520 | tf_op jit(solution)/shard_map/conv1_forward/pallas_call | solution.py:545
  108.0 26.2 %conv2_forward.1 = (f32[2048,512]{1,0:T(8,128)}, bf16[2048,512]{1,0:T(8,128)(2,1)}, f32[2,32,512]{2,1,0:T(8,128)}) custom-call(s32[4]{0:T(128)} %pad_add_fusion.position, s32[64]{0:T(128)} %get-tuple-element.55.slot_tile, s32[64]{0:T(128)} %get-tuple-element.56.slot_crop, f32[16,512]{1,0:T(8,128)} %get-tuple-element.61.par.rest_0_, ...), custom_call_target="tpu_custom_call" | custom-call | flops 9663676416 | bytes 16777216 | tf_op jit(solution)/shard_map/conv2_forward/pallas_call | solution.py:638
  135.1 50.6 %attention.1 = (bf16[2048,256]{1,0:T(8,128)(2,1)}, bf16[2048,256]{1,0:T(8,128)(2,1)}, bf16[4,256,512]{2,1,0:T(8,128)(2,1)}, bf16[4,256,512]{2,1,0:T(8,128)(2,1)}...) custom-call(s32[4]{0:T(128)} %pad_add_fusion.position, ...), custom_call_target="tpu_custom_call" | custom-call | flops 32212254720 | bytes 25165824 | tf_op jit(solution)/shard_map/attention/pallas_call | solution.py:864
  185.8 22.8 %conv2_input_grad.1 = (bf16[10,10,32,512]{3,2,1,0:T(8,128)(2,1)}, f32[16,512]{1,0:T(8,128)}) custom-call(s32[4]{0:T(128)} %pad_add_fusion.position, s32[64]{0:T(128)} %get-tuple-element.55.slot_tile, s32[64]{0:T(128)} %get-tuple-element.56.slot_crop, f32[16,512]{1,0:T(8,128)} %get-tuple-element.61.par.rest_0_, f32[2,32,512]{2,1,0:T(8,128)} %get-tuple-element.74.stats2, ...), custom_call_target="tpu_custom_call" | custom-call | flops 9663676416 | bytes 16777216 | tf_op jit(solution)/shard_map/conv2_input_grad/pallas_call | solution.py:998
  208.6 22.9 %conv1_input_grad.1 = (f32[2048,256]{1,0:T(8,128)}, bf16[2048,256]{1,0:T(8,128)(2,1)}, f32[16,512]{1,0:T(8,128)}) custom-call(s32[4]{0:T(128)} %pad_add_fusion.position, s32[64]{0:T(128)} %get-tuple-element.55.slot_tile, s32[64]{0:T(128)} %get-tuple-element.56.slot_crop, f32[16,512]{1,0:T(8,128)} %get-tuple-element.61.par.rest_0_, ...), custom_call_target="tpu_custom_call" | custom-call | flops 9663676416 | bytes 16777216 | tf_op jit(solution)/shard_map/conv1_input_grad/pallas_call | solution.py:1084
  235.0 2.5 collective-permute-done.24
  238.1 17.5 %conv2_weight_grad.1 = (bf16[9,256,512]{2,1,0:T(8,128)(2,1)}, bf16[9,256,512]{2,1,0:T(8,128)(2,1)}) custom-call(s32[4]{0:T(128)} %pad_add_fusion.position, bf16[10,10,32,512]{3,2,1,0:T(8,128)(2,1)} %get-tuple-element.63.pad_hbm.active, bf16[10,10,32,512]{3,2,1,0:T(8,128)(2,1)} %get-tuple-element.75.pad_hbm.grad), custom_call_target="tpu_custom_call" | custom-call | flops 9663676416 | bytes 12582912 | tf_op jit(solution)/shard_map/conv2_weight_grad/pallas_call | solution.py:913
  257.8 17.9 %conv1_weight_grad.1 = (bf16[9,256,512]{2,1,0:T(8,128)(2,1)}, bf16[9,256,512]{2,1,0:T(8,128)(2,1)}) custom-call(s32[4]{0:T(128)} %pad_add_fusion.position, bf16[10,10,32,512]{3,2,1,0:T(8,128)(2,1)} %get-tuple-element.84.active, bf16[10,10,32,512]{3,2,1,0:T(8,128)(2,1)} %get-tuple-element.77.pad_hbm.grad), custom_call_target="tpu_custom_call" | custom-call | flops 9663676416 | bytes 12582912 | tf_op jit(solution)/shard_map/conv1_weight_grad/pallas_call | solution.py:913
  279.8 47.8 %collective-permute-done.65 = bf16[2,2,2,32,512]{4,3,0,2,1:T(8,128)(2,1)S(1)} collective-permute-done((bf16[2,2,2,32,512]{4,3,0,2,1:T(8,128)(2,1)S(1)}, bf16[2,2,2,32,512]{4,3,0,2,1:T(8,128)(2,1)S(1)}, u32[]{:S(2)}, u32[]{:S(2)}) %collective-permute-start.65) | collective-permute-done | bytes 262176 | tf_op jit(solution)/shard_map/ppermute | solution.py:1109
  329.5 3.2 collective-permute-done.69
  333.2 4.4 collective-permute-done.66
  339.0 2.8 collective-permute-done.70
  343.6 2.5 collective-permute-done.67
  346.1 10.2 %collective-permute-start.27 = (f32[16,512]{1,0:T(8,128)S(1)}, f32[16,512]{1,0:T(8,128)S(1)}, u32[]{:S(2)}, u32[]{:S(2)}) collective-permute-start(f32[16,512]{1,0:T(8,128)S(1)} %add.140), channel_id=1, source_target_pairs={{0,16},{2,18},{4,20},{6,22},{8,24},{10,26},{12,28},{14,30},{16,0},... | collective-permute-start | bytes 98312 | tf_op jit(solution)/shard_map/ppermute | solution.py:1106
  360.4 7.2 %collective-permute-done.53 = bf16[3,2,2,32,512]{4,3,0,2,1:T(8,128)(2,1)S(1)} collective-permute-done((bf16[3,2,2,32,512]{4,3,0,2,1:T(8,128)(2,1)S(1)}, bf16[3,2,2,32,512]{4,3,0,2,1:T(8,128)(2,1)S(1)}, u32[]{:S(2)}, u32[]{:S(2)}) %collective-permute-start.53) | collective-permute-done | bytes 393248 | tf_op jit(solution)/shard_map/ppermute | solution.py:1106
  370.1 8.2 %collective-permute-done.50 = bf16[3,2,2,32,512]{4,3,0,1,2:T(8,128)(2,1)S(1)} collective-permute-done((bf16[3,2,2,32,512]{4,3,0,1,2:T(8,128)(2,1)S(1)}, bf16[3,2,2,32,512]{4,3,0,1,2:T(8,128)(2,1)S(1)}, u32[]{:S(2)}, u32[]{:S(2)}) %collective-permute-start.50) | collective-permute-done | bytes 393248 | tf_op jit(solution)/shard_map/ppermute | solution.py:1106
  380.9 7.2 %collective-permute-done.29 = bf16[3,2,2,32,512]{4,3,0,2,1:T(8,128)(2,1)S(1)} collective-permute-done((bf16[3,2,2,32,512]{4,3,0,2,1:T(8,128)(2,1)S(1)}, bf16[3,2,2,32,512]{4,3,0,2,1:T(8,128)(2,1)S(1)}, u32[]{:S(2)}, u32[]{:S(2)}) %collective-permute-start.29) | collective-permute-done | bytes 393248 | tf_op jit(solution)/shard_map/ppermute | solution.py:1109
  389.9 6.0 %collective-permute-done.32 = bf16[3,2,2,32,512]{4,3,0,1,2:T(8,128)(2,1)S(1)} collective-permute-done((bf16[3,2,2,32,512]{4,3,0,1,2:T(8,128)(2,1)S(1)}, bf16[3,2,2,32,512]{4,3,0,1,2:T(8,128)(2,1)S(1)}, u32[]{:S(2)}, u32[]{:S(2)}) %collective-permute-start.32) | collective-permute-done | bytes 393248 | tf_op jit(solution)/shard_map/ppermute | solution.py:1106
  396.9 5.5 %collective-permute-done.54 = bf16[3,2,32,512]{3,2,0,1:T(8,128)(2,1)S(1)} collective-permute-done((bf16[3,2,32,512]{3,2,0,1:T(8,128)(2,1)S(1)}, bf16[3,2,32,512]{3,2,0,1:T(8,128)(2,1)S(1)}, u32[]{:S(2)}, u32[]{:S(2)}) %collective-permute-start.54) | collective-permute-done | bytes 196640 | tf_op jit(solution)/shard_map/ppermute | solution.py:1109
  403.3 4.8 collective-permute-done.48
  410.0 3.7 collective-permute-done.51
  414.4 5.0 collective-permute-done.36
  420.3 5.8 %collective-permute-done.30 = bf16[3,2,32,512]{3,2,0,1:T(8,128)(2,1)S(1)} collective-permute-done((bf16[3,2,32,512]{3,2,0,1:T(8,128)(2,1)S(1)}, bf16[3,2,32,512]{3,2,0,1:T(8,128)(2,1)S(1)}, u32[]{:S(2)}, u32[]{:S(2)}) %collective-permute-start.30) | collective-permute-done | bytes 196640 | tf_op jit(solution)/shard_map/ppermute | solution.py:1106
  428.1 4.0 collective-permute-done.33
  432.7 4.0 collective-permute-done.55
  438.4 3.6 collective-permute-done.49
  442.3 4.4 collective-permute-done.52
  446.9 4.4 collective-permute-done.37
  453.3 2.6 collective-permute-done.31
  456.3 4.3 collective-permute-done.34
  463.9 10.6 %collective-permute-done.56 = bf16[9,32,512]{2,1,0:T(8,128)(2,1)S(1)} collective-permute-done((bf16[9,32,512]{2,1,0:T(8,128)(2,1)S(1)}, bf16[9,32,512]{2,1,0:T(8,128)(2,1)S(1)}, u32[]{:S(2)}, u32[]{:S(2)}) %collective-permute-start.56) | collective-permute-done | bytes 294944 | tf_op jit(solution)/shard_map/ppermute | solution.py:1106
  474.7 4.8 collective-permute-done.72.rest_1_
  487.5 4.7 collective-permute-done.57.rest_1_
  493.0 4.4 collective-permute-done.39.rest_1_
  498.3 5.5 %unpack_output.1 = bf16[256,4096]{1,0:T(8,128)(2,1)} custom-call(s32[4]{0:T(128)} %pad_add_fusion.position, s32[64]{0:T(128)} %get-tuple-element.55.slot_tile, bf16[2048,256]{1,0:T(8,128)(2,1)} %get-tuple-element.71.rest_0_, bf16[2048,256]{1,0:T(8,128)(2,1)} %copy-done.46), custom_call_target="tpu_custom_call" | custom-call | flops 4294967296 | bytes 8388608 | tf_op jit(solution)/shard_map/unpack_output/pallas_call | solution.py:454
  505.1 5.5 %collective-permute-done.41.rest_3_ = bf16[9,32,512]{2,1,0:T(8,128)(2,1)S(1)} collective-permute-done((bf16[9,32,512]{2,1,0:T(8,128)(2,1)S(1)}, bf16[9,32,512]{2,1,0:T(8,128)(2,1)S(1)}, u32[]{:S(2)}, u32[]{:S(2)}) %collective-permute-start.41) | collective-permute-done | bytes 294944 | tf_op jit(solution)/shard_map/ppermute | solution.py:1106
  510.6 10.9 %unpack_input_grad.1 = f32[256,4096]{1,0:T(8,128)} custom-call(s32[4]{0:T(128)} %pad_add_fusion.position, s32[64]{0:T(128)} %get-tuple-element.55.slot_tile, f32[2048,256]{1,0:T(8,128)} %get-tuple-element.79.rest_0_, bf16[2048,256]{1,0:T(8,128)(2,1)} %copy-done.45), custom_call_target="tpu_custom_call" | custom-call | flops 4294967296 | bytes 8388608 | tf_op jit(solution)/shard_map/unpack_input_grad/pallas_call | solution.py:454
  521.6 2.8 small_grads.1
  524.4 2.9 slice_bitcast_fusion
  528.0 4.1 conv2_grads.1
  533.7 4.1 conv1_grads.1
  (326 shorter events, 82.2 us)
Async XLA Ops:
  10.3 65.3 %collective-permute-start = (bf16[2048,256]{1,0:T(8,128)(2,1)}, bf16[2048,256]{1,0:T(8,128)(2,1)S(1)}, u32[]{:S(2)}, u32[]{:S(2)}) collective-permute-start(bf16[2048,256]{1,0:T(8,128)(2,1)} %get-tuple-element.60), channel_id=1, source_target_pairs={{0,1},{1,0},{2,3},{3,2},{4,5},{5,4},{6,7},{7,6},{8,9},{9,8},{10,11... | collective-permute-start | bytes 3145736 | tf_op jit(solution)/shard_map/ppermute | solution.py:1109
  14.2 29.5 %collective-permute-start.10 = (bf16[9,32,512]{2,1,0:T(8,128)(2,1)S(1)}, bf16[9,32,512]{2,1,0:T(8,128)(2,1)S(1)}, u32[]{:S(2)}, u32[]{:S(2)}) collective-permute-start(bf16[9,32,512]{2,1,0:T(8,128)(2,1)S(1)} %constant_dynamic-slice_fusion.1), channel_id=1, source_target_pairs={{0,1},{1,0},{2,3},{3,2},{4,5},{5,4},{6,7},{7,6},{8,9},{9,8},{10,11... | collective-permute-start | bytes 884744 | tf_op jit(solution)/shard_map/ppermute | solution.py:1109
  15.3 33.9 %collective-permute-start.2 = (bf16[9,32,512]{2,1,0:T(8,128)(2,1)S(1)}, bf16[9,32,512]{2,1,0:T(8,128)(2,1)S(1)}, u32[]{:S(2)}, u32[]{:S(2)}) collective-permute-start(bf16[9,32,512]{2,1,0:T(8,128)(2,1)S(1)} %constant_dynamic-slice_fusion.2), channel_id=1, source_target_pairs={{0,1},{1,0},{2,3},{3,2},{4,5},{5,4},{6,7},{7,6},{8,9},{9,8},{10,11... | collective-permute-start | bytes 884744 | tf_op jit(solution)/shard_map/ppermute | solution.py:1109
  43.8 11.5 %collective-permute-start.14 = (bf16[9,32,512]{2,1,0:T(8,128)(2,1)S(1)}, bf16[9,32,512]{2,1,0:T(8,128)(2,1)S(1)}, u32[]{:S(2)}, u32[]{:S(2)}) collective-permute-start(bf16[9,32,512]{2,1,0:T(8,128)(2,1)S(1)} %collective-permute-done.10.rest_1_), channel_id=1, source_target_pairs={{0,2},{2,0},{4,6},{6,4},{8,10},{10,8},{12,14},{14,12},{16,18},{18,... | collective-permute-start | bytes 884744 | tf_op jit(solution)/shard_map/ppermute | solution.py:1106
  49.3 9.9 %collective-permute-start.3 = (bf16[9,32,512]{2,1,0:T(8,128)(2,1)S(1)}, bf16[9,32,512]{2,1,0:T(8,128)(2,1)S(1)}, u32[]{:S(2)}, u32[]{:S(2)}) collective-permute-start(bf16[9,32,512]{2,1,0:T(8,128)(2,1)S(1)} %collective-permute-done.2.rest_5_.rest_1_), channel_id=1, source_target_pairs={{0,8},{2,10},{4,12},{6,14},{8,0},{10,2},{12,4},{14,6},{16,24},{18,... | collective-permute-start | bytes 884744 | tf_op jit(solution)/shard_map/ppermute | solution.py:1106
  52.8 9.9 %collective-permute-start.12 = (bf16[9,32,512]{2,1,0:T(8,128)(2,1)S(1)}, bf16[9,32,512]{2,1,0:T(8,128)(2,1)S(1)}, u32[]{:S(2)}, u32[]{:S(2)}) collective-permute-start(bf16[9,32,512]{2,1,0:T(8,128)(2,1)S(1)} %collective-permute-done.10.rest_1_), channel_id=1, source_target_pairs={{0,4},{2,6},{4,0},{6,2},{8,12},{10,14},{12,8},{14,10},{16,20},{18,... | collective-permute-start | bytes 884744 | tf_op jit(solution)/shard_map/ppermute | solution.py:1106
  55.3 13.9 %collective-permute-start.4 = (bf16[9,32,512]{2,1,0:T(8,128)(2,1)S(1)}, bf16[9,32,512]{2,1,0:T(8,128)(2,1)}, u32[]{:S(2)}, u32[]{:S(2)}) collective-permute-start(bf16[9,32,512]{2,1,0:T(8,128)(2,1)S(1)} %collective-permute-done.2.rest_5_.rest_1_), channel_id=1, source_target_pairs={{0,4},{2,6},{4,0},{6,2},{8,12},{10,14},{12,8},{14,10},{16,20},{18,... | collective-permute-start | bytes 884744 | tf_op jit(solution)/shard_map/ppermute | solution.py:1106
  59.2 16.3 %collective-permute-start.5 = (bf16[9,32,512]{2,1,0:T(8,128)(2,1)S(1)}, bf16[9,32,512]{2,1,0:T(8,128)(2,1)}, u32[]{:S(2)}, u32[]{:S(2)}) collective-permute-start(bf16[9,32,512]{2,1,0:T(8,128)(2,1)S(1)} %collective-permute-done.3.rest_6_.rest_2_), channel_id=1, source_target_pairs={{0,4},{2,6},{4,0},{6,2},{8,12},{10,14},{12,8},{14,10},{16,20},{18,... | collective-permute-start | bytes 884744 | tf_op jit(solution)/shard_map/ppermute | solution.py:1106
  62.8 18.8 %collective-permute-start.6 = (bf16[9,32,512]{2,1,0:T(8,128)(2,1)S(1)}, bf16[9,32,512]{2,1,0:T(8,128)(2,1)}, u32[]{:S(2)}, u32[]{:S(2)}) collective-permute-start(bf16[9,32,512]{2,1,0:T(8,128)(2,1)S(1)} %collective-permute-done.2.rest_5_.rest_1_), channel_id=1, source_target_pairs={{0,2},{2,0},{4,6},{6,4},{8,10},{10,8},{12,14},{14,12},{16,18},{18,... | collective-permute-start | bytes 884744 | tf_op jit(solution)/shard_map/ppermute | solution.py:1106
  63.9 18.9 %collective-permute-start.7 = (bf16[9,32,512]{2,1,0:T(8,128)(2,1)S(1)}, bf16[9,32,512]{2,1,0:T(8,128)(2,1)}, u32[]{:S(2)}, u32[]{:S(2)}) collective-permute-start(bf16[9,32,512]{2,1,0:T(8,128)(2,1)S(1)} %collective-permute-done.3.rest_6_.rest_2_), channel_id=1, source_target_pairs={{0,2},{2,0},{4,6},{6,4},{8,10},{10,8},{12,14},{14,12},{16,18},{18,... | collective-permute-start | bytes 884744 | tf_op jit(solution)/shard_map/ppermute | solution.py:1106
  69.2 12.8 %collective-permute-start.13 = (bf16[9,32,512]{2,1,0:T(8,128)(2,1)}, bf16[9,32,512]{2,1,0:T(8,128)(2,1)}, u32[]{:S(2)}, u32[]{:S(2)}) collective-permute-start(bf16[9,32,512]{2,1,0:T(8,128)(2,1)} %collective-permute-done.11.rest_2_), channel_id=1, source_target_pairs={{0,4},{2,6},{4,0},{6,2},{8,12},{10,14},{12,8},{14,10},{16,20},{18,... | collective-permute-start | bytes 884744 | tf_op jit(solution)/shard_map/ppermute | solution.py:1106
  81.6 25.6 %collective-permute-start.15 = (bf16[9,32,512]{2,1,0:T(8,128)(2,1)}, bf16[9,32,512]{2,1,0:T(8,128)(2,1)S(1)}, u32[]{:S(2)}, u32[]{:S(2)}) collective-permute-start(bf16[9,32,512]{2,1,0:T(8,128)(2,1)} %collective-permute-done.11.rest_2_), channel_id=1, source_target_pairs={{0,2},{2,0},{4,6},{6,4},{8,10},{10,8},{12,14},{14,12},{16,18},{18,... | collective-permute-start | bytes 884744 | tf_op jit(solution)/shard_map/ppermute | solution.py:1106
  82.3 24.9 %collective-permute-start.16 = (bf16[9,32,512]{2,1,0:T(8,128)(2,1)S(1)}, bf16[9,32,512]{2,1,0:T(8,128)(2,1)}, u32[]{:S(2)}, u32[]{:S(2)}) collective-permute-start(bf16[9,32,512]{2,1,0:T(8,128)(2,1)S(1)} %copy-done.56), channel_id=1, source_target_pairs={{0,2},{2,0},{4,6},{6,4},{8,10},{10,8},{12,14},{14,12},{16,18},{18,... | collective-permute-start | bytes 884744 | tf_op jit(solution)/shard_map/ppermute | solution.py:1106
  82.6 24.6 %collective-permute-start.17 = (bf16[9,32,512]{2,1,0:T(8,128)(2,1)}, bf16[9,32,512]{2,1,0:T(8,128)(2,1)}, u32[]{:S(2)}, u32[]{:S(2)}) collective-permute-start(bf16[9,32,512]{2,1,0:T(8,128)(2,1)} %collective-permute-done.13.rest_4_), channel_id=1, source_target_pairs={{0,2},{2,0},{4,6},{6,4},{8,10},{10,8},{12,14},{14,12},{16,18},{18,... | collective-permute-start | bytes 884744 | tf_op jit(solution)/shard_map/ppermute | solution.py:1106
  82.8 24.3 %collective-permute-start.19 = (bf16[4,128,512]{2,1,0:T(8,128)(2,1)S(1)}, bf16[4,128,512]{2,1,0:T(8,128)(2,1)S(1)}, u32[]{:S(2)}, u32[]{:S(2)}) collective-permute-start(bf16[4,128,512]{2,1,0:T(8,128)(2,1)S(1)} %constant_dynamic-slice_fusion), channel_id=1, source_target_pairs={{0,1},{1,0},{2,3},{3,2},{4,5},{5,4},{6,7},{7,6},{8,9},{9,8},{10,11... | collective-permute-start | bytes 1572872 | tf_op jit(solution)/shard_map/ppermute | solution.py:1109
  83.3 50.9 %collective-permute-start.18 = (bf16[2048,256]{1,0:T(8,128)(2,1)S(1)}, bf16[2048,256]{1,0:T(8,128)(2,1)}, u32[]{:S(2)}, u32[]{:S(2)}) collective-permute-start(bf16[2048,256]{1,0:T(8,128)(2,1)S(1)} %copy-done.48), channel_id=1, source_target_pairs={{0,1},{1,0},{2,3},{3,2},{4,5},{5,4},{6,7},{7,6},{8,9},{9,8},{10,11... | collective-permute-start | bytes 3145736 | tf_op jit(solution)/shard_map/ppermute | solution.py:1109
  107.1 27.1 %collective-permute-start.20 = (bf16[4,128,512]{2,1,0:T(8,128)(2,1)S(1)}, bf16[4,128,512]{2,1,0:T(8,128)(2,1)S(1)}, u32[]{:S(2)}, u32[]{:S(2)}) collective-permute-start(bf16[4,128,512]{2,1,0:T(8,128)(2,1)S(1)} %collective-permute-done.19.rest_7_), channel_id=1, source_target_pairs={{0,2},{2,0},{4,6},{6,4},{8,10},{10,8},{12,14},{14,12},{16,18},{18,... | collective-permute-start | bytes 1572872 | tf_op jit(solution)/shard_map/ppermute | solution.py:1106
  185.7 70.0 %collective-permute-start.64 = (bf16[4,256,512]{2,1,0:T(8,128)(2,1)}, bf16[4,256,512]{2,1,0:T(8,128)(2,1)S(1)}, u32[]{:S(2)}, u32[]{:S(2)}) collective-permute-start(bf16[4,256,512]{2,1,0:T(8,128)(2,1)} %get-tuple-element.90), channel_id=1, source_target_pairs={{0,2},{2,0},{4,6},{6,4},{8,10},{10,8},{12,14},{14,12},{16,18},{18,... | collective-permute-start | bytes 3145736 | tf_op jit(solution)/shard_map/ppermute | solution.py:1106
  237.5 18.1 %collective-permute-start.25 = (f32[16,512]{1,0:T(8,128)S(1)}, f32[16,512]{1,0:T(8,128)S(1)}, u32[]{:S(2)}, u32[]{:S(2)}) collective-permute-start(f32[16,512]{1,0:T(8,128)S(1)} %add.138), channel_id=1, source_target_pairs={{0,4},{2,6},{4,0},{6,2},{8,12},{10,14},{12,8},{14,10},{16,20},{18,... | collective-permute-start | bytes 98312 | tf_op jit(solution)/shard_map/ppermute | solution.py:1106
  255.6 22.1 %collective-permute-start.26 = (f32[16,512]{1,0:T(8,128)S(1)}, f32[16,512]{1,0:T(8,128)S(1)}, u32[]{:S(2)}, u32[]{:S(2)}) collective-permute-start(f32[16,512]{1,0:T(8,128)S(1)} %add.139), channel_id=1, source_target_pairs={{0,8},{2,10},{4,12},{6,14},{8,0},{10,2},{12,4},{14,6},{16,24},{18,... | collective-permute-start | bytes 98312 | tf_op jit(solution)/shard_map/ppermute | solution.py:1106
  256.2 22.1 %collective-permute-start.68 = (bf16[2,2,2,32,512]{4,3,0,1,2:T(8,128)(2,1)S(1)}, bf16[2,2,2,32,512]{4,3,0,1,2:T(8,128)(2,1)S(1)}, u32[]{:S(2)}, u32[]{:S(2)}) collective-permute-start(bf16[2,2,2,32,512]{4,3,0,1,2:T(8,128)(2,1)S(1)} %bitcast.241), channel_id=1, source_target_pairs={{0,4},{2,6},{4,0},{6,2},{8,12},{10,14},{12,8},{14,10},{16,20},{18,... | collective-permute-start | bytes 786440 | tf_op jit(solution)/shard_map/ppermute | solution.py:1106
  275.7 198.9 %collective-permute-start.21 = (bf16[2048,256]{1,0:T(8,128)(2,1)}, bf16[2048,256]{1,0:T(8,128)(2,1)S(1)}, u32[]{:S(2)}, u32[]{:S(2)}) collective-permute-start(bf16[2048,256]{1,0:T(8,128)(2,1)} %get-tuple-element.72), channel_id=1, source_target_pairs={{0,1},{1,0},{2,3},{3,2},{4,5},{5,4},{6,7},{7,6},{8,9},{9,8},{10,11... | collective-permute-start | bytes 3145736 | tf_op jit(solution)/shard_map/ppermute | solution.py:1109
  277.1 203.1 %collective-permute-start.22 = (bf16[2048,256]{1,0:T(8,128)(2,1)}, bf16[2048,256]{1,0:T(8,128)(2,1)S(1)}, u32[]{:S(2)}, u32[]{:S(2)}) collective-permute-start(bf16[2048,256]{1,0:T(8,128)(2,1)} %get-tuple-element.80), channel_id=1, source_target_pairs={{0,1},{1,0},{2,3},{3,2},{4,5},{5,4},{6,7},{7,6},{8,9},{9,8},{10,11... | collective-permute-start | bytes 3145736 | tf_op jit(solution)/shard_map/ppermute | solution.py:1109
  277.7 78.7 %collective-permute-start.46 = (bf16[9,256,512]{2,1,0:T(8,128)(2,1)S(1)}, bf16[9,256,512]{2,1,0:T(8,128)(2,1)S(1)}, u32[]{:S(2)}, u32[]{:S(2)}) collective-permute-start(bf16[9,256,512]{2,1,0:T(8,128)(2,1)S(1)} %copy-done.44), channel_id=1, source_target_pairs={{0,2},{2,0},{4,6},{6,4},{8,10},{10,8},{12,14},{14,12},{16,18},{18,... | collective-permute-start | bytes 7077896 | tf_op jit(solution)/shard_map/ppermute | solution.py:1106
  277.7 80.3 %collective-permute-start.28 = (bf16[9,256,512]{2,1,0:T(8,128)(2,1)}, bf16[9,256,512]{2,1,0:T(8,128)(2,1)S(1)}, u32[]{:S(2)}, u32[]{:S(2)}) collective-permute-start(bf16[9,256,512]{2,1,0:T(8,128)(2,1)} %get-tuple-element.86), channel_id=1, source_target_pairs={{0,2},{2,0},{4,6},{6,4},{8,10},{10,8},{12,14},{14,12},{16,18},{18,... | collective-permute-start | bytes 7077896 | tf_op jit(solution)/shard_map/ppermute | solution.py:1106
  278.3 49.4 %collective-permute-start.65 = (bf16[2,2,2,32,512]{4,3,0,2,1:T(8,128)(2,1)S(1)}, bf16[2,2,2,32,512]{4,3,0,2,1:T(8,128)(2,1)S(1)}, u32[]{:S(2)}, u32[]{:S(2)}) collective-permute-start(bf16[2,2,2,32,512]{4,3,0,2,1:T(8,128)(2,1)S(1)} %bitcast.242), channel_id=1, source_target_pairs={{0,1},{1,0},{2,3},{3,2},{4,5},{5,4},{6,7},{7,6},{8,9},{9,8},{10,11... | collective-permute-start | bytes 786440 | tf_op jit(solution)/shard_map/ppermute | solution.py:1109
  346.1 117.5 %collective-permute-start.27 = (f32[16,512]{1,0:T(8,128)S(1)}, f32[16,512]{1,0:T(8,128)S(1)}, u32[]{:S(2)}, u32[]{:S(2)}) collective-permute-start(f32[16,512]{1,0:T(8,128)S(1)} %add.140), channel_id=1, source_target_pairs={{0,16},{2,18},{4,20},{6,22},{8,24},{10,26},{12,28},{14,30},{16,0},... | collective-permute-start | bytes 98312 | tf_op jit(solution)/shard_map/ppermute | solution.py:1106
  357.5 10.0 %collective-permute-start.53 = (bf16[3,2,2,32,512]{4,3,0,2,1:T(8,128)(2,1)S(1)}, bf16[3,2,2,32,512]{4,3,0,2,1:T(8,128)(2,1)S(1)}, u32[]{:S(2)}, u32[]{:S(2)}) collective-permute-start(bf16[3,2,2,32,512]{4,3,0,2,1:T(8,128)(2,1)S(1)} %bitcast.239), channel_id=1, source_target_pairs={{0,8},{2,10},{4,12},{6,14},{8,0},{10,2},{12,4},{14,6},{16,24},{18,... | collective-permute-start | bytes 1179656 | tf_op jit(solution)/shard_map/ppermute | solution.py:1106
  358.0 11.1 %collective-permute-start.47 = (bf16[3,2,2,32,512]{4,3,0,2,1:T(8,128)(2,1)S(1)}, bf16[3,2,2,32,512]{4,3,0,2,1:T(8,128)(2,1)S(1)}, u32[]{:S(2)}, u32[]{:S(2)}) collective-permute-start(bf16[3,2,2,32,512]{4,3,0,2,1:T(8,128)(2,1)S(1)} %bitcast.235), channel_id=1, source_target_pairs={{0,1},{1,0},{2,3},{3,2},{4,5},{5,4},{6,7},{7,6},{8,9},{9,8},{10,11... | collective-permute-start | bytes 1179656 | tf_op jit(solution)/shard_map/ppermute | solution.py:1109
  367.5 10.7 %collective-permute-start.50 = (bf16[3,2,2,32,512]{4,3,0,1,2:T(8,128)(2,1)S(1)}, bf16[3,2,2,32,512]{4,3,0,1,2:T(8,128)(2,1)S(1)}, u32[]{:S(2)}, u32[]{:S(2)}) collective-permute-start(bf16[3,2,2,32,512]{4,3,0,1,2:T(8,128)(2,1)S(1)} %bitcast.238), channel_id=1, source_target_pairs={{0,4},{2,6},{4,0},{6,2},{8,12},{10,14},{12,8},{14,10},{16,20},{18,... | collective-permute-start | bytes 1179656 | tf_op jit(solution)/shard_map/ppermute | solution.py:1106
  369.2 10.3 %collective-permute-start.35 = (bf16[3,2,2,32,512]{4,3,0,2,1:T(8,128)(2,1)S(1)}, bf16[3,2,2,32,512]{4,3,0,2,1:T(8,128)(2,1)S(1)}, u32[]{:S(2)}, u32[]{:S(2)}) collective-permute-start(bf16[3,2,2,32,512]{4,3,0,2,1:T(8,128)(2,1)S(1)} %bitcast.240), channel_id=1, source_target_pairs={{0,8},{2,10},{4,12},{6,14},{8,0},{10,2},{12,4},{14,6},{16,24},{18,... | collective-permute-start | bytes 1179656 | tf_op jit(solution)/shard_map/ppermute | solution.py:1106
  379.5 82.1 %collective-permute-start.71 = (bf16[4,32,512]{2,1,0:T(8,128)(2,1)S(1)}, bf16[4,32,512]{2,1,0:T(8,128)(2,1)S(1)}, u32[]{:S(2)}, u32[]{:S(2)}) collective-permute-start(bf16[4,32,512]{2,1,0:T(8,128)(2,1)S(1)} %pad_maximum_fusion.3), channel_id=1, source_target_pairs={{0,16},{2,18},{4,20},{6,22},{8,24},{10,26},{12,28},{14,30},{16,0},... | collective-permute-start | bytes 393224 | tf_op jit(solution)/shard_map/ppermute | solution.py:1106
  460.5 13.9 %collective-permute-start.56 = (bf16[9,32,512]{2,1,0:T(8,128)(2,1)S(1)}, bf16[9,32,512]{2,1,0:T(8,128)(2,1)S(1)}, u32[]{:S(2)}, u32[]{:S(2)}) collective-permute-start(bf16[9,32,512]{2,1,0:T(8,128)(2,1)S(1)} %pad_maximum_fusion.2), channel_id=1, source_target_pairs={{0,16},{2,18},{4,20},{6,22},{8,24},{10,26},{12,28},{14,30},{16,0},... | collective-permute-start | bytes 884744 | tf_op jit(solution)/shard_map/ppermute | solution.py:1106
  461.6 18.1 %collective-permute-start.38 = (bf16[9,32,512]{2,1,0:T(8,128)(2,1)S(1)}, bf16[9,32,512]{2,1,0:T(8,128)(2,1)S(1)}, u32[]{:S(2)}, u32[]{:S(2)}) collective-permute-start(bf16[9,32,512]{2,1,0:T(8,128)(2,1)S(1)} %pad_maximum_fusion.1), channel_id=1, source_target_pairs={{0,16},{2,18},{4,20},{6,22},{8,24},{10,26},{12,28},{14,30},{16,0},... | collective-permute-start | bytes 884744 | tf_op jit(solution)/shard_map/ppermute | solution.py:1106
  463.6 15.8 %collective-permute-start.73 = (bf16[4,32,512]{2,1,0:T(8,128)(2,1)S(1)}, bf16[4,32,512]{2,1,0:T(8,128)(2,1)S(1)}, u32[]{:S(2)}, u32[]{:S(2)}) collective-permute-start(bf16[4,32,512]{2,1,0:T(8,128)(2,1)S(1)} %add_convert_fusion.5.rest_0_), channel_id=1, source_target_pairs={{0,4},{2,6},{4,0},{6,2},{8,12},{10,14},{12,8},{14,10},{16,20},{18,... | collective-permute-start | bytes 393224 | tf_op jit(solution)/shard_map/ppermute | solution.py:1106
  480.1 12.0 %collective-permute-start.60 = (bf16[9,32,512]{2,1,0:T(8,128)(2,1)S(1)}, bf16[9,32,512]{2,1,0:T(8,128)(2,1)S(1)}, u32[]{:S(2)}, u32[]{:S(2)}) collective-permute-start(bf16[9,32,512]{2,1,0:T(8,128)(2,1)S(1)} %add_convert_fusion.3.rest_0_), channel_id=1, source_target_pairs={{0,2},{2,0},{4,6},{6,4},{8,10},{10,8},{12,14},{14,12},{16,18},{18,... | collective-permute-start | bytes 884744 | tf_op jit(solution)/shard_map/ppermute | solution.py:1106
  480.4 12.4 %collective-permute-start.58 = (bf16[9,32,512]{2,1,0:T(8,128)(2,1)S(1)}, bf16[9,32,512]{2,1,0:T(8,128)(2,1)S(1)}, u32[]{:S(2)}, u32[]{:S(2)}) collective-permute-start(bf16[9,32,512]{2,1,0:T(8,128)(2,1)S(1)} %add_convert_fusion.3.rest_0_), channel_id=1, source_target_pairs={{0,4},{2,6},{4,0},{6,2},{8,12},{10,14},{12,8},{14,10},{16,20},{18,... | collective-permute-start | bytes 884744 | tf_op jit(solution)/shard_map/ppermute | solution.py:1106
  482.9 14.5 %collective-permute-start.39 = (bf16[9,32,512]{2,1,0:T(8,128)(2,1)S(1)}, bf16[9,32,512]{2,1,0:T(8,128)(2,1)S(1)}, u32[]{:S(2)}, u32[]{:S(2)}) collective-permute-start(bf16[9,32,512]{2,1,0:T(8,128)(2,1)S(1)} %add_convert_fusion.4.rest_0_), channel_id=1, source_target_pairs={{0,8},{2,10},{4,12},{6,14},{8,0},{10,2},{12,4},{14,6},{16,24},{18,... | collective-permute-start | bytes 884744 | tf_op jit(solution)/shard_map/ppermute | solution.py:1106
  487.3 16.6 %collective-permute-start.40 = (bf16[9,32,512]{2,1,0:T(8,128)(2,1)S(1)}, bf16[9,32,512]{2,1,0:T(8,128)(2,1)S(1)}, u32[]{:S(2)}, u32[]{:S(2)}) collective-permute-start(bf16[9,32,512]{2,1,0:T(8,128)(2,1)S(1)} %add_convert_fusion.4.rest_0_), channel_id=1, source_target_pairs={{0,4},{2,6},{4,0},{6,2},{8,12},{10,14},{12,8},{14,10},{16,20},{18,... | collective-permute-start | bytes 884744 | tf_op jit(solution)/shard_map/ppermute | solution.py:1106
  492.1 12.4 %collective-permute-start.61 = (bf16[9,32,512]{2,1,0:T(8,128)(2,1)S(1)}, bf16[9,32,512]{2,1,0:T(8,128)(2,1)S(1)}, u32[]{:S(2)}, u32[]{:S(2)}) collective-permute-start(bf16[9,32,512]{2,1,0:T(8,128)(2,1)S(1)} %collective-permute-done.57.rest_1_), channel_id=1, source_target_pairs={{0,2},{2,0},{4,6},{6,4},{8,10},{10,8},{12,14},{14,12},{16,18},{18,... | collective-permute-start | bytes 884744 | tf_op jit(solution)/shard_map/ppermute | solution.py:1106
  492.2 12.6 %collective-permute-start.59 = (bf16[9,32,512]{2,1,0:T(8,128)(2,1)S(1)}, bf16[9,32,512]{2,1,0:T(8,128)(2,1)S(1)}, u32[]{:S(2)}, u32[]{:S(2)}) collective-permute-start(bf16[9,32,512]{2,1,0:T(8,128)(2,1)S(1)} %collective-permute-done.57.rest_1_), channel_id=1, source_target_pairs={{0,4},{2,6},{4,0},{6,2},{8,12},{10,14},{12,8},{14,10},{16,20},{18,... | collective-permute-start | bytes 884744 | tf_op jit(solution)/shard_map/ppermute | solution.py:1106
  492.8 11.2 %collective-permute-start.62 = (bf16[9,32,512]{2,1,0:T(8,128)(2,1)S(1)}, bf16[9,32,512]{2,1,0:T(8,128)(2,1)S(1)}, u32[]{:S(2)}, u32[]{:S(2)}) collective-permute-start(bf16[9,32,512]{2,1,0:T(8,128)(2,1)S(1)} %collective-permute-done.58.rest_2_), channel_id=1, source_target_pairs={{0,2},{2,0},{4,6},{6,4},{8,10},{10,8},{12,14},{14,12},{16,18},{18,... | collective-permute-start | bytes 884744 | tf_op jit(solution)/shard_map/ppermute | solution.py:1106
  497.4 13.3 %collective-permute-start.41 = (bf16[9,32,512]{2,1,0:T(8,128)(2,1)S(1)}, bf16[9,32,512]{2,1,0:T(8,128)(2,1)S(1)}, u32[]{:S(2)}, u32[]{:S(2)}) collective-permute-start(bf16[9,32,512]{2,1,0:T(8,128)(2,1)S(1)} %collective-permute-done.39.rest_1_), channel_id=1, source_target_pairs={{0,4},{2,6},{4,0},{6,2},{8,12},{10,14},{12,8},{14,10},{16,20},{18,... | collective-permute-start | bytes 884744 | tf_op jit(solution)/shard_map/ppermute | solution.py:1106
  503.9 28.1 %collective-permute-start.42 = (bf16[9,32,512]{2,1,0:T(8,128)(2,1)S(1)}, bf16[9,32,512]{2,1,0:T(8,128)(2,1)S(1)}, u32[]{:S(2)}, u32[]{:S(2)}) collective-permute-start(bf16[9,32,512]{2,1,0:T(8,128)(2,1)S(1)} %add_convert_fusion.4.rest_0_), channel_id=1, source_target_pairs={{0,2},{2,0},{4,6},{6,4},{8,10},{10,8},{12,14},{14,12},{16,18},{18,... | collective-permute-start | bytes 884744 | tf_op jit(solution)/shard_map/ppermute | solution.py:1106
  504.0 28.0 %collective-permute-start.43 = (bf16[9,32,512]{2,1,0:T(8,128)(2,1)S(1)}, bf16[9,32,512]{2,1,0:T(8,128)(2,1)S(1)}, u32[]{:S(2)}, u32[]{:S(2)}) collective-permute-start(bf16[9,32,512]{2,1,0:T(8,128)(2,1)S(1)} %collective-permute-done.39.rest_1_), channel_id=1, source_target_pairs={{0,2},{2,0},{4,6},{6,4},{8,10},{10,8},{12,14},{14,12},{16,18},{18,... | collective-permute-start | bytes 884744 | tf_op jit(solution)/shard_map/ppermute | solution.py:1106
  504.6 27.5 %collective-permute-start.44 = (bf16[9,32,512]{2,1,0:T(8,128)(2,1)S(1)}, bf16[9,32,512]{2,1,0:T(8,128)(2,1)S(1)}, u32[]{:S(2)}, u32[]{:S(2)}) collective-permute-start(bf16[9,32,512]{2,1,0:T(8,128)(2,1)S(1)} %collective-permute-done.40.rest_2_), channel_id=1, source_target_pairs={{0,2},{2,0},{4,6},{6,4},{8,10},{10,8},{12,14},{14,12},{16,18},{18,... | collective-permute-start | bytes 884744 | tf_op jit(solution)/shard_map/ppermute | solution.py:1106
  504.8 22.5 %collective-permute-start.63 = (bf16[9,32,512]{2,1,0:T(8,128)(2,1)S(1)}, bf16[9,32,512]{2,1,0:T(8,128)(2,1)S(1)}, u32[]{:S(2)}, u32[]{:S(2)}) collective-permute-start(bf16[9,32,512]{2,1,0:T(8,128)(2,1)S(1)} %collective-permute-done.59.rest_3_), channel_id=1, source_target_pairs={{0,2},{2,0},{4,6},{6,4},{8,10},{10,8},{12,14},{14,12},{16,18},{18,... | collective-permute-start | bytes 884744 | tf_op jit(solution)/shard_map/ppermute | solution.py:1106
  510.6 21.5 %collective-permute-start.45 = (bf16[9,32,512]{2,1,0:T(8,128)(2,1)S(1)}, bf16[9,32,512]{2,1,0:T(8,128)(2,1)S(1)}, u32[]{:S(2)}, u32[]{:S(2)}) collective-permute-start(bf16[9,32,512]{2,1,0:T(8,128)(2,1)S(1)} %collective-permute-done.41.rest_3_), channel_id=1, source_target_pairs={{0,2},{2,0},{4,6},{6,4},{8,10},{10,8},{12,14},{14,12},{16,18},{18,... | collective-permute-start | bytes 884744 | tf_op jit(solution)/shard_map/ppermute | solution.py:1106
  (90 other events, 1484.6 us)

commit v2 on v1

--- a/solution.py
+++ b/solution.py
@@ -147,15 +147,11 @@
         self.same = (self.crop_col == self.crop_row[:, 0:slots]).astype(F32)
 
 
-def place_of(position):
-    return position[0], position[1], position[2], position[3]
-
-
 def group_total(value):
     width = CH // GROUPS
     lane = lax.broadcasted_iota(jnp.int32, (value.shape[0], 128), 1)
     parts = []
-    for at in range(0, CH, 128):
+    for at in range(0, value.shape[1], 128):
         part = value[:, at : at + 128]
         step = 1
         while step < width:
@@ -173,23 +169,33 @@
     return total / count
 
 
-def slab_sum(pixels, slots, term):
-    def step(at, total):
-        return total + term(at)
-
-    return lax.fori_loop(0, pixels, step, jnp.zeros((slots, CH), F32), unroll=8)
-
-
-def stats_slabs(ref, same):
-    pixels, slots, _ = ref.shape
-    mean = crop_mean(same, slab_sum(pixels, slots, lambda at: ref[at]))
-
-    def square(at):
-        centred = ref[at] - mean
+def lanes_of(width):
+    return [slice(at, at + 128) for at in range(0, width, 128)]
+
+
+def slab_sum(pixels, slots, width, term):
+    parts = []
+    for lanes in lanes_of(width):
+
+        def step(at, total):
+            return total + term(at, lanes)
+
+        parts.append(lax.fori_loop(0, pixels, step, jnp.zeros((slots, 128), F32), unroll=8))
+    return jnp.concatenate(parts, axis=1)
+
+
+def slab_stats(pixels, slots, slab, same):
+    mean = crop_mean(same, slab_sum(pixels, slots, CH, slab))
+
+    def square(at, lanes):
+        centred = slab(at, lanes) - mean[:, lanes]
         return centred * centred
 
-    inverse = lax.rsqrt(crop_mean(same, slab_sum(pixels, slots, square)) + EPS)
-    return mean, inverse
+    return mean, lax.rsqrt(crop_mean(same, slab_sum(pixels, slots, CH, square)) + EPS)
+
+
+def sigmoid(value):
+    return 0.5 * jnp.tanh(0.5 * value) + 0.5
 
 
 def fill_halo(pad, plan):
@@ -227,23 +233,31 @@
 
 
 class WeightLoad:
-    def __init__(self, position, pieces, target, sem):
+    def __init__(self, position, pieces, target, sem, columns=None):
         self.copies = []
-        if len(pieces) == 1:
-            self.copies.append(pltpu.make_async_copy(pieces[0], target, sem.at[0]))
-        else:
-            me = position[0]
+        views = [(pieces[0], None)]
+        if len(pieces) > 1:
+            me, core = position[0], position[1]
             half = pieces[0].shape[1]
-            width = pieces[1].shape[1]
-            mine = position[1] if len(pieces) == 9 else position[2]
-            spots = [me * half]
-            for at in range(len(pieces) - 1):
-                spots.append((1 - me) * half + (mine ^ at) * width)
-            for at, (piece, spot) in enumerate(zip(pieces, spots)):
-                rows = pl.ds(pl.multiple_of(spot, width), piece.shape[1])
-                self.copies.append(
-                    pltpu.make_async_copy(piece, target.at[:, rows, :], sem.at[at])
-                )
+            views = [(pieces[0], me * half)]
+            part = half // (len(pieces) - 1)
+            for number, piece in enumerate(pieces[1:]):
+                spot = (1 - me) * half
+                if len(pieces) == 3:
+                    spot = spot + (core ^ number) * part
+                if len(piece.shape) == 3:
+                    views.append((piece, spot))
+                    continue
+                for at in range(piece.shape[0]):
+                    views.append((piece.at[at], spot + at * piece.shape[2]))
+        for at, (piece, spot) in enumerate(views):
+            width = piece.shape[1]
+            rows = slice(None)
+            if spot is not None:
+                rows = pl.ds(pl.multiple_of(spot, 32), width)
+            if columns is not None:
+                piece = piece.at[:, :, columns]
+            self.copies.append(pltpu.make_async_copy(piece, target.at[:, rows, :], sem.at[at]))
 
     def start(self):
         for copy in self.copies:
@@ -255,26 +269,46 @@
 
 
 def weight_sems(pieces):
-    return pltpu.SemaphoreType.DMA((len(pieces),))
-
-
-def store_grad(grad, outs, work, position, number):
+    return pltpu.SemaphoreType.DMA((9,))
+
+
+BLOCK = CH // 16
+
+
+def store_grad(grad, outs, work, position, unit, first, count, front=True):
     if len(outs) == 1:
-        outs[0][number] = grad.astype(BF16)
+        outs[0][unit] = grad.astype(BF16)
+        return
+    work[...] = grad
+    me, core, quad = position[0], position[1], position[2]
+    for half, out in enumerate(outs):
+        for c in range(2):
+            for q in range(4):
+                row = (me ^ c) * (CH // 2) + (core ^ half) * (CH // 4) + (quad ^ q) * BLOCK
+                part = work[pl.ds(pl.multiple_of(row, BLOCK), BLOCK), :]
+                if front:
+                    to = ((c * 4 + q) * first + unit) * BLOCK
+                else:
+                    to = (8 * first + (q * 2 + c) * (count - first) + unit - first) * BLOCK
+                out[pl.ds(pl.multiple_of(to, BLOCK), BLOCK), :] = part.astype(BF16)
+
+
+def store_vectors(vecs, out, me):
+    if len(out.shape) == 2:
+        out[...] = vecs[...]
     else:
-        work[...] = grad
-        mine = position[3]
-        width = CH // 16
-        for at in range(16):
-            rows = pl.ds(pl.multiple_of((mine ^ at) * width, width), width)
-            part = work[rows, :].astype(BF16)
-            core, spot = (at // 4) % 2, (at // 8) * 4 + at % 4
-            outs[core][number, spot * width : (spot + 1) * width, :] = part
+        half = out.shape[2]
+        out[0] = vecs[:, pl.ds(pl.multiple_of(me * half, half), half)]
+        out[1] = vecs[:, pl.ds(pl.multiple_of((1 - me) * half, half), half)]
+
+
+def vector_shape(paired):
+    return shape((2, 16, CH // 2) if paired else (16, CH), F32)
 
 
 def grad_shapes(count, paired):
     if paired:
-        return [shape((count, CH // 2, CH), BF16)] * 2
+        return [shape((8 * count * BLOCK, CH), BF16)] * 2
     return [shape((count, CH, CH), BF16)]
 
 
@@ -314,6 +348,18 @@
     return [table[k] for k in kinds]
 
 
+ROOM = {
+    "unpack_output": 18,
+    "unpack_input_grad": 18,
+    "conv2_weight_grad": 24,
+    "conv1_weight_grad": 22,
+    "conv2_input_grad": 24,
+    "conv1_input_grad": 20,
+    "conv2_grads": 16,
+    "conv1_grads": 14,
+}
+
+
 def call(body, ins, outs, shapes, scratch, name, flops, moved):
     return pl.pallas_call(
         body,
@@ -321,7 +367,7 @@
         out_specs=tuple(specs(outs)),
         out_shape=tuple(shapes),
         scratch_shapes=list(scratch),
-        compiler_params=pltpu.CompilerParams(vmem_limit_bytes=60 << 20),
+        compiler_params=pltpu.CompilerParams(vmem_limit_bytes=ROOM.get(name, 60) << 20),
         cost_estimate=pl.CostEstimate(
             flops=int(flops), bytes_accessed=int(moved), transcendentals=0
         ),
@@ -407,7 +453,7 @@
         [shape((rows, local), BF16)] * devices,
         [vmem((local // 128, pixels, 128), F32), vmem((local // 128, rows, 128), F32)],
         name,
-        4 << 30,
+        40 << 30,
         6 << 20,
     )(position, slot_tile, signal)
 
@@ -466,16 +512,21 @@
 (G1, B1, C1, G2, B2, C2, G3, B3, QB, VB, PB) = range(11)
 
 
-def norm_swish_pad(source, mean, inverse, gain, bias, pad, slots):
+def norm_swish_pad(slab, mean, inverse, gain, bias, pad, copy=None):
     scaled = inverse * gain
-
-    def step(row, carry):
-        for col in range(TILE):
-            before = (source[row * TILE + col] - mean) * scaled + bias
-            pad[row + 1, col + 1] = (before * jax.nn.sigmoid(before)).astype(BF16)
-        return carry
-
-    lax.fori_loop(0, TILE, step, 0)
+    for lanes in lanes_of(CH):
+        centre, factor, offset = mean[:, lanes], scaled[:, lanes], bias[:, lanes]
+
+        def step(row, carry):
+            for col in range(TILE):
+                value = slab(row * TILE + col, lanes)
+                before = (value - centre) * factor + offset
+                pad[row + 1, col + 1, :, lanes] = (before * sigmoid(before)).astype(BF16)
+                if copy is not None:
+                    copy[row * TILE + col, :, lanes] = value.astype(BF16)
+            return carry
+
+        lax.fori_loop(0, TILE, step, 0)
 
 
 def first_kernel(parts, count, position, slot_tile, slot_crop, *rest):
@@ -483,8 +534,8 @@
     par_parts, rest = rest[:parts], rest[parts:]
     pieces, rest = rest[:count], rest[count:]
     (par, feats_hbm, pad1_hbm, hidden_hbm, pad2_hbm, stats1, stats2) = rest[:7]
-    feats, wide, hidden, pad1, pad2, weight, weight_sem, sem = rest[7:]
-    pixels, slots, _ = wide.shape
+    feats, rounded, hidden, pad1, pad2, weight, weight_sem, sem = rest[7:]
+    pixels, slots, _ = hidden.shape
     load_weight = WeightLoad(position, pieces, weight, weight_sem)
     load_weight.start()
 
@@ -500,17 +551,14 @@
     save_feats = pltpu.make_async_copy(feats, feats_hbm, sem.at[1])
     save_feats.start()
 
-    def widen(at, carry):
-        wide[at] = feats[pl.ds(pl.multiple_of(at * slots, slots), slots), :].astype(F32)
-        return carry
-
-    lax.fori_loop(0, pixels, widen, 0, unroll=4)
     plan = Plan(position[0], slot_tile, slot_crop, slots)
-    mean, inverse = stats_slabs(wide, plan.same)
+
+    def slab1(at, lanes):
+        return feats[pl.ds(pl.multiple_of(at * slots, slots), slots), lanes].astype(F32)
+
+    mean, inverse = slab_stats(pixels, slots, slab1, plan.same)
     stats1[0], stats1[1] = mean, inverse
-    norm_swish_pad(
-        wide, mean, inverse, par[G1 : G1 + 1, :], par[B1 : B1 + 1, :], pad1, slots
-    )
+    norm_swish_pad(slab1, mean, inverse, par[G1 : G1 + 1, :], par[B1 : B1 + 1, :], pad1)
     fill_halo(pad1, plan)
     save_pad1 = pltpu.make_async_copy(pad1, pad1_hbm, sem.at[2])
     save_pad1.start()
@@ -522,13 +570,17 @@
         return carry
 
     lax.fori_loop(0, TILE, step, 0)
-    save_hidden = pltpu.make_async_copy(hidden, hidden_hbm, sem.at[3])
-    save_hidden.start()
-    mean, inverse = stats_slabs(hidden, plan.same)
+
+    def slab2(at, lanes):
+        return hidden[at, :, lanes]
+
+    mean, inverse = slab_stats(pixels, slots, slab2, plan.same)
     stats2[0], stats2[1] = mean, inverse
     norm_swish_pad(
-        hidden, mean, inverse, par[G2 : G2 + 1, :], par[B2 : B2 + 1, :], pad2, slots
+        slab2, mean, inverse, par[G2 : G2 + 1, :], par[B2 : B2 + 1, :], pad2, rounded
     )
+    save_hidden = pltpu.make_async_copy(rounded, hidden_hbm, sem.at[3])
+    save_hidden.start()
     fill_halo(pad2, plan)
     save_pad2 = pltpu.make_async_copy(pad2, pad2_hbm, sem.at[4])
     save_pad2.start()
@@ -550,14 +602,14 @@
             shape((16, CH), F32),
             shape((rows, CH), BF16),
             shape(pad, BF16),
-            shape((pixels, slots, CH), F32),
+            shape((pixels, slots, CH), BF16),
             shape(pad, BF16),
             shape((2, slots, CH), F32),
             shape((2, slots, CH), F32),
         ],
         [
             vmem((rows, CH), BF16),
-            vmem((pixels, slots, CH), F32),
+            vmem((pixels, slots, CH), BF16),
             vmem((pixels, slots, CH), F32),
             vmem(pad, BF16),
             vmem(pad, BF16),
@@ -597,33 +649,25 @@
 
     lax.fori_loop(0, TILE, step, 0)
 
-    def slab(at):
-        span = pl.ds(pl.multiple_of(at * slots, slots), slots)
-        return jnp.concatenate([resid[col, span, :] for col in range(CH // 128)], axis=1)
-
-    mean = crop_mean(same, slab_sum(pixels, slots, slab))
-
-    def square(at):
-        centred = slab(at) - mean
-        return centred * centred
-
-    inverse = lax.rsqrt(crop_mean(same, slab_sum(pixels, slots, square)) + EPS)
+    def slab(at, lanes):
+        return resid[lanes.start // 128, pl.ds(pl.multiple_of(at * slots, slots), slots), :]
+
+    mean, inverse = slab_stats(pixels, slots, slab, same)
     stats3[0], stats3[1] = mean, inverse
     rows_scr[0], rows_scr[1] = mean, inverse * par[G3 : G3 + 1, :]
     bias = par[B3 : B3 + 1, :]
 
     def tile_step(slot, carry):
-        value = jnp.concatenate(
-            [resid[col, pl.ds(slot, pixels, stride=slots), :] for col in range(CH // 128)],
-            axis=1,
-        )
         at = pl.ds(pl.multiple_of(slot * pixels, pixels), pixels)
-        resid_tile[at, :] = value
-        row = pl.ds(slot, 1)
-        normed[at, :] = ((value - rows_scr[0, row]) * rows_scr[1, row] + bias).astype(BF16)
+        centre, factor = rows_scr[0, pl.ds(slot, 1)], rows_scr[1, pl.ds(slot, 1)]
+        for col, lanes in enumerate(lanes_of(CH)):
+            value = resid[col, pl.ds(slot, pixels, stride=slots), :]
+            resid_tile[at, lanes] = value.astype(BF16)
+            scaled = (value - centre[:, lanes]) * factor[:, lanes]
+            normed[at, lanes] = (scaled + bias[:, lanes]).astype(BF16)
         return carry
 
-    lax.fori_loop(0, slots, tile_step, 0)
+    lax.fori_loop(0, slots, tile_step, 0, unroll=2)
     save_resid = pltpu.make_async_copy(resid_tile, resid_hbm, sem.at[2])
     save_normed = pltpu.make_async_copy(normed, normed_hbm, sem.at[3])
     save_resid.start()
@@ -639,10 +683,10 @@
         functools.partial(second_kernel, len(weight)),
         "sssvvh" + "h" * len(weight),
         "hhv",
-        [shape((rows, CH), F32), shape((rows, CH), BF16), shape((2, slots, CH), F32)],
+        [shape((rows, CH), BF16), shape((rows, CH), BF16), shape((2, slots, CH), F32)],
         [
             vmem((CH // 128, rows, 128), F32),
-            vmem((rows, CH), F32),
+            vmem((rows, CH), BF16),
             vmem((rows, CH), BF16),
             vmem(pad.shape, BF16),
             vmem((9, CH, CH), BF16),
@@ -662,9 +706,9 @@
     pieces, rest = rest[:count], rest[count:]
     out_parts, rest = rest[:outs], rest[outs:]
     grad_outs, rest = rest[:outs], rest[outs:]
-    vecs, resid_grad, pad = rest[:3]
-    (tangent, query, key, value, mixed_grad, mixed, query_grad, key_grad, value_grad) = rest[3:12]
-    normed_grad, by_tile, rows_scr, weight, key_crop, work, weight_sem = rest[12:]
+    vecs_out, pad = rest[:2]
+    (tangent, query, key, value, mixed_grad, mixed, query_grad, key_grad, value_grad) = rest[2:11]
+    normed_grad, by_tile, rows_scr, weight, key_crop, work, vecs, weight_sem = rest[11:]
     load_weight = WeightLoad(position, pieces, weight, weight_sem)
     load_weight.start()
     wq, wk, wv, wp = (weight.at[k] for k in range(4))
@@ -766,7 +810,7 @@
         total += jnp.dot(dv, wv[...], preferred_element_type=F32)
         normed_grad[span, :] = total
         result = lax.dot_general(mixed[span, :], wp[...], NT, preferred_element_type=F32)
-        result = (result + par[PB : PB + 1, :] + resid[span, :]).astype(BF16)
+        result = (result + par[PB : PB + 1, :] + resid[span, :].astype(F32)).astype(BF16)
         if outs == 1:
             out_parts[0][span, :] = result
         else:
@@ -790,20 +834,22 @@
     left = normed[...]
     for number, grad in enumerate((query_grad, key, value)):
         total = lax.dot_general(grad[...], left, TN, preferred_element_type=F32)
-        store_grad(total, grad_outs, work, position, number)
+        store_grad(total, grad_outs, work, position, number, 4, 4)
     total = lax.dot_general(tangent[...], mixed[...], TN, preferred_element_type=F32)
-    store_grad(total, grad_outs, work, position, 3)
-
-    def hat_of(slot, span):
-        row = pl.ds(slot, 1)
-        return (resid[span, :] - stats3[0, row]) * stats3[1, row]
+    store_grad(total, grad_outs, work, position, 3, 4, 4)
 
     def sums(slot, carry):
         span = pl.ds(pl.multiple_of(slot * pixels, pixels), pixels)
-        upstream = normed_grad[span, :]
         row = pl.ds(slot, 1)
-        rows_scr[0, row] = jnp.sum(upstream, axis=0, keepdims=True)
-        rows_scr[1, row] = jnp.sum(upstream * hat_of(slot, span), axis=0, keepdims=True)
+        centre, factor = stats3[0, row], stats3[1, row]
+        plains, crosseds = [], []
+        for lanes in lanes_of(CH):
+            upstream = normed_grad[span, lanes]
+            hat = (resid[span, lanes].astype(F32) - centre[:, lanes]) * factor[:, lanes]
+            plains.append(jnp.sum(upstream, axis=0, keepdims=True))
+            crosseds.append(jnp.sum(upstream * hat, axis=0, keepdims=True))
+        rows_scr[0, row] = jnp.concatenate(plains, axis=1)
+        rows_scr[1, row] = jnp.concatenate(crosseds, axis=1)
         return carry
 
     lax.fori_loop(0, slots, sums, 0)
@@ -822,11 +868,15 @@
     def apply(slot, carry):
         span = pl.ds(pl.multiple_of(slot * pixels, pixels), pixels)
         row = pl.ds(slot, 1)
-        scaled = normed_grad[span, :] * gain
-        centred = scaled - rows_scr[0, row] - hat_of(slot, span) * rows_scr[1, row]
-        result = tangent[span, :].astype(F32) + stats3[1, row] * centred
-        for col in range(CH // 128):
-            by_tile[col, span, :] = result[:, col * 128 : (col + 1) * 128]
+        centre, factor = stats3[0, row], stats3[1, row]
+        slope = factor * gain
+        level = factor * rows_scr[0, row]
+        tilt = factor * factor * rows_scr[1, row]
+        for col, lanes in enumerate(lanes_of(CH)):
+            centred = resid[span, lanes].astype(F32) - centre[:, lanes]
+            grad = normed_grad[span, lanes] * slope[:, lanes] - level[:, lanes]
+            grad = grad - centred * tilt[:, lanes]
+            by_tile[col, span, :] = tangent[span, lanes].astype(F32) + grad
         return carry
 
     lax.fori_loop(0, slots, apply, 0)
@@ -841,13 +891,13 @@
                 ],
                 axis=1,
             )
-            resid_grad[at] = slab
             rounded = slab.astype(BF16)
             pad[row + 1, col + 1] = rounded
             total += jnp.sum(rounded.astype(F32), axis=0, keepdims=True)
         return total
 
     vecs[C2 : C2 + 1, :] = lax.fori_loop(0, TILE, spread, zero)
+    store_vectors(vecs, vecs_out, me)
     fill_halo(pad, plan)
 
 
@@ -864,14 +914,15 @@
     result = call(
         functools.partial(attention_kernel, parts, outs, len(weight)),
         "sssss" + "v" * (4 + parts) + "h" * len(weight),
-        "v" * (2 * outs + 3),
+        "v" * (2 * outs + 2),
         out_shapes
         + grad_shapes(4, outs == 2)
-        + [shape((16, CH), F32), shape((pixels, slots, CH), F32), shape(pad, BF16)],
+        + [vector_shape(outs == 2), shape(pad, BF16)],
         [vmem((rows, CH), BF16)] * 7
         + [vmem((rows, CH), F32)] * 3
         + [vmem((CH // 128, rows, 128), F32), vmem((2, slots, CH), F32)]
         + [vmem((4, CH, CH), BF16), vmem((1, rows), jnp.int32), vmem((CH, CH), F32)]
+        + [vmem((16, CH), F32)]
         + [weight_sems(weight)],
         "attention",
         30 << 30,
@@ -889,60 +940,101 @@
     return result[:outs], result[outs : 2 * outs], result[2 * outs :]
 
 
-def weight_grad_kernel(outs, begin, position, active, grad, *rest):
-    out_parts, (flipped, work) = rest[:outs], rest[outs:]
+def weight_grad_kernel(paired, first, extra, position, active, grad, *rest):
+    outs = 2 if paired else 1
+    extras, rest = rest[: outs if extra else 0], rest[outs if extra else 0 :]
+    out_parts, (flipped, work, sem) = rest[:outs], rest[outs:]
+    copies = []
+    for half, part in enumerate(extras):
+        for at in range(8):
+            source = part.at[pl.ds(at * extra * BLOCK, extra * BLOCK)]
+            target = out_parts[half].at[pl.ds(at * first * BLOCK, extra * BLOCK)]
+            copies.append(pltpu.make_async_copy(source, target, sem.at[half, at]))
+    for copy in copies:
+        copy.start()
     slots = active.shape[2]
     wide = TILE * slots
     for row in range(TILE):
         left = grad[row + 1, 1 : TILE + 1].reshape(wide, CH)
         flipped[:, row * wide : (row + 1) * wide] = left.T
 
-    def step(number, carry):
-        tap = begin + number
+    def step(front, tap, carry):
         right = active[pl.ds(tap // 3, TILE), pl.ds(tap % 3, TILE)].reshape(TILE * wide, CH)
         total = jnp.dot(flipped[...], right, preferred_element_type=F32)
-        store_grad(total, out_parts, work, position, number)
+        store_grad(total, out_parts, work, position, tap + extra, first, 9 + extra, front)
         return carry
 
-    lax.fori_loop(0, out_parts[0].shape[0], step, 0)
-
-
-def weight_grad(position, active, grad, paired, slots, name, begin=0, count=9):
+    lax.fori_loop(0, first - extra, functools.partial(step, True), 0)
+    if first - extra < 9:
+        lax.fori_loop(first - extra, 9, functools.partial(step, False), 0)
+    for copy in copies:
+        copy.wait()
+
+
+def weight_grad(position, active, grad, paired, slots, name, first=9, extras=()):
     rows = TILE * TILE * slots
-    shapes = grad_shapes(count, paired)
+    extra = 4 if extras else 0
+    shapes = grad_shapes(9 + extra, paired)
     return call(
-        functools.partial(weight_grad_kernel, len(shapes), begin),
-        "svv",
+        functools.partial(weight_grad_kernel, paired, first, extra),
+        "svv" + "h" * len(extras),
         "v" * len(shapes),
         shapes,
-        [vmem((CH, rows), BF16), vmem((CH, CH), F32)],
+        [
+            vmem((CH, rows), BF16),
+            vmem((CH, CH), F32),
+            pltpu.SemaphoreType.DMA((2, 8)),
+        ],
         name,
-        2 * rows * CH * CH * count,
+        2 * rows * CH * CH * 9,
         12 << 20,
-    )(position, active, grad)
+    )(position, active, grad, *extras)
 
 
 def swish_back(upstream, before):
-    gate = jax.nn.sigmoid(before)
+    gate = sigmoid(before)
     return upstream * (gate + before * gate * (1.0 - gate))
 
 
 def norm_back_sums(source, upstream, mean, inverse, gain, bias, slots):
-    def step(at, carry):
-        plain, crossed = carry
-        hat = (source(at) - mean) * inverse
-        grad = swish_back(upstream[at], hat * gain + bias)
-        upstream[at] = grad
-        return plain + grad, crossed + grad * hat
-
-    zero = jnp.zeros((slots, CH), F32)
-    return lax.fori_loop(0, TILE * TILE, step, (zero, zero), unroll=2)
+    plains, crosseds = [], []
+    for lanes in lanes_of(upstream.shape[2]):
+        centre, factor = mean[:, lanes], inverse[:, lanes]
+        slope, offset = gain[:, lanes], bias[:, lanes]
+
+        def step(at, carry):
+            plain, crossed = carry
+            hat = (source(at, lanes) - centre) * factor
+            grad = swish_back(upstream[at, :, lanes], hat * slope + offset)
+            upstream[at, :, lanes] = grad
+            return plain + grad, crossed + grad * hat
+
+        zero = jnp.zeros((slots, 128), F32)
+        plain, crossed = lax.fori_loop(0, TILE * TILE, step, (zero, zero), unroll=4)
+        plains.append(plain)
+        crosseds.append(crossed)
+    return jnp.concatenate(plains, axis=1), jnp.concatenate(crosseds, axis=1)
+
+
+def norm_back_apply(source, upstream, mean, inverse, gain, plain, crossed, put):
+    for lanes in lanes_of(upstream.shape[2]):
+        centre, factor = mean[:, lanes], inverse[:, lanes]
+        slope = factor * gain[:, lanes]
+        level = factor * plain[:, lanes]
+        tilt = factor * factor * crossed[:, lanes]
+
+        def step(at, carry):
+            centred = source(at, lanes) - centre
+            put(at, lanes, upstream[at, :, lanes] * slope - level - centred * tilt)
+            return carry
+
+        lax.fori_loop(0, TILE * TILE, step, 0, unroll=8)
 
 
 def middle_kernel(count, position, slot_tile, slot_crop, par, stats2, pad_hbm, hidden_hbm, *rest):
     pieces, rest = rest[:count], rest[count:]
-    pad_out_hbm, vecs = rest[:2]
-    pad, weight, hidden, upstream, pad_out, weight_sem, sem = rest[2:]
+    pad_out_hbm, vecs_out = rest[:2]
+    pad, weight, hidden, upstream, pad_out, vecs, totals, weight_sem, sem = rest[2:]
     slots = pad.shape[2]
     load_pad = pltpu.make_async_copy(pad_hbm, pad, sem.at[0])
     load_weight = WeightLoad(position, pieces, weight, weight_sem)
@@ -964,8 +1056,12 @@
     load_hidden.wait()
     mean, inverse = stats2[0], stats2[1]
     gain, bias = par[G2 : G2 + 1, :], par[B2 : B2 + 1, :]
+
+    def source(at, lanes):
+        return hidden[at, :, lanes].astype(F32)
+
     plain, crossed = norm_back_sums(
-        lambda at: hidden[at], upstream, mean, inverse, gain, bias, slots
+        source, upstream, mean, inverse, gain, bias, slots
     )
     vecs[...] = jnp.zeros_like(vecs)
     vecs[G2 : G2 + 1, :] = jnp.sum(crossed, axis=0, keepdims=True)
@@ -973,19 +1069,16 @@
     plain = crop_mean(same, plain * gain)
     crossed = crop_mean(same, crossed * gain)
 
-    def apply(row, carry):
-        total = carry
-        for col in range(TILE):
-            at = row * TILE + col
-            hat = (hidden[at] - mean) * inverse
-            grad = inverse * (upstream[at] * gain - plain - hat * crossed)
-            rounded = grad.astype(BF16)
-            pad_out[row + 1, col + 1] = rounded
-            total += rounded.astype(F32)
-        return total
-
-    total = lax.fori_loop(0, TILE, apply, jnp.zeros((slots, CH), F32))
-    vecs[C1 : C1 + 1, :] = jnp.sum(total, axis=0, keepdims=True)
+    totals[...] = jnp.zeros_like(totals)
+
+    def put(at, lanes, grad):
+        rounded = grad.astype(BF16)
+        pad_out[at // TILE + 1, at % TILE + 1, :, lanes] = rounded
+        totals[:, lanes] += rounded.astype(F32)
+
+    norm_back_apply(source, upstream, mean, inverse, gain, plain, crossed, put)
+    vecs[C1 : C1 + 1, :] = jnp.sum(totals[...], axis=0, keepdims=True)
+    store_vectors(vecs, vecs_out, position[0])
     fill_halo(pad_out, plan)
     save = pltpu.make_async_copy(pad_out, pad_out_hbm, sem.at[3])
     save.start()
@@ -999,13 +1092,15 @@
         functools.partial(middle_kernel, len(weight)),
         "sssvvhh" + "h" * len(weight),
         "hv",
-        [shape(pad.shape, BF16), shape((16, CH), F32)],
+        [shape(pad.shape, BF16), vector_shape(len(weight) > 1)],
         [
             vmem(pad.shape, BF16),
             vmem((9, CH, CH), BF16),
-            vmem((pixels, slots, CH), F32),
+            vmem((pixels, slots, CH), BF16),
             vmem((pixels, slots, CH), F32),
             vmem(pad.shape, BF16),
+            vmem((16, CH), F32),
+            vmem((slots, CH), F32),
             weight_sems(weight),
             pltpu.SemaphoreType.DMA((4,)),
         ],
@@ -1016,18 +1111,27 @@
 
 
 def last_kernel(
-    outs, count, position, slot_tile, slot_crop, par, stats1, feats, pad_hbm, resid_hbm, *rest
+    whose, count, position, slot_tile, slot_crop, par, stats1, vecs2, vecs3, *rest
 ):
-    pieces, rest = rest[:count], rest[count:]
-    out_parts, (vecs, pad, weight, resid, upstream, weight_sem, sem) = rest[:outs], rest[outs:]
+    feats_hbm, pad_hbm, resid_hbm = rest[:3]
+    pieces, rest = rest[3 : 3 + count], rest[3 + count :]
+    out, vecs, pad, weight, feats, resid, upstream, weight_sem, sem = rest
     slots = pad.shape[2]
+    width = upstream.shape[2]
     pixels = TILE * TILE
     me = position[0]
+    columns = None
+    span = pl.ds(0, width)
+    if width < CH:
+        columns = span = pl.ds(pl.multiple_of((me ^ whose) * width, width), width)
+    load_weight = WeightLoad(position, pieces, weight, weight_sem, columns)
     load_pad = pltpu.make_async_copy(pad_hbm, pad, sem.at[0])
-    load_weight = WeightLoad(position, pieces, weight, weight_sem)
-    load_resid = pltpu.make_async_copy(resid_hbm, resid, sem.at[2])
+    inner = pl.ds(1, TILE)
+    load_resid = pltpu.make_async_copy(resid_hbm.at[inner, inner, :, span], resid, sem.at[1])
+    load_feats = pltpu.make_async_copy(feats_hbm.at[:, span], feats, sem.at[2])
     load_pad.start()
     load_weight.start()
+    load_feats.start()
     load_resid.start()
     plan = Plan(me, slot_tile, slot_crop, slots)
     same = plan.same
@@ -1036,159 +1140,207 @@
 
     def step(row, carry):
         total = conv_rows(pad, weight, row, slots, NN, True)
-        upstream[pl.ds(row * TILE, TILE)] = total.reshape(TILE, slots, CH)
+        upstream[pl.ds(row * TILE, TILE)] = total.reshape(TILE, slots, width)
         return carry
 
     lax.fori_loop(0, TILE, step, 0)
+    load_feats.wait()
     load_resid.wait()
-    mean, inverse = stats1[0], stats1[1]
-    gain, bias = par[G1 : G1 + 1, :], par[B1 : B1 + 1, :]
-
-    def source(at):
-        return feats[pl.ds(pl.multiple_of(at * slots, slots), slots), :].astype(F32)
+    mean, inverse = stats1[0, :, span], stats1[1, :, span]
+    gain, bias = par[G1 : G1 + 1, span], par[B1 : B1 + 1, span]
+
+    def source(at, lanes):
+        return feats[pl.ds(pl.multiple_of(at * slots, slots), slots), lanes].astype(F32)
 
     plain, crossed = norm_back_sums(source, upstream, mean, inverse, gain, bias, slots)
-    vecs[...] = jnp.zeros_like(vecs)
+    vecs[...] = vecs2[...] + vecs3[...] if width == CH else vecs2[whose] + vecs3[whose]
     vecs[G1 : G1 + 1, :] = jnp.sum(crossed, axis=0, keepdims=True)
     vecs[B1 : B1 + 1, :] = jnp.sum(plain, axis=0, keepdims=True)
+    if out.shape[0] > pixels * slots:
+        begin = pixels * slots
+        out[begin : begin + 16, :] = vecs[...].astype(BF16)
+        out[begin + 16 : begin + 32, :] = jnp.zeros((16, width), BF16)
     plain = crop_mean(same, plain * gain)
     crossed = crop_mean(same, crossed * gain)
 
-    def apply(at, carry):
-        hat = (source(at) - mean) * inverse
-        grad = resid[at] + inverse * (upstream[at] * gain - plain - hat * crossed)
-        if outs == 1:
-            span = pl.ds(pl.multiple_of(at * slots, slots), slots)
-            out_parts[0][span, :] = grad.astype(BF16)
-        else:
-            upstream[at] = grad
-        return carry
-
-    lax.fori_loop(0, pixels, apply, 0, unroll=2)
-    if outs == 2:
-        local = out_parts[0].shape[1]
-        own = pl.ds(pl.multiple_of(me * local, local), local)
-        other = pl.ds(pl.multiple_of((1 - me) * local, local), local)
-        out_parts[0][...] = upstream[:, :, own].reshape(pixels * slots, local)
-        out_parts[1][...] = upstream[:, :, other].reshape(pixels * slots, local).astype(BF16)
-
-
-def last(position, tables, par, stats1, feats, pad, weight, resid_grad, parts, slots):
+    def put(at, lanes, grad):
+        rows = pl.ds(pl.multiple_of(at * slots, slots), slots)
+        grad = resid[at // TILE, at % TILE, :, lanes].astype(F32) + grad
+        out[rows, lanes] = grad.astype(out.dtype)
+
+    norm_back_apply(source, upstream, mean, inverse, gain, plain, crossed, put)
+
+
+def last(position, tables, par, stats1, vecs, feats, pad, weight, resid_grad, whose, slots):
     pixels = TILE * TILE
     rows = pixels * slots
-    if parts == 2:
-        out_shapes = [shape((rows, CH // 2), F32), shape((rows, CH // 2), BF16)]
-    else:
-        out_shapes = [shape((rows, CH), BF16)]
-    outs = len(out_shapes)
-    result = call(
-        functools.partial(last_kernel, outs, len(weight)),
-        "sssvvvhh" + "h" * len(weight),
-        "v" * (outs + 1),
-        out_shapes + [shape((16, CH), F32)],
+    width = CH // 2 if len(weight) > 1 else CH
+    return call(
+        functools.partial(last_kernel, whose, len(weight)),
+        "sssvvvvhhh" + "h" * len(weight),
+        "vv",
+        [
+            shape((rows + (32 if whose else 0), width), F32 if width < CH and whose == 0 else BF16),
+            shape((16, width), F32),
+        ],
         [
             vmem(pad.shape, BF16),
-            vmem((9, CH, CH), BF16),
-            vmem((pixels, slots, CH), F32),
-            vmem((pixels, slots, CH), F32),
+            vmem((9, CH, width), BF16),
+            vmem((rows, width), BF16),
+            vmem((TILE, TILE, slots, width), BF16),
+            vmem((pixels, slots, width), F32),
             weight_sems(weight),
             pltpu.SemaphoreType.DMA((3,)),
         ],
         "conv1_input_grad",
-        2 * rows * CH * CH * 9,
-        16 << 20,
-    )(position, *tables[:2], par, stats1, feats, pad, resid_grad, *weight)
-    return result[:outs], result[outs]
-
-
-class Links:
-    def flip(self, value, bit):
-        return lax.ppermute(value, "dp", [(at, at ^ bit) for at in range(16)])
-
-    def chan(self, value):
-        return lax.ppermute(value, "chan", [(0, 1), (1, 0)])
-
-    def core(self, value):
-        return self.flip(value, 1)
-
-    def down(self, value):
-        return self.flip(value, 2)
-
-    def near(self, value):
-        return self.flip(value, 4)
-
-    def far(self, value):
-        return self.flip(value, 8)
-
-    def spread(self, value):
-        parts = [value, self.near(value), self.down(value)]
-        parts.append(self.down(parts[1]))
-        return parts + [self.core(part) for part in parts]
-
-    def gather_eighths(self, weight, piece):
-        width = weight.shape[1] // 8
-        own = lax.dynamic_slice_in_dim(weight, piece * width, width, 1)
-        return [weight] + self.spread(self.chan(own))
-
-    def gather_halves(self, weight, core):
-        width = weight.shape[1] // 2
-        own = self.chan(lax.dynamic_slice_in_dim(weight, core * width, width, 1))
-        return [weight, own, self.core(own)]
-
-    def add(self, left, right):
-        return (left.astype(F32) + right.astype(F32)).astype(BF16)
-
-    def reduce(self, halves):
-        count = halves[0].shape[0]
-        value = self.add(halves[0], self.core(halves[1]))
-        value = value.reshape(count, 2, 2, 2, CH // 16, CH)
-        third = -(-count // 3)
-        orders = (("chan", "down", "near"), ("down", "near", "chan"), ("near", "chan", "down"))
-        done = []
-        for number, order in enumerate(orders):
-            part = value[number * third : (number + 1) * third]
-            if part.shape[0] == 0:
-                continue
-            names = ["chan", "down", "near"]
-            for name in order:
-                at = 1 + names.index(name)
-                names.remove(name)
-                keep = lax.index_in_dim(part, 0, at, keepdims=False)
-                send = lax.index_in_dim(part, 1, at, keepdims=False)
-                part = self.add(keep, getattr(self, name)(send))
-            done.append(part)
-        value = jnp.concatenate(done, axis=0)
-        return self.spread(self.add(value, self.far(value)))
-
-    def total(self, value):
-        for step in (self.core, self.chan, self.down, self.near, self.far):
-            value = value + step(value)
-        return value
-
-
-def assemble_kernel(position, *rest):
-    parts, out = rest[:-1], rest[-1]
-    width = parts[0].shape[1]
-    for at, part in enumerate(parts):
-        rows = pl.ds(pl.multiple_of((position[1] ^ at) * width, width), width)
-        out[:, rows, :] = part[...].astype(F32)
-
-
-def assemble(position, parts, name):
-    count, width, _ = parts[0].shape
+        2 * rows * CH * width * 9,
+        10 << 20,
+    )(position, *tables[:2], par, stats1, *vecs, feats, pad, resid_grad, *weight)
+
+
+def after(value, *others):
+    flat, tree = jax.tree.flatten(value)
+    extra = jax.tree.leaves(others)
+    held = lax.optimization_barrier(tuple(flat) + tuple(extra))
+    return jax.tree.unflatten(tree, list(held[: len(flat)]))
+
+
+def add(*terms):
+    total = terms[0].astype(F32)
+    for term in terms[1:]:
+        total = total + term.astype(F32)
+    return total
+
+
+def swap(value, axis):
+    return lax.ppermute(value, axis, [(0, 1), (1, 0)])
+
+
+def to_all(value, axes, count):
+    return lax.all_to_all(jnp.broadcast_to(value[None], (count,) + value.shape), axes, 0, 0)
+
+
+QUAD = ("y", "near")
+
+
+def from_quad(values):
+    return [
+        lax.ppermute(value, ("near", "y"), [(at, at ^ bits) for at in range(4)])
+        for bits, value in zip((2, 1, 3), values)
+    ]
+
+
+def rounded_sum(terms):
+    total = terms[0].astype(F32)
+    for term in terms[1:]:
+        total = total + term.astype(F32)
+    return total.astype(BF16)
+
+
+def vector_rows(vectors):
+    rows, width = vectors.shape
+    return jnp.pad(vectors.astype(BF16), ((0, BLOCK - rows), (0, CH - width)))
+
+
+class Reduction:
+    def __init__(self, halves, first, count):
+        self.stage, self.first, self.count = 0, first, count
+        self.state = (halves[0], halves[1], swap(halves[1], "core"))
+
+    def advance(self, *others, vectors=None):
+        if others:
+            self.state = after(self.state, *others)
+        self.stage += 1
+        front = self.first * BLOCK
+        back = (self.count - self.first) * BLOCK
+        state = self.state
+        if self.stage == 1:
+            mine, _, came = state
+
+            def part(begin, size):
+                span = slice(begin, begin + size)
+                return rounded_sum([mine[span], came[span]])
+
+            start = 8 * front
+            keep = part(0, 4 * front), part(start, 2 * back)
+            sent_front = part(4 * front, 4 * front)
+            sent_back = [part(start + q * 2 * back, 2 * back) for q in (1, 2, 3)]
+            self.state = keep, (swap(sent_front, "chan"), from_quad(sent_back))
+            return sent_front, sent_back
+        if self.stage == 2:
+            (mine_front, mine_back), (came_front, came_back) = state
+            piece = [slice(q * front, (q + 1) * front) for q in range(4)]
+            sent_front = [rounded_sum([mine_front[piece[q]], came_front[piece[q]]]) for q in (1, 2, 3)]
+            sent_back = rounded_sum([mine_back[back:]] + [value[back:] for value in came_back])
+            keep_front = [mine_front[:front], came_front[:front]]
+            keep_back = [mine_back[:back]] + [value[:back] for value in came_back]
+            self.state = keep_front, keep_back, (from_quad(sent_front), swap(sent_back, "chan"))
+            return sent_front, sent_back
+        if self.stage == 3:
+            mine_front, mine_back, (came_front, came_back) = state
+            parts = [rounded_sum(mine_front + came_front), rounded_sum(mine_back + [came_back])]
+            if vectors is not None:
+                parts.append(vector_rows(vectors))
+            value = jnp.concatenate(parts, axis=0)
+            self.state = value, swap(value, "far")
+            return value
+        if self.stage == 4:
+            value = rounded_sum(list(state))
+            self.state = [value] + from_quad([value] * 3)
+            return value
+        if self.stage == 5:
+            mine = jnp.concatenate(state, axis=0)
+            self.state = mine, swap(mine, "core")
+            return mine
+
+    @property
+    def pieces(self):
+        return list(self.state)
+
+
+def assemble_kernel(sizes, position, mine, other, *outs):
+    units = mine.shape[0] // (4 * BLOCK)
+    vectors = None
+    for number, part in enumerate((mine, other)):
+        for at in range(4):
+            row = ((position[1] ^ number) * 4 + (position[2] ^ at)) * BLOCK
+            rows = pl.ds(pl.multiple_of(row, BLOCK), BLOCK)
+            unit = 0
+            for out, size in zip(outs, sizes):
+                for index in range(max(size, 1)):
+                    begin = (at * units + unit) * BLOCK
+                    value = part[begin : begin + BLOCK, :].astype(F32)
+                    if size:
+                        out[index, rows, :] = value
+                    else:
+                        out[rows, :] = value
+                    unit += 1
+            if unit < units:
+                begin = (at * units + unit) * BLOCK
+                term = part[begin : begin + BLOCK, :].astype(F32)
+                vectors = term if vectors is None else vectors + term
+    if vectors is not None:
+        outs[-1][...] = vectors
+
+
+def assemble(position, pieces, sizes, vectors, name):
+    shapes = [shape(((size,) if size else ()) + (8 * BLOCK, CH), F32) for size in sizes]
+    if vectors:
+        shapes.append(shape((BLOCK, CH), F32))
     return call(
-        assemble_kernel,
-        "s" + "v" * len(parts),
-        "v",
-        [shape((count, width * len(parts), CH), F32)],
+        functools.partial(assemble_kernel, sizes),
+        "svv",
+        "v" * len(shapes),
+        shapes,
         [],
         name,
-        1 << 20,
+        4 << 30,
         6 << 20,
-    )(position, *parts)[0]
+    )(position, *pieces)
 
 
 def body(
+    paired,
     features,
     crop_ids,
     cotangent,
@@ -1212,20 +1364,20 @@
 ):
     _, local, pixels = features.shape
     devices = lax.axis_size("chan")
-    copies = lax.axis_size("dp")
     index = lax.axis_index("chan").astype(jnp.int32)
     tiles = pixels // (TILE * TILE)
     slots = tiles if devices == 1 else tiles // 2
-    paired = devices == 2 and copies == 16
-    links = Links()
-    turn = lax.axis_index("dp").astype(jnp.int32)
-    core, down, near = turn & 1, (turn >> 1) & 1, (turn >> 2) & 1
-    piece = core * 4 + down * 2 + near
-    position = jnp.stack([index, piece, core, index * 8 + piece])
+    if paired:
+        core, down, near = [lax.axis_index(a).astype(jnp.int32) for a in ("core", "y", "near")]
+        quad = down * 2 + near
+        piece = core * 4 + quad
+    else:
+        core = quad = jnp.int32(0)
+    position = jnp.stack([index, core, quad])
 
     def exchange(parts):
         if paired:
-            return [parts[0], links.chan(parts[1])]
+            return [parts[0], swap(parts[1], "chan")]
         if devices == 2:
             parts = [jnp.where(index == 0, parts[k], parts[1 - k]) for k in range(2)]
         moved = lax.all_to_all(jnp.stack(parts), "chan", 0, 0)
@@ -1233,7 +1385,7 @@
 
     def give_back(parts):
         if paired:
-            return [parts[0], links.chan(parts[1])]
+            return [parts[0], swap(parts[1], "chan")]
         whole = parts[0].reshape(parts[0].shape[0], devices, local)
         moved = lax.all_to_all(jnp.transpose(whole, (1, 0, 2)), "chan", 0, 0)
         parts = [moved[at] for at in range(devices)]
@@ -1273,53 +1425,95 @@
     )
     small = jnp.stack([query_weight, key_weight, value_weight, proj_weight])
     if paired:
-        weight1 = links.gather_eighths(conv1_weight, piece)
-        weight2 = links.gather_eighths(conv2_weight, piece)
-        par_parts = [vectors, links.chan(vectors)]
+        eighth = local // 8
+        part = lax.dynamic_slice_in_dim(conv1_weight, piece * eighth, eighth, 1)
+        eighth1 = swap(part, "chan")
+        part = lax.dynamic_slice_in_dim(conv2_weight, piece * eighth, eighth, 1)
+        eighth2 = swap(part, "chan")
+        par_parts = [vectors, swap(vectors, "chan")]
     else:
         par_parts = [lax.all_gather(vectors, "chan", axis=1, tiled=True)]
         weight1 = [lax.all_gather(conv1_weight, "chan", axis=1, tiled=True)]
-        weight2 = [lax.all_gather(conv2_weight, "chan", axis=1, tiled=True)]
     tables, packed = pack_first(
         position, crop_ids[0], widened(features[0]), devices, slots, "pack_features"
     )
     feature_parts = exchange(narrowed(packed))
+    if paired:
+        eighth1, par_parts[1] = after((eighth1, par_parts[1]), packed[1])
+        mine = to_all(eighth1, QUAD, 4)
+        weight1 = [conv1_weight, mine, swap(mine, "core")]
     packed = pack(
         position, tables[0], widened(cotangent[0]), False, devices, slots, "pack_cotangent"
     )
     packed = list(packed)
     if paired:
-        small, packed[1], _ = lax.optimization_barrier((small, packed[1], feature_parts[1]))
-        weight3 = links.gather_halves(small, core)
+        eighth2, small = after((eighth2, small), feature_parts[1], weight1[1], packed[1])
+        weight2 = [conv2_weight, to_all(eighth2, ("core",) + QUAD, 8)]
+        part = lax.dynamic_slice_in_dim(small, core * (local // 2), local // 2, 1)
+        own_small = swap(part, "chan")
     else:
+        weight2 = [lax.all_gather(conv2_weight, "chan", axis=1, tiled=True)]
         weight3 = [lax.all_gather(small, "chan", axis=1, tiled=True)]
-    tangent_parts = exchange(narrowed(packed))
+        tangent_parts = exchange(narrowed(packed))
     par, feats, pad1, hidden, pad2, stats1, stats2 = first(
         position, tables, par_parts, feature_parts, weight1, slots
     )
+    if paired:
+        own_small, packed[1] = after((own_small, packed[1]), pad2)
+        tangent_parts = [packed[0], swap(packed[1], "chan")]
+        weight3 = [small, own_small, swap(own_small, "core")]
     resid, normed, stats3 = second(position, tables, par, feats, pad2, weight2, slots)
-    out_parts, small_grads, (vecs3, resid_grad, grad2) = attention(
+    if paired:
+        weight3 = after(weight3, normed)
+    out_parts, small_grads, (vecs3, grad2) = attention(
         position, tables, par, normed, resid, stats3, tangent_parts, weight3, slots
     )
     out_parts = give_back(out_parts)
-    output = unpack_lanes(out_parts, False, BF16, "unpack_output")
-    grads2 = weight_grad(position, pad2, grad2, paired, slots, "conv2_weight_grad")
-    grad1, vecs2 = middle(position, tables, par, stats2, grad2, weight2, hidden, slots)
-    grads1 = weight_grad(position, pad1, grad1, paired, slots, "conv1_weight_grad")
-    in_parts, vecs1 = last(
-        position, tables, par, stats1, feats, grad1, weight1, resid_grad, len(feature_parts), slots
-    )
-    in_parts = give_back(in_parts)
-    input_grad = unpack_lanes(in_parts, True, F32, "unpack_input_grad")
-
-    vecs = vecs1 + vecs2 + vecs3
     if paired:
-        small_grads = assemble(position, links.reduce(small_grads), "small_grads")
-        weight2_grad = assemble(position, links.reduce(grads2), "conv2_grads")
-        weight1_grad = assemble(position, links.reduce(grads1), "conv1_grads")
-        vecs = links.total(vecs)
-        vecs = lax.dynamic_slice_in_dim(vecs, index * local, local, 1)
+        resid_grad = grad2
+        halves = weight_grad(
+            position, pad2, grad2, True, slots, "conv2_weight_grad", 8, small_grads
+        )
+        chain2 = Reduction(halves, 8, 13)
+        grad2 = after(grad2, halves[1])
+        grad1, vecs2 = middle(position, tables, par, stats2, grad2, weight2, hidden, slots)
+        back = functools.partial(last, position, tables, par, stats1, (vecs2, vecs3), feats)
+        sent = chain2.advance(grad1, out_parts[1])
+        halves = weight_grad(
+            position, pad1, after(grad1, sent), True, slots, "conv1_weight_grad", 5
+        )
+        sent = chain2.advance(halves[1])
+        chain1 = Reduction(after(halves, sent), 5, 9)
+        grad1 = after(grad1, sent, halves[1])
+        in_other, _ = back(grad1, weight1, resid_grad, 1, slots)
+        sent = chain1.advance(in_other, chain2.state)
+        in_got = swap(in_other, "chan")
+        grad1 = after(grad1, sent, in_other)
+        in_own, vecs_own = back(grad1, weight1, resid_grad, 0, slots)
+        sent = chain1.advance(in_own), chain2.advance(in_own)
+        output = unpack_lanes(after(out_parts, sent), False, BF16, "unpack_output")
+        rows = in_own.shape[0]
+        vecs = vecs_own + in_got[rows : rows + 16].astype(F32)
+        sent = chain1.advance(output, in_got, vectors=vecs), chain2.advance(output)
+        in_parts = after([in_own, in_got], sent)
+        input_grad = unpack_lanes(in_parts, True, F32, "unpack_input_grad")
+        sent = chain1.advance(input_grad), chain2.advance(input_grad)
+        sent = chain1.advance()
+        small_grads = assemble(
+            position, after(chain2.pieces, sent), [0, 0, 0, 0, 9], False, "conv2_grads"
+        )
+        small_grads, weight2_grad = small_grads[:4], small_grads[4]
+        weight1_grad, vecs = assemble(position, chain1.pieces, [9], True, "conv1_grads")
+        vecs = vecs[:16, :local]
     else:
+        output = unpack_lanes(out_parts, False, BF16, "unpack_output")
+        grads2 = weight_grad(position, pad2, grad2, False, slots, "conv2_weight_grad")
+        grad1, vecs2 = middle(position, tables, par, stats2, grad2, weight2, hidden, slots)
+        grads1 = weight_grad(position, pad1, grad1, False, slots, "conv1_weight_grad")
+        in_all, vecs1 = last(
+            position, tables, par, stats1, (vecs2, vecs3), feats, grad1, weight1, grad2, 0, slots
+        )
+        input_grad = unpack_lanes(give_back([in_all]), True, F32, "unpack_input_grad")
 
         def total(grad, axis):
             part = lax.psum_scatter(grad, "chan", scatter_dimension=axis, tiled=True)
@@ -1328,8 +1522,8 @@
         small_grads, weight2_grad, weight1_grad = [
             total(g[0], 1) for g in (small_grads, grads2, grads1)
         ]
-        vecs = total(vecs, 1)
-    gq, gk, gv, gp = [small_grads[k] for k in range(4)]
+        vecs = total(vecs1, 1)
+    gq, gk, gv, gp = small_grads if paired else [small_grads[k] for k in range(4)]
     return (
         output[None],
         input_grad[None],
@@ -1354,12 +1548,17 @@
 
 
 def solution(mesh):
-    canvas = P("dp", "chan", None)
+    paired = mesh.shape["dp"] == 16 and mesh.shape["chan"] == 2
+    rows = "dp"
+    if paired:
+        rows = ("far", "near", "y", "core")
+        mesh = jax.sharding.Mesh(mesh.devices.reshape((2,) * 5), rows + ("chan",))
+    canvas = P(rows, "chan", None)
     vector = P("chan")
     conv = P(None, "chan", None)
     matrix = P("chan", None)
     placed = (
-        (canvas, P("dp", None, None), canvas)
+        (canvas, P(rows, None, None), canvas)
         + (vector, vector, conv, vector, vector, vector, conv, vector, vector, vector)
         + (matrix, vector, matrix, matrix, vector, matrix, vector)
     )
@@ -1367,4 +1566,4 @@
         (canvas, canvas, vector, vector, conv, vector, vector, vector, conv, vector)
         + (vector, vector, matrix, vector, matrix, matrix, vector, matrix, vector)
     )
-    return jax.shard_map(body, mesh=mesh, in_specs=placed, out_specs=results, check_vma=False)
+    return jax.shard_map(functools.partial(body, paired), mesh=mesh, in_specs=placed, out_specs=results, check_vma=False)

time: 549 us -> 355 us (0.65)
  waiting for transfers between devices: 225 us -> 67 us
  starting transfers between devices: 71.6 us -> 52.4 us
  Pallas kernels: 222 us -> 207 us
    ppermute x79 -> x38, waiting for transfers between devices: 225 us -> 66.9 us  [the longest x20 51.5 us: swap(): return lax.ppermute(value, axis, [(0, 1), (1, 0)])]
    ppermute x79 -> x38, starting transfers between devices: 71.6 us -> 44.3 us  [the longest x18 24.1 us: from_quad(): lax.ppermute(value, ('near', 'y'), [(at, at ^ bits) for at in range(4)])]
    pallas_call x6, Pallas kernels: 69.2 us -> 60.3 us  [the longest x2 29.3 us: weight_grad(): call(functools.partial(weight_grad_kernel, paired, first, extra), 'svv' +...]
    all_to_all x0 -> x2, starting transfers between devices: none -> 8.11 us  [to_all(): lax.all_to_all(jnp.broadcast_to(value[None], (count,) + value.shape), axe...]
  transfers between devices with their start and end apart: 79 -> 40, of which waited for: 39 -> 14; matrix products, arithmetic and copies ran while one was open for 2% -> 2% of each run, Pallas kernels for 29% -> 40%
where the time goes in v2:
time: 355 us; the launch traced here: 348 us
  Pallas kernels  207 us (58%)
  waiting for transfers between devices  67 us (19%)
  starting transfers between devices  52.4 us (15%)
  local copies, waits for them, and re-layouts  14.4 us (4%)
  other arithmetic  4.61 us (1%)
    ppermute x20, waiting for transfers between devices, swap(): return lax.ppermute(value, axis, [(0, 1), (1, 0)])  51.5 us
    pallas_call x1, Pallas kernels, attention(): call(functools.partial(attention_kernel, parts, outs, len(weight)), 'ssss...  50.1 us
    pallas_call x2, Pallas kernels, weight_grad(): call(functools.partial(weight_grad_kernel, paired, first, extra), 'svv' +...  29.3 us
    pallas_call x1, Pallas kernels, first(): call(functools.partial(first_kernel, len(parts), len(weight)), 'sss' + 'v...  24.9 us
    pallas_call x1, Pallas kernels, second(): call(functools.partial(second_kernel, len(weight)), 'sssvvh' + 'h' * len(...  24.7 us
    pallas_call x2, Pallas kernels, last(): call(functools.partial(last_kernel, whose, len(weight)), 'sssvvvvhhh' + '...  24.1 us
    ppermute x18, starting transfers between devices, from_quad(): lax.ppermute(value, ('near', 'y'), [(at, at ^ bits) for at in range(4)])  24.1 us
    ppermute x20, starting transfers between devices, swap(): return lax.ppermute(value, axis, [(0, 1), (1, 0)])  20.2 us
  transfers between devices with their start and end apart: 40, of which 14 were waited for; matrix products, arithmetic and copies ran while one was open for 2% of the time, Pallas kernels for 40%

profile of v2, /device:TPU:0, one launch (start us, length us, event | category | flops | bytes accessed | tf_op | source)
XLA Modules:
  0.0 347.7 jit_solution(9481075273526103773)
XLA Ops:
  0.7 1.5 stack.82.rest_2_
  2.2 3.0 collective-permute-start.2
  7.3 2.1 collective-permute-start.4
  10.0 8.8 %pack_features.1 = (s32[64]{0:T(128)}, s32[64]{0:T(128)}, s32[16]{0:T(128)}, s32[16]{0:T(128)}, bf16[2048,256]{1,0:T(8,128)(2,1)}, /*index=5*/bf16[2048,256]{1,0:T(8,128)(2,1)}) custom-call(s32[3]{0:T(128)} %pad_add_fusion.position, s32[64,64]{1,0:T(8,128)} %bitcast.62, s32[2578]{0:T(1024)} %constant.33.clone.table, bf16[256,4096]{1,0:T(8,128)(2,1)} %bitcast.60), custom_call_target="tpu_custom_call" | custom-call | flops 4294967296 | bytes 6291456 | tf_op jit(solution)/shard_map/pack_features/pallas_call | solution.py:431
  20.1 4.3 %all-to-all-start = ((bf16[4,9,32,512]{3,2,1,0:T(8,128)(2,1)}), bf16[4,9,32,512]{3,2,1,0:T(8,128)(2,1)S(1)}, u32[]{:S(2)}, u32[]{:S(2)}) async-start(bf16[4,9,32,512]{3,2,1,0:T(8,128)(2,1)} %broadcast_in_dim.8), calls=%async_computation | async-start | bytes 2359296 | tf_op jit(solution)/shard_map/all_to_all | solution.py:1220
  24.4 5.3 %pack_cotangent.1 = (bf16[2048,256]{1,0:T(8,128)(2,1)}, bf16[2048,256]{1,0:T(8,128)(2,1)}) custom-call(s32[3]{0:T(128)} %pad_add_fusion.position, s32[64]{0:T(128)} %get-tuple-element.124.slot_tile, bf16[256,4096]{1,0:T(8,128)(2,1)} %bitcast.61), custom_call_target="tpu_custom_call" | custom-call | flops 42949672960 | bytes 6291456 | tf_op jit(solution)/shard_map/pack_cotangent/pallas_call | solution.py:449
  30.8 12.8 %collective-permute-done.rest_1_ = bf16[2048,256]{1,0:T(8,128)(2,1)S(1)} collective-permute-done((bf16[2048,256]{1,0:T(8,128)(2,1)}, bf16[2048,256]{1,0:T(8,128)(2,1)S(1)}, u32[]{:S(2)}, u32[]{:S(2)}) %collective-permute-start) | collective-permute-done | bytes 1048608 | tf_op jit(solution)/shard_map/ppermute | solution.py:1216
  43.6 1.9 broadcast_in_dim.9
  45.4 3.8 %all-to-all-start.1 = ((bf16[8,9,32,512]{3,2,1,0:T(8,128)(2,1)}), bf16[8,9,32,512]{3,2,1,0:T(8,128)(2,1)S(1)}, u32[]{:S(2)}, u32[]{:S(2)}) async-start(bf16[8,9,32,512]{3,2,1,0:T(8,128)(2,1)} %broadcast_in_dim.9), calls=%async_computation.1 | async-start | bytes 4718592 | tf_op jit(solution)/shard_map/all_to_all | solution.py:1220
  52.6 24.9 %conv1_forward.1 = (f32[16,512]{1,0:T(8,128)}, bf16[2048,512]{1,0:T(8,128)(2,1)}, bf16[10,10,32,512]{3,2,1,0:T(8,128)(2,1)}, bf16[64,32,512]{2,1,0:T(8,128)(2,1)...) custom-call(s32[3]{0:T(128)} %pad_add_fusion.position, ...), custom_call_target="tpu_custom_call" | custom-call | flops 9663676416 | bytes 20971520 | tf_op jit(solution)/shard_map/conv1_forward/pallas_call | solution.py:597
  78.2 1.4 copy-done
  79.6 24.7 %conv2_forward.1 = (bf16[2048,512]{1,0:T(8,128)(2,1)}, bf16[2048,512]{1,0:T(8,128)(2,1)}, f32[2,32,512]{2,1,0:T(8,128)}) custom-call(s32[3]{0:T(128)} %pad_add_fusion.position, s32[64]{0:T(128)} %get-tuple-element.124.slot_tile, s32[64]{0:T(128)} %get-tuple-element.125.slot_crop, f32[16,512]{1,0:T(8,128)} %get-tuple-element.132.par.rest_0_, ...), custom_call_target="tpu_custom_call" | custom-call | flops 9663676416 | bytes 16777216 | tf_op jit(solution)/shard_map/conv2_forward/pallas_call | solution.py:682
  104.4 50.1 %attention.1 = (bf16[2048,256]{1,0:T(8,128)(2,1)}, bf16[2048,256]{1,0:T(8,128)(2,1)}, bf16[1024,512]{1,0:T(8,128)(2,1)}, bf16[1024,512]{1,0:T(8,128)(2,1)}, f32[...) custom-call(s32[3]{0:T(128)} %pad_add_fusion.position, s32[64]{0:T(128)} %get-tuple-element.124.slot_tile, ...), custom_call_target="tpu_custom_call" | custom-call | flops 32212254720 | bytes 25165824 | tf_op jit(solution)/shard_map/attention/pallas_call | solution.py:914
  154.5 1.9 copy-done.7
  156.4 1.2 copy-done.17
  159.0 16.0 %conv2_weight_grad.1 = (bf16[3328,512]{1,0:T(8,128)(2,1)S(1)}, bf16[3328,512]{1,0:T(8,128)(2,1)S(1)}) custom-call(s32[3]{0:T(128)S(1)} %copy-done.6, bf16[10,10,32,512]{3,2,1,0:T(8,128)(2,1)S(1)} %copy-done.12, bf16[10,10,32,512]{3,2,1,0:T(8,128)(2,1)S(1)} %copy-done.7, bf16[1024,512]{1,0:T(8,128)(2,1)S(1)} %copy-done.17, bf16[1024,512]{1,0:T(8,128)(2,1)S(1)} %copy-done.18), custom_call_target="tpu_custom_call" | custom-call | flops 9663676416 | bytes 12582912 | tf_op jit(solution)/shard_map/conv2_weight_grad/pallas_call | solution.py:978
  175.1 1.5 collective-permute-start.8
  176.6 19.3 %conv2_input_grad.1 = (bf16[10,10,32,512]{3,2,1,0:T(8,128)(2,1)S(1)}, f32[2,16,256]{2,1,0:T(8,128)S(1)}) custom-call(s32[3]{0:T(128)S(1)} %copy-done.6, s32[64]{0:T(128)S(1)} %copy-done.20, s32[64]{0:T(128)S(1)} %copy-done.21, f32[16,512]{1,0:T(8,128)S(1)} %copy-done.15, f32[2,32,512]{2,1,0:T(8,128)S(1)} %copy-done.19, ...), custom_call_target="tpu_custom_call" | custom-call | flops 9663676416 | bytes 16777216 | tf_op jit(solution)/shard_map/conv2_input_grad/pallas_call | solution.py:1091
  195.9 4.7 %collective-permute-done.8.rest_1_ = bf16[2048,256]{1,0:T(8,128)(2,1)S(1)} collective-permute-done((bf16[2048,256]{1,0:T(8,128)(2,1)S(1)}, bf16[2048,256]{1,0:T(8,128)(2,1)S(1)}, u32[]{:S(2)}, u32[]{:S(2)}) %collective-permute-start.8) | collective-permute-done | bytes 1048608 | tf_op jit(solution)/shard_map/ppermute | solution.py:1216
  201.2 1.5 collective-permute-start.10
  204.6 2.1 collective-permute-start.11
  206.7 13.3 %conv1_weight_grad.1 = (bf16[2304,512]{1,0:T(8,128)(2,1)S(1)}, bf16[2304,512]{1,0:T(8,128)(2,1)S(1)}) custom-call(s32[3]{0:T(128)S(1)} %copy-done.6, bf16[10,10,32,512]{3,2,1,0:T(8,128)(2,1)S(1)} %copy-done.13, bf16[10,10,32,512]{3,2,1,0:T(8,128)(2,1)S(1)} %get-tuple-element.179.grad.rest_1_), custom_call_target="tpu_custom_call" | custom-call | flops 9663676416 | bytes 12582912 | tf_op jit(solution)/shard_map/conv1_weight_grad/pallas_call | solution.py:978
  220.2 5.8 %collective-permute-done.10 = bf16[1024,512]{1,0:T(8,128)(2,1)S(1)} collective-permute-done((bf16[1024,512]{1,0:T(8,128)(2,1)S(1)}, bf16[1024,512]{1,0:T(8,128)(2,1)S(1)}, u32[]{:S(2)}, u32[]{:S(2)}) %collective-permute-start.10) | collective-permute-done | bytes 1048608 | tf_op jit(solution)/shard_map/ppermute | solution.py:1216
  226.4 1.5 collective-permute-start.18
  228.9 2.5 collective-permute-start.15
  231.4 12.4 %conv1_input_grad.2 = (bf16[2080,256]{1,0:T(8,128)(2,1)S(1)}, f32[16,256]{1,0:T(8,128)}) custom-call(s32[3]{0:T(128)S(1)} %copy-done.6, s32[64]{0:T(128)S(1)} %copy-done.20, s32[64]{0:T(128)S(1)} %copy-done.21, f32[16,512]{1,0:T(8,128)S(1)} %copy-done.15, f32[2,32,512]{2,1,0:T(8,128)S(1)} %copy-done.11, f32[2,16,256]{2,1,0:T(8,128)S(1)} %get-tuple-element.173.vecs2, ...), custom_call_target="tpu_custom_call" | custom-call | flops 4831838208 | bytes 10485760 | tf_op jit(solution)/shard_map/conv1_input_grad/pallas_call | solution.py:1178
  246.8 2.0 collective-permute-start.20
  248.8 1.5 collective-permute-start.19
  250.3 11.7 %conv1_input_grad.3 = (f32[2048,256]{1,0:T(8,128)S(1)}, f32[16,256]{1,0:T(8,128)S(1)}) custom-call(s32[3]{0:T(128)S(1)} %copy-done.6, s32[64]{0:T(128)S(1)} %copy-done.20, s32[64]{0:T(128)S(1)} %copy-done.21, f32[16,512]{1,0:T(8,128)S(1)} %copy-done.15, f32[2,32,512]{2,1,0:T(8,128)S(1)} %copy-done.11, f32[2,16,256]{2,1,0:T(8,128)S(1)} %get-tuple-element.173.vecs2, ...), custom_call_target="tpu_custom_call" | custom-call | flops 4831838208 | bytes 10485760 | tf_op jit(solution)/shard_map/conv1_input_grad/pallas_call | solution.py:1178
  262.5 8.0 %collective-permute-done.23.rest_1_ = bf16[2080,256]{1,0:T(8,128)(2,1)S(1)} collective-permute-done((bf16[2080,256]{1,0:T(8,128)(2,1)S(1)}, bf16[2080,256]{1,0:T(8,128)(2,1)S(1)}, u32[]{:S(2)}, u32[]{:S(2)}) %collective-permute-start.23) | collective-permute-done | bytes 1064992 | tf_op jit(solution)/shard_map/ppermute | solution.py:1216
  270.4 3.4 collective-permute-start.28
  273.9 8.9 %collective-permute-done.19 = bf16[640,512]{1,0:T(8,128)(2,1)S(1)} collective-permute-done((bf16[640,512]{1,0:T(8,128)(2,1)S(1)}, bf16[640,512]{1,0:T(8,128)(2,1)S(1)}, u32[]{:S(2)}, u32[]{:S(2)}) %collective-permute-start.19) | collective-permute-done | bytes 655392 | tf_op jit(solution)/shard_map/ppermute | solution.py:1216
  284.2 1.2 collective-permute-start.25
  285.4 1.7 collective-permute-start.24
  287.2 4.5 %unpack_output.1 = bf16[256,4096]{1,0:T(8,128)(2,1)} custom-call(s32[3]{0:T(128)S(1)} %copy-done.6, s32[64]{0:T(128)S(1)} %copy-done.20, bf16[2048,256]{1,0:T(8,128)(2,1)S(1)} %copy-done.10, bf16[2048,256]{1,0:T(8,128)(2,1)S(1)} %collective-permute-done.8.rest_1_), custom_call_target="tpu_custom_call" | custom-call | flops 4294967296 | bytes 8388608 | tf_op jit(solution)/shard_map/unpack_output/pallas_call | solution.py:500
  292.5 1.2 collective-permute-start.35
  293.7 1.7 collective-permute-start.34
  295.4 1.9 collective-permute-done.24
  297.6 1.7 collective-permute-start.29
  299.3 9.5 %unpack_input_grad.1 = f32[256,4096]{1,0:T(8,128)} custom-call(s32[3]{0:T(128)S(1)} %copy-done.6, s32[64]{0:T(128)S(1)} %copy-done.20, f32[2048,256]{1,0:T(8,128)S(1)} %get-tuple-element.212.rest_0_, bf16[2080,256]{1,0:T(8,128)(2,1)S(1)} %collective-permute-done.23.rest_1_), custom_call_target="tpu_custom_call" | custom-call | flops 4294967296 | bytes 8388608 | tf_op jit(solution)/shard_map/unpack_input_grad/pallas_call | solution.py:500
  308.8 7.7 %collective-permute-done.29 = bf16[320,512]{1,0:T(8,128)(2,1)S(1)} collective-permute-done((bf16[320,512]{1,0:T(8,128)(2,1)S(1)}, bf16[320,512]{1,0:T(8,128)(2,1)S(1)}, u32[]{:S(2)}, u32[]{:S(2)}) %collective-permute-start.29) | collective-permute-done | bytes 327712 | tf_op jit(solution)/shard_map/ppermute | solution.py:1216
  316.6 5.9 %collective-permute-start.32 = (bf16[320,512]{1,0:T(8,128)(2,1)S(1)}, bf16[320,512]{1,0:T(8,128)(2,1)S(1)}, u32[]{:S(2)}, u32[]{:S(2)}) collective-permute-start(bf16[320,512]{1,0:T(8,128)(2,1)S(1)} %add_convert_fusion.5), channel_id=1, source_target_pairs={{0,12},{4,8},{8,4},{12,0},{1,13},{5,9},{9,5},{13,1},{2,14},{6,10},... | collective-permute-start | bytes 983048 | tf_op jit(solution)/shard_map/ppermute | solution.py:1228
  323.2 7.9 %collective-permute-done.32 = bf16[320,512]{1,0:T(8,128)(2,1)S(1)} collective-permute-done((bf16[320,512]{1,0:T(8,128)(2,1)S(1)}, bf16[320,512]{1,0:T(8,128)(2,1)S(1)}, u32[]{:S(2)}, u32[]{:S(2)}) %collective-permute-start.32) | collective-permute-done | bytes 327712 | tf_op jit(solution)/shard_map/ppermute | solution.py:1228
  331.1 4.0 %collective-permute-done.31 = bf16[320,512]{1,0:T(8,128)(2,1)S(1)} collective-permute-done((bf16[320,512]{1,0:T(8,128)(2,1)S(1)}, bf16[320,512]{1,0:T(8,128)(2,1)S(1)}, u32[]{:S(2)}, u32[]{:S(2)}) %collective-permute-start.31) | collective-permute-done | bytes 327712 | tf_op jit(solution)/shard_map/ppermute | solution.py:1228
  335.1 1.5 collective-permute-done.30
  337.4 2.4 collective-permute-done.33.other
  339.8 3.0 conv1_grads.1
  343.5 3.8 %conv2_grads.1 = (f32[256,512]{1,0:T(8,128)}, f32[256,512]{1,0:T(8,128)}, f32[256,512]{1,0:T(8,128)}, f32[256,512]{1,0:T(8,128)}, f32[9,256,512]{2,1,0:T(8,128)}) custom-call(s32[3]{0:T(128)S(1)} %copy-done.6, bf16[1664,512]{1,0:T(8,128)(2,1)S(1)} %constant_dynamic-update-slice_fusion.mine, bf16[1664,512]{1,0:T(8,128)(2,1)S(1)} %collective-permute-done.37.other), custom_call_target="tpu_custom_call" | custom-call | flops 4294967296 | bytes 6291456 | tf_op jit(solution)/shard_map/conv2_grads/pallas_call | solution.py:1330
  (174 shorter events, 22.1 us)
Async XLA Ops:
  2.2 16.7 %collective-permute-start.2 = (f32[16,256]{1,0:T(8,128)S(1)}, f32[16,256]{1,0:T(8,128)S(1)}, u32[]{:S(2)}, u32[]{:S(2)}) collective-permute-start(f32[16,256]{1,0:T(8,128)S(1)} %stack.82.rest_2_), channel_id=1, source_target_pairs={{0,1},{1,0},{2,3},{3,2},{4,5},{5,4},{6,7},{7,6},{8,9},{9,8},{10,11... | collective-permute-start | bytes 49160 | tf_op jit(solution)/shard_map/ppermute | solution.py:1216
  6.2 12.7 %collective-permute-start.1 = (bf16[9,32,512]{2,1,0:T(8,128)(2,1)S(1)}, bf16[9,32,512]{2,1,0:T(8,128)(2,1)S(1)}, u32[]{:S(2)}, u32[]{:S(2)}) collective-permute-start(bf16[9,32,512]{2,1,0:T(8,128)(2,1)S(1)} %constant_dynamic-slice_fusion.2), channel_id=1, source_target_pairs={{0,1},{1,0},{2,3},{3,2},{4,5},{5,4},{6,7},{7,6},{8,9},{9,8},{10,11... | collective-permute-start | bytes 884744 | tf_op jit(solution)/shard_map/ppermute | solution.py:1216
  7.3 23.5 %collective-permute-start.4 = (bf16[9,32,512]{2,1,0:T(8,128)(2,1)S(1)}, bf16[9,32,512]{2,1,0:T(8,128)(2,1)S(1)}, u32[]{:S(2)}, u32[]{:S(2)}) collective-permute-start(bf16[9,32,512]{2,1,0:T(8,128)(2,1)S(1)} %constant_dynamic-slice_fusion.1), channel_id=1, source_target_pairs={{0,1},{1,0},{2,3},{3,2},{4,5},{5,4},{6,7},{7,6},{8,9},{9,8},{10,11... | collective-permute-start | bytes 884744 | tf_op jit(solution)/shard_map/ppermute | solution.py:1216
  18.8 24.8 %collective-permute-start = (bf16[2048,256]{1,0:T(8,128)(2,1)}, bf16[2048,256]{1,0:T(8,128)(2,1)S(1)}, u32[]{:S(2)}, u32[]{:S(2)}) collective-permute-start(bf16[2048,256]{1,0:T(8,128)(2,1)} %get-tuple-element.129), channel_id=1, source_target_pairs={{0,1},{1,0},{2,3},{3,2},{4,5},{5,4},{6,7},{7,6},{8,9},{9,8},{10,11... | collective-permute-start | bytes 3145736 | tf_op jit(solution)/shard_map/ppermute | solution.py:1216
  20.1 23.5 %all-to-all-start = ((bf16[4,9,32,512]{3,2,1,0:T(8,128)(2,1)}), bf16[4,9,32,512]{3,2,1,0:T(8,128)(2,1)S(1)}, u32[]{:S(2)}, u32[]{:S(2)}) async-start(bf16[4,9,32,512]{3,2,1,0:T(8,128)(2,1)} %broadcast_in_dim.8), calls=%async_computation | async-start | bytes 2359296 | tf_op jit(solution)/shard_map/all_to_all | solution.py:1220
  45.4 32.7 %all-to-all-start.1 = ((bf16[8,9,32,512]{3,2,1,0:T(8,128)(2,1)}), bf16[8,9,32,512]{3,2,1,0:T(8,128)(2,1)S(1)}, u32[]{:S(2)}, u32[]{:S(2)}) async-start(bf16[8,9,32,512]{3,2,1,0:T(8,128)(2,1)} %broadcast_in_dim.9), calls=%async_computation.1 | async-start | bytes 4718592 | tf_op jit(solution)/shard_map/all_to_all | solution.py:1220
  49.3 3.4 collective-permute-start.3
  50.8 26.7 %collective-permute-start.5 = (bf16[4,128,512]{2,1,0:T(8,128)(2,1)S(1)}, bf16[4,128,512]{2,1,0:T(8,128)(2,1)}, u32[]{:S(2)}, u32[]{:S(2)}) collective-permute-start(bf16[4,128,512]{2,1,0:T(8,128)(2,1)S(1)} %constant_dynamic-slice_fusion), channel_id=1, source_target_pairs={{0,1},{1,0},{2,3},{3,2},{4,5},{5,4},{6,7},{7,6},{8,9},{9,8},{10,11... | collective-permute-start | bytes 1572872 | tf_op jit(solution)/shard_map/ppermute | solution.py:1216
  52.6 24.9 %copy-start.34 = (bf16[2048,256]{1,0:T(8,128)(2,1)S(1)}, bf16[2048,256]{1,0:T(8,128)(2,1)}, u32[]{:S(2)}) copy-start(bf16[2048,256]{1,0:T(8,128)(2,1)} %get-tuple-element.142) | copy-start | bytes 3145732
  77.5 26.8 %collective-permute-start.6 = (bf16[2048,256]{1,0:T(8,128)(2,1)S(1)}, bf16[2048,256]{1,0:T(8,128)(2,1)}, u32[]{:S(2)}, u32[]{:S(2)}) collective-permute-start(bf16[2048,256]{1,0:T(8,128)(2,1)S(1)} %copy-done.34), channel_id=1, source_target_pairs={{0,1},{1,0},{2,3},{3,2},{4,5},{5,4},{6,7},{7,6},{8,9},{9,8},{10,11... | collective-permute-start | bytes 3145736 | tf_op jit(solution)/shard_map/ppermute | solution.py:1216
  78.1 26.2 %collective-permute-start.7 = (bf16[4,128,512]{2,1,0:T(8,128)(2,1)}, bf16[4,128,512]{2,1,0:T(8,128)(2,1)}, u32[]{:S(2)}, u32[]{:S(2)}) collective-permute-start(bf16[4,128,512]{2,1,0:T(8,128)(2,1)} %collective-permute-done.5.rest_7_), channel_id=1, source_target_pairs={{0,2},{2,0},{1,3},{3,1},{4,6},{6,4},{5,7},{7,5},{8,10},{10,8},{9,1... | collective-permute-start | bytes 1572872 | tf_op jit(solution)/shard_map/ppermute | solution.py:1216
  104.3 50.2 %copy-start.6 = (s32[3]{0:T(128)S(1)}, s32[3]{0:T(128)}, u32[]{:S(2)}) copy-start(s32[3]{0:T(128)} %pad_add_fusion.position) | copy-start | bytes 40
  104.3 50.2 %copy-start.12 = (bf16[10,10,32,512]{3,2,1,0:T(8,128)(2,1)S(1)}, bf16[10,10,32,512]{3,2,1,0:T(8,128)(2,1)}, u32[]{:S(2)}) copy-start(bf16[10,10,32,512]{3,2,1,0:T(8,128)(2,1)} %get-tuple-element.134.pad_hbm.active) | copy-start | bytes 9830404
  175.0 25.7 %collective-permute-start.9 = (bf16[3328,512]{1,0:T(8,128)(2,1)S(1)}, bf16[3328,512]{1,0:T(8,128)(2,1)S(1)}, u32[]{:S(2)}, u32[]{:S(2)}) collective-permute-start(bf16[3328,512]{1,0:T(8,128)(2,1)S(1)} %get-tuple-element.154), channel_id=1, source_target_pairs={{0,2},{2,0},{1,3},{3,1},{4,6},{6,4},{5,7},{7,5},{8,10},{10,8},{9,1... | collective-permute-start | bytes 10223624 | tf_op jit(solution)/shard_map/ppermute | solution.py:1216
  175.1 25.6 %collective-permute-start.8 = (bf16[2048,256]{1,0:T(8,128)(2,1)S(1)}, bf16[2048,256]{1,0:T(8,128)(2,1)S(1)}, u32[]{:S(2)}, u32[]{:S(2)}) collective-permute-start(bf16[2048,256]{1,0:T(8,128)(2,1)S(1)} %copy-done.36), channel_id=1, source_target_pairs={{0,1},{1,0},{2,3},{3,2},{4,5},{5,4},{6,7},{7,6},{8,9},{9,8},{10,11... | collective-permute-start | bytes 3145736 | tf_op jit(solution)/shard_map/ppermute | solution.py:1216
  201.2 24.8 %collective-permute-start.10 = (bf16[1024,512]{1,0:T(8,128)(2,1)S(1)}, bf16[1024,512]{1,0:T(8,128)(2,1)S(1)}, u32[]{:S(2)}, u32[]{:S(2)}) collective-permute-start(bf16[1024,512]{1,0:T(8,128)(2,1)S(1)} %get-tuple-element.234), channel_id=1, source_target_pairs={{0,1},{1,0},{2,3},{3,2},{4,5},{5,4},{6,7},{7,6},{8,9},{9,8},{10,11... | collective-permute-start | bytes 3145736 | tf_op jit(solution)/shard_map/ppermute | solution.py:1216
  203.2 17.0 %collective-permute-start.13 = (bf16[320,512]{1,0:T(8,128)(2,1)S(1)}, bf16[320,512]{1,0:T(8,128)(2,1)S(1)}, u32[]{:S(2)}, u32[]{:S(2)}) collective-permute-start(bf16[320,512]{1,0:T(8,128)(2,1)S(1)} %get-tuple-element.230), channel_id=1, source_target_pairs={{0,12},{4,8},{8,4},{12,0},{1,13},{5,9},{9,5},{13,1},{2,14},{6,10},... | collective-permute-start | bytes 983048 | tf_op jit(solution)/shard_map/ppermute | solution.py:1228
  204.0 16.1 %collective-permute-start.12 = (bf16[320,512]{1,0:T(8,128)(2,1)S(1)}, bf16[320,512]{1,0:T(8,128)(2,1)S(1)}, u32[]{:S(2)}, u32[]{:S(2)}) collective-permute-start(bf16[320,512]{1,0:T(8,128)(2,1)S(1)} %get-tuple-element.231), channel_id=1, source_target_pairs={{0,4},{4,0},{8,12},{12,8},{1,5},{5,1},{9,13},{13,9},{2,6},{6,2},{1... | collective-permute-start | bytes 983048 | tf_op jit(solution)/shard_map/ppermute | solution.py:1228
  204.6 15.6 %collective-permute-start.11 = (bf16[320,512]{1,0:T(8,128)(2,1)S(1)}, bf16[320,512]{1,0:T(8,128)(2,1)S(1)}, u32[]{:S(2)}, u32[]{:S(2)}) collective-permute-start(bf16[320,512]{1,0:T(8,128)(2,1)S(1)} %get-tuple-element.232), channel_id=1, source_target_pairs={{0,8},{4,12},{8,0},{12,4},{1,9},{5,13},{9,1},{13,5},{2,10},{6,14},... | collective-permute-start | bytes 983048 | tf_op jit(solution)/shard_map/ppermute | solution.py:1228
  206.7 24.7 %copy-start.5 = (bf16[9,256,512]{2,1,0:T(8,128)(2,1)S(1)}, bf16[9,256,512]{2,1,0:T(8,128)(2,1)}, u32[]{:S(2)}) copy-start(bf16[9,256,512]{2,1,0:T(8,128)(2,1)} %rest_3_.3) | copy-start | bytes 7077892
  206.7 24.7 %copy-start.8 = (bf16[10,10,32,512]{3,2,1,0:T(8,128)(2,1)S(1)}, bf16[10,10,32,512]{3,2,1,0:T(8,128)(2,1)}, u32[]{:S(2)}) copy-start(bf16[10,10,32,512]{3,2,1,0:T(8,128)(2,1)} %get-tuple-element.155.grad.pad_hbm.rest_2_) | copy-start | bytes 9830404
  206.7 24.7 %copy-start.9 = (bf16[2048,512]{1,0:T(8,128)(2,1)S(1)}, bf16[2048,512]{1,0:T(8,128)(2,1)}, u32[]{:S(2)}) copy-start(bf16[2048,512]{1,0:T(8,128)(2,1)} %get-tuple-element.133.feats.rest_0_) | copy-start | bytes 6291460
  220.1 23.8 %copy-start.25 = (bf16[320,512]{1,0:T(8,128)(2,1)}, bf16[320,512]{1,0:T(8,128)(2,1)S(1)}, u32[]{:S(2)}) copy-start(bf16[320,512]{1,0:T(8,128)(2,1)S(1)} %collective-permute-done.13) | copy-start | bytes 983044
  226.3 18.3 %collective-permute-start.14 = (bf16[2304,512]{1,0:T(8,128)(2,1)S(1)}, bf16[2304,512]{1,0:T(8,128)(2,1)S(1)}, u32[]{:S(2)}, u32[]{:S(2)}) collective-permute-start(bf16[2304,512]{1,0:T(8,128)(2,1)S(1)} %get-tuple-element.171), channel_id=1, source_target_pairs={{0,2},{2,0},{1,3},{3,1},{4,6},{6,4},{5,7},{7,5},{8,10},{10,8},{9,1... | collective-permute-start | bytes 7077896 | tf_op jit(solution)/shard_map/ppermute | solution.py:1216
  226.4 17.5 %collective-permute-start.18 = (bf16[160,512]{1,0:T(8,128)(2,1)S(1)}, bf16[160,512]{1,0:T(8,128)(2,1)S(1)}, u32[]{:S(2)}, u32[]{:S(2)}) collective-permute-start(bf16[160,512]{1,0:T(8,128)(2,1)S(1)} %add_convert_fusion.23), channel_id=1, source_target_pairs={{0,1},{1,0},{2,3},{3,2},{4,5},{5,4},{6,7},{7,6},{8,9},{9,8},{10,11... | collective-permute-start | bytes 491528 | tf_op jit(solution)/shard_map/ppermute | solution.py:1216
  227.9 16.6 %collective-permute-start.17 = (bf16[256,512]{1,0:T(8,128)(2,1)S(1)}, bf16[256,512]{1,0:T(8,128)(2,1)S(1)}, u32[]{:S(2)}, u32[]{:S(2)}) collective-permute-start(bf16[256,512]{1,0:T(8,128)(2,1)S(1)} %get-tuple-element.241), channel_id=1, source_target_pairs={{0,12},{4,8},{8,4},{12,0},{1,13},{5,9},{9,5},{13,1},{2,14},{6,10},... | collective-permute-start | bytes 786440 | tf_op jit(solution)/shard_map/ppermute | solution.py:1228
  228.7 15.8 %collective-permute-start.16 = (bf16[256,512]{1,0:T(8,128)(2,1)S(1)}, bf16[256,512]{1,0:T(8,128)(2,1)S(1)}, u32[]{:S(2)}, u32[]{:S(2)}) collective-permute-start(bf16[256,512]{1,0:T(8,128)(2,1)S(1)} %get-tuple-element.242), channel_id=1, source_target_pairs={{0,4},{4,0},{8,12},{12,8},{1,5},{5,1},{9,13},{13,9},{2,6},{6,2},{1... | collective-permute-start | bytes 786440 | tf_op jit(solution)/shard_map/ppermute | solution.py:1228
  228.9 15.7 %collective-permute-start.15 = (bf16[256,512]{1,0:T(8,128)(2,1)S(1)}, bf16[256,512]{1,0:T(8,128)(2,1)S(1)}, u32[]{:S(2)}, u32[]{:S(2)}) collective-permute-start(bf16[256,512]{1,0:T(8,128)(2,1)S(1)} %get-tuple-element.243), channel_id=1, source_target_pairs={{0,8},{4,12},{8,0},{12,4},{1,9},{5,13},{9,1},{13,5},{2,10},{6,14},... | collective-permute-start | bytes 786440 | tf_op jit(solution)/shard_map/ppermute | solution.py:1228
  243.9 26.5 %collective-permute-start.23 = (bf16[2080,256]{1,0:T(8,128)(2,1)S(1)}, bf16[2080,256]{1,0:T(8,128)(2,1)S(1)}, u32[]{:S(2)}, u32[]{:S(2)}) collective-permute-start(bf16[2080,256]{1,0:T(8,128)(2,1)S(1)} %get-tuple-element.176), channel_id=1, source_target_pairs={{0,1},{1,0},{2,3},{3,2},{4,5},{5,4},{6,7},{7,6},{8,9},{9,8},{10,11... | collective-permute-start | bytes 3194888 | tf_op jit(solution)/shard_map/ppermute | solution.py:1216
  245.2 28.6 %collective-permute-start.22 = (bf16[256,512]{1,0:T(8,128)(2,1)S(1)}, bf16[256,512]{1,0:T(8,128)(2,1)S(1)}, u32[]{:S(2)}, u32[]{:S(2)}) collective-permute-start(bf16[256,512]{1,0:T(8,128)(2,1)S(1)} %get-tuple-element.235), channel_id=1, source_target_pairs={{0,12},{4,8},{8,4},{12,0},{1,13},{5,9},{9,5},{13,1},{2,14},{6,10},... | collective-permute-start | bytes 786440 | tf_op jit(solution)/shard_map/ppermute | solution.py:1228
  245.8 28.0 %collective-permute-start.21 = (bf16[256,512]{1,0:T(8,128)(2,1)S(1)}, bf16[256,512]{1,0:T(8,128)(2,1)S(1)}, u32[]{:S(2)}, u32[]{:S(2)}) collective-permute-start(bf16[256,512]{1,0:T(8,128)(2,1)S(1)} %get-tuple-element.236), channel_id=1, source_target_pairs={{0,4},{4,0},{8,12},{12,8},{1,5},{5,1},{9,13},{13,9},{2,6},{6,2},{1... | collective-permute-start | bytes 786440 | tf_op jit(solution)/shard_map/ppermute | solution.py:1228
  246.8 27.0 %collective-permute-start.20 = (bf16[256,512]{1,0:T(8,128)(2,1)S(1)}, bf16[256,512]{1,0:T(8,128)(2,1)S(1)}, u32[]{:S(2)}, u32[]{:S(2)}) collective-permute-start(bf16[256,512]{1,0:T(8,128)(2,1)S(1)} %get-tuple-element.237), channel_id=1, source_target_pairs={{0,8},{4,12},{8,0},{12,4},{1,9},{5,13},{9,1},{13,5},{2,10},{6,14},... | collective-permute-start | bytes 786440 | tf_op jit(solution)/shard_map/ppermute | solution.py:1228
  248.8 34.0 %collective-permute-start.19 = (bf16[640,512]{1,0:T(8,128)(2,1)S(1)}, bf16[640,512]{1,0:T(8,128)(2,1)S(1)}, u32[]{:S(2)}, u32[]{:S(2)}) collective-permute-start(bf16[640,512]{1,0:T(8,128)(2,1)S(1)} %get-tuple-element.239), channel_id=1, source_target_pairs={{0,1},{1,0},{2,3},{3,2},{4,5},{5,4},{6,7},{7,6},{8,9},{9,8},{10,11... | collective-permute-start | bytes 1966088 | tf_op jit(solution)/shard_map/ppermute | solution.py:1216
  262.5 24.7 %copy-start.10 = (bf16[2048,256]{1,0:T(8,128)(2,1)S(1)}, bf16[2048,256]{1,0:T(8,128)(2,1)}, u32[]{:S(2)}) copy-start(bf16[2048,256]{1,0:T(8,128)(2,1)} %get-tuple-element.197.rest_0_) | copy-start | bytes 3145732
  270.4 21.3 %collective-permute-start.28 = (bf16[416,512]{1,0:T(8,128)(2,1)S(1)}, bf16[416,512]{1,0:T(8,128)(2,1)S(1)}, u32[]{:S(2)}, u32[]{:S(2)}) collective-permute-start(bf16[416,512]{1,0:T(8,128)(2,1)S(1)} %pad_maximum_fusion.2), channel_id=1, source_target_pairs={{0,16},{16,0},{1,17},{17,1},{2,18},{18,2},{3,19},{19,3},{4,20},{20... | collective-permute-start | bytes 1277960 | tf_op jit(solution)/shard_map/ppermute | solution.py:1216
  283.0 9.4 %collective-permute-start.27 = (bf16[128,512]{1,0:T(8,128)(2,1)S(1)}, bf16[128,512]{1,0:T(8,128)(2,1)S(1)}, u32[]{:S(2)}, u32[]{:S(2)}) collective-permute-start(bf16[128,512]{1,0:T(8,128)(2,1)S(1)} %add_convert_fusion.25), channel_id=1, source_target_pairs={{0,1},{1,0},{2,3},{3,2},{4,5},{5,4},{6,7},{7,6},{8,9},{9,8},{10,11... | collective-permute-start | bytes 393224 | tf_op jit(solution)/shard_map/ppermute | solution.py:1216
  283.7 10.1 %collective-permute-start.26 = (bf16[160,512]{1,0:T(8,128)(2,1)S(1)}, bf16[160,512]{1,0:T(8,128)(2,1)S(1)}, u32[]{:S(2)}, u32[]{:S(2)}) collective-permute-start(bf16[160,512]{1,0:T(8,128)(2,1)S(1)} %get-tuple-element.244), channel_id=1, source_target_pairs={{0,12},{4,8},{8,4},{12,0},{1,13},{5,9},{9,5},{13,1},{2,14},{6,10},... | collective-permute-start | bytes 491528 | tf_op jit(solution)/shard_map/ppermute | solution.py:1228
  284.2 11.2 %collective-permute-start.25 = (bf16[160,512]{1,0:T(8,128)(2,1)S(1)}, bf16[160,512]{1,0:T(8,128)(2,1)S(1)}, u32[]{:S(2)}, u32[]{:S(2)}) collective-permute-start(bf16[160,512]{1,0:T(8,128)(2,1)S(1)} %get-tuple-element.245), channel_id=1, source_target_pairs={{0,4},{4,0},{8,12},{12,8},{1,5},{5,1},{9,13},{13,9},{2,6},{6,2},{1... | collective-permute-start | bytes 491528 | tf_op jit(solution)/shard_map/ppermute | solution.py:1228
  285.4 11.9 %collective-permute-start.24 = (bf16[160,512]{1,0:T(8,128)(2,1)S(1)}, bf16[160,512]{1,0:T(8,128)(2,1)S(1)}, u32[]{:S(2)}, u32[]{:S(2)}) collective-permute-start(bf16[160,512]{1,0:T(8,128)(2,1)S(1)} %get-tuple-element.246), channel_id=1, source_target_pairs={{0,8},{4,12},{8,0},{12,4},{1,9},{5,13},{9,1},{13,5},{2,10},{6,14},... | collective-permute-start | bytes 491528 | tf_op jit(solution)/shard_map/ppermute | solution.py:1228
  291.9 30.9 %collective-permute-start.36 = (bf16[416,512]{1,0:T(8,128)(2,1)S(1)}, bf16[416,512]{1,0:T(8,128)(2,1)S(1)}, u32[]{:S(2)}, u32[]{:S(2)}) collective-permute-start(bf16[416,512]{1,0:T(8,128)(2,1)S(1)} %add_convert_fusion.4), channel_id=1, source_target_pairs={{0,12},{4,8},{8,4},{12,0},{1,13},{5,9},{9,5},{13,1},{2,14},{6,10},... | collective-permute-start | bytes 1277960 | tf_op jit(solution)/shard_map/ppermute | solution.py:1228
  292.5 30.7 %collective-permute-start.35 = (bf16[416,512]{1,0:T(8,128)(2,1)S(1)}, bf16[416,512]{1,0:T(8,128)(2,1)S(1)}, u32[]{:S(2)}, u32[]{:S(2)}) collective-permute-start(bf16[416,512]{1,0:T(8,128)(2,1)S(1)} %add_convert_fusion.4), channel_id=1, source_target_pairs={{0,4},{4,0},{8,12},{12,8},{1,5},{5,1},{9,13},{13,9},{2,6},{6,2},{1... | collective-permute-start | bytes 1277960 | tf_op jit(solution)/shard_map/ppermute | solution.py:1228
  293.7 29.4 %collective-permute-start.34 = (bf16[416,512]{1,0:T(8,128)(2,1)S(1)}, bf16[416,512]{1,0:T(8,128)(2,1)S(1)}, u32[]{:S(2)}, u32[]{:S(2)}) collective-permute-start(bf16[416,512]{1,0:T(8,128)(2,1)S(1)} %add_convert_fusion.4), channel_id=1, source_target_pairs={{0,8},{4,12},{8,0},{12,4},{1,9},{5,13},{9,1},{13,5},{2,10},{6,14},... | collective-permute-start | bytes 1277960 | tf_op jit(solution)/shard_map/ppermute | solution.py:1228
  297.6 19.0 %collective-permute-start.29 = (bf16[320,512]{1,0:T(8,128)(2,1)S(1)}, bf16[320,512]{1,0:T(8,128)(2,1)S(1)}, u32[]{:S(2)}, u32[]{:S(2)}) collective-permute-start(bf16[320,512]{1,0:T(8,128)(2,1)S(1)} %fusion.1), channel_id=1, source_target_pairs={{0,16},{16,0},{1,17},{17,1},{2,18},{18,2},{3,19},{19,3},{4,20},{20... | collective-permute-start | bytes 983048 | tf_op jit(solution)/shard_map/ppermute | solution.py:1216
  316.6 14.5 %collective-permute-start.32 = (bf16[320,512]{1,0:T(8,128)(2,1)S(1)}, bf16[320,512]{1,0:T(8,128)(2,1)S(1)}, u32[]{:S(2)}, u32[]{:S(2)}) collective-permute-start(bf16[320,512]{1,0:T(8,128)(2,1)S(1)} %add_convert_fusion.5), channel_id=1, source_target_pairs={{0,12},{4,8},{8,4},{12,0},{1,13},{5,9},{9,5},{13,1},{2,14},{6,10},... | collective-permute-start | bytes 983048 | tf_op jit(solution)/shard_map/ppermute | solution.py:1228
  322.5 12.6 %collective-permute-start.31 = (bf16[320,512]{1,0:T(8,128)(2,1)S(1)}, bf16[320,512]{1,0:T(8,128)(2,1)S(1)}, u32[]{:S(2)}, u32[]{:S(2)}) collective-permute-start(bf16[320,512]{1,0:T(8,128)(2,1)S(1)} %add_convert_fusion.5), channel_id=1, source_target_pairs={{0,4},{4,0},{8,12},{12,8},{1,5},{5,1},{9,13},{13,9},{2,6},{6,2},{1... | collective-permute-start | bytes 983048 | tf_op jit(solution)/shard_map/ppermute | solution.py:1228
  322.8 13.8 %collective-permute-start.30 = (bf16[320,512]{1,0:T(8,128)(2,1)S(1)}, bf16[320,512]{1,0:T(8,128)(2,1)S(1)}, u32[]{:S(2)}, u32[]{:S(2)}) collective-permute-start(bf16[320,512]{1,0:T(8,128)(2,1)S(1)} %add_convert_fusion.5), channel_id=1, source_target_pairs={{0,8},{4,12},{8,0},{12,4},{1,9},{5,13},{9,1},{13,5},{2,10},{6,14},... | collective-permute-start | bytes 983048 | tf_op jit(solution)/shard_map/ppermute | solution.py:1228
  336.7 3.1 collective-permute-start.33
  336.9 6.6 %collective-permute-start.37 = (bf16[1664,512]{1,0:T(8,128)(2,1)S(1)}, bf16[1664,512]{1,0:T(8,128)(2,1)S(1)}, u32[]{:S(2)}, u32[]{:S(2)}) collective-permute-start(bf16[1664,512]{1,0:T(8,128)(2,1)S(1)} %constant_dynamic-update-slice_fusion.mine), channel_id=1, source_target_pairs={{0,2},{2,0},{1,3},{3,1},{4,6},{6,4},{5,7},{7,5},{8,10},{10,8},{9,1... | collective-permute-start | bytes 5111816 | tf_op jit(solution)/shard_map/ppermute | solution.py:1216
  (37 other events, 425.3 us)

commit v3 on v2

--- a/solution.py
+++ b/solution.py
@@ -33,8 +33,63 @@
     ]
 
 
+PITCH = 8
+QUERIES = 8
+KEYS = 8
+
+
+def window_cost(starts, sizes, slots):
+    total = 0.0
+    for block in range(0, slots, QUERIES):
+        inside = [
+            (starts <= at) & (at < starts + sizes) for at in (block, block + QUERIES - 1)
+        ]
+        low = (starts * inside[0]).sum(axis=-1) // 2 * 2
+        high = ((starts + sizes) * inside[1]).sum(axis=-1)
+        total = total + (high - low + KEYS - 1) // KEYS + 0.25
+    return total
+
+
+def best_starts(sizes, slots):
+    layouts = sizes.shape[0]
+    masks = np.arange(1 << (CROPS - 1), dtype=np.int32)
+    bits = ((masks[None, :] >> np.arange(CROPS)[:, None]) & 1).astype(np.float32)
+    picks = []
+    for row in sizes.astype(np.float32):
+        filled, squares = row @ bits, (row * row) @ bits
+        cost = np.abs(squares - (row * row).sum() / 2) + 1e6 * np.abs(filled - slots)
+        picks.append(bits[:, np.argpartition(cost, 4)[:4]].T)
+        picks[-1] = picks[-1][(picks[-1] @ row) == slots]
+        picks[-1] = picks[-1][np.arange(4) % len(picks[-1])]
+    halves = np.array(picks, np.int32)
+    halves = np.stack([1 - halves, halves], axis=2)
+    held = halves * sizes[:, None, None, :]
+    draw = np.random.RandomState(0)
+    best = np.full((layouts, 4, 2), 1e9, np.float32)
+    chosen = np.zeros(held.shape, np.int32)
+    for trial in range(20):
+        key = draw.rand(CROPS)[None, None, None, :] + 0.0 * held
+        if trial == 0:
+            key = -held + 0.01 * key
+        elif trial < 8:
+            key = key + 2.0 * (held % QUERIES != 0)
+        order = np.argsort(key, axis=-1)
+        ordered = np.take_along_axis(held, order, axis=-1)
+        begin = np.cumsum(ordered, axis=-1) - ordered
+        starts = np.zeros_like(held)
+        np.put_along_axis(starts, order, begin, axis=-1)
+        cost = window_cost(starts, held, slots)
+        better = cost < best
+        best = np.where(better, cost, best)
+        chosen = np.where(better[..., None], starts, chosen)
+    pick = np.argmin(best.max(axis=2), axis=1)
+    rows = np.arange(layouts)
+    owner, starts = halves[rows, pick, 1], chosen[rows, pick]
+    return np.where(owner == 1, starts[:, 1] + slots, starts[:, 0])
+
+
 @functools.lru_cache(maxsize=None)
-def owner_tables(devices, units, slots):
+def start_tables(devices, units, slots):
     layouts = band_layouts(units)
     rank = np.zeros(1 << (units - 1), np.int32)
     for number, sizes in enumerate(layouts):
@@ -43,36 +98,26 @@
     sizes = np.array(
         [[r * c for r in rows for c in cols] for rows in layouts for cols in layouts], np.int32
     )
-    owners = np.zeros(sizes.shape, np.int32)
     if devices == 2:
-        masks = np.arange(1 << (CROPS - 1), dtype=np.int32)
-        bits = ((masks[None, :] >> np.arange(CROPS)[:, None]) & 1).astype(np.float32)
-        for at, row in enumerate(sizes.astype(np.float32)):
-            filled = row @ bits
-            squares = (row * row) @ bits
-            cost = np.abs(squares - (row * row).sum() / 2) + 1e6 * np.abs(filled - slots)
-            owners[at] = bits[:, int(np.argmin(cost))].astype(np.int32)
+        starts = best_starts(sizes, slots)
     else:
+        starts = np.zeros(sizes.shape, np.int32)
         for at, row in enumerate(sizes):
             loads = [0] * devices
             for crop in sorted(range(CROPS), key=lambda c: -row[c]):
                 device = loads.index(min(loads))
-                owners[at, crop] = device
+                starts[at, crop] = device * slots + loads[device]
                 loads[device] += int(row[crop])
-    for device in range(devices):
-        assert (np.where(owners == device, sizes, 0).sum(axis=1) <= slots).all()
-    return rank, owners
+    assert ((starts % slots) + sizes <= slots).all() and starts.max() < 256
+    return rank, starts
 
 
 def packed_tables(devices, units, slots):
-    rank, owners = owner_tables(devices, units, slots)
-    shifts = np.arange(0, 32, 4, dtype=np.int64)
-    words = (owners.reshape(-1, 2, 8).astype(np.int64) << shifts).sum(axis=2)
+    rank, starts = start_tables(devices, units, slots)
+    shifts = np.arange(0, 32, 8, dtype=np.int64)
+    words = (starts.reshape(-1, 4, 4).astype(np.int64) << shifts).sum(axis=2)
     words = np.where(words >= 1 << 31, words - (1 << 32), words)
     return np.concatenate([rank, words.reshape(-1).astype(np.int32)])
-
-
-WINDOWS = (8, 16, 24, 32)
 
 
 def write_plan(devices, slots, ids, table, slot_tile, slot_crop, starts, ends):
@@ -93,11 +138,7 @@
         return ids[0, TILE * step]
 
     layout = code(row_id) * layouts + code(col_id)
-    words = [table[(1 << (units - 1)) + 2 * layout + half] for half in range(2)]
-    heights, widths = [], []
-    for band in range(BANDS):
-        heights.append(sum(jnp.where(row_id(k) // BANDS == band, 1, 0) for k in range(units)))
-        widths.append(sum(jnp.where(col_id(k) % BANDS == band, 1, 0) for k in range(units)))
+    words = [table[(1 << (units - 1)) + 4 * layout + part] for part in range(4)]
     if devices * slots > count:
 
         def clear(at, carry):
@@ -106,17 +147,10 @@
             return carry
 
         lax.fori_loop(0, devices * slots, clear, 0)
-    filled = [jnp.int32(device * slots) for device in range(devices)]
     for crop in range(CROPS):
-        owner = lax.shift_right_logical(words[crop // 8], jnp.int32(4 * (crop % 8))) & 15
-        size = heights[crop // BANDS] * widths[crop % BANDS]
-        start = filled[0]
-        for device in range(1, devices):
-            start = jnp.where(owner == device, filled[device], start)
+        start = lax.shift_right_logical(words[crop // 4], jnp.int32(8 * (crop % 4))) & 255
         starts[crop] = start
         ends[crop] = start
-        for device in range(devices):
-            filled[device] = filled[device] + jnp.where(owner == device, size, 0)
 
     def place(row, carry):
         for col in range(units):
@@ -407,21 +441,31 @@
                     value = raster[col, pl.ds(pl.multiple_of(start + row * side, TILE), TILE), :]
                     value = jnp.where(keep, value, 0.0)
                     if by_pixel:
-                        stage[col, pl.ds(row * TILE * slots + slot, TILE, stride=slots), :] = value
+                        pitch = slots + PITCH
+                        to = pl.ds(row * TILE * pitch + slot, TILE, stride=pitch)
+                        stage[col, to, :] = value
                     else:
                         at = pl.multiple_of(slot * (TILE * TILE) + row * TILE, TILE)
                         stage[col, pl.ds(at, TILE), :] = value
             return carry
 
         lax.fori_loop(0, slots, step, 0)
-        for at in range(0, stage.shape[1], chunk):
+        size = slots if by_pixel else TILE * TILE
+        pitch = size + PITCH if by_pixel else size
+        for number in range(out.shape[0] // size):
             for col in range(cols):
                 span = slice(col * 128, (col + 1) * 128)
-                out[at : at + chunk, span] = stage[col, at : at + chunk, :].astype(BF16)
+                value = stage[col, number * pitch : number * pitch + size, :]
+                out[number * size : (number + 1) * size, span] = value.astype(BF16)
 
 
 def pack_base(position, number, devices, slots):
     return (position[0] ^ number if devices == 2 else number) * slots
+
+
+def pack_scratch(local, pixels, slots):
+    rows = TILE * TILE * (slots + PITCH)
+    return [vmem((local // 128, pixels, 128), F32), vmem((local // 128, rows, 128), F32)]
 
 
 def pack_first(position, ids, signal, devices, slots, name):
@@ -435,7 +479,7 @@
         [shape((devices * slots,), jnp.int32)] * 2
         + [shape((CROPS,), jnp.int32)] * 2
         + [shape((rows, local), BF16)] * devices,
-        [vmem((local // 128, pixels, 128), F32), vmem((local // 128, rows, 128), F32)],
+        pack_scratch(local, pixels, slots),
         name,
         4 << 30,
         6 << 20,
@@ -451,7 +495,7 @@
         "ssv",
         "v" * devices,
         [shape((rows, local), BF16)] * devices,
-        [vmem((local // 128, pixels, 128), F32), vmem((local // 128, rows, 128), F32)],
+        pack_scratch(local, pixels, slots),
         name,
         40 << 30,
         6 << 20,
@@ -465,10 +509,13 @@
     chunk = 512
     cols = local // 128
     for number, part in enumerate(ins):
-        for at in range(0, stage.shape[1], chunk):
+        size = slots if by_pixel else TILE * TILE
+        pitch = size + PITCH if by_pixel else size
+        for at in range(part.shape[0] // size):
             for col in range(cols):
                 span = slice(col * 128, (col + 1) * 128)
-                stage[col, at : at + chunk, :] = part[at : at + chunk, span].astype(F32)
+                value = part[at * size : (at + 1) * size, span]
+                stage[col, at * pitch : at * pitch + size, :] = value.astype(F32)
 
         def step(slot, carry):
             tile = slot_tile[pack_base(position, number, len(ins), slots) + slot]
@@ -480,7 +527,7 @@
                     to = pl.ds(pl.multiple_of(start + row * side, TILE), TILE)
                     for col in range(cols):
                         if by_pixel:
-                            at = pl.ds(row * TILE * slots + slot, TILE, stride=slots)
+                            at = pl.ds(row * TILE * pitch + slot, TILE, stride=pitch)
                         else:
                             first = pl.multiple_of(slot * (TILE * TILE) + row * TILE, TILE)
                             at = pl.ds(first, TILE)
@@ -502,7 +549,7 @@
         "ss" + "v" * len(parts),
         "v",
         [shape((local, pixels), dtype)],
-        [vmem((local // 128, pixels, 128), F32), vmem((local // 128, rows, 128), F32)],
+        pack_scratch(local, pixels, slots),
         name,
         4 << 30,
         8 << 20,
@@ -644,13 +691,17 @@
         total = conv_rows(pad, weight, row, slots, NT, False) + par[C2 : C2 + 1, :]
         total = total + feats[at, :].astype(F32)
         for col in range(CH // 128):
-            resid[col, at, :] = total[:, col * 128 : (col + 1) * 128]
+            for x in range(TILE):
+                to = pl.multiple_of((row * TILE + x) * (slots + PITCH), 8)
+                part = total[x * slots : (x + 1) * slots, col * 128 : (col + 1) * 128]
+                resid[col, pl.ds(to, slots), :] = part
         return carry
 
     lax.fori_loop(0, TILE, step, 0)
 
     def slab(at, lanes):
-        return resid[lanes.start // 128, pl.ds(pl.multiple_of(at * slots, slots), slots), :]
+        begin = pl.multiple_of(at * (slots + PITCH), 8)
+        return resid[lanes.start // 128, pl.ds(begin, slots), :]
 
     mean, inverse = slab_stats(pixels, slots, slab, same)
     stats3[0], stats3[1] = mean, inverse
@@ -661,7 +712,7 @@
         at = pl.ds(pl.multiple_of(slot * pixels, pixels), pixels)
         centre, factor = rows_scr[0, pl.ds(slot, 1)], rows_scr[1, pl.ds(slot, 1)]
         for col, lanes in enumerate(lanes_of(CH)):
-            value = resid[col, pl.ds(slot, pixels, stride=slots), :]
+            value = resid[col, pl.ds(slot, pixels, stride=slots + PITCH), :]
             resid_tile[at, lanes] = value.astype(BF16)
             scaled = (value - centre[:, lanes]) * factor[:, lanes]
             normed[at, lanes] = (scaled + bias[:, lanes]).astype(BF16)
@@ -685,7 +736,7 @@
         "hhv",
         [shape((rows, CH), BF16), shape((rows, CH), BF16), shape((2, slots, CH), F32)],
         [
-            vmem((CH // 128, rows, 128), F32),
+            vmem((CH // 128, pixels * (slots + PITCH), 128), F32),
             vmem((rows, CH), BF16),
             vmem((rows, CH), BF16),
             vmem(pad.shape, BF16),
@@ -701,14 +752,16 @@
 
 
 def attention_kernel(parts, outs, count, position, slot_tile, slot_crop, starts, ends, *rest):
-    par, normed, resid, stats3 = rest[:4]
+    par, normed, resid_hbm, stats3 = rest[:4]
     tangent_parts, rest = rest[4 : 4 + parts], rest[4 + parts :]
     pieces, rest = rest[:count], rest[count:]
-    out_parts, rest = rest[:outs], rest[outs:]
-    grad_outs, rest = rest[:outs], rest[outs:]
+    out_hbm, rest = rest[:outs], rest[outs:]
+    grads_hbm, rest = rest[:outs], rest[outs:]
     vecs_out, pad = rest[:2]
     (tangent, query, key, value, mixed_grad, mixed, query_grad, key_grad, value_grad) = rest[2:11]
-    normed_grad, by_tile, rows_scr, weight, key_crop, work, vecs, weight_sem = rest[11:]
+    normed_grad, by_tile, rows_scr, weight, key_crop, work, vecs = rest[11:18]
+    scores_scr, prob_grads, sums, weight_sem, sem, resid = rest[18:24]
+    grad_outs = rest[24:]
     load_weight = WeightLoad(position, pieces, weight, weight_sem)
     load_weight.start()
     wq, wk, wv, wp = (weight.at[k] for k in range(4))
@@ -717,8 +770,8 @@
     slots = rows // pixels
     me = position[0]
     base = me * slots
-    block = 256
-    per_block = block // pixels
+    per_block = QUERIES
+    block = per_block * pixels
     plan = Plan(me, slot_tile, slot_crop, slots)
     lane_slot = lax.broadcasted_iota(jnp.int32, (1, rows), 1) // pixels
     crops = jnp.zeros((1, rows), jnp.int32)
@@ -726,11 +779,28 @@
         crops = jnp.where(lane_slot == slot, slot_crop[base + slot], crops)
     key_crop[...] = crops
 
-    def put(columns, part):
-        tangent[:, columns] = part
-
-    load_full(tangent_parts, me, BF16, put)
+    half = CH // outs
+    columns = [pl.ds(0, CH)]
+    if outs == 2:
+        columns = [pl.ds(pl.multiple_of((me ^ k) * half, half), half) for k in range(2)]
+    load_tangent = [
+        pltpu.make_async_copy(part, tangent.at[:, columns[k]], sem.at[k])
+        for k, part in enumerate(tangent_parts)
+    ]
+    load_resid = pltpu.make_async_copy(resid_hbm, resid, sem.at[2])
+    save_out = [
+        pltpu.make_async_copy(query.at[:, columns[k]], part, sem.at[3 + k])
+        for k, part in enumerate(out_hbm)
+    ]
+    save_grads = [
+        pltpu.make_async_copy(part, grads_hbm[k], sem.at[5 + k])
+        for k, part in enumerate(grad_outs)
+    ]
+    for copy in load_tangent + [load_resid]:
+        copy.start()
     load_weight.wait()
+    for copy in load_tangent:
+        copy.wait()
 
     def project(at, carry):
         span = pl.ds(pl.multiple_of(at * block, block), block)
@@ -749,50 +819,69 @@
 
     lax.fori_loop(0, rows // block, project, 0)
 
-    def attend(at, begin, width):
+    def attend_step(at, carry):
         span = pl.ds(pl.multiple_of(at * block, block), block)
-        keys = pl.ds(pl.multiple_of(begin, 128), width)
-        q, g = query[span, :], mixed_grad[span, :]
-        scores = lax.dot_general(q, key[keys, :], NT, preferred_element_type=F32) * SCALE
-        down = lax.broadcasted_iota(jnp.int32, (block, 1), 0) // pixels
-        own_crop = jnp.zeros((block, 1), jnp.int32)
-        for slot in range(per_block):
-            own_crop = jnp.where(down == slot, slot_crop[base + at * per_block + slot], own_crop)
-        scores = jnp.where(own_crop == key_crop[:, keys], scores, -1e30)
-        top = jnp.max(scores, axis=1, keepdims=True)
-        exponent = jnp.exp(scores - top)
-        total = jnp.sum(exponent, axis=1, keepdims=True)
-        prob = exponent * (1.0 / total)
-        rounded = prob.astype(BF16)
-        mixed[span, :] = jnp.dot(
-            rounded, value[keys, :], preferred_element_type=F32
-        ).astype(BF16)
-        prob_grad = lax.dot_general(g, value[keys, :], NT, preferred_element_type=F32)
-        inner = jnp.sum(prob * prob_grad, axis=1, keepdims=True)
-        score_grad = (prob * (prob_grad - inner)).astype(BF16)
-        query_grad[span, :] = (
-            jnp.dot(score_grad, key[keys, :], preferred_element_type=F32) * SCALE
-        ).astype(BF16)
-        key_grad[keys, :] += lax.dot_general(score_grad, q, TN, preferred_element_type=F32)
-        value_grad[keys, :] += lax.dot_general(rounded, g, TN, preferred_element_type=F32)
-
-    def attend_step(at, carry):
         low_crop = slot_crop[base + at * per_block]
         high_crop = slot_crop[base + at * per_block + per_block - 1]
         low = starts[jnp.maximum(low_crop, 0)] - base
         low = jnp.where(low_crop < 0, at * per_block, low) // 2 * 2
         high = jnp.where(high_crop < 0, slots, ends[jnp.maximum(high_crop, 0)] - base)
-        kind = sum(jnp.where(high - low > width, 1, 0) for width in WINDOWS[:-1])
-        span = jnp.int32(WINDOWS[0])
-        for number, width in enumerate(WINDOWS):
-            span = jnp.where(kind == number, width, span)
-        begin = jnp.minimum(low, slots - span) * pixels
-        for number, width in enumerate(WINDOWS):
-
-            @pl.when(kind == number)
-            def _():
-                attend(at, begin, width * pixels)
-
+        count = (high - low + KEYS - 1) // KEYS
+        begin = jnp.minimum(low, slots - KEYS * count) * pixels
+        down = lax.broadcasted_iota(jnp.int32, (block, 1), 0) // pixels
+        own_crop = jnp.zeros((block, 1), jnp.int32)
+        for slot in range(per_block):
+            own_crop = jnp.where(down == slot, slot_crop[base + at * per_block + slot], own_crop)
+
+        def keys_of(number):
+            return pl.ds(pl.multiple_of(begin + number * (KEYS * pixels), 128), KEYS * pixels)
+
+        def score(number, top):
+            keys = keys_of(number)
+            scores = lax.dot_general(
+                query[span, :], key[keys, :], NT, preferred_element_type=F32
+            )
+            scores = jnp.where(own_crop == key_crop[:, keys], scores * SCALE, -1e30)
+            scores_scr[number] = scores
+            prob_grads[number] = lax.dot_general(
+                mixed_grad[span, :], value[keys, :], NT, preferred_element_type=F32
+            )
+            return jnp.maximum(top, jnp.max(scores, axis=1, keepdims=True))
+
+        top = lax.fori_loop(0, count, score, jnp.full((block, 1), -1e30, F32))
+
+        def weigh(number, carry):
+            total, inner = carry
+            exponent = jnp.exp(scores_scr[number] - top)
+            scores_scr[number] = exponent
+            total += jnp.sum(exponent, axis=1, keepdims=True)
+            inner += jnp.sum(exponent * prob_grads[number], axis=1, keepdims=True)
+            return total, inner
+
+        zero = jnp.zeros((block, 1), F32)
+        total, inner = lax.fori_loop(0, count, weigh, (zero, zero))
+        share = 1.0 / total
+        inner = inner * share
+        sums[...] = jnp.zeros_like(sums)
+
+        def spread_back(number, carry):
+            keys = keys_of(number)
+            prob = scores_scr[number] * share
+            rounded = prob.astype(BF16)
+            score_grad = (prob * (prob_grads[number] - inner)).astype(BF16)
+            sums[0] += jnp.dot(rounded, value[keys, :], preferred_element_type=F32)
+            sums[1] += jnp.dot(score_grad, key[keys, :], preferred_element_type=F32)
+            key_grad[keys, :] += lax.dot_general(
+                score_grad, query[span, :], TN, preferred_element_type=F32
+            )
+            value_grad[keys, :] += lax.dot_general(
+                rounded, mixed_grad[span, :], TN, preferred_element_type=F32
+            )
+            return carry
+
+        lax.fori_loop(0, count, spread_back, 0)
+        mixed[span, :] = sums[0].astype(BF16)
+        query_grad[span, :] = (sums[1] * SCALE).astype(BF16)
         return carry
 
     lax.fori_loop(0, rows // block, attend_step, 0)
@@ -811,34 +900,29 @@
         normed_grad[span, :] = total
         result = lax.dot_general(mixed[span, :], wp[...], NT, preferred_element_type=F32)
         result = (result + par[PB : PB + 1, :] + resid[span, :].astype(F32)).astype(BF16)
-        if outs == 1:
-            out_parts[0][span, :] = result
-        else:
-            mixed_scr = query
-            mixed_scr[span, :] = result
+        query[span, :] = result
         query_bias += jnp.sum(dq.astype(F32), axis=0, keepdims=True)
         value_bias += jnp.sum(dv.astype(F32), axis=0, keepdims=True)
         tangent_sum += jnp.sum(tangent[span, :].astype(F32), axis=0, keepdims=True)
         return query_bias, value_bias, tangent_sum
 
+    load_resid.wait()
     zero = jnp.zeros((1, CH), F32)
     query_bias, value_bias, tangent_sum = lax.fori_loop(
         0, rows // block, back, (zero, zero, zero)
     )
-    if outs == 2:
-        local = out_parts[0].shape[1]
-        own = pl.ds(pl.multiple_of(me * local, local), local)
-        other = pl.ds(pl.multiple_of((1 - me) * local, local), local)
-        out_parts[0][...] = query[:, own]
-        out_parts[1][...] = query[:, other]
+    for copy in save_out:
+        copy.start()
     left = normed[...]
     for number, grad in enumerate((query_grad, key, value)):
         total = lax.dot_general(grad[...], left, TN, preferred_element_type=F32)
         store_grad(total, grad_outs, work, position, number, 4, 4)
     total = lax.dot_general(tangent[...], mixed[...], TN, preferred_element_type=F32)
     store_grad(total, grad_outs, work, position, 3, 4, 4)
-
-    def sums(slot, carry):
+    for copy in save_grads:
+        copy.start()
+
+    def tile_sums(slot, carry):
         span = pl.ds(pl.multiple_of(slot * pixels, pixels), pixels)
         row = pl.ds(slot, 1)
         centre, factor = stats3[0, row], stats3[1, row]
@@ -852,7 +936,7 @@
         rows_scr[1, row] = jnp.concatenate(crosseds, axis=1)
         return carry
 
-    lax.fori_loop(0, slots, sums, 0)
+    lax.fori_loop(0, slots, tile_sums, 0)
     same = plan.same
     gain = par[G3 : G3 + 1, :]
     plain, crossed = rows_scr[0], rows_scr[1]
@@ -867,6 +951,7 @@
 
     def apply(slot, carry):
         span = pl.ds(pl.multiple_of(slot * pixels, pixels), pixels)
+        padded = pl.ds(pl.multiple_of(slot * (pixels + PITCH), 8), pixels)
         row = pl.ds(slot, 1)
         centre, factor = stats3[0, row], stats3[1, row]
         slope = factor * gain
@@ -876,7 +961,7 @@
             centred = resid[span, lanes].astype(F32) - centre[:, lanes]
             grad = normed_grad[span, lanes] * slope[:, lanes] - level[:, lanes]
             grad = grad - centred * tilt[:, lanes]
-            by_tile[col, span, :] = tangent[span, lanes].astype(F32) + grad
+            by_tile[col, padded, :] = tangent[span, lanes].astype(F32) + grad
         return carry
 
     lax.fori_loop(0, slots, apply, 0)
@@ -887,7 +972,7 @@
             at = row * TILE + col
             slab = jnp.concatenate(
                 [
-                    by_tile[c, pl.ds(at, slots, stride=pixels), :] for c in range(CH // 128)
+                    by_tile[c, pl.ds(at, slots, stride=pixels + PITCH), :] for c in range(CH // 128)
                 ],
                 axis=1,
             )
@@ -899,6 +984,8 @@
     vecs[C2 : C2 + 1, :] = lax.fori_loop(0, TILE, spread, zero)
     store_vectors(vecs, vecs_out, me)
     fill_halo(pad, plan)
+    for copy in save_out + save_grads:
+        copy.wait()
 
 
 def attention(position, tables, par, normed, resid, stats3, tangent_parts, weight, slots):
@@ -913,17 +1000,20 @@
     outs = len(out_shapes)
     result = call(
         functools.partial(attention_kernel, parts, outs, len(weight)),
-        "sssss" + "v" * (4 + parts) + "h" * len(weight),
-        "v" * (2 * outs + 2),
+        "sssssvvhv" + "h" * parts + "h" * len(weight),
+        "h" * (2 * outs) + "vv",
         out_shapes
         + grad_shapes(4, outs == 2)
         + [vector_shape(outs == 2), shape(pad, BF16)],
         [vmem((rows, CH), BF16)] * 7
         + [vmem((rows, CH), F32)] * 3
-        + [vmem((CH // 128, rows, 128), F32), vmem((2, slots, CH), F32)]
+        + [vmem((CH // 128, slots * (pixels + PITCH), 128), F32), vmem((2, slots, CH), F32)]
         + [vmem((4, CH, CH), BF16), vmem((1, rows), jnp.int32), vmem((CH, CH), F32)]
         + [vmem((16, CH), F32)]
-        + [weight_sems(weight)],
+        + [vmem((slots // KEYS, QUERIES * pixels, KEYS * pixels), F32)] * 2
+        + [vmem((2, QUERIES * pixels, CH), F32)]
+        + [weight_sems(weight), pltpu.SemaphoreType.DMA((7,)), vmem((rows, CH), BF16)]
+        + [vmem(part.shape, BF16) for part in grad_shapes(4, outs == 2)],
         "attention",
         30 << 30,
         24 << 20,
@@ -964,7 +1054,8 @@
         store_grad(total, out_parts, work, position, tap + extra, first, 9 + extra, front)
         return carry
 
-    lax.fori_loop(0, first - extra, functools.partial(step, True), 0)
+    if first > extra:
+        lax.fori_loop(0, first - extra, functools.partial(step, True), 0)
     if first - extra < 9:
         lax.fori_loop(first - extra, 9, functools.partial(step, False), 0)
     for copy in copies:
@@ -1156,10 +1247,6 @@
     vecs[...] = vecs2[...] + vecs3[...] if width == CH else vecs2[whose] + vecs3[whose]
     vecs[G1 : G1 + 1, :] = jnp.sum(crossed, axis=0, keepdims=True)
     vecs[B1 : B1 + 1, :] = jnp.sum(plain, axis=0, keepdims=True)
-    if out.shape[0] > pixels * slots:
-        begin = pixels * slots
-        out[begin : begin + 16, :] = vecs[...].astype(BF16)
-        out[begin + 16 : begin + 32, :] = jnp.zeros((16, width), BF16)
     plain = crop_mean(same, plain * gain)
     crossed = crop_mean(same, crossed * gain)
 
@@ -1180,7 +1267,7 @@
         "sssvvvvhhh" + "h" * len(weight),
         "vv",
         [
-            shape((rows + (32 if whose else 0), width), F32 if width < CH and whose == 0 else BF16),
+            shape((rows, width), F32 if width < CH and whose == 0 else BF16),
             shape((16, width), F32),
         ],
         [
@@ -1262,25 +1349,31 @@
                 return rounded_sum([mine[span], came[span]])
 
             start = 8 * front
-            keep = part(0, 4 * front), part(start, 2 * back)
-            sent_front = part(4 * front, 4 * front)
+            keep = part(0, 4 * front) if front else None, part(start, 2 * back)
+            sent_front = part(4 * front, 4 * front) if front else None
             sent_back = [part(start + q * 2 * back, 2 * back) for q in (1, 2, 3)]
-            self.state = keep, (swap(sent_front, "chan"), from_quad(sent_back))
+            came_front = swap(sent_front, "chan") if front else None
+            self.state = keep, (came_front, from_quad(sent_back))
             return sent_front, sent_back
         if self.stage == 2:
             (mine_front, mine_back), (came_front, came_back) = state
             piece = [slice(q * front, (q + 1) * front) for q in range(4)]
-            sent_front = [rounded_sum([mine_front[piece[q]], came_front[piece[q]]]) for q in (1, 2, 3)]
+            sent_front, keep_front = [], None
+            if front:
+                terms = [[mine_front[span], came_front[span]] for span in piece]
+                keep_front, sent_front = terms[0], [rounded_sum(term) for term in terms[1:]]
             sent_back = rounded_sum([mine_back[back:]] + [value[back:] for value in came_back])
-            keep_front = [mine_front[:front], came_front[:front]]
+            if vectors is not None:
+                sent_back = jnp.concatenate([sent_back, vector_rows(vectors)], axis=0)
             keep_back = [mine_back[:back]] + [value[:back] for value in came_back]
             self.state = keep_front, keep_back, (from_quad(sent_front), swap(sent_back, "chan"))
             return sent_front, sent_back
         if self.stage == 3:
             mine_front, mine_back, (came_front, came_back) = state
-            parts = [rounded_sum(mine_front + came_front), rounded_sum(mine_back + [came_back])]
+            parts = [rounded_sum(mine_front + came_front)] if front else []
+            parts.append(rounded_sum(mine_back + [came_back[:back]]))
             if vectors is not None:
-                parts.append(vector_rows(vectors))
+                parts.append(rounded_sum([vector_rows(vectors), came_back[back:]]))
             value = jnp.concatenate(parts, axis=0)
             self.state = value, swap(value, "far")
             return value
@@ -1480,21 +1573,20 @@
         back = functools.partial(last, position, tables, par, stats1, (vecs2, vecs3), feats)
         sent = chain2.advance(grad1, out_parts[1])
         halves = weight_grad(
-            position, pad1, after(grad1, sent), True, slots, "conv1_weight_grad", 5
+            position, pad1, after(grad1, sent), True, slots, "conv1_weight_grad", 0
         )
         sent = chain2.advance(halves[1])
-        chain1 = Reduction(after(halves, sent), 5, 9)
+        chain1 = Reduction(after(halves, sent), 0, 9)
         grad1 = after(grad1, sent, halves[1])
-        in_other, _ = back(grad1, weight1, resid_grad, 1, slots)
-        sent = chain1.advance(in_other, chain2.state)
-        in_got = swap(in_other, "chan")
+        in_other, vecs_other = back(grad1, weight1, resid_grad, 1, slots)
+        sent = chain1.advance(in_other, chain2.state), chain2.advance(in_other)
+        in_got = swap(after(in_other, sent), "chan")
         grad1 = after(grad1, sent, in_other)
         in_own, vecs_own = back(grad1, weight1, resid_grad, 0, slots)
-        sent = chain1.advance(in_own), chain2.advance(in_own)
-        output = unpack_lanes(after(out_parts, sent), False, BF16, "unpack_output")
-        rows = in_own.shape[0]
-        vecs = vecs_own + in_got[rows : rows + 16].astype(F32)
-        sent = chain1.advance(output, in_got, vectors=vecs), chain2.advance(output)
+        sent = chain1.advance(in_own, vectors=vecs_other), chain2.advance(in_own)
+        out_parts = after(out_parts, sent, in_own, in_got)
+        output = unpack_lanes(out_parts, False, BF16, "unpack_output")
+        sent = chain1.advance(output, vectors=vecs_own)
         in_parts = after([in_own, in_got], sent)
         input_grad = unpack_lanes(in_parts, True, F32, "unpack_input_grad")
         sent = chain1.advance(input_grad), chain2.advance(input_grad)

time: 355 us -> 333 us (0.938); the launches traced: 348 us -> 335 us
  Pallas kernels: 207 us -> 192 us
  starting transfers between devices: 52.4 us -> 61.1 us
  waiting for transfers between devices: 67 us -> 61.6 us
    ppermute x20 -> x19, waiting for transfers between devices: 51.5 us -> 25.8 us  [swap(): return lax.ppermute(value, axis, [(0, 1), (1, 0)])]
    ppermute x18 -> x15, waiting for transfers between devices: 15.4 us -> 35.8 us  [from_quad(): lax.ppermute(value, ('near', 'y'), [(at, at ^ bits) for at in range(4)])]
    ppermute x18 -> x15, starting transfers between devices: 24.1 us -> 36.1 us  [from_quad(): lax.ppermute(value, ('near', 'y'), [(at, at ^ bits) for at in range(4)])]
    pallas_call x1, Pallas kernels: 50.1 us -> 43.6 us  [attention(): call(functools.partial(attention_kernel, parts, outs, len(weight)), 'ssss...]
    ppermute x20 -> x19, starting transfers between devices: 20.2 us -> 16.9 us  [swap(): return lax.ppermute(value, axis, [(0, 1), (1, 0)])]
  transfers between devices with their start and end apart: 40 -> 36, of which waited for: 14 -> 14; matrix products, arithmetic and copies ran while one was open for 2% -> 2% of each run, Pallas kernels for 40% -> 38%
where the time goes in v3:
time: 333 us; the launch traced here: 335 us
  Pallas kernels  192 us (58%)
  waiting for transfers between devices  61.6 us (18%)
  starting transfers between devices  61.1 us (18%)
  local copies, waits for them, and re-layouts  14.9 us (4%)
  other arithmetic  4.66 us (1%)
    pallas_call x1, Pallas kernels, attention(): call(functools.partial(attention_kernel, parts, outs, len(weight)), 'ssss...  43.6 us
    ppermute x15, starting transfers between devices, from_quad(): lax.ppermute(value, ('near', 'y'), [(at, at ^ bits) for at in range(4)])  36.1 us
    ppermute x15, waiting for transfers between devices, from_quad(): lax.ppermute(value, ('near', 'y'), [(at, at ^ bits) for at in range(4)])  35.8 us
    pallas_call x2, Pallas kernels, weight_grad(): call(functools.partial(weight_grad_kernel, paired, first, extra), 'svv' +...  29.4 us
    ppermute x19, waiting for transfers between devices, swap(): return lax.ppermute(value, axis, [(0, 1), (1, 0)])  25.8 us
    pallas_call x1, Pallas kernels, first(): call(functools.partial(first_kernel, len(parts), len(weight)), 'sss' + 'v...  24.8 us
    pallas_call x2, Pallas kernels, last(): call(functools.partial(last_kernel, whose, len(weight)), 'sssvvvvhhh' + '...  23.5 us
    pallas_call x1, Pallas kernels, second(): call(functools.partial(second_kernel, len(weight)), 'sssvvh' + 'h' * len(...  22.3 us
  transfers between devices with their start and end apart: 36, of which 14 were waited for; matrix products, arithmetic and copies ran while one was open for 2% of the time, Pallas kernels for 38%

profile of v3, /device:TPU:0, one launch (start us, length us, event | category | flops | bytes accessed | tf_op | source)
XLA Modules:
  0.0 335.4 jit_solution(5943746803607317130)
XLA Ops:
  0.7 1.5 stack.82.rest_2_
  2.2 3.0 collective-permute-start.2
  7.3 2.1 collective-permute-start.4
  10.0 6.0 %pack_features.1 = (s32[64]{0:T(128)}, s32[64]{0:T(128)}, s32[16]{0:T(128)}, s32[16]{0:T(128)}, bf16[2048,256]{1,0:T(8,128)(2,1)}, /*index=5*/bf16[2048,256]{1,0:T(8,128)(2,1)}) custom-call(s32[3]{0:T(128)} %pad_add_fusion.position, s32[64,64]{1,0:T(8,128)} %bitcast.62, s32[5028]{0:T(1024)} %constant.33.clone.table, bf16[256,4096]{1,0:T(8,128)(2,1)} %bitcast.60), custom_call_target="tpu_custom_call" | custom-call | flops 4294967296 | bytes 6291456 | tf_op jit(solution)/shard_map/pack_features/pallas_call | solution.py:475
  17.4 4.2 %all-to-all-start = ((bf16[4,9,32,512]{3,2,1,0:T(8,128)(2,1)}), bf16[4,9,32,512]{3,2,1,0:T(8,128)(2,1)S(1)}, u32[]{:S(2)}, u32[]{:S(2)}) async-start(bf16[4,9,32,512]{3,2,1,0:T(8,128)(2,1)} %broadcast_in_dim.8), calls=%async_computation | async-start | bytes 2359296 | tf_op jit(solution)/shard_map/all_to_all | solution.py:1307
  21.6 5.2 %pack_cotangent.1 = (bf16[2048,256]{1,0:T(8,128)(2,1)}, bf16[2048,256]{1,0:T(8,128)(2,1)}) custom-call(s32[3]{0:T(128)} %pad_add_fusion.position, s32[64]{0:T(128)} %get-tuple-element.119.slot_tile, bf16[256,4096]{1,0:T(8,128)(2,1)} %bitcast.61), custom_call_target="tpu_custom_call" | custom-call | flops 42949672960 | bytes 6291456 | tf_op jit(solution)/shard_map/pack_cotangent/pallas_call | solution.py:493
  28.0 15.6 %collective-permute-done.rest_1_ = bf16[2048,256]{1,0:T(8,128)(2,1)S(1)} collective-permute-done((bf16[2048,256]{1,0:T(8,128)(2,1)}, bf16[2048,256]{1,0:T(8,128)(2,1)S(1)}, u32[]{:S(2)}, u32[]{:S(2)}) %collective-permute-start) | collective-permute-done | bytes 1048608 | tf_op jit(solution)/shard_map/ppermute | solution.py:1303
  43.6 1.9 broadcast_in_dim.9
  45.4 3.8 %all-to-all-start.1 = ((bf16[8,9,32,512]{3,2,1,0:T(8,128)(2,1)}), bf16[8,9,32,512]{3,2,1,0:T(8,128)(2,1)S(1)}, u32[]{:S(2)}, u32[]{:S(2)}) async-start(bf16[8,9,32,512]{3,2,1,0:T(8,128)(2,1)} %broadcast_in_dim.9), calls=%async_computation.1 | async-start | bytes 4718592 | tf_op jit(solution)/shard_map/all_to_all | solution.py:1307
  51.4 1.2 collective-permute-done.3.rest_6_.rest_5_
  52.6 24.8 %conv1_forward.1 = (f32[16,512]{1,0:T(8,128)}, bf16[2048,512]{1,0:T(8,128)(2,1)}, bf16[10,10,32,512]{3,2,1,0:T(8,128)(2,1)}, bf16[64,32,512]{2,1,0:T(8,128)(2,1)...) custom-call(s32[3]{0:T(128)} %pad_add_fusion.position, ...), custom_call_target="tpu_custom_call" | custom-call | flops 9663676416 | bytes 20971520 | tf_op jit(solution)/shard_map/conv1_forward/pallas_call | solution.py:644
  78.2 1.4 copy-done
  79.6 22.3 %conv2_forward.1 = (bf16[2048,512]{1,0:T(8,128)(2,1)}, bf16[2048,512]{1,0:T(8,128)(2,1)}, f32[2,32,512]{2,1,0:T(8,128)}) custom-call(s32[3]{0:T(128)} %pad_add_fusion.position, s32[64]{0:T(128)} %get-tuple-element.119.slot_tile, s32[64]{0:T(128)} %get-tuple-element.120.slot_crop, f32[16,512]{1,0:T(8,128)} %get-tuple-element.127.par.rest_0_, ...), custom_call_target="tpu_custom_call" | custom-call | flops 9663676416 | bytes 16777216 | tf_op jit(solution)/shard_map/conv2_forward/pallas_call | solution.py:733
  102.9 43.6 %attention.1 = (bf16[2048,256]{1,0:T(8,128)(2,1)}, bf16[2048,256]{1,0:T(8,128)(2,1)}, bf16[1024,512]{1,0:T(8,128)(2,1)}, bf16[1024,512]{1,0:T(8,128)(2,1)}, f32[...) custom-call(s32[3]{0:T(128)} %pad_add_fusion.position, s32[64]{0:T(128)} %get-tuple-element.119.slot_tile, ...), custom_call_target="tpu_custom_call" | custom-call | flops 32212254720 | bytes 25165824 | tf_op jit(solution)/shard_map/attention/pallas_call | solution.py:1001
  146.6 1.9 copy-done.7
  148.5 1.2 copy-done.17
  149.7 1.2 copy-done.18
  151.0 16.0 %conv2_weight_grad.1 = (bf16[3328,512]{1,0:T(8,128)(2,1)S(1)}, bf16[3328,512]{1,0:T(8,128)(2,1)S(1)}) custom-call(s32[3]{0:T(128)S(1)} %copy-done.6, bf16[10,10,32,512]{3,2,1,0:T(8,128)(2,1)S(1)} %copy-done.12, bf16[10,10,32,512]{3,2,1,0:T(8,128)(2,1)S(1)} %copy-done.7, bf16[1024,512]{1,0:T(8,128)(2,1)S(1)} %copy-done.17, bf16[1024,512]{1,0:T(8,128)(2,1)S(1)} %copy-done.18), custom_call_target="tpu_custom_call" | custom-call | flops 9663676416 | bytes 12582912 | tf_op jit(solution)/shard_map/conv2_weight_grad/pallas_call | solution.py:1069
  167.7 19.3 %conv2_input_grad.1 = (bf16[10,10,32,512]{3,2,1,0:T(8,128)(2,1)S(1)}, f32[2,16,256]{2,1,0:T(8,128)S(1)}) custom-call(s32[3]{0:T(128)S(1)} %copy-done.6, s32[64]{0:T(128)S(1)} %copy-done.20, s32[64]{0:T(128)S(1)} %copy-done.21, f32[16,512]{1,0:T(8,128)S(1)} %copy-done.15, f32[2,32,512]{2,1,0:T(8,128)S(1)} %copy-done.19, ...), custom_call_target="tpu_custom_call" | custom-call | flops 9663676416 | bytes 16777216 | tf_op jit(solution)/shard_map/conv2_input_grad/pallas_call | solution.py:1182
  187.0 5.6 %collective-permute-done.8.rest_1_ = bf16[2048,256]{1,0:T(8,128)(2,1)S(1)} collective-permute-done((bf16[2048,256]{1,0:T(8,128)(2,1)S(1)}, bf16[2048,256]{1,0:T(8,128)(2,1)S(1)}, u32[]{:S(2)}, u32[]{:S(2)}) %collective-permute-start.8) | collective-permute-done | bytes 1048608 | tf_op jit(solution)/shard_map/ppermute | solution.py:1303
  194.2 7.6 %collective-permute-start.13 = (bf16[320,512]{1,0:T(8,128)(2,1)S(1)}, bf16[320,512]{1,0:T(8,128)(2,1)S(1)}, u32[]{:S(2)}, u32[]{:S(2)}) collective-permute-start(bf16[320,512]{1,0:T(8,128)(2,1)S(1)} %get-tuple-element.219), channel_id=1, source_target_pairs={{0,12},{4,8},{8,4},{12,0},{1,13},{5,9},{9,5},{13,1},{2,14},{6,10},... | collective-permute-start | bytes 983048 | tf_op jit(solution)/shard_map/ppermute | solution.py:1315
  201.8 3.3 collective-permute-start.12
  205.1 1.4 collective-permute-start.11
  206.5 13.3 %conv1_weight_grad.1 = (bf16[2304,512]{1,0:T(8,128)(2,1)S(1)}, bf16[2304,512]{1,0:T(8,128)(2,1)S(1)}) custom-call(s32[3]{0:T(128)S(1)} %copy-done.6, bf16[10,10,32,512]{3,2,1,0:T(8,128)(2,1)S(1)} %copy-done.13, bf16[10,10,32,512]{3,2,1,0:T(8,128)(2,1)S(1)} %get-tuple-element.184.grad.rest_1_), custom_call_target="tpu_custom_call" | custom-call | flops 9663676416 | bytes 12582912 | tf_op jit(solution)/shard_map/conv1_weight_grad/pallas_call | solution.py:1069
  220.8 1.5 collective-permute-start.18
  222.3 4.4 %collective-permute-start.17 = (bf16[256,512]{1,0:T(8,128)(2,1)S(1)}, bf16[256,512]{1,0:T(8,128)(2,1)S(1)}, u32[]{:S(2)}, u32[]{:S(2)}) collective-permute-start(bf16[256,512]{1,0:T(8,128)(2,1)S(1)} %get-tuple-element.229), channel_id=1, source_target_pairs={{0,12},{4,8},{8,4},{12,0},{1,13},{5,9},{9,5},{13,1},{2,14},{6,10},... | collective-permute-start | bytes 786440 | tf_op jit(solution)/shard_map/ppermute | solution.py:1315
  226.7 2.9 collective-permute-start.16
  229.7 1.5 collective-permute-start.15
  231.2 11.8 %conv1_input_grad.2 = (bf16[2048,256]{1,0:T(8,128)(2,1)S(1)}, f32[16,256]{1,0:T(8,128)S(1)}) custom-call(s32[3]{0:T(128)S(1)} %copy-done.6, s32[64]{0:T(128)S(1)} %copy-done.20, s32[64]{0:T(128)S(1)} %copy-done.21, f32[16,512]{1,0:T(8,128)S(1)} %copy-done.15, f32[2,32,512]{2,1,0:T(8,128)S(1)} %copy-done.11, f32[2,16,256]{2,1,0:T(8,128)S(1)} %get-tuple-element.168.vecs2, ...), custom_call_target="tpu_custom_call" | custom-call | flops 4831838208 | bytes 10485760 | tf_op jit(solution)/shard_map/conv1_input_grad/pallas_call | solution.py:1265
  243.5 3.8 %collective-permute-start.22 = (bf16[416,512]{1,0:T(8,128)(2,1)S(1)}, bf16[416,512]{1,0:T(8,128)(2,1)S(1)}, u32[]{:S(2)}, u32[]{:S(2)}) collective-permute-start(bf16[416,512]{1,0:T(8,128)(2,1)S(1)} %pad_maximum_fusion.2), channel_id=1, source_target_pairs={{0,16},{16,0},{1,17},{17,1},{2,18},{18,2},{3,19},{19,3},{4,20},{20... | collective-permute-start | bytes 1277960 | tf_op jit(solution)/shard_map/ppermute | solution.py:1303
  248.0 3.0 collective-permute-start.21
  251.6 1.6 collective-permute-start.23
  253.2 11.7 %conv1_input_grad.3 = (f32[2048,256]{1,0:T(8,128)S(1)}, f32[16,256]{1,0:T(8,128)S(1)}) custom-call(s32[3]{0:T(128)S(1)} %copy-done.6, s32[64]{0:T(128)S(1)} %copy-done.20, s32[64]{0:T(128)S(1)} %copy-done.21, f32[16,512]{1,0:T(8,128)S(1)} %copy-done.15, f32[2,32,512]{2,1,0:T(8,128)S(1)} %copy-done.11, f32[2,16,256]{2,1,0:T(8,128)S(1)} %get-tuple-element.168.vecs2, ...), custom_call_target="tpu_custom_call" | custom-call | flops 4831838208 | bytes 10485760 | tf_op jit(solution)/shard_map/conv1_input_grad/pallas_call | solution.py:1265
  264.9 1.2 collective-permute-done.22
  266.3 1.8 collective-permute-start.32
  268.1 5.4 %collective-permute-done.21 = bf16[576,512]{1,0:T(8,128)(2,1)S(1)} collective-permute-done((bf16[576,512]{1,0:T(8,128)(2,1)S(1)}, bf16[576,512]{1,0:T(8,128)(2,1)S(1)}, u32[]{:S(2)}, u32[]{:S(2)}) %collective-permute-start.21) | collective-permute-done | bytes 589856 | tf_op jit(solution)/shard_map/ppermute | solution.py:1315
  273.5 2.0 collective-permute-start.31
  276.3 4.1 %collective-permute-start.30 = (bf16[416,512]{1,0:T(8,128)(2,1)S(1)}, bf16[416,512]{1,0:T(8,128)(2,1)S(1)}, u32[]{:S(2)}, u32[]{:S(2)}) collective-permute-start(bf16[416,512]{1,0:T(8,128)(2,1)S(1)} %add_convert_fusion.6), channel_id=1, source_target_pairs={{0,8},{4,12},{8,0},{12,4},{1,9},{5,13},{9,1},{13,5},{2,10},{6,14},... | collective-permute-start | bytes 1277960 | tf_op jit(solution)/shard_map/ppermute | solution.py:1315
  280.4 6.2 %collective-permute-done.19 = bf16[576,512]{1,0:T(8,128)(2,1)S(1)} collective-permute-done((bf16[576,512]{1,0:T(8,128)(2,1)S(1)}, bf16[576,512]{1,0:T(8,128)(2,1)S(1)}, u32[]{:S(2)}, u32[]{:S(2)}) %collective-permute-start.19) | collective-permute-done | bytes 589856 | tf_op jit(solution)/shard_map/ppermute | solution.py:1315
  287.5 1.6 collective-permute-start.24
  289.1 4.5 %unpack_output.1 = bf16[256,4096]{1,0:T(8,128)(2,1)} custom-call(s32[3]{0:T(128)S(1)} %copy-done.6, s32[64]{0:T(128)S(1)} %copy-done.20, bf16[2048,256]{1,0:T(8,128)(2,1)S(1)} %copy-done.10, bf16[2048,256]{1,0:T(8,128)(2,1)S(1)} %collective-permute-done.8.rest_1_), custom_call_target="tpu_custom_call" | custom-call | flops 4294967296 | bytes 8388608 | tf_op jit(solution)/shard_map/unpack_output/pallas_call | solution.py:547
  294.9 6.2 %unpack_input_grad.1 = f32[256,4096]{1,0:T(8,128)} custom-call(s32[3]{0:T(128)S(1)} %copy-done.6, s32[64]{0:T(128)S(1)} %copy-done.20, f32[2048,256]{1,0:T(8,128)S(1)} %get-tuple-element.202.rest_0_, bf16[2048,256]{1,0:T(8,128)(2,1)S(1)} %collective-permute-done.23.rest_1_), custom_call_target="tpu_custom_call" | custom-call | flops 4294967296 | bytes 8388608 | tf_op jit(solution)/shard_map/unpack_input_grad/pallas_call | solution.py:547
  301.1 9.0 %collective-permute-done.30 = bf16[416,512]{1,0:T(8,128)(2,1)S(1)} collective-permute-done((bf16[416,512]{1,0:T(8,128)(2,1)S(1)}, bf16[416,512]{1,0:T(8,128)(2,1)S(1)}, u32[]{:S(2)}, u32[]{:S(2)}) %collective-permute-start.30) | collective-permute-done | bytes 426016 | tf_op jit(solution)/shard_map/ppermute | solution.py:1315
  310.9 3.1 collective-permute-start.26
  314.0 8.0 %collective-permute-done.28 = bf16[320,512]{1,0:T(8,128)(2,1)S(1)} collective-permute-done((bf16[320,512]{1,0:T(8,128)(2,1)S(1)}, bf16[320,512]{1,0:T(8,128)(2,1)S(1)}, u32[]{:S(2)}, u32[]{:S(2)}) %collective-permute-start.28) | collective-permute-done | bytes 327712 | tf_op jit(solution)/shard_map/ppermute | solution.py:1315
  322.0 5.8 %collective-permute-done.27 = bf16[320,512]{1,0:T(8,128)(2,1)S(1)} collective-permute-done((bf16[320,512]{1,0:T(8,128)(2,1)S(1)}, bf16[320,512]{1,0:T(8,128)(2,1)S(1)}, u32[]{:S(2)}, u32[]{:S(2)}) %collective-permute-start.27) | collective-permute-done | bytes 327712 | tf_op jit(solution)/shard_map/ppermute | solution.py:1315
  327.9 3.8 %conv2_grads.1 = (f32[256,512]{1,0:T(8,128)}, f32[256,512]{1,0:T(8,128)}, f32[256,512]{1,0:T(8,128)}, f32[256,512]{1,0:T(8,128)}, f32[9,256,512]{2,1,0:T(8,128)}) custom-call(s32[3]{0:T(128)S(1)} %copy-done.6, bf16[1664,512]{1,0:T(8,128)(2,1)S(1)} %constant_dynamic-update-slice_fusion.mine, bf16[1664,512]{1,0:T(8,128)(2,1)S(1)} %collective-permute-done.33.other), custom_call_target="tpu_custom_call" | custom-call | flops 4294967296 | bytes 6291456 | tf_op jit(solution)/shard_map/conv2_grads/pallas_call | solution.py:1423
  331.7 3.0 conv1_grads.1
  (152 shorter events, 18.5 us)
Async XLA Ops:
  2.2 13.9 %collective-permute-start.2 = (f32[16,256]{1,0:T(8,128)S(1)}, f32[16,256]{1,0:T(8,128)S(1)}, u32[]{:S(2)}, u32[]{:S(2)}) collective-permute-start(f32[16,256]{1,0:T(8,128)S(1)} %stack.82.rest_2_), channel_id=1, source_target_pairs={{0,1},{1,0},{2,3},{3,2},{4,5},{5,4},{6,7},{7,6},{8,9},{9,8},{10,11... | collective-permute-start | bytes 49160 | tf_op jit(solution)/shard_map/ppermute | solution.py:1303
  6.2 10.0 %collective-permute-start.1 = (bf16[9,32,512]{2,1,0:T(8,128)(2,1)S(1)}, bf16[9,32,512]{2,1,0:T(8,128)(2,1)S(1)}, u32[]{:S(2)}, u32[]{:S(2)}) collective-permute-start(bf16[9,32,512]{2,1,0:T(8,128)(2,1)S(1)} %constant_dynamic-slice_fusion.2), channel_id=1, source_target_pairs={{0,1},{1,0},{2,3},{3,2},{4,5},{5,4},{6,7},{7,6},{8,9},{9,8},{10,11... | collective-permute-start | bytes 884744 | tf_op jit(solution)/shard_map/ppermute | solution.py:1303
  7.3 20.7 %collective-permute-start.4 = (bf16[9,32,512]{2,1,0:T(8,128)(2,1)S(1)}, bf16[9,32,512]{2,1,0:T(8,128)(2,1)S(1)}, u32[]{:S(2)}, u32[]{:S(2)}) collective-permute-start(bf16[9,32,512]{2,1,0:T(8,128)(2,1)S(1)} %constant_dynamic-slice_fusion.1), channel_id=1, source_target_pairs={{0,1},{1,0},{2,3},{3,2},{4,5},{5,4},{6,7},{7,6},{8,9},{9,8},{10,11... | collective-permute-start | bytes 884744 | tf_op jit(solution)/shard_map/ppermute | solution.py:1303
  16.0 27.5 %collective-permute-start = (bf16[2048,256]{1,0:T(8,128)(2,1)}, bf16[2048,256]{1,0:T(8,128)(2,1)S(1)}, u32[]{:S(2)}, u32[]{:S(2)}) collective-permute-start(bf16[2048,256]{1,0:T(8,128)(2,1)} %get-tuple-element.124), channel_id=1, source_target_pairs={{0,1},{1,0},{2,3},{3,2},{4,5},{5,4},{6,7},{7,6},{8,9},{9,8},{10,11... | collective-permute-start | bytes 3145736 | tf_op jit(solution)/shard_map/ppermute | solution.py:1303
  17.4 26.2 %all-to-all-start = ((bf16[4,9,32,512]{3,2,1,0:T(8,128)(2,1)}), bf16[4,9,32,512]{3,2,1,0:T(8,128)(2,1)S(1)}, u32[]{:S(2)}, u32[]{:S(2)}) async-start(bf16[4,9,32,512]{3,2,1,0:T(8,128)(2,1)} %broadcast_in_dim.8), calls=%async_computation | async-start | bytes 2359296 | tf_op jit(solution)/shard_map/all_to_all | solution.py:1307
  45.4 32.7 %all-to-all-start.1 = ((bf16[8,9,32,512]{3,2,1,0:T(8,128)(2,1)}), bf16[8,9,32,512]{3,2,1,0:T(8,128)(2,1)S(1)}, u32[]{:S(2)}, u32[]{:S(2)}) async-start(bf16[8,9,32,512]{3,2,1,0:T(8,128)(2,1)} %broadcast_in_dim.9), calls=%async_computation.1 | async-start | bytes 4718592 | tf_op jit(solution)/shard_map/all_to_all | solution.py:1307
  49.3 3.4 %collective-permute-start.3 = (bf16[4,9,32,512]{3,2,1,0:T(8,128)(2,1)S(1)}, bf16[4,9,32,512]{3,2,1,0:T(8,128)(2,1)}, u32[]{:S(2)}, u32[]{:S(2)}) collective-permute-start(bf16[4,9,32,512]{3,2,1,0:T(8,128)(2,1)S(1)} %all-to-all-done.rest_5_.rest_4_), channel_id=1, source_target_pairs={{0,2},{2,0},{1,3},{3,1},{4,6},{6,4},{5,7},{7,5},{8,10},{10,8},{9,1... | collective-permute-start | bytes 3538952 | tf_op jit(solution)/shard_map/ppermute | solution.py:1303
  50.8 26.7 %collective-permute-start.5 = (bf16[4,128,512]{2,1,0:T(8,128)(2,1)S(1)}, bf16[4,128,512]{2,1,0:T(8,128)(2,1)}, u32[]{:S(2)}, u32[]{:S(2)}) collective-permute-start(bf16[4,128,512]{2,1,0:T(8,128)(2,1)S(1)} %constant_dynamic-slice_fusion), channel_id=1, source_target_pairs={{0,1},{1,0},{2,3},{3,2},{4,5},{5,4},{6,7},{7,6},{8,9},{9,8},{10,11... | collective-permute-start | bytes 1572872 | tf_op jit(solution)/shard_map/ppermute | solution.py:1303
  52.6 24.9 %copy-start.30 = (bf16[2048,256]{1,0:T(8,128)(2,1)S(1)}, bf16[2048,256]{1,0:T(8,128)(2,1)}, u32[]{:S(2)}) copy-start(bf16[2048,256]{1,0:T(8,128)(2,1)} %get-tuple-element.137) | copy-start | bytes 3145732
  77.5 25.4 %collective-permute-start.6 = (bf16[2048,256]{1,0:T(8,128)(2,1)S(1)}, bf16[2048,256]{1,0:T(8,128)(2,1)}, u32[]{:S(2)}, u32[]{:S(2)}) collective-permute-start(bf16[2048,256]{1,0:T(8,128)(2,1)S(1)} %copy-done.30), channel_id=1, source_target_pairs={{0,1},{1,0},{2,3},{3,2},{4,5},{5,4},{6,7},{7,6},{8,9},{9,8},{10,11... | collective-permute-start | bytes 3145736 | tf_op jit(solution)/shard_map/ppermute | solution.py:1303
  78.1 23.7 %collective-permute-start.7 = (bf16[4,128,512]{2,1,0:T(8,128)(2,1)}, bf16[4,128,512]{2,1,0:T(8,128)(2,1)}, u32[]{:S(2)}, u32[]{:S(2)}) collective-permute-start(bf16[4,128,512]{2,1,0:T(8,128)(2,1)} %collective-permute-done.5.rest_7_), channel_id=1, source_target_pairs={{0,2},{2,0},{1,3},{3,1},{4,6},{6,4},{5,7},{7,5},{8,10},{10,8},{9,1... | collective-permute-start | bytes 1572872 | tf_op jit(solution)/shard_map/ppermute | solution.py:1303
  102.9 43.6 %copy-start.6 = (s32[3]{0:T(128)S(1)}, s32[3]{0:T(128)}, u32[]{:S(2)}) copy-start(s32[3]{0:T(128)} %pad_add_fusion.position) | copy-start | bytes 40
  102.9 43.6 %copy-start.12 = (bf16[10,10,32,512]{3,2,1,0:T(8,128)(2,1)S(1)}, bf16[10,10,32,512]{3,2,1,0:T(8,128)(2,1)}, u32[]{:S(2)}) copy-start(bf16[10,10,32,512]{3,2,1,0:T(8,128)(2,1)} %get-tuple-element.129.pad_hbm.active) | copy-start | bytes 9830404
  150.9 16.8 %copy-start.1 = (bf16[8,9,32,512]{3,2,1,0:T(8,128)(2,1)S(1)}, bf16[8,9,32,512]{3,2,1,0:T(8,128)(2,1)}, u32[]{:S(2)}) copy-start(bf16[8,9,32,512]{3,2,1,0:T(8,128)(2,1)} %copy-done) | copy-start | bytes 7077892
  150.9 16.8 %copy-start.4 = (bf16[9,256,512]{2,1,0:T(8,128)(2,1)S(1)}, bf16[9,256,512]{2,1,0:T(8,128)(2,1)}, u32[]{:S(2)}) copy-start(bf16[9,256,512]{2,1,0:T(8,128)(2,1)} %rest_0_.3) | copy-start | bytes 7077892
  150.9 16.8 %copy-start.14 = (bf16[64,32,512]{2,1,0:T(8,128)(2,1)S(1)}, bf16[64,32,512]{2,1,0:T(8,128)(2,1)}, u32[]{:S(2)}) copy-start(bf16[64,32,512]{2,1,0:T(8,128)(2,1)} %get-tuple-element.151.hidden_hbm) | copy-start | bytes 6291460
  150.9 16.8 %copy-start.15 = (f32[16,512]{1,0:T(8,128)S(1)}, f32[16,512]{1,0:T(8,128)}, u32[]{:S(2)}) copy-start(f32[16,512]{1,0:T(8,128)} %get-tuple-element.127.par.rest_0_) | copy-start | bytes 98308
  150.9 16.8 %copy-start.19 = (f32[2,32,512]{2,1,0:T(8,128)S(1)}, f32[2,32,512]{2,1,0:T(8,128)}, u32[]{:S(2)}) copy-start(f32[2,32,512]{2,1,0:T(8,128)} %get-tuple-element.145.stats2) | copy-start | bytes 393220
  151.0 16.8 %copy-start.20 = (s32[64]{0:T(128)S(1)}, s32[64]{0:T(128)}, u32[]{:S(2)}) copy-start(s32[64]{0:T(128)} %get-tuple-element.119.slot_tile) | copy-start | bytes 772
  167.0 25.7 %collective-permute-start.9 = (bf16[3328,512]{1,0:T(8,128)(2,1)S(1)}, bf16[3328,512]{1,0:T(8,128)(2,1)S(1)}, u32[]{:S(2)}, u32[]{:S(2)}) collective-permute-start(bf16[3328,512]{1,0:T(8,128)(2,1)S(1)} %get-tuple-element.149), channel_id=1, source_target_pairs={{0,2},{2,0},{1,3},{3,1},{4,6},{6,4},{5,7},{7,5},{8,10},{10,8},{9,1... | collective-permute-start | bytes 10223624 | tf_op jit(solution)/shard_map/ppermute | solution.py:1303
  167.1 25.6 %collective-permute-start.8 = (bf16[2048,256]{1,0:T(8,128)(2,1)S(1)}, bf16[2048,256]{1,0:T(8,128)(2,1)S(1)}, u32[]{:S(2)}, u32[]{:S(2)}) collective-permute-start(bf16[2048,256]{1,0:T(8,128)(2,1)S(1)} %copy-done.32), channel_id=1, source_target_pairs={{0,1},{1,0},{2,3},{3,2},{4,5},{5,4},{6,7},{7,6},{8,9},{9,8},{10,11... | collective-permute-start | bytes 3145736 | tf_op jit(solution)/shard_map/ppermute | solution.py:1303
  193.3 27.2 %collective-permute-start.10 = (bf16[1024,512]{1,0:T(8,128)(2,1)S(1)}, bf16[1024,512]{1,0:T(8,128)(2,1)S(1)}, u32[]{:S(2)}, u32[]{:S(2)}) collective-permute-start(bf16[1024,512]{1,0:T(8,128)(2,1)S(1)} %get-tuple-element.223), channel_id=1, source_target_pairs={{0,1},{1,0},{2,3},{3,2},{4,5},{5,4},{6,7},{7,6},{8,9},{9,8},{10,11... | collective-permute-start | bytes 3145736 | tf_op jit(solution)/shard_map/ppermute | solution.py:1303
  194.2 25.6 %collective-permute-start.13 = (bf16[320,512]{1,0:T(8,128)(2,1)S(1)}, bf16[320,512]{1,0:T(8,128)(2,1)S(1)}, u32[]{:S(2)}, u32[]{:S(2)}) collective-permute-start(bf16[320,512]{1,0:T(8,128)(2,1)S(1)} %get-tuple-element.219), channel_id=1, source_target_pairs={{0,12},{4,8},{8,4},{12,0},{1,13},{5,9},{9,5},{13,1},{2,14},{6,10},... | collective-permute-start | bytes 983048 | tf_op jit(solution)/shard_map/ppermute | solution.py:1315
  201.8 18.1 %collective-permute-start.12 = (bf16[320,512]{1,0:T(8,128)(2,1)S(1)}, bf16[320,512]{1,0:T(8,128)(2,1)S(1)}, u32[]{:S(2)}, u32[]{:S(2)}) collective-permute-start(bf16[320,512]{1,0:T(8,128)(2,1)S(1)} %get-tuple-element.221), channel_id=1, source_target_pairs={{0,4},{4,0},{8,12},{12,8},{1,5},{5,1},{9,13},{13,9},{2,6},{6,2},{1... | collective-permute-start | bytes 983048 | tf_op jit(solution)/shard_map/ppermute | solution.py:1315
  205.1 15.3 %collective-permute-start.11 = (bf16[320,512]{1,0:T(8,128)(2,1)S(1)}, bf16[320,512]{1,0:T(8,128)(2,1)S(1)}, u32[]{:S(2)}, u32[]{:S(2)}) collective-permute-start(bf16[320,512]{1,0:T(8,128)(2,1)S(1)} %get-tuple-element.222), channel_id=1, source_target_pairs={{0,8},{4,12},{8,0},{12,4},{1,9},{5,13},{9,1},{13,5},{2,10},{6,14},... | collective-permute-start | bytes 983048 | tf_op jit(solution)/shard_map/ppermute | solution.py:1315
  206.5 24.6 %copy-start.5 = (bf16[9,256,512]{2,1,0:T(8,128)(2,1)S(1)}, bf16[9,256,512]{2,1,0:T(8,128)(2,1)}, u32[]{:S(2)}) copy-start(bf16[9,256,512]{2,1,0:T(8,128)(2,1)} %rest_3_.3) | copy-start | bytes 7077892
  206.5 24.6 %copy-start.8 = (bf16[10,10,32,512]{3,2,1,0:T(8,128)(2,1)S(1)}, bf16[10,10,32,512]{3,2,1,0:T(8,128)(2,1)}, u32[]{:S(2)}) copy-start(bf16[10,10,32,512]{3,2,1,0:T(8,128)(2,1)} %get-tuple-element.150.grad.pad_hbm.rest_2_) | copy-start | bytes 9830404
  206.5 24.6 %copy-start.9 = (bf16[2048,512]{1,0:T(8,128)(2,1)S(1)}, bf16[2048,512]{1,0:T(8,128)(2,1)}, u32[]{:S(2)}) copy-start(bf16[2048,512]{1,0:T(8,128)(2,1)} %get-tuple-element.128.feats.rest_0_) | copy-start | bytes 6291460
  220.7 26.5 %collective-permute-start.14 = (bf16[2304,512]{1,0:T(8,128)(2,1)S(1)}, bf16[2304,512]{1,0:T(8,128)(2,1)S(1)}, u32[]{:S(2)}, u32[]{:S(2)}) collective-permute-start(bf16[2304,512]{1,0:T(8,128)(2,1)S(1)} %get-tuple-element.166), channel_id=1, source_target_pairs={{0,2},{2,0},{1,3},{3,1},{4,6},{6,4},{5,7},{7,5},{8,10},{10,8},{9,1... | collective-permute-start | bytes 7077896 | tf_op jit(solution)/shard_map/ppermute | solution.py:1303
  220.8 22.3 %collective-permute-start.18 = (bf16[160,512]{1,0:T(8,128)(2,1)S(1)}, bf16[160,512]{1,0:T(8,128)(2,1)S(1)}, u32[]{:S(2)}, u32[]{:S(2)}) collective-permute-start(bf16[160,512]{1,0:T(8,128)(2,1)S(1)} %add_convert_fusion.19), channel_id=1, source_target_pairs={{0,1},{1,0},{2,3},{3,2},{4,5},{5,4},{6,7},{7,6},{8,9},{9,8},{10,11... | collective-permute-start | bytes 491528 | tf_op jit(solution)/shard_map/ppermute | solution.py:1303
  222.3 20.8 %collective-permute-start.17 = (bf16[256,512]{1,0:T(8,128)(2,1)S(1)}, bf16[256,512]{1,0:T(8,128)(2,1)S(1)}, u32[]{:S(2)}, u32[]{:S(2)}) collective-permute-start(bf16[256,512]{1,0:T(8,128)(2,1)S(1)} %get-tuple-element.229), channel_id=1, source_target_pairs={{0,12},{4,8},{8,4},{12,0},{1,13},{5,9},{9,5},{13,1},{2,14},{6,10},... | collective-permute-start | bytes 786440 | tf_op jit(solution)/shard_map/ppermute | solution.py:1315
  226.7 16.4 %collective-permute-start.16 = (bf16[256,512]{1,0:T(8,128)(2,1)S(1)}, bf16[256,512]{1,0:T(8,128)(2,1)S(1)}, u32[]{:S(2)}, u32[]{:S(2)}) collective-permute-start(bf16[256,512]{1,0:T(8,128)(2,1)S(1)} %get-tuple-element.230), channel_id=1, source_target_pairs={{0,4},{4,0},{8,12},{12,8},{1,5},{5,1},{9,13},{13,9},{2,6},{6,2},{1... | collective-permute-start | bytes 786440 | tf_op jit(solution)/shard_map/ppermute | solution.py:1315
  229.7 13.5 %collective-permute-start.15 = (bf16[256,512]{1,0:T(8,128)(2,1)S(1)}, bf16[256,512]{1,0:T(8,128)(2,1)S(1)}, u32[]{:S(2)}, u32[]{:S(2)}) collective-permute-start(bf16[256,512]{1,0:T(8,128)(2,1)S(1)} %get-tuple-element.231), channel_id=1, source_target_pairs={{0,8},{4,12},{8,0},{12,4},{1,9},{5,13},{9,1},{13,5},{2,10},{6,14},... | collective-permute-start | bytes 786440 | tf_op jit(solution)/shard_map/ppermute | solution.py:1315
  243.5 22.7 %collective-permute-start.22 = (bf16[416,512]{1,0:T(8,128)(2,1)S(1)}, bf16[416,512]{1,0:T(8,128)(2,1)S(1)}, u32[]{:S(2)}, u32[]{:S(2)}) collective-permute-start(bf16[416,512]{1,0:T(8,128)(2,1)S(1)} %pad_maximum_fusion.2), channel_id=1, source_target_pairs={{0,16},{16,0},{1,17},{17,1},{2,18},{18,2},{3,19},{19,3},{4,20},{20... | collective-permute-start | bytes 1277960 | tf_op jit(solution)/shard_map/ppermute | solution.py:1303
  248.0 25.6 %collective-permute-start.21 = (bf16[576,512]{1,0:T(8,128)(2,1)S(1)}, bf16[576,512]{1,0:T(8,128)(2,1)S(1)}, u32[]{:S(2)}, u32[]{:S(2)}) collective-permute-start(bf16[576,512]{1,0:T(8,128)(2,1)S(1)} %get-tuple-element.225), channel_id=1, source_target_pairs={{0,12},{4,8},{8,4},{12,0},{1,13},{5,9},{9,5},{13,1},{2,14},{6,10},... | collective-permute-start | bytes 1769480 | tf_op jit(solution)/shard_map/ppermute | solution.py:1315
  251.0 25.4 %collective-permute-start.20 = (bf16[576,512]{1,0:T(8,128)(2,1)S(1)}, bf16[576,512]{1,0:T(8,128)(2,1)S(1)}, u32[]{:S(2)}, u32[]{:S(2)}) collective-permute-start(bf16[576,512]{1,0:T(8,128)(2,1)S(1)} %get-tuple-element.226), channel_id=1, source_target_pairs={{0,4},{4,0},{8,12},{12,8},{1,5},{5,1},{9,13},{13,9},{2,6},{6,2},{1... | collective-permute-start | bytes 1769480 | tf_op jit(solution)/shard_map/ppermute | solution.py:1315
  251.0 35.7 %collective-permute-start.19 = (bf16[576,512]{1,0:T(8,128)(2,1)S(1)}, bf16[576,512]{1,0:T(8,128)(2,1)S(1)}, u32[]{:S(2)}, u32[]{:S(2)}) collective-permute-start(bf16[576,512]{1,0:T(8,128)(2,1)S(1)} %get-tuple-element.227), channel_id=1, source_target_pairs={{0,8},{4,12},{8,0},{12,4},{1,9},{5,13},{9,1},{13,5},{2,10},{6,14},... | collective-permute-start | bytes 1769480 | tf_op jit(solution)/shard_map/ppermute | solution.py:1315
  251.6 37.4 %collective-permute-start.23 = (bf16[2048,256]{1,0:T(8,128)(2,1)S(1)}, bf16[2048,256]{1,0:T(8,128)(2,1)S(1)}, u32[]{:S(2)}, u32[]{:S(2)}) collective-permute-start(bf16[2048,256]{1,0:T(8,128)(2,1)S(1)} %get-tuple-element.193), channel_id=1, source_target_pairs={{0,1},{1,0},{2,3},{3,2},{4,5},{5,4},{6,7},{7,6},{8,9},{9,8},{10,11... | collective-permute-start | bytes 3145736 | tf_op jit(solution)/shard_map/ppermute | solution.py:1303
  266.3 34.8 %collective-permute-start.32 = (bf16[416,512]{1,0:T(8,128)(2,1)S(1)}, bf16[416,512]{1,0:T(8,128)(2,1)S(1)}, u32[]{:S(2)}, u32[]{:S(2)}) collective-permute-start(bf16[416,512]{1,0:T(8,128)(2,1)S(1)} %add_convert_fusion.6), channel_id=1, source_target_pairs={{0,12},{4,8},{8,4},{12,0},{1,13},{5,9},{9,5},{13,1},{2,14},{6,10},... | collective-permute-start | bytes 1277960 | tf_op jit(solution)/shard_map/ppermute | solution.py:1315
  273.5 27.6 %collective-permute-start.31 = (bf16[416,512]{1,0:T(8,128)(2,1)S(1)}, bf16[416,512]{1,0:T(8,128)(2,1)S(1)}, u32[]{:S(2)}, u32[]{:S(2)}) collective-permute-start(bf16[416,512]{1,0:T(8,128)(2,1)S(1)} %add_convert_fusion.6), channel_id=1, source_target_pairs={{0,4},{4,0},{8,12},{12,8},{1,5},{5,1},{9,13},{13,9},{2,6},{6,2},{1... | collective-permute-start | bytes 1277960 | tf_op jit(solution)/shard_map/ppermute | solution.py:1315
  276.3 33.8 %collective-permute-start.30 = (bf16[416,512]{1,0:T(8,128)(2,1)S(1)}, bf16[416,512]{1,0:T(8,128)(2,1)S(1)}, u32[]{:S(2)}, u32[]{:S(2)}) collective-permute-start(bf16[416,512]{1,0:T(8,128)(2,1)S(1)} %add_convert_fusion.6), channel_id=1, source_target_pairs={{0,8},{4,12},{8,0},{12,4},{1,9},{5,13},{9,1},{13,5},{2,10},{6,14},... | collective-permute-start | bytes 1277960 | tf_op jit(solution)/shard_map/ppermute | solution.py:1315
  287.5 7.1 %collective-permute-start.24 = (bf16[320,512]{1,0:T(8,128)(2,1)S(1)}, bf16[320,512]{1,0:T(8,128)(2,1)S(1)}, u32[]{:S(2)}, u32[]{:S(2)}) collective-permute-start(bf16[320,512]{1,0:T(8,128)(2,1)S(1)} %fusion.1), channel_id=1, source_target_pairs={{0,1},{1,0},{2,3},{3,2},{4,5},{5,4},{6,7},{7,6},{8,9},{9,8},{10,11... | collective-permute-start | bytes 983048 | tf_op jit(solution)/shard_map/ppermute | solution.py:1303
  294.8 15.6 %collective-permute-start.25 = (bf16[320,512]{1,0:T(8,128)(2,1)S(1)}, bf16[320,512]{1,0:T(8,128)(2,1)S(1)}, u32[]{:S(2)}, u32[]{:S(2)}) collective-permute-start(bf16[320,512]{1,0:T(8,128)(2,1)S(1)} %pad_maximum_fusion.3), channel_id=1, source_target_pairs={{0,16},{16,0},{1,17},{17,1},{2,18},{18,2},{3,19},{19,3},{4,20},{20... | collective-permute-start | bytes 983048 | tf_op jit(solution)/shard_map/ppermute | solution.py:1303
  310.3 17.6 %collective-permute-start.33 = (bf16[1664,512]{1,0:T(8,128)(2,1)S(1)}, bf16[1664,512]{1,0:T(8,128)(2,1)S(1)}, u32[]{:S(2)}, u32[]{:S(2)}) collective-permute-start(bf16[1664,512]{1,0:T(8,128)(2,1)S(1)} %constant_dynamic-update-slice_fusion.mine), channel_id=1, source_target_pairs={{0,2},{2,0},{1,3},{3,1},{4,6},{6,4},{5,7},{7,5},{8,10},{10,8},{9,1... | collective-permute-start | bytes 5111816 | tf_op jit(solution)/shard_map/ppermute | solution.py:1303
  310.5 11.5 %collective-permute-start.28 = (bf16[320,512]{1,0:T(8,128)(2,1)S(1)}, bf16[320,512]{1,0:T(8,128)(2,1)S(1)}, u32[]{:S(2)}, u32[]{:S(2)}) collective-permute-start(bf16[320,512]{1,0:T(8,128)(2,1)S(1)} %add_convert_fusion.7), channel_id=1, source_target_pairs={{0,12},{4,8},{8,4},{12,0},{1,13},{5,9},{9,5},{13,1},{2,14},{6,10},... | collective-permute-start | bytes 983048 | tf_op jit(solution)/shard_map/ppermute | solution.py:1315
  310.6 17.2 %collective-permute-start.27 = (bf16[320,512]{1,0:T(8,128)(2,1)S(1)}, bf16[320,512]{1,0:T(8,128)(2,1)S(1)}, u32[]{:S(2)}, u32[]{:S(2)}) collective-permute-start(bf16[320,512]{1,0:T(8,128)(2,1)S(1)} %add_convert_fusion.7), channel_id=1, source_target_pairs={{0,4},{4,0},{8,12},{12,8},{1,5},{5,1},{9,13},{13,9},{2,6},{6,2},{1... | collective-permute-start | bytes 983048 | tf_op jit(solution)/shard_map/ppermute | solution.py:1315
  310.9 16.8 %collective-permute-start.26 = (bf16[320,512]{1,0:T(8,128)(2,1)S(1)}, bf16[320,512]{1,0:T(8,128)(2,1)S(1)}, u32[]{:S(2)}, u32[]{:S(2)}) collective-permute-start(bf16[320,512]{1,0:T(8,128)(2,1)S(1)} %add_convert_fusion.7), channel_id=1, source_target_pairs={{0,8},{4,12},{8,0},{12,4},{1,9},{5,13},{9,1},{13,5},{2,10},{6,14},... | collective-permute-start | bytes 983048 | tf_op jit(solution)/shard_map/ppermute | solution.py:1315
  327.8 3.9 %collective-permute-start.29 = (bf16[1280,512]{1,0:T(8,128)(2,1)S(1)}, bf16[1280,512]{1,0:T(8,128)(2,1)S(1)}, u32[]{:S(2)}, u32[]{:S(2)}) collective-permute-start(bf16[1280,512]{1,0:T(8,128)(2,1)S(1)} %pad_maximum_fusion.mine), channel_id=1, source_target_pairs={{0,2},{2,0},{1,3},{3,1},{4,6},{6,4},{5,7},{7,5},{8,10},{10,8},{9,1... | collective-permute-start | bytes 3932168 | tf_op jit(solution)/shard_map/ppermute | solution.py:1303
  (25 other events, 177.4 us)

commit v4 on v3

--- a/solution.py
+++ b/solution.py
@@ -1540,9 +1540,9 @@
     )
     packed = list(packed)
     if paired:
-        eighth2, small = after((eighth2, small), feature_parts[1], weight1[1], packed[1])
+        part = lax.dynamic_slice_in_dim(small, core * (local // 2), local // 2, 1)
+        eighth2, part = after((eighth2, part), feature_parts[1], weight1[1], packed[1])
         weight2 = [conv2_weight, to_all(eighth2, ("core",) + QUAD, 8)]
-        part = lax.dynamic_slice_in_dim(small, core * (local // 2), local // 2, 1)
         own_small = swap(part, "chan")
     else:
         weight2 = [lax.all_gather(conv2_weight, "chan", axis=1, tiled=True)]
@@ -1589,12 +1589,13 @@
         sent = chain1.advance(output, vectors=vecs_own)
         in_parts = after([in_own, in_got], sent)
         input_grad = unpack_lanes(in_parts, True, F32, "unpack_input_grad")
-        sent = chain1.advance(input_grad), chain2.advance(input_grad)
-        sent = chain1.advance()
+        sent = chain1.advance(input_grad)
+        sent = sent, chain2.advance(sent)
         small_grads = assemble(
             position, after(chain2.pieces, sent), [0, 0, 0, 0, 9], False, "conv2_grads"
         )
         small_grads, weight2_grad = small_grads[:4], small_grads[4]
+        chain1.advance(weight2_grad)
         weight1_grad, vecs = assemble(position, chain1.pieces, [9], True, "conv1_grads")
         vecs = vecs[:16, :local]
     else:

time: 333 us -> 335 us (level)
  Pallas kernels: 192 us -> 185 us
  waiting for transfers between devices: 61.6 us -> 66.1 us
    ppermute x19, waiting for transfers between devices: 25.8 us -> 41.8 us  [swap(): return lax.ppermute(value, axis, [(0, 1), (1, 0)])]
    ppermute x15, waiting for transfers between devices: 35.8 us -> 24.3 us  [from_quad(): lax.ppermute(value, ('near', 'y'), [(at, at ^ bits) for at in range(4)])]
    pallas_call x1, Pallas kernels: 43.6 us -> 38.2 us  [attention(): call(functools.partial(attention_kernel, parts, outs, len(weight)), 'ssss...]
    ppermute x19, starting transfers between devices: 16.9 us -> 20.8 us  [swap(): return lax.ppermute(value, axis, [(0, 1), (1, 0)])]
    unnamed x71 -> x80, local copies, waits for them, and re-layouts: 6.57 us -> 7.93 us
  transfers between devices with their start and end apart: 36 -> 36, of which waited for: 14 -> 16; matrix products, arithmetic and copies ran while one was open for 2% -> 2% of each run, Pallas kernels for 38% -> 38%
where the time goes in v4:
time: 335 us; the launch traced here: 334 us
  Pallas kernels  185 us (55%)
  waiting for transfers between devices  66.1 us (20%)
  starting transfers between devices  62 us (19%)
  local copies, waits for them, and re-layouts  16.1 us (5%)
  other arithmetic  3.85 us (1%)
    ppermute x19, waiting for transfers between devices, swap(): return lax.ppermute(value, axis, [(0, 1), (1, 0)])  41.8 us
    pallas_call x1, Pallas kernels, attention(): call(functools.partial(attention_kernel, parts, outs, len(weight)), 'ssss...  38.2 us
    ppermute x15, starting transfers between devices, from_quad(): lax.ppermute(value, ('near', 'y'), [(at, at ^ bits) for at in range(4)])  33.1 us
    pallas_call x2, Pallas kernels, weight_grad(): call(functools.partial(weight_grad_kernel, paired, first, extra), 'svv' +...  29.5 us
    pallas_call x1, Pallas kernels, first(): call(functools.partial(first_kernel, len(parts), len(weight)), 'sss' + 'v...  24.8 us
    ppermute x15, waiting for transfers between devices, from_quad(): lax.ppermute(value, ('near', 'y'), [(at, at ^ bits) for at in range(4)])  24.3 us
    pallas_call x1, Pallas kernels, second(): call(functools.partial(second_kernel, len(weight)), 'sssvvh' + 'h' * len(...  22.3 us
    pallas_call x2, Pallas kernels, last(): call(functools.partial(last_kernel, whose, len(weight)), 'sssvvvvhhh' + '...  21.7 us
  transfers between devices with their start and end apart: 36, of which 16 were waited for; matrix products, arithmetic and copies ran while one was open for 2% of the time, Pallas kernels for 38%

profile of v4, /device:TPU:0, one launch (start us, length us, event | category | flops | bytes accessed | tf_op | source)
XLA Modules:
  0.0 334.1 jit_solution(6086353240976262014)
XLA Ops:
  0.7 1.5 stack.82.rest_2_
  2.2 3.0 collective-permute-start.2
  7.3 2.1 collective-permute-start.4
  10.0 6.0 %pack_features.1 = (s32[64]{0:T(128)}, s32[64]{0:T(128)}, s32[16]{0:T(128)}, s32[16]{0:T(128)}, bf16[2048,256]{1,0:T(8,128)(2,1)}, /*index=5*/bf16[2048,256]{1,0:T(8,128)(2,1)}) custom-call(s32[3]{0:T(128)} %pad_add_fusion.position, s32[64,64]{1,0:T(8,128)} %bitcast.62, s32[5028]{0:T(1024)} %constant.33.clone.table, bf16[256,4096]{1,0:T(8,128)(2,1)} %bitcast.60), custom_call_target="tpu_custom_call" | custom-call | flops 4294967296 | bytes 6291456 | tf_op jit(solution)/shard_map/pack_features/pallas_call | solution.py:475
  17.4 4.2 %all-to-all-start = ((bf16[4,9,32,512]{3,2,1,0:T(8,128)(2,1)}), bf16[4,9,32,512]{3,2,1,0:T(8,128)(2,1)S(1)}, u32[]{:S(2)}, u32[]{:S(2)}) async-start(bf16[4,9,32,512]{3,2,1,0:T(8,128)(2,1)} %broadcast_in_dim.8), calls=%async_computation | async-start | bytes 2359296 | tf_op jit(solution)/shard_map/all_to_all | solution.py:1307
  21.6 5.3 %pack_cotangent.1 = (bf16[2048,256]{1,0:T(8,128)(2,1)}, bf16[2048,256]{1,0:T(8,128)(2,1)}) custom-call(s32[3]{0:T(128)} %pad_add_fusion.position, s32[64]{0:T(128)} %get-tuple-element.123.slot_tile, bf16[256,4096]{1,0:T(8,128)(2,1)} %bitcast.61), custom_call_target="tpu_custom_call" | custom-call | flops 42949672960 | bytes 6291456 | tf_op jit(solution)/shard_map/pack_cotangent/pallas_call | solution.py:493
  28.2 15.5 %collective-permute-done.rest_1_ = bf16[2048,256]{1,0:T(8,128)(2,1)} collective-permute-done((bf16[2048,256]{1,0:T(8,128)(2,1)}, bf16[2048,256]{1,0:T(8,128)(2,1)}, u32[]{:S(2)}, u32[]{:S(2)}) %collective-permute-start) | collective-permute-done | bytes 1048608 | tf_op jit(solution)/shard_map/ppermute | solution.py:1303
  43.7 1.8 broadcast_in_dim.9
  45.5 3.8 %all-to-all-start.1 = ((bf16[8,9,32,512]{3,2,1,0:T(8,128)(2,1)}), bf16[8,9,32,512]{3,2,1,0:T(8,128)(2,1)S(1)}, u32[]{:S(2)}, u32[]{:S(2)}) async-start(bf16[8,9,32,512]{3,2,1,0:T(8,128)(2,1)} %broadcast_in_dim.9), calls=%async_computation.1 | async-start | bytes 4718592 | tf_op jit(solution)/shard_map/all_to_all | solution.py:1307
  50.3 2.2 collective-permute-done.3.rest_6_.rest_5_
  53.6 24.8 %conv1_forward.1 = (f32[16,512]{1,0:T(8,128)}, bf16[2048,512]{1,0:T(8,128)(2,1)}, bf16[10,10,32,512]{3,2,1,0:T(8,128)(2,1)}, bf16[64,32,512]{2,1,0:T(8,128)(2,1)...) custom-call(s32[3]{0:T(128)} %pad_add_fusion.position, ...), custom_call_target="tpu_custom_call" | custom-call | flops 9663676416 | bytes 20971520 | tf_op jit(solution)/shard_map/conv1_forward/pallas_call | solution.py:644
  79.0 1.4 copy-done
  80.4 22.3 %conv2_forward.1 = (bf16[2048,512]{1,0:T(8,128)(2,1)}, bf16[2048,512]{1,0:T(8,128)(2,1)}, f32[2,32,512]{2,1,0:T(8,128)}) custom-call(s32[3]{0:T(128)} %pad_add_fusion.position, s32[64]{0:T(128)} %get-tuple-element.123.slot_tile, s32[64]{0:T(128)} %get-tuple-element.124.slot_crop, f32[16,512]{1,0:T(8,128)} %get-tuple-element.131.par.rest_0_, ...), custom_call_target="tpu_custom_call" | custom-call | flops 9663676416 | bytes 16777216 | tf_op jit(solution)/shard_map/conv2_forward/pallas_call | solution.py:733
  103.8 38.2 %attention.1 = (bf16[2048,256]{1,0:T(8,128)(2,1)}, bf16[2048,256]{1,0:T(8,128)(2,1)}, bf16[1024,512]{1,0:T(8,128)(2,1)}, bf16[1024,512]{1,0:T(8,128)(2,1)}, f32[...) custom-call(s32[3]{0:T(128)} %pad_add_fusion.position, s32[64]{0:T(128)} %get-tuple-element.123.slot_tile, ...), custom_call_target="tpu_custom_call" | custom-call | flops 32212254720 | bytes 25165824 | tf_op jit(solution)/shard_map/attention/pallas_call | solution.py:1001
  142.1 1.9 copy-done.9
  144.0 1.2 copy-done.19
  146.5 16.0 %conv2_weight_grad.1 = (bf16[3328,512]{1,0:T(8,128)(2,1)S(1)}, bf16[3328,512]{1,0:T(8,128)(2,1)S(1)}) custom-call(s32[3]{0:T(128)S(1)} %copy-done.6, bf16[10,10,32,512]{3,2,1,0:T(8,128)(2,1)S(1)} %copy-done.14, bf16[10,10,32,512]{3,2,1,0:T(8,128)(2,1)S(1)} %copy-done.9, bf16[1024,512]{1,0:T(8,128)(2,1)S(1)} %copy-done.19, bf16[1024,512]{1,0:T(8,128)(2,1)S(1)} %copy-done.20), custom_call_target="tpu_custom_call" | custom-call | flops 9663676416 | bytes 12582912 | tf_op jit(solution)/shard_map/conv2_weight_grad/pallas_call | solution.py:1069
  162.5 4.5 %collective-permute-start.9 = (bf16[3328,512]{1,0:T(8,128)(2,1)S(1)}, bf16[3328,512]{1,0:T(8,128)(2,1)S(1)}, u32[]{:S(2)}, u32[]{:S(2)}) collective-permute-start(bf16[3328,512]{1,0:T(8,128)(2,1)S(1)} %get-tuple-element.153), channel_id=1, source_target_pairs={{0,2},{2,0},{1,3},{3,1},{4,6},{6,4},{5,7},{7,5},{8,10},{10,8},{9,1... | collective-permute-start | bytes 10223624 | tf_op jit(solution)/shard_map/ppermute | solution.py:1303
  167.0 19.2 %conv2_input_grad.1 = (bf16[10,10,32,512]{3,2,1,0:T(8,128)(2,1)S(1)}, f32[2,16,256]{2,1,0:T(8,128)S(1)}) custom-call(s32[3]{0:T(128)S(1)} %copy-done.6, s32[64]{0:T(128)S(1)} %copy-done.22, s32[64]{0:T(128)S(1)} %copy-done.23, f32[16,512]{1,0:T(8,128)S(1)} %copy-done.17, f32[2,32,512]{2,1,0:T(8,128)S(1)} %copy-done.21, ...), custom_call_target="tpu_custom_call" | custom-call | flops 9663676416 | bytes 16777216 | tf_op jit(solution)/shard_map/conv2_input_grad/pallas_call | solution.py:1182
  186.3 5.9 %collective-permute-done.8.rest_1_ = bf16[2048,256]{1,0:T(8,128)(2,1)S(1)} collective-permute-done((bf16[2048,256]{1,0:T(8,128)(2,1)S(1)}, bf16[2048,256]{1,0:T(8,128)(2,1)S(1)}, u32[]{:S(2)}, u32[]{:S(2)}) %collective-permute-start.8) | collective-permute-done | bytes 1048608 | tf_op jit(solution)/shard_map/ppermute | solution.py:1303
  193.6 4.0 %collective-permute-start.13 = (bf16[320,512]{1,0:T(8,128)(2,1)S(1)}, bf16[320,512]{1,0:T(8,128)(2,1)S(1)}, u32[]{:S(2)}, u32[]{:S(2)}) collective-permute-start(bf16[320,512]{1,0:T(8,128)(2,1)S(1)} %get-tuple-element.227), channel_id=1, source_target_pairs={{0,12},{4,8},{8,4},{12,0},{1,13},{5,9},{9,5},{13,1},{2,14},{6,10},... | collective-permute-start | bytes 983048 | tf_op jit(solution)/shard_map/ppermute | solution.py:1315
  197.6 4.1 %collective-permute-start.12 = (bf16[320,512]{1,0:T(8,128)(2,1)S(1)}, bf16[320,512]{1,0:T(8,128)(2,1)S(1)}, u32[]{:S(2)}, u32[]{:S(2)}) collective-permute-start(bf16[320,512]{1,0:T(8,128)(2,1)S(1)} %get-tuple-element.229), channel_id=1, source_target_pairs={{0,4},{4,0},{8,12},{12,8},{1,5},{5,1},{9,13},{13,9},{2,6},{6,2},{1... | collective-permute-start | bytes 983048 | tf_op jit(solution)/shard_map/ppermute | solution.py:1315
  201.8 1.4 collective-permute-start.11
  203.2 13.5 %conv1_weight_grad.1 = (bf16[2304,512]{1,0:T(8,128)(2,1)S(1)}, bf16[2304,512]{1,0:T(8,128)(2,1)S(1)}) custom-call(s32[3]{0:T(128)S(1)} %copy-done.6, bf16[10,10,32,512]{3,2,1,0:T(8,128)(2,1)S(1)} %copy-done.15, bf16[10,10,32,512]{3,2,1,0:T(8,128)(2,1)S(1)} %get-tuple-element.188.grad.rest_1_), custom_call_target="tpu_custom_call" | custom-call | flops 9663676416 | bytes 12582912 | tf_op jit(solution)/shard_map/conv1_weight_grad/pallas_call | solution.py:1069
  218.3 3.8 %collective-permute-start.17 = (bf16[256,512]{1,0:T(8,128)(2,1)S(1)}, bf16[256,512]{1,0:T(8,128)(2,1)S(1)}, u32[]{:S(2)}, u32[]{:S(2)}) collective-permute-start(bf16[256,512]{1,0:T(8,128)(2,1)S(1)} %get-tuple-element.237), channel_id=1, source_target_pairs={{0,12},{4,8},{8,4},{12,0},{1,13},{5,9},{9,5},{13,1},{2,14},{6,10},... | collective-permute-start | bytes 786440 | tf_op jit(solution)/shard_map/ppermute | solution.py:1315
  222.1 4.3 %collective-permute-start.16 = (bf16[256,512]{1,0:T(8,128)(2,1)S(1)}, bf16[256,512]{1,0:T(8,128)(2,1)S(1)}, u32[]{:S(2)}, u32[]{:S(2)}) collective-permute-start(bf16[256,512]{1,0:T(8,128)(2,1)S(1)} %get-tuple-element.238), channel_id=1, source_target_pairs={{0,4},{4,0},{8,12},{12,8},{1,5},{5,1},{9,13},{13,9},{2,6},{6,2},{1... | collective-permute-start | bytes 786440 | tf_op jit(solution)/shard_map/ppermute | solution.py:1315
  226.4 1.5 collective-permute-start.15
  227.9 10.9 %conv1_input_grad.2 = (bf16[2048,256]{1,0:T(8,128)(2,1)S(1)}, f32[16,256]{1,0:T(8,128)S(1)}) custom-call(s32[3]{0:T(128)S(1)} %copy-done.6, s32[64]{0:T(128)S(1)} %copy-done.22, s32[64]{0:T(128)S(1)} %copy-done.23, f32[16,512]{1,0:T(8,128)S(1)} %copy-done.17, f32[2,32,512]{2,1,0:T(8,128)S(1)} %copy-done.13, f32[2,16,256]{2,1,0:T(8,128)S(1)} %get-tuple-element.172.vecs2, ...), custom_call_target="tpu_custom_call" | custom-call | flops 4831838208 | bytes 10485760 | tf_op jit(solution)/shard_map/conv1_input_grad/pallas_call | solution.py:1265
  240.2 6.9 %collective-permute-start.22 = (bf16[416,512]{1,0:T(8,128)(2,1)S(1)}, bf16[416,512]{1,0:T(8,128)(2,1)S(1)}, u32[]{:S(2)}, u32[]{:S(2)}) collective-permute-start(bf16[416,512]{1,0:T(8,128)(2,1)S(1)} %pad_maximum_fusion.1), channel_id=1, source_target_pairs={{0,16},{16,0},{1,17},{17,1},{2,18},{18,2},{3,19},{19,3},{4,20},{20... | collective-permute-start | bytes 1277960 | tf_op jit(solution)/shard_map/ppermute | solution.py:1303
  247.8 3.0 collective-permute-start.21
  252.1 10.8 %conv1_input_grad.3 = (f32[2048,256]{1,0:T(8,128)S(1)}, f32[16,256]{1,0:T(8,128)S(1)}) custom-call(s32[3]{0:T(128)S(1)} %copy-done.6, s32[64]{0:T(128)S(1)} %copy-done.22, s32[64]{0:T(128)S(1)} %copy-done.23, f32[16,512]{1,0:T(8,128)S(1)} %copy-done.17, f32[2,32,512]{2,1,0:T(8,128)S(1)} %copy-done.13, f32[2,16,256]{2,1,0:T(8,128)S(1)} %get-tuple-element.172.vecs2, ...), custom_call_target="tpu_custom_call" | custom-call | flops 4831838208 | bytes 10485760 | tf_op jit(solution)/shard_map/conv1_input_grad/pallas_call | solution.py:1265
  262.9 3.1 collective-permute-done.22
  266.2 1.4 collective-permute-start.31
  267.6 5.4 %collective-permute-done.21 = bf16[576,512]{1,0:T(8,128)(2,1)S(1)} collective-permute-done((bf16[576,512]{1,0:T(8,128)(2,1)S(1)}, bf16[576,512]{1,0:T(8,128)(2,1)S(1)}, u32[]{:S(2)}, u32[]{:S(2)}) %collective-permute-start.21) | collective-permute-done | bytes 589856 | tf_op jit(solution)/shard_map/ppermute | solution.py:1315
  273.0 2.0 collective-permute-start.30
  275.0 1.3 collective-permute-done.20
  276.3 3.4 %collective-permute-start.29 = (bf16[416,512]{1,0:T(8,128)(2,1)S(1)}, bf16[416,512]{1,0:T(8,128)(2,1)S(1)}, u32[]{:S(2)}, u32[]{:S(2)}) collective-permute-start(bf16[416,512]{1,0:T(8,128)(2,1)S(1)} %add_convert_fusion.6), channel_id=1, source_target_pairs={{0,8},{4,12},{8,0},{12,4},{1,9},{5,13},{9,1},{13,5},{2,10},{6,14},... | collective-permute-start | bytes 1277960 | tf_op jit(solution)/shard_map/ppermute | solution.py:1315
  279.8 6.4 %collective-permute-done.19 = bf16[576,512]{1,0:T(8,128)(2,1)S(1)} collective-permute-done((bf16[576,512]{1,0:T(8,128)(2,1)S(1)}, bf16[576,512]{1,0:T(8,128)(2,1)S(1)}, u32[]{:S(2)}, u32[]{:S(2)}) %collective-permute-start.19) | collective-permute-done | bytes 589856 | tf_op jit(solution)/shard_map/ppermute | solution.py:1315
  287.7 4.5 %unpack_output.1 = bf16[256,4096]{1,0:T(8,128)(2,1)} custom-call(s32[3]{0:T(128)S(1)} %copy-done.6, s32[64]{0:T(128)S(1)} %copy-done.22, bf16[2048,256]{1,0:T(8,128)(2,1)S(1)} %copy-done.12, bf16[2048,256]{1,0:T(8,128)(2,1)S(1)} %collective-permute-done.8.rest_1_), custom_call_target="tpu_custom_call" | custom-call | flops 4294967296 | bytes 8388608 | tf_op jit(solution)/shard_map/unpack_output/pallas_call | solution.py:547
  292.2 1.9 collective-permute-done.24
  294.5 6.2 %unpack_input_grad.1 = f32[256,4096]{1,0:T(8,128)} custom-call(s32[3]{0:T(128)S(1)} %copy-done.6, s32[64]{0:T(128)S(1)} %copy-done.22, f32[2048,256]{1,0:T(8,128)S(1)} %get-tuple-element.206.rest_0_, bf16[2048,256]{1,0:T(8,128)(2,1)S(1)} %collective-permute-done.23.rest_1_), custom_call_target="tpu_custom_call" | custom-call | flops 4294967296 | bytes 8388608 | tf_op jit(solution)/shard_map/unpack_input_grad/pallas_call | solution.py:547
  300.7 8.9 %collective-permute-done.25 = bf16[320,512]{1,0:T(8,128)(2,1)S(1)} collective-permute-done((bf16[320,512]{1,0:T(8,128)(2,1)S(1)}, bf16[320,512]{1,0:T(8,128)(2,1)S(1)}, u32[]{:S(2)}, u32[]{:S(2)}) %collective-permute-start.25) | collective-permute-done | bytes 327712 | tf_op jit(solution)/shard_map/ppermute | solution.py:1303
  310.8 2.8 collective-permute-start.26
  313.6 3.8 %conv2_grads.1 = (f32[256,512]{1,0:T(8,128)}, f32[256,512]{1,0:T(8,128)}, f32[256,512]{1,0:T(8,128)}, f32[256,512]{1,0:T(8,128)}, f32[9,256,512]{2,1,0:T(8,128)}) custom-call(s32[3]{0:T(128)S(1)} %copy-done.6, bf16[1664,512]{1,0:T(8,128)(2,1)S(1)} %constant_dynamic-update-slice_fusion.mine, bf16[1664,512]{1,0:T(8,128)(2,1)S(1)} %collective-permute-done.32.other), custom_call_target="tpu_custom_call" | custom-call | flops 4294967296 | bytes 6291456 | tf_op jit(solution)/shard_map/conv2_grads/pallas_call | solution.py:1423
  317.4 4.1 %collective-permute-done.28 = bf16[320,512]{1,0:T(8,128)(2,1)S(1)} collective-permute-done((bf16[320,512]{1,0:T(8,128)(2,1)S(1)}, bf16[320,512]{1,0:T(8,128)(2,1)S(1)}, u32[]{:S(2)}, u32[]{:S(2)}) %collective-permute-start.28) | collective-permute-done | bytes 327712 | tf_op jit(solution)/shard_map/ppermute | solution.py:1315
  321.5 5.7 %collective-permute-done.27 = bf16[320,512]{1,0:T(8,128)(2,1)S(1)} collective-permute-done((bf16[320,512]{1,0:T(8,128)(2,1)S(1)}, bf16[320,512]{1,0:T(8,128)(2,1)S(1)}, u32[]{:S(2)}, u32[]{:S(2)}) %collective-permute-start.27) | collective-permute-done | bytes 327712 | tf_op jit(solution)/shard_map/ppermute | solution.py:1315
  327.4 3.0 collective-permute-done.33.other
  330.4 3.0 conv1_grads.1
  (162 shorter events, 20.6 us)
Async XLA Ops:
  2.2 13.9 %collective-permute-start.2 = (f32[16,256]{1,0:T(8,128)S(1)}, f32[16,256]{1,0:T(8,128)S(1)}, u32[]{:S(2)}, u32[]{:S(2)}) collective-permute-start(f32[16,256]{1,0:T(8,128)S(1)} %stack.82.rest_2_), channel_id=1, source_target_pairs={{0,1},{1,0},{2,3},{3,2},{4,5},{5,4},{6,7},{7,6},{8,9},{9,8},{10,11... | collective-permute-start | bytes 49160 | tf_op jit(solution)/shard_map/ppermute | solution.py:1303
  6.2 10.0 %collective-permute-start.1 = (bf16[9,32,512]{2,1,0:T(8,128)(2,1)S(1)}, bf16[9,32,512]{2,1,0:T(8,128)(2,1)S(1)}, u32[]{:S(2)}, u32[]{:S(2)}) collective-permute-start(bf16[9,32,512]{2,1,0:T(8,128)(2,1)S(1)} %constant_dynamic-slice_fusion.2), channel_id=1, source_target_pairs={{0,1},{1,0},{2,3},{3,2},{4,5},{5,4},{6,7},{7,6},{8,9},{9,8},{10,11... | collective-permute-start | bytes 884744 | tf_op jit(solution)/shard_map/ppermute | solution.py:1303
  7.3 20.6 %collective-permute-start.4 = (bf16[9,32,512]{2,1,0:T(8,128)(2,1)S(1)}, bf16[9,32,512]{2,1,0:T(8,128)(2,1)S(1)}, u32[]{:S(2)}, u32[]{:S(2)}) collective-permute-start(bf16[9,32,512]{2,1,0:T(8,128)(2,1)S(1)} %constant_dynamic-slice_fusion.1), channel_id=1, source_target_pairs={{0,1},{1,0},{2,3},{3,2},{4,5},{5,4},{6,7},{7,6},{8,9},{9,8},{10,11... | collective-permute-start | bytes 884744 | tf_op jit(solution)/shard_map/ppermute | solution.py:1303
  16.0 27.7 %collective-permute-start = (bf16[2048,256]{1,0:T(8,128)(2,1)}, bf16[2048,256]{1,0:T(8,128)(2,1)}, u32[]{:S(2)}, u32[]{:S(2)}) collective-permute-start(bf16[2048,256]{1,0:T(8,128)(2,1)} %get-tuple-element.128), channel_id=1, source_target_pairs={{0,1},{1,0},{2,3},{3,2},{4,5},{5,4},{6,7},{7,6},{8,9},{9,8},{10,11... | collective-permute-start | bytes 3145736 | tf_op jit(solution)/shard_map/ppermute | solution.py:1303
  17.4 26.3 %all-to-all-start = ((bf16[4,9,32,512]{3,2,1,0:T(8,128)(2,1)}), bf16[4,9,32,512]{3,2,1,0:T(8,128)(2,1)S(1)}, u32[]{:S(2)}, u32[]{:S(2)}) async-start(bf16[4,9,32,512]{3,2,1,0:T(8,128)(2,1)} %broadcast_in_dim.8), calls=%async_computation | async-start | bytes 2359296 | tf_op jit(solution)/shard_map/all_to_all | solution.py:1307
  45.5 33.6 %all-to-all-start.1 = ((bf16[8,9,32,512]{3,2,1,0:T(8,128)(2,1)}), bf16[8,9,32,512]{3,2,1,0:T(8,128)(2,1)S(1)}, u32[]{:S(2)}, u32[]{:S(2)}) async-start(bf16[8,9,32,512]{3,2,1,0:T(8,128)(2,1)} %broadcast_in_dim.9), calls=%async_computation.1 | async-start | bytes 4718592 | tf_op jit(solution)/shard_map/all_to_all | solution.py:1307
  49.3 3.3 collective-permute-start.3
  49.8 28.6 %collective-permute-start.5 = (bf16[4,128,512]{2,1,0:T(8,128)(2,1)}, bf16[4,128,512]{2,1,0:T(8,128)(2,1)}, u32[]{:S(2)}, u32[]{:S(2)}) collective-permute-start(bf16[4,128,512]{2,1,0:T(8,128)(2,1)} %constant_dynamic-slice_fusion), channel_id=1, source_target_pairs={{0,1},{1,0},{2,3},{3,2},{4,5},{5,4},{6,7},{7,6},{8,9},{9,8},{10,11... | collective-permute-start | bytes 1572872 | tf_op jit(solution)/shard_map/ppermute | solution.py:1303
  53.5 24.9 %copy-start.34 = (bf16[2048,256]{1,0:T(8,128)(2,1)S(1)}, bf16[2048,256]{1,0:T(8,128)(2,1)}, u32[]{:S(2)}) copy-start(bf16[2048,256]{1,0:T(8,128)(2,1)} %get-tuple-element.141) | copy-start | bytes 3145732
  78.4 25.4 %collective-permute-start.6 = (bf16[2048,256]{1,0:T(8,128)(2,1)S(1)}, bf16[2048,256]{1,0:T(8,128)(2,1)}, u32[]{:S(2)}, u32[]{:S(2)}) collective-permute-start(bf16[2048,256]{1,0:T(8,128)(2,1)S(1)} %copy-done.34), channel_id=1, source_target_pairs={{0,1},{1,0},{2,3},{3,2},{4,5},{5,4},{6,7},{7,6},{8,9},{9,8},{10,11... | collective-permute-start | bytes 3145736 | tf_op jit(solution)/shard_map/ppermute | solution.py:1303
  79.0 23.7 %collective-permute-start.7 = (bf16[4,128,512]{2,1,0:T(8,128)(2,1)}, bf16[4,128,512]{2,1,0:T(8,128)(2,1)}, u32[]{:S(2)}, u32[]{:S(2)}) collective-permute-start(bf16[4,128,512]{2,1,0:T(8,128)(2,1)} %collective-permute-done.5.rest_7_), channel_id=1, source_target_pairs={{0,2},{2,0},{1,3},{3,1},{4,6},{6,4},{5,7},{7,5},{8,10},{10,8},{9,1... | collective-permute-start | bytes 1572872 | tf_op jit(solution)/shard_map/ppermute | solution.py:1303
  103.8 38.2 %copy-start.6 = (s32[3]{0:T(128)S(1)}, s32[3]{0:T(128)}, u32[]{:S(2)}) copy-start(s32[3]{0:T(128)} %pad_add_fusion.position) | copy-start | bytes 40
  103.8 38.3 %copy-start.14 = (bf16[10,10,32,512]{3,2,1,0:T(8,128)(2,1)S(1)}, bf16[10,10,32,512]{3,2,1,0:T(8,128)(2,1)}, u32[]{:S(2)}) copy-start(bf16[10,10,32,512]{3,2,1,0:T(8,128)(2,1)} %get-tuple-element.133.pad_hbm.active) | copy-start | bytes 9830404
  146.4 20.6 %copy-start.16 = (bf16[64,32,512]{2,1,0:T(8,128)(2,1)S(1)}, bf16[64,32,512]{2,1,0:T(8,128)(2,1)}, u32[]{:S(2)}) copy-start(bf16[64,32,512]{2,1,0:T(8,128)(2,1)} %get-tuple-element.155.hidden_hbm) | copy-start | bytes 6291460
  146.4 20.6 %copy-start.17 = (f32[16,512]{1,0:T(8,128)S(1)}, f32[16,512]{1,0:T(8,128)}, u32[]{:S(2)}) copy-start(f32[16,512]{1,0:T(8,128)} %get-tuple-element.131.par.rest_0_) | copy-start | bytes 98308
  146.5 20.6 %copy-start.21 = (f32[2,32,512]{2,1,0:T(8,128)S(1)}, f32[2,32,512]{2,1,0:T(8,128)}, u32[]{:S(2)}) copy-start(f32[2,32,512]{2,1,0:T(8,128)} %get-tuple-element.149.stats2) | copy-start | bytes 393220
  146.5 20.6 %copy-start.22 = (s32[64]{0:T(128)S(1)}, s32[64]{0:T(128)}, u32[]{:S(2)}) copy-start(s32[64]{0:T(128)} %get-tuple-element.123.slot_tile) | copy-start | bytes 772
  146.5 20.6 %copy-start.23 = (s32[64]{0:T(128)S(1)}, s32[64]{0:T(128)}, u32[]{:S(2)}) copy-start(s32[64]{0:T(128)} %get-tuple-element.124.slot_crop) | copy-start | bytes 772
  162.5 29.6 %collective-permute-start.9 = (bf16[3328,512]{1,0:T(8,128)(2,1)S(1)}, bf16[3328,512]{1,0:T(8,128)(2,1)S(1)}, u32[]{:S(2)}, u32[]{:S(2)}) collective-permute-start(bf16[3328,512]{1,0:T(8,128)(2,1)S(1)} %get-tuple-element.153), channel_id=1, source_target_pairs={{0,2},{2,0},{1,3},{3,1},{4,6},{6,4},{5,7},{7,5},{8,10},{10,8},{9,1... | collective-permute-start | bytes 10223624 | tf_op jit(solution)/shard_map/ppermute | solution.py:1303
  167.0 25.1 %collective-permute-start.8 = (bf16[2048,256]{1,0:T(8,128)(2,1)S(1)}, bf16[2048,256]{1,0:T(8,128)(2,1)S(1)}, u32[]{:S(2)}, u32[]{:S(2)}) collective-permute-start(bf16[2048,256]{1,0:T(8,128)(2,1)S(1)} %copy-done.35), channel_id=1, source_target_pairs={{0,1},{1,0},{2,3},{3,2},{4,5},{5,4},{6,7},{7,6},{8,9},{9,8},{10,11... | collective-permute-start | bytes 3145736 | tf_op jit(solution)/shard_map/ppermute | solution.py:1303
  192.8 24.4 %collective-permute-start.10 = (bf16[1024,512]{1,0:T(8,128)(2,1)S(1)}, bf16[1024,512]{1,0:T(8,128)(2,1)S(1)}, u32[]{:S(2)}, u32[]{:S(2)}) collective-permute-start(bf16[1024,512]{1,0:T(8,128)(2,1)S(1)} %get-tuple-element.231), channel_id=1, source_target_pairs={{0,1},{1,0},{2,3},{3,2},{4,5},{5,4},{6,7},{7,6},{8,9},{9,8},{10,11... | collective-permute-start | bytes 3145736 | tf_op jit(solution)/shard_map/ppermute | solution.py:1303
  193.6 23.1 %collective-permute-start.13 = (bf16[320,512]{1,0:T(8,128)(2,1)S(1)}, bf16[320,512]{1,0:T(8,128)(2,1)S(1)}, u32[]{:S(2)}, u32[]{:S(2)}) collective-permute-start(bf16[320,512]{1,0:T(8,128)(2,1)S(1)} %get-tuple-element.227), channel_id=1, source_target_pairs={{0,12},{4,8},{8,4},{12,0},{1,13},{5,9},{9,5},{13,1},{2,14},{6,10},... | collective-permute-start | bytes 983048 | tf_op jit(solution)/shard_map/ppermute | solution.py:1315
  197.6 19.1 %collective-permute-start.12 = (bf16[320,512]{1,0:T(8,128)(2,1)S(1)}, bf16[320,512]{1,0:T(8,128)(2,1)S(1)}, u32[]{:S(2)}, u32[]{:S(2)}) collective-permute-start(bf16[320,512]{1,0:T(8,128)(2,1)S(1)} %get-tuple-element.229), channel_id=1, source_target_pairs={{0,4},{4,0},{8,12},{12,8},{1,5},{5,1},{9,13},{13,9},{2,6},{6,2},{1... | collective-permute-start | bytes 983048 | tf_op jit(solution)/shard_map/ppermute | solution.py:1315
  201.8 15.4 %collective-permute-start.11 = (bf16[320,512]{1,0:T(8,128)(2,1)S(1)}, bf16[320,512]{1,0:T(8,128)(2,1)S(1)}, u32[]{:S(2)}, u32[]{:S(2)}) collective-permute-start(bf16[320,512]{1,0:T(8,128)(2,1)S(1)} %get-tuple-element.230), channel_id=1, source_target_pairs={{0,8},{4,12},{8,0},{12,4},{1,9},{5,13},{9,1},{13,5},{2,10},{6,14},... | collective-permute-start | bytes 983048 | tf_op jit(solution)/shard_map/ppermute | solution.py:1315
  203.1 24.7 %copy-start.5 = (bf16[9,256,512]{2,1,0:T(8,128)(2,1)S(1)}, bf16[9,256,512]{2,1,0:T(8,128)(2,1)}, u32[]{:S(2)}) copy-start(bf16[9,256,512]{2,1,0:T(8,128)(2,1)} %rest_3_.3) | copy-start | bytes 7077892
  203.2 24.7 %copy-start.10 = (bf16[10,10,32,512]{3,2,1,0:T(8,128)(2,1)S(1)}, bf16[10,10,32,512]{3,2,1,0:T(8,128)(2,1)}, u32[]{:S(2)}) copy-start(bf16[10,10,32,512]{3,2,1,0:T(8,128)(2,1)} %get-tuple-element.154.grad.pad_hbm.rest_2_) | copy-start | bytes 9830404
  203.2 24.7 %copy-start.11 = (bf16[2048,512]{1,0:T(8,128)(2,1)S(1)}, bf16[2048,512]{1,0:T(8,128)(2,1)}, u32[]{:S(2)}) copy-start(bf16[2048,512]{1,0:T(8,128)(2,1)} %get-tuple-element.132.feats.rest_0_) | copy-start | bytes 6291460
  217.2 21.6 %copy-start.28 = (bf16[320,512]{1,0:T(8,128)(2,1)}, bf16[320,512]{1,0:T(8,128)(2,1)S(1)}, u32[]{:S(2)}) copy-start(bf16[320,512]{1,0:T(8,128)(2,1)S(1)} %collective-permute-done.11) | copy-start | bytes 983044
  217.5 29.5 %collective-permute-start.14 = (bf16[2304,512]{1,0:T(8,128)(2,1)S(1)}, bf16[2304,512]{1,0:T(8,128)(2,1)S(1)}, u32[]{:S(2)}, u32[]{:S(2)}) collective-permute-start(bf16[2304,512]{1,0:T(8,128)(2,1)S(1)} %get-tuple-element.170), channel_id=1, source_target_pairs={{0,2},{2,0},{1,3},{3,1},{4,6},{6,4},{5,7},{7,5},{8,10},{10,8},{9,1... | collective-permute-start | bytes 7077896 | tf_op jit(solution)/shard_map/ppermute | solution.py:1303
  217.6 21.3 %collective-permute-start.18 = (bf16[160,512]{1,0:T(8,128)(2,1)S(1)}, bf16[160,512]{1,0:T(8,128)(2,1)S(1)}, u32[]{:S(2)}, u32[]{:S(2)}) collective-permute-start(bf16[160,512]{1,0:T(8,128)(2,1)S(1)} %add_convert_fusion.19), channel_id=1, source_target_pairs={{0,1},{1,0},{2,3},{3,2},{4,5},{5,4},{6,7},{7,6},{8,9},{9,8},{10,11... | collective-permute-start | bytes 491528 | tf_op jit(solution)/shard_map/ppermute | solution.py:1303
  218.3 20.6 %collective-permute-start.17 = (bf16[256,512]{1,0:T(8,128)(2,1)S(1)}, bf16[256,512]{1,0:T(8,128)(2,1)S(1)}, u32[]{:S(2)}, u32[]{:S(2)}) collective-permute-start(bf16[256,512]{1,0:T(8,128)(2,1)S(1)} %get-tuple-element.237), channel_id=1, source_target_pairs={{0,12},{4,8},{8,4},{12,0},{1,13},{5,9},{9,5},{13,1},{2,14},{6,10},... | collective-permute-start | bytes 786440 | tf_op jit(solution)/shard_map/ppermute | solution.py:1315
  222.1 16.8 %collective-permute-start.16 = (bf16[256,512]{1,0:T(8,128)(2,1)S(1)}, bf16[256,512]{1,0:T(8,128)(2,1)S(1)}, u32[]{:S(2)}, u32[]{:S(2)}) collective-permute-start(bf16[256,512]{1,0:T(8,128)(2,1)S(1)} %get-tuple-element.238), channel_id=1, source_target_pairs={{0,4},{4,0},{8,12},{12,8},{1,5},{5,1},{9,13},{13,9},{2,6},{6,2},{1... | collective-permute-start | bytes 786440 | tf_op jit(solution)/shard_map/ppermute | solution.py:1315
  226.4 13.5 %collective-permute-start.15 = (bf16[256,512]{1,0:T(8,128)(2,1)S(1)}, bf16[256,512]{1,0:T(8,128)(2,1)S(1)}, u32[]{:S(2)}, u32[]{:S(2)}) collective-permute-start(bf16[256,512]{1,0:T(8,128)(2,1)S(1)} %get-tuple-element.239), channel_id=1, source_target_pairs={{0,8},{4,12},{8,0},{12,4},{1,9},{5,13},{9,1},{13,5},{2,10},{6,14},... | collective-permute-start | bytes 786440 | tf_op jit(solution)/shard_map/ppermute | solution.py:1315
  240.2 25.9 %collective-permute-start.22 = (bf16[416,512]{1,0:T(8,128)(2,1)S(1)}, bf16[416,512]{1,0:T(8,128)(2,1)S(1)}, u32[]{:S(2)}, u32[]{:S(2)}) collective-permute-start(bf16[416,512]{1,0:T(8,128)(2,1)S(1)} %pad_maximum_fusion.1), channel_id=1, source_target_pairs={{0,16},{16,0},{1,17},{17,1},{2,18},{18,2},{3,19},{19,3},{4,20},{20... | collective-permute-start | bytes 1277960 | tf_op jit(solution)/shard_map/ppermute | solution.py:1303
  247.8 25.2 %collective-permute-start.21 = (bf16[576,512]{1,0:T(8,128)(2,1)S(1)}, bf16[576,512]{1,0:T(8,128)(2,1)S(1)}, u32[]{:S(2)}, u32[]{:S(2)}) collective-permute-start(bf16[576,512]{1,0:T(8,128)(2,1)S(1)} %get-tuple-element.233), channel_id=1, source_target_pairs={{0,12},{4,8},{8,4},{12,0},{1,13},{5,9},{9,5},{13,1},{2,14},{6,10},... | collective-permute-start | bytes 1769480 | tf_op jit(solution)/shard_map/ppermute | solution.py:1315
  250.8 25.5 %collective-permute-start.20 = (bf16[576,512]{1,0:T(8,128)(2,1)S(1)}, bf16[576,512]{1,0:T(8,128)(2,1)S(1)}, u32[]{:S(2)}, u32[]{:S(2)}) collective-permute-start(bf16[576,512]{1,0:T(8,128)(2,1)S(1)} %get-tuple-element.234), channel_id=1, source_target_pairs={{0,4},{4,0},{8,12},{12,8},{1,5},{5,1},{9,13},{13,9},{2,6},{6,2},{1... | collective-permute-start | bytes 1769480 | tf_op jit(solution)/shard_map/ppermute | solution.py:1315
  251.0 35.2 %collective-permute-start.19 = (bf16[576,512]{1,0:T(8,128)(2,1)S(1)}, bf16[576,512]{1,0:T(8,128)(2,1)S(1)}, u32[]{:S(2)}, u32[]{:S(2)}) collective-permute-start(bf16[576,512]{1,0:T(8,128)(2,1)S(1)} %get-tuple-element.235), channel_id=1, source_target_pairs={{0,8},{4,12},{8,0},{12,4},{1,9},{5,13},{9,1},{13,5},{2,10},{6,14},... | collective-permute-start | bytes 1769480 | tf_op jit(solution)/shard_map/ppermute | solution.py:1315
  251.5 36.2 %collective-permute-start.23 = (bf16[2048,256]{1,0:T(8,128)(2,1)S(1)}, bf16[2048,256]{1,0:T(8,128)(2,1)S(1)}, u32[]{:S(2)}, u32[]{:S(2)}) collective-permute-start(bf16[2048,256]{1,0:T(8,128)(2,1)S(1)} %get-tuple-element.197), channel_id=1, source_target_pairs={{0,1},{1,0},{2,3},{3,2},{4,5},{5,4},{6,7},{7,6},{8,9},{9,8},{10,11... | collective-permute-start | bytes 3145736 | tf_op jit(solution)/shard_map/ppermute | solution.py:1303
  266.2 43.5 %collective-permute-start.31 = (bf16[416,512]{1,0:T(8,128)(2,1)S(1)}, bf16[416,512]{1,0:T(8,128)(2,1)S(1)}, u32[]{:S(2)}, u32[]{:S(2)}) collective-permute-start(bf16[416,512]{1,0:T(8,128)(2,1)S(1)} %add_convert_fusion.6), channel_id=1, source_target_pairs={{0,12},{4,8},{8,4},{12,0},{1,13},{5,9},{9,5},{13,1},{2,14},{6,10},... | collective-permute-start | bytes 1277960 | tf_op jit(solution)/shard_map/ppermute | solution.py:1315
  273.0 36.7 %collective-permute-start.30 = (bf16[416,512]{1,0:T(8,128)(2,1)S(1)}, bf16[416,512]{1,0:T(8,128)(2,1)S(1)}, u32[]{:S(2)}, u32[]{:S(2)}) collective-permute-start(bf16[416,512]{1,0:T(8,128)(2,1)S(1)} %add_convert_fusion.6), channel_id=1, source_target_pairs={{0,4},{4,0},{8,12},{12,8},{1,5},{5,1},{9,13},{13,9},{2,6},{6,2},{1... | collective-permute-start | bytes 1277960 | tf_op jit(solution)/shard_map/ppermute | solution.py:1315
  276.3 33.5 %collective-permute-start.29 = (bf16[416,512]{1,0:T(8,128)(2,1)S(1)}, bf16[416,512]{1,0:T(8,128)(2,1)S(1)}, u32[]{:S(2)}, u32[]{:S(2)}) collective-permute-start(bf16[416,512]{1,0:T(8,128)(2,1)S(1)} %add_convert_fusion.6), channel_id=1, source_target_pairs={{0,8},{4,12},{8,0},{12,4},{1,9},{5,13},{9,1},{13,5},{2,10},{6,14},... | collective-permute-start | bytes 1277960 | tf_op jit(solution)/shard_map/ppermute | solution.py:1315
  287.0 7.1 %collective-permute-start.24 = (bf16[320,512]{1,0:T(8,128)(2,1)S(1)}, bf16[320,512]{1,0:T(8,128)(2,1)S(1)}, u32[]{:S(2)}, u32[]{:S(2)}) collective-permute-start(bf16[320,512]{1,0:T(8,128)(2,1)S(1)} %fusion.1), channel_id=1, source_target_pairs={{0,1},{1,0},{2,3},{3,2},{4,5},{5,4},{6,7},{7,6},{8,9},{9,8},{10,11... | collective-permute-start | bytes 983048 | tf_op jit(solution)/shard_map/ppermute | solution.py:1303
  294.4 15.2 %collective-permute-start.25 = (bf16[320,512]{1,0:T(8,128)(2,1)S(1)}, bf16[320,512]{1,0:T(8,128)(2,1)S(1)}, u32[]{:S(2)}, u32[]{:S(2)}) collective-permute-start(bf16[320,512]{1,0:T(8,128)(2,1)S(1)} %pad_maximum_fusion.2), channel_id=1, source_target_pairs={{0,16},{16,0},{1,17},{17,1},{2,18},{18,2},{3,19},{19,3},{4,20},{20... | collective-permute-start | bytes 983048 | tf_op jit(solution)/shard_map/ppermute | solution.py:1303
  309.9 3.7 %collective-permute-start.32 = (bf16[1664,512]{1,0:T(8,128)(2,1)S(1)}, bf16[1664,512]{1,0:T(8,128)(2,1)S(1)}, u32[]{:S(2)}, u32[]{:S(2)}) collective-permute-start(bf16[1664,512]{1,0:T(8,128)(2,1)S(1)} %constant_dynamic-update-slice_fusion.mine), channel_id=1, source_target_pairs={{0,2},{2,0},{1,3},{3,1},{4,6},{6,4},{5,7},{7,5},{8,10},{10,8},{9,1... | collective-permute-start | bytes 5111816 | tf_op jit(solution)/shard_map/ppermute | solution.py:1303
  310.0 11.5 %collective-permute-start.28 = (bf16[320,512]{1,0:T(8,128)(2,1)S(1)}, bf16[320,512]{1,0:T(8,128)(2,1)S(1)}, u32[]{:S(2)}, u32[]{:S(2)}) collective-permute-start(bf16[320,512]{1,0:T(8,128)(2,1)S(1)} %add_convert_fusion.7), channel_id=1, source_target_pairs={{0,12},{4,8},{8,4},{12,0},{1,13},{5,9},{9,5},{13,1},{2,14},{6,10},... | collective-permute-start | bytes 983048 | tf_op jit(solution)/shard_map/ppermute | solution.py:1315
  310.4 16.8 %collective-permute-start.27 = (bf16[320,512]{1,0:T(8,128)(2,1)S(1)}, bf16[320,512]{1,0:T(8,128)(2,1)S(1)}, u32[]{:S(2)}, u32[]{:S(2)}) collective-permute-start(bf16[320,512]{1,0:T(8,128)(2,1)S(1)} %add_convert_fusion.7), channel_id=1, source_target_pairs={{0,4},{4,0},{8,12},{12,8},{1,5},{5,1},{9,13},{13,9},{2,6},{6,2},{1... | collective-permute-start | bytes 983048 | tf_op jit(solution)/shard_map/ppermute | solution.py:1315
  310.8 16.4 %collective-permute-start.26 = (bf16[320,512]{1,0:T(8,128)(2,1)S(1)}, bf16[320,512]{1,0:T(8,128)(2,1)S(1)}, u32[]{:S(2)}, u32[]{:S(2)}) collective-permute-start(bf16[320,512]{1,0:T(8,128)(2,1)S(1)} %add_convert_fusion.7), channel_id=1, source_target_pairs={{0,8},{4,12},{8,0},{12,4},{1,9},{5,13},{9,1},{13,5},{2,10},{6,14},... | collective-permute-start | bytes 983048 | tf_op jit(solution)/shard_map/ppermute | solution.py:1315
  327.3 3.1 collective-permute-start.33
  (29 other events, 212.5 us)

commit v5 on v4

--- a/solution.py
+++ b/solution.py
@@ -1500,22 +1500,24 @@
         whole = unpack(position, tables[0], parts, pixels, by_pixel, dtype, slots, name)
         return whole[:local]
 
-    vectors = jnp.stack(
-        [
-            norm1_gain,
-            norm1_bias,
-            conv1_bias,
-            norm2_gain,
-            norm2_bias,
-            conv2_bias,
-            norm3_gain,
-            norm3_bias,
-            query_bias,
-            value_bias,
-            proj_bias,
-        ]
-        + [jnp.zeros_like(proj_bias)] * 5
-    )
+    def vector_table(norm1_gain):
+        return jnp.stack(
+            [
+                norm1_gain,
+                norm1_bias,
+                conv1_bias,
+                norm2_gain,
+                norm2_bias,
+                conv2_bias,
+                norm3_gain,
+                norm3_bias,
+                query_bias,
+                value_bias,
+                proj_bias,
+            ]
+            + [jnp.zeros_like(proj_bias)] * 5
+        )
+
     small = jnp.stack([query_weight, key_weight, value_weight, proj_weight])
     if paired:
         eighth = local // 8
@@ -1523,18 +1525,19 @@
         eighth1 = swap(part, "chan")
         part = lax.dynamic_slice_in_dim(conv2_weight, piece * eighth, eighth, 1)
         eighth2 = swap(part, "chan")
-        par_parts = [vectors, swap(vectors, "chan")]
     else:
-        par_parts = [lax.all_gather(vectors, "chan", axis=1, tiled=True)]
+        par_parts = [lax.all_gather(vector_table(norm1_gain), "chan", axis=1, tiled=True)]
         weight1 = [lax.all_gather(conv1_weight, "chan", axis=1, tiled=True)]
     tables, packed = pack_first(
         position, crop_ids[0], widened(features[0]), devices, slots, "pack_features"
     )
     feature_parts = exchange(narrowed(packed))
     if paired:
-        eighth1, par_parts[1] = after((eighth1, par_parts[1]), packed[1])
+        eighth1 = after(eighth1, packed[1])
         mine = to_all(eighth1, QUAD, 4)
         weight1 = [conv1_weight, mine, swap(mine, "core")]
+        vectors = vector_table(after(norm1_gain, eighth1))
+        par_parts = [vectors, swap(vectors, "chan")]
     packed = pack(
         position, tables[0], widened(cotangent[0]), False, devices, slots, "pack_cotangent"
     )

time: 335 us -> 337 us (level)
  Pallas kernels: 185 us -> 191 us
  waiting for transfers between devices: 66.1 us -> 61 us
    pallas_call x1, Pallas kernels: 38.2 us -> 43.2 us  [attention(): call(functools.partial(attention_kernel, parts, outs, len(weight)), 'ssss...]
    unnamed x80 -> x76, local copies, waits for them, and re-layouts: 7.93 us -> 7.5 us
  transfers between devices with their start and end apart: 36 -> 36, of which waited for: 16 -> 13; matrix products, arithmetic and copies ran while one was open for 2% -> 3% of each run, Pallas kernels for 38% -> 38%
where the time goes in v5:
time: 337 us; the launch traced here: 336 us
  Pallas kernels  191 us (57%)
  starting transfers between devices  61 us (18%)
  waiting for transfers between devices  61 us (18%)
  local copies, waits for them, and re-layouts  17.6 us (5%)
  other arithmetic  3.8 us (1%)
    pallas_call x1, Pallas kernels, attention(): call(functools.partial(attention_kernel, parts, outs, len(weight)), 'ssss...  43.2 us
    ppermute x19, waiting for transfers between devices, swap(): return lax.ppermute(value, axis, [(0, 1), (1, 0)])  38.6 us
    ppermute x15, starting transfers between devices, from_quad(): lax.ppermute(value, ('near', 'y'), [(at, at ^ bits) for at in range(4)])  31.4 us
    pallas_call x2, Pallas kernels, weight_grad(): call(functools.partial(weight_grad_kernel, paired, first, extra), 'svv' +...  29.5 us
    pallas_call x1, Pallas kernels, first(): call(functools.partial(first_kernel, len(parts), len(weight)), 'sss' + 'v...  24.8 us
    pallas_call x2, Pallas kernels, last(): call(functools.partial(last_kernel, whose, len(weight)), 'sssvvvvhhh' + '...  23.5 us
    ppermute x15, waiting for transfers between devices, from_quad(): lax.ppermute(value, ('near', 'y'), [(at, at ^ bits) for at in range(4)])  22.4 us
    pallas_call x1, Pallas kernels, second(): call(functools.partial(second_kernel, len(weight)), 'sssvvh' + 'h' * len(...  22.3 us
  transfers between devices with their start and end apart: 36, of which 13 were waited for; matrix products, arithmetic and copies ran while one was open for 3% of the time, Pallas kernels for 38%

profile of v5, /device:TPU:0, one launch (start us, length us, event | category | flops | bytes accessed | tf_op | source)
XLA Modules:
  0.0 336.2 jit_solution(6611260698050882185)
XLA Ops:
  1.7 3.0 collective-permute-start.1
  6.3 6.0 %pack_features.1 = (s32[64]{0:T(128)}, s32[64]{0:T(128)}, s32[16]{0:T(128)}, s32[16]{0:T(128)}, bf16[2048,256]{1,0:T(8,128)(2,1)}, /*index=5*/bf16[2048,256]{1,0:T(8,128)(2,1)}) custom-call(s32[3]{0:T(128)} %pad_add_fusion.position, s32[64,64]{1,0:T(8,128)} %bitcast.62, s32[5028]{0:T(1024)} %constant.33.clone.table, bf16[256,4096]{1,0:T(8,128)(2,1)} %bitcast.60), custom_call_target="tpu_custom_call" | custom-call | flops 4294967296 | bytes 6291456 | tf_op jit(solution)/shard_map/pack_features/pallas_call | solution.py:475
  12.4 2.1 collective-permute-start
  14.4 1.2 broadcast_in_dim.8
  15.6 3.8 %all-to-all-start = ((bf16[4,9,32,512]{3,2,1,0:T(8,128)(2,1)}), bf16[4,9,32,512]{3,2,1,0:T(8,128)(2,1)S(1)}, u32[]{:S(2)}, u32[]{:S(2)}) async-start(bf16[4,9,32,512]{3,2,1,0:T(8,128)(2,1)} %broadcast_in_dim.8), calls=%async_computation | async-start | bytes 2359296 | tf_op jit(solution)/shard_map/all_to_all | solution.py:1307
  19.4 5.2 %pack_cotangent.1 = (bf16[2048,256]{1,0:T(8,128)(2,1)}, bf16[2048,256]{1,0:T(8,128)(2,1)}) custom-call(s32[3]{0:T(128)} %pad_add_fusion.position, s32[64]{0:T(128)} %get-tuple-element.123.slot_tile, bf16[256,4096]{1,0:T(8,128)(2,1)} %bitcast.61), custom_call_target="tpu_custom_call" | custom-call | flops 42949672960 | bytes 6291456 | tf_op jit(solution)/shard_map/pack_cotangent/pallas_call | solution.py:493
  25.9 14.6 %collective-permute-done.rest_1_ = bf16[2048,256]{1,0:T(8,128)(2,1)} collective-permute-done((bf16[2048,256]{1,0:T(8,128)(2,1)}, bf16[2048,256]{1,0:T(8,128)(2,1)}, u32[]{:S(2)}, u32[]{:S(2)}) %collective-permute-start) | collective-permute-done | bytes 1048608 | tf_op jit(solution)/shard_map/ppermute | solution.py:1303
  40.6 1.8 broadcast_in_dim.9
  42.4 4.1 %all-to-all-start.1 = ((bf16[8,9,32,512]{3,2,1,0:T(8,128)(2,1)}), bf16[8,9,32,512]{3,2,1,0:T(8,128)(2,1)S(1)}, u32[]{:S(2)}, u32[]{:S(2)}) async-start(bf16[8,9,32,512]{3,2,1,0:T(8,128)(2,1)} %broadcast_in_dim.9), calls=%async_computation.1 | async-start | bytes 4718592 | tf_op jit(solution)/shard_map/all_to_all | solution.py:1307
  48.1 1.6 stack.82.rest_2_
  49.7 1.6 collective-permute-start.2
  51.8 1.7 collective-permute-done.2.rest_3_
  54.1 24.8 %conv1_forward.1 = (f32[16,512]{1,0:T(8,128)}, bf16[2048,512]{1,0:T(8,128)(2,1)}, bf16[10,10,32,512]{3,2,1,0:T(8,128)(2,1)}, bf16[64,32,512]{2,1,0:T(8,128)(2,1)...) custom-call(s32[3]{0:T(128)} %pad_add_fusion.position, ...), custom_call_target="tpu_custom_call" | custom-call | flops 9663676416 | bytes 20971520 | tf_op jit(solution)/shard_map/conv1_forward/pallas_call | solution.py:644
  79.0 1.6 collective-permute-start.6
  80.6 1.4 copy-done
  82.0 22.3 %conv2_forward.1 = (bf16[2048,512]{1,0:T(8,128)(2,1)}, bf16[2048,512]{1,0:T(8,128)(2,1)}, f32[2,32,512]{2,1,0:T(8,128)}) custom-call(s32[3]{0:T(128)} %pad_add_fusion.position, s32[64]{0:T(128)} %get-tuple-element.123.slot_tile, s32[64]{0:T(128)} %get-tuple-element.124.slot_crop, f32[16,512]{1,0:T(8,128)} %get-tuple-element.131.par.rest_0_, ...), custom_call_target="tpu_custom_call" | custom-call | flops 9663676416 | bytes 16777216 | tf_op jit(solution)/shard_map/conv2_forward/pallas_call | solution.py:733
  104.3 43.2 %attention.1 = (bf16[2048,256]{1,0:T(8,128)(2,1)}, bf16[2048,256]{1,0:T(8,128)(2,1)}, bf16[1024,512]{1,0:T(8,128)(2,1)}, bf16[1024,512]{1,0:T(8,128)(2,1)}, f32[...) custom-call(s32[3]{0:T(128)} %pad_add_fusion.position, s32[64]{0:T(128)} %get-tuple-element.123.slot_tile, ...), custom_call_target="tpu_custom_call" | custom-call | flops 32212254720 | bytes 25165824 | tf_op jit(solution)/shard_map/attention/pallas_call | solution.py:1001
  147.6 1.9 copy-done.7
  149.5 1.2 copy-done.17
  150.7 1.2 copy-done.18
  152.0 16.0 %conv2_weight_grad.1 = (bf16[3328,512]{1,0:T(8,128)(2,1)S(1)}, bf16[3328,512]{1,0:T(8,128)(2,1)S(1)}) custom-call(s32[3]{0:T(128)S(1)} %copy-done.6, bf16[10,10,32,512]{3,2,1,0:T(8,128)(2,1)S(1)} %copy-done.12, bf16[10,10,32,512]{3,2,1,0:T(8,128)(2,1)S(1)} %copy-done.7, bf16[1024,512]{1,0:T(8,128)(2,1)S(1)} %copy-done.17, bf16[1024,512]{1,0:T(8,128)(2,1)S(1)} %copy-done.18), custom_call_target="tpu_custom_call" | custom-call | flops 9663676416 | bytes 12582912 | tf_op jit(solution)/shard_map/conv2_weight_grad/pallas_call | solution.py:1069
  168.2 19.2 %conv2_input_grad.1 = (bf16[10,10,32,512]{3,2,1,0:T(8,128)(2,1)S(1)}, f32[2,16,256]{2,1,0:T(8,128)S(1)}) custom-call(s32[3]{0:T(128)S(1)} %copy-done.6, s32[64]{0:T(128)S(1)} %copy-done.20, s32[64]{0:T(128)S(1)} %copy-done.21, f32[16,512]{1,0:T(8,128)S(1)} %copy-done.15, f32[2,32,512]{2,1,0:T(8,128)S(1)} %copy-done.19, ...), custom_call_target="tpu_custom_call" | custom-call | flops 9663676416 | bytes 16777216 | tf_op jit(solution)/shard_map/conv2_input_grad/pallas_call | solution.py:1182
  187.4 6.2 %collective-permute-done.8.rest_1_ = bf16[2048,256]{1,0:T(8,128)(2,1)S(1)} collective-permute-done((bf16[2048,256]{1,0:T(8,128)(2,1)S(1)}, bf16[2048,256]{1,0:T(8,128)(2,1)S(1)}, u32[]{:S(2)}, u32[]{:S(2)}) %collective-permute-start.8) | collective-permute-done | bytes 1048608 | tf_op jit(solution)/shard_map/ppermute | solution.py:1303
  195.1 7.8 %collective-permute-start.13 = (bf16[320,512]{1,0:T(8,128)(2,1)S(1)}, bf16[320,512]{1,0:T(8,128)(2,1)S(1)}, u32[]{:S(2)}, u32[]{:S(2)}) collective-permute-start(bf16[320,512]{1,0:T(8,128)(2,1)S(1)} %get-tuple-element.227), channel_id=1, source_target_pairs={{0,12},{4,8},{8,4},{12,0},{1,13},{5,9},{9,5},{13,1},{2,14},{6,10},... | collective-permute-start | bytes 983048 | tf_op jit(solution)/shard_map/ppermute | solution.py:1315
  203.6 13.5 %conv1_weight_grad.1 = (bf16[2304,512]{1,0:T(8,128)(2,1)S(1)}, bf16[2304,512]{1,0:T(8,128)(2,1)S(1)}) custom-call(s32[3]{0:T(128)S(1)} %copy-done.6, bf16[10,10,32,512]{3,2,1,0:T(8,128)(2,1)S(1)} %copy-done.13, bf16[10,10,32,512]{3,2,1,0:T(8,128)(2,1)S(1)} %get-tuple-element.188.grad.rest_1_), custom_call_target="tpu_custom_call" | custom-call | flops 9663676416 | bytes 12582912 | tf_op jit(solution)/shard_map/conv1_weight_grad/pallas_call | solution.py:1069
  217.2 1.9 collective-permute-done.10
  220.0 7.2 %collective-permute-start.17 = (bf16[256,512]{1,0:T(8,128)(2,1)S(1)}, bf16[256,512]{1,0:T(8,128)(2,1)S(1)}, u32[]{:S(2)}, u32[]{:S(2)}) collective-permute-start(bf16[256,512]{1,0:T(8,128)(2,1)S(1)} %get-tuple-element.237), channel_id=1, source_target_pairs={{0,12},{4,8},{8,4},{12,0},{1,13},{5,9},{9,5},{13,1},{2,14},{6,10},... | collective-permute-start | bytes 786440 | tf_op jit(solution)/shard_map/ppermute | solution.py:1315
  227.8 11.8 %conv1_input_grad.2 = (bf16[2048,256]{1,0:T(8,128)(2,1)S(1)}, f32[16,256]{1,0:T(8,128)S(1)}) custom-call(s32[3]{0:T(128)S(1)} %copy-done.6, s32[64]{0:T(128)S(1)} %copy-done.20, s32[64]{0:T(128)S(1)} %copy-done.21, f32[16,512]{1,0:T(8,128)S(1)} %copy-done.15, f32[2,32,512]{2,1,0:T(8,128)S(1)} %copy-done.11, f32[2,16,256]{2,1,0:T(8,128)S(1)} %get-tuple-element.172.vecs2, ...), custom_call_target="tpu_custom_call" | custom-call | flops 4831838208 | bytes 10485760 | tf_op jit(solution)/shard_map/conv1_input_grad/pallas_call | solution.py:1265
  240.9 8.0 %collective-permute-start.22 = (bf16[416,512]{1,0:T(8,128)(2,1)S(1)}, bf16[416,512]{1,0:T(8,128)(2,1)S(1)}, u32[]{:S(2)}, u32[]{:S(2)}) collective-permute-start(bf16[416,512]{1,0:T(8,128)(2,1)S(1)} %pad_maximum_fusion.1), channel_id=1, source_target_pairs={{0,16},{16,0},{1,17},{17,1},{2,18},{18,2},{3,19},{19,3},{4,20},{20... | collective-permute-start | bytes 1277960 | tf_op jit(solution)/shard_map/ppermute | solution.py:1303
  249.7 2.8 collective-permute-start.21
  253.2 1.6 collective-permute-start.23
  254.9 11.7 %conv1_input_grad.3 = (f32[2048,256]{1,0:T(8,128)S(1)}, f32[16,256]{1,0:T(8,128)S(1)}) custom-call(s32[3]{0:T(128)S(1)} %copy-done.6, s32[64]{0:T(128)S(1)} %copy-done.20, s32[64]{0:T(128)S(1)} %copy-done.21, f32[16,512]{1,0:T(8,128)S(1)} %copy-done.15, f32[2,32,512]{2,1,0:T(8,128)S(1)} %copy-done.11, f32[2,16,256]{2,1,0:T(8,128)S(1)} %get-tuple-element.172.vecs2, ...), custom_call_target="tpu_custom_call" | custom-call | flops 4831838208 | bytes 10485760 | tf_op jit(solution)/shard_map/conv1_input_grad/pallas_call | solution.py:1265
  267.8 1.9 collective-permute-start.31
  269.7 5.6 %collective-permute-done.21 = bf16[576,512]{1,0:T(8,128)(2,1)S(1)} collective-permute-done((bf16[576,512]{1,0:T(8,128)(2,1)S(1)}, bf16[576,512]{1,0:T(8,128)(2,1)S(1)}, u32[]{:S(2)}, u32[]{:S(2)}) %collective-permute-start.21) | collective-permute-done | bytes 589856 | tf_op jit(solution)/shard_map/ppermute | solution.py:1315
  275.3 2.0 collective-permute-start.30
  277.9 4.2 %collective-permute-start.29 = (bf16[416,512]{1,0:T(8,128)(2,1)S(1)}, bf16[416,512]{1,0:T(8,128)(2,1)S(1)}, u32[]{:S(2)}, u32[]{:S(2)}) collective-permute-start(bf16[416,512]{1,0:T(8,128)(2,1)S(1)} %add_convert_fusion.6), channel_id=1, source_target_pairs={{0,8},{4,12},{8,0},{12,4},{1,9},{5,13},{9,1},{13,5},{2,10},{6,14},... | collective-permute-start | bytes 1277960 | tf_op jit(solution)/shard_map/ppermute | solution.py:1315
  282.1 6.3 %collective-permute-done.19 = bf16[576,512]{1,0:T(8,128)(2,1)S(1)} collective-permute-done((bf16[576,512]{1,0:T(8,128)(2,1)S(1)}, bf16[576,512]{1,0:T(8,128)(2,1)S(1)}, u32[]{:S(2)}, u32[]{:S(2)}) %collective-permute-start.19) | collective-permute-done | bytes 589856 | tf_op jit(solution)/shard_map/ppermute | solution.py:1315
  289.3 1.5 collective-permute-start.24
  290.8 4.5 %unpack_output.1 = bf16[256,4096]{1,0:T(8,128)(2,1)} custom-call(s32[3]{0:T(128)S(1)} %copy-done.6, s32[64]{0:T(128)S(1)} %copy-done.20, bf16[2048,256]{1,0:T(8,128)(2,1)S(1)} %copy-done.10, bf16[2048,256]{1,0:T(8,128)(2,1)S(1)} %collective-permute-done.8.rest_1_), custom_call_target="tpu_custom_call" | custom-call | flops 4294967296 | bytes 8388608 | tf_op jit(solution)/shard_map/unpack_output/pallas_call | solution.py:547
  295.2 1.2 collective-permute-done.24
  296.7 6.2 %unpack_input_grad.1 = f32[256,4096]{1,0:T(8,128)} custom-call(s32[3]{0:T(128)S(1)} %copy-done.6, s32[64]{0:T(128)S(1)} %copy-done.20, f32[2048,256]{1,0:T(8,128)S(1)} %get-tuple-element.206.rest_0_, bf16[2048,256]{1,0:T(8,128)(2,1)S(1)} %collective-permute-done.23.rest_1_), custom_call_target="tpu_custom_call" | custom-call | flops 4294967296 | bytes 8388608 | tf_op jit(solution)/shard_map/unpack_input_grad/pallas_call | solution.py:547
  303.0 8.8 %collective-permute-done.25 = bf16[320,512]{1,0:T(8,128)(2,1)S(1)} collective-permute-done((bf16[320,512]{1,0:T(8,128)(2,1)S(1)}, bf16[320,512]{1,0:T(8,128)(2,1)S(1)}, u32[]{:S(2)}, u32[]{:S(2)}) %collective-permute-start.25) | collective-permute-done | bytes 327712 | tf_op jit(solution)/shard_map/ppermute | solution.py:1303
  312.5 3.2 collective-permute-start.26
  315.8 3.8 %conv2_grads.1 = (f32[256,512]{1,0:T(8,128)}, f32[256,512]{1,0:T(8,128)}, f32[256,512]{1,0:T(8,128)}, f32[256,512]{1,0:T(8,128)}, f32[9,256,512]{2,1,0:T(8,128)}) custom-call(s32[3]{0:T(128)S(1)} %copy-done.6, bf16[1664,512]{1,0:T(8,128)(2,1)S(1)} %constant_dynamic-update-slice_fusion.mine, bf16[1664,512]{1,0:T(8,128)(2,1)S(1)} %collective-permute-done.32.other), custom_call_target="tpu_custom_call" | custom-call | flops 4294967296 | bytes 6291456 | tf_op jit(solution)/shard_map/conv2_grads/pallas_call | solution.py:1423
  319.6 4.1 %collective-permute-done.28 = bf16[320,512]{1,0:T(8,128)(2,1)S(1)} collective-permute-done((bf16[320,512]{1,0:T(8,128)(2,1)S(1)}, bf16[320,512]{1,0:T(8,128)(2,1)S(1)}, u32[]{:S(2)}, u32[]{:S(2)}) %collective-permute-start.28) | collective-permute-done | bytes 327712 | tf_op jit(solution)/shard_map/ppermute | solution.py:1315
  323.7 5.6 %collective-permute-done.27 = bf16[320,512]{1,0:T(8,128)(2,1)S(1)} collective-permute-done((bf16[320,512]{1,0:T(8,128)(2,1)S(1)}, bf16[320,512]{1,0:T(8,128)(2,1)S(1)}, u32[]{:S(2)}, u32[]{:S(2)}) %collective-permute-start.27) | collective-permute-done | bytes 327712 | tf_op jit(solution)/shard_map/ppermute | solution.py:1315
  329.5 3.0 collective-permute-done.33.other
  332.5 3.0 conv1_grads.1
  (158 shorter events, 17.6 us)
Async XLA Ops:
  1.7 12.8 %collective-permute-start.1 = (bf16[9,32,512]{2,1,0:T(8,128)(2,1)S(1)}, bf16[9,32,512]{2,1,0:T(8,128)(2,1)S(1)}, u32[]{:S(2)}, u32[]{:S(2)}) collective-permute-start(bf16[9,32,512]{2,1,0:T(8,128)(2,1)S(1)} %constant_dynamic-slice_fusion.2), channel_id=1, source_target_pairs={{0,1},{1,0},{2,3},{3,2},{4,5},{5,4},{6,7},{7,6},{8,9},{9,8},{10,11... | collective-permute-start | bytes 884744 | tf_op jit(solution)/shard_map/ppermute | solution.py:1303
  5.7 20.0 %collective-permute-start.4 = (bf16[9,32,512]{2,1,0:T(8,128)(2,1)S(1)}, bf16[9,32,512]{2,1,0:T(8,128)(2,1)S(1)}, u32[]{:S(2)}, u32[]{:S(2)}) collective-permute-start(bf16[9,32,512]{2,1,0:T(8,128)(2,1)S(1)} %constant_dynamic-slice_fusion.1), channel_id=1, source_target_pairs={{0,1},{1,0},{2,3},{3,2},{4,5},{5,4},{6,7},{7,6},{8,9},{9,8},{10,11... | collective-permute-start | bytes 884744 | tf_op jit(solution)/shard_map/ppermute | solution.py:1303
  12.4 28.2 %collective-permute-start = (bf16[2048,256]{1,0:T(8,128)(2,1)}, bf16[2048,256]{1,0:T(8,128)(2,1)}, u32[]{:S(2)}, u32[]{:S(2)}) collective-permute-start(bf16[2048,256]{1,0:T(8,128)(2,1)} %get-tuple-element.128), channel_id=1, source_target_pairs={{0,1},{1,0},{2,3},{3,2},{4,5},{5,4},{6,7},{7,6},{8,9},{9,8},{10,11... | collective-permute-start | bytes 3145736 | tf_op jit(solution)/shard_map/ppermute | solution.py:1303
  15.6 25.0 %all-to-all-start = ((bf16[4,9,32,512]{3,2,1,0:T(8,128)(2,1)}), bf16[4,9,32,512]{3,2,1,0:T(8,128)(2,1)S(1)}, u32[]{:S(2)}, u32[]{:S(2)}) async-start(bf16[4,9,32,512]{3,2,1,0:T(8,128)(2,1)} %broadcast_in_dim.8), calls=%async_computation | async-start | bytes 2359296 | tf_op jit(solution)/shard_map/all_to_all | solution.py:1307
  42.4 38.2 %all-to-all-start.1 = ((bf16[8,9,32,512]{3,2,1,0:T(8,128)(2,1)}), bf16[8,9,32,512]{3,2,1,0:T(8,128)(2,1)S(1)}, u32[]{:S(2)}, u32[]{:S(2)}) async-start(bf16[8,9,32,512]{3,2,1,0:T(8,128)(2,1)} %broadcast_in_dim.9), calls=%async_computation.1 | async-start | bytes 4718592 | tf_op jit(solution)/shard_map/all_to_all | solution.py:1307
  46.4 7.1 %collective-permute-start.3 = (bf16[4,9,32,512]{3,2,1,0:T(8,128)(2,1)S(1)}, bf16[4,9,32,512]{3,2,1,0:T(8,128)(2,1)}, u32[]{:S(2)}, u32[]{:S(2)}) collective-permute-start(bf16[4,9,32,512]{3,2,1,0:T(8,128)(2,1)S(1)} %all-to-all-done.rest_5_.rest_4_), channel_id=1, source_target_pairs={{0,2},{2,0},{1,3},{3,1},{4,6},{6,4},{5,7},{7,5},{8,10},{10,8},{9,1... | collective-permute-start | bytes 3538952 | tf_op jit(solution)/shard_map/ppermute | solution.py:1303
  49.7 3.8 %collective-permute-start.2 = (f32[16,256]{1,0:T(8,128)S(1)}, f32[16,256]{1,0:T(8,128)S(1)}, u32[]{:S(2)}, u32[]{:S(2)}) collective-permute-start(f32[16,256]{1,0:T(8,128)S(1)} %stack.82.rest_2_), channel_id=1, source_target_pairs={{0,1},{1,0},{2,3},{3,2},{4,5},{5,4},{6,7},{7,6},{8,9},{9,8},{10,11... | collective-permute-start | bytes 49160 | tf_op jit(solution)/shard_map/ppermute | solution.py:1303
  51.2 27.7 %collective-permute-start.5 = (bf16[4,128,512]{2,1,0:T(8,128)(2,1)}, bf16[4,128,512]{2,1,0:T(8,128)(2,1)}, u32[]{:S(2)}, u32[]{:S(2)}) collective-permute-start(bf16[4,128,512]{2,1,0:T(8,128)(2,1)} %constant_dynamic-slice_fusion), channel_id=1, source_target_pairs={{0,1},{1,0},{2,3},{3,2},{4,5},{5,4},{6,7},{7,6},{8,9},{9,8},{10,11... | collective-permute-start | bytes 1572872 | tf_op jit(solution)/shard_map/ppermute | solution.py:1303
  54.1 24.9 %copy-start.32 = (bf16[2048,256]{1,0:T(8,128)(2,1)S(1)}, bf16[2048,256]{1,0:T(8,128)(2,1)}, u32[]{:S(2)}) copy-start(bf16[2048,256]{1,0:T(8,128)(2,1)} %get-tuple-element.141) | copy-start | bytes 3145732
  79.0 25.3 %collective-permute-start.6 = (bf16[2048,256]{1,0:T(8,128)(2,1)S(1)}, bf16[2048,256]{1,0:T(8,128)(2,1)}, u32[]{:S(2)}, u32[]{:S(2)}) collective-permute-start(bf16[2048,256]{1,0:T(8,128)(2,1)S(1)} %copy-done.32), channel_id=1, source_target_pairs={{0,1},{1,0},{2,3},{3,2},{4,5},{5,4},{6,7},{7,6},{8,9},{9,8},{10,11... | collective-permute-start | bytes 3145736 | tf_op jit(solution)/shard_map/ppermute | solution.py:1303
  80.6 23.7 %collective-permute-start.7 = (bf16[4,128,512]{2,1,0:T(8,128)(2,1)}, bf16[4,128,512]{2,1,0:T(8,128)(2,1)}, u32[]{:S(2)}, u32[]{:S(2)}) collective-permute-start(bf16[4,128,512]{2,1,0:T(8,128)(2,1)} %collective-permute-done.5.rest_7_), channel_id=1, source_target_pairs={{0,2},{2,0},{1,3},{3,1},{4,6},{6,4},{5,7},{7,5},{8,10},{10,8},{9,1... | collective-permute-start | bytes 1572872 | tf_op jit(solution)/shard_map/ppermute | solution.py:1303
  104.3 43.2 %copy-start.6 = (s32[3]{0:T(128)S(1)}, s32[3]{0:T(128)}, u32[]{:S(2)}) copy-start(s32[3]{0:T(128)} %pad_add_fusion.position) | copy-start | bytes 40
  104.3 43.2 %copy-start.12 = (bf16[10,10,32,512]{3,2,1,0:T(8,128)(2,1)S(1)}, bf16[10,10,32,512]{3,2,1,0:T(8,128)(2,1)}, u32[]{:S(2)}) copy-start(bf16[10,10,32,512]{3,2,1,0:T(8,128)(2,1)} %get-tuple-element.133.pad_hbm.active) | copy-start | bytes 9830404
  151.9 16.2 %copy-start.14 = (bf16[64,32,512]{2,1,0:T(8,128)(2,1)S(1)}, bf16[64,32,512]{2,1,0:T(8,128)(2,1)}, u32[]{:S(2)}) copy-start(bf16[64,32,512]{2,1,0:T(8,128)(2,1)} %get-tuple-element.155.hidden_hbm) | copy-start | bytes 6291460
  151.9 16.2 %copy-start.15 = (f32[16,512]{1,0:T(8,128)S(1)}, f32[16,512]{1,0:T(8,128)}, u32[]{:S(2)}) copy-start(f32[16,512]{1,0:T(8,128)} %get-tuple-element.131.par.rest_0_) | copy-start | bytes 98308
  152.0 16.2 %copy-start.19 = (f32[2,32,512]{2,1,0:T(8,128)S(1)}, f32[2,32,512]{2,1,0:T(8,128)}, u32[]{:S(2)}) copy-start(f32[2,32,512]{2,1,0:T(8,128)} %get-tuple-element.149.stats2) | copy-start | bytes 393220
  152.0 16.2 %copy-start.20 = (s32[64]{0:T(128)S(1)}, s32[64]{0:T(128)}, u32[]{:S(2)}) copy-start(s32[64]{0:T(128)} %get-tuple-element.123.slot_tile) | copy-start | bytes 772
  152.0 16.2 %copy-start.21 = (s32[64]{0:T(128)S(1)}, s32[64]{0:T(128)}, u32[]{:S(2)}) copy-start(s32[64]{0:T(128)} %get-tuple-element.124.slot_crop) | copy-start | bytes 772
  168.0 25.7 %collective-permute-start.9 = (bf16[3328,512]{1,0:T(8,128)(2,1)S(1)}, bf16[3328,512]{1,0:T(8,128)(2,1)S(1)}, u32[]{:S(2)}, u32[]{:S(2)}) collective-permute-start(bf16[3328,512]{1,0:T(8,128)(2,1)S(1)} %get-tuple-element.153), channel_id=1, source_target_pairs={{0,2},{2,0},{1,3},{3,1},{4,6},{6,4},{5,7},{7,5},{8,10},{10,8},{9,1... | collective-permute-start | bytes 10223624 | tf_op jit(solution)/shard_map/ppermute | solution.py:1303
  168.1 25.6 %collective-permute-start.8 = (bf16[2048,256]{1,0:T(8,128)(2,1)S(1)}, bf16[2048,256]{1,0:T(8,128)(2,1)S(1)}, u32[]{:S(2)}, u32[]{:S(2)}) collective-permute-start(bf16[2048,256]{1,0:T(8,128)(2,1)S(1)} %copy-done.33), channel_id=1, source_target_pairs={{0,1},{1,0},{2,3},{3,2},{4,5},{5,4},{6,7},{7,6},{8,9},{9,8},{10,11... | collective-permute-start | bytes 3145736 | tf_op jit(solution)/shard_map/ppermute | solution.py:1303
  194.3 24.8 %collective-permute-start.10 = (bf16[1024,512]{1,0:T(8,128)(2,1)S(1)}, bf16[1024,512]{1,0:T(8,128)(2,1)S(1)}, u32[]{:S(2)}, u32[]{:S(2)}) collective-permute-start(bf16[1024,512]{1,0:T(8,128)(2,1)S(1)} %get-tuple-element.231), channel_id=1, source_target_pairs={{0,1},{1,0},{2,3},{3,2},{4,5},{5,4},{6,7},{7,6},{8,9},{9,8},{10,11... | collective-permute-start | bytes 3145736 | tf_op jit(solution)/shard_map/ppermute | solution.py:1303
  195.1 22.1 %collective-permute-start.13 = (bf16[320,512]{1,0:T(8,128)(2,1)S(1)}, bf16[320,512]{1,0:T(8,128)(2,1)S(1)}, u32[]{:S(2)}, u32[]{:S(2)}) collective-permute-start(bf16[320,512]{1,0:T(8,128)(2,1)S(1)} %get-tuple-element.227), channel_id=1, source_target_pairs={{0,12},{4,8},{8,4},{12,0},{1,13},{5,9},{9,5},{13,1},{2,14},{6,10},... | collective-permute-start | bytes 983048 | tf_op jit(solution)/shard_map/ppermute | solution.py:1315
  202.9 14.2 %collective-permute-start.12 = (bf16[320,512]{1,0:T(8,128)(2,1)S(1)}, bf16[320,512]{1,0:T(8,128)(2,1)S(1)}, u32[]{:S(2)}, u32[]{:S(2)}) collective-permute-start(bf16[320,512]{1,0:T(8,128)(2,1)S(1)} %get-tuple-element.229), channel_id=1, source_target_pairs={{0,4},{4,0},{8,12},{12,8},{1,5},{5,1},{9,13},{13,9},{2,6},{6,2},{1... | collective-permute-start | bytes 983048 | tf_op jit(solution)/shard_map/ppermute | solution.py:1315
  202.9 14.2 %collective-permute-start.11 = (bf16[320,512]{1,0:T(8,128)(2,1)S(1)}, bf16[320,512]{1,0:T(8,128)(2,1)S(1)}, u32[]{:S(2)}, u32[]{:S(2)}) collective-permute-start(bf16[320,512]{1,0:T(8,128)(2,1)S(1)} %get-tuple-element.230), channel_id=1, source_target_pairs={{0,8},{4,12},{8,0},{12,4},{1,9},{5,13},{9,1},{13,5},{2,10},{6,14},... | collective-permute-start | bytes 983048 | tf_op jit(solution)/shard_map/ppermute | solution.py:1315
  203.6 24.2 %copy-start.5 = (bf16[9,256,512]{2,1,0:T(8,128)(2,1)S(1)}, bf16[9,256,512]{2,1,0:T(8,128)(2,1)}, u32[]{:S(2)}) copy-start(bf16[9,256,512]{2,1,0:T(8,128)(2,1)} %rest_3_.3) | copy-start | bytes 7077892
  203.6 24.2 %copy-start.8 = (bf16[10,10,32,512]{3,2,1,0:T(8,128)(2,1)S(1)}, bf16[10,10,32,512]{3,2,1,0:T(8,128)(2,1)}, u32[]{:S(2)}) copy-start(bf16[10,10,32,512]{3,2,1,0:T(8,128)(2,1)} %get-tuple-element.154.grad.pad_hbm.rest_2_) | copy-start | bytes 9830404
  203.6 24.2 %copy-start.9 = (bf16[2048,512]{1,0:T(8,128)(2,1)S(1)}, bf16[2048,512]{1,0:T(8,128)(2,1)}, u32[]{:S(2)}) copy-start(bf16[2048,512]{1,0:T(8,128)(2,1)} %get-tuple-element.132.feats.rest_0_) | copy-start | bytes 6291460
  217.2 22.4 %copy-start.26 = (bf16[320,512]{1,0:T(8,128)(2,1)}, bf16[320,512]{1,0:T(8,128)(2,1)S(1)}, u32[]{:S(2)}) copy-start(bf16[320,512]{1,0:T(8,128)(2,1)S(1)} %collective-permute-done.11) | copy-start | bytes 983044
  219.4 29.4 %collective-permute-start.14 = (bf16[2304,512]{1,0:T(8,128)(2,1)S(1)}, bf16[2304,512]{1,0:T(8,128)(2,1)S(1)}, u32[]{:S(2)}, u32[]{:S(2)}) collective-permute-start(bf16[2304,512]{1,0:T(8,128)(2,1)S(1)} %get-tuple-element.170), channel_id=1, source_target_pairs={{0,2},{2,0},{1,3},{3,1},{4,6},{6,4},{5,7},{7,5},{8,10},{10,8},{9,1... | collective-permute-start | bytes 7077896 | tf_op jit(solution)/shard_map/ppermute | solution.py:1303
  219.5 20.2 %collective-permute-start.18 = (bf16[160,512]{1,0:T(8,128)(2,1)S(1)}, bf16[160,512]{1,0:T(8,128)(2,1)S(1)}, u32[]{:S(2)}, u32[]{:S(2)}) collective-permute-start(bf16[160,512]{1,0:T(8,128)(2,1)S(1)} %add_convert_fusion.19), channel_id=1, source_target_pairs={{0,1},{1,0},{2,3},{3,2},{4,5},{5,4},{6,7},{7,6},{8,9},{9,8},{10,11... | collective-permute-start | bytes 491528 | tf_op jit(solution)/shard_map/ppermute | solution.py:1303
  220.0 19.7 %collective-permute-start.17 = (bf16[256,512]{1,0:T(8,128)(2,1)S(1)}, bf16[256,512]{1,0:T(8,128)(2,1)S(1)}, u32[]{:S(2)}, u32[]{:S(2)}) collective-permute-start(bf16[256,512]{1,0:T(8,128)(2,1)S(1)} %get-tuple-element.237), channel_id=1, source_target_pairs={{0,12},{4,8},{8,4},{12,0},{1,13},{5,9},{9,5},{13,1},{2,14},{6,10},... | collective-permute-start | bytes 786440 | tf_op jit(solution)/shard_map/ppermute | solution.py:1315
  227.2 12.6 %collective-permute-start.16 = (bf16[256,512]{1,0:T(8,128)(2,1)S(1)}, bf16[256,512]{1,0:T(8,128)(2,1)S(1)}, u32[]{:S(2)}, u32[]{:S(2)}) collective-permute-start(bf16[256,512]{1,0:T(8,128)(2,1)S(1)} %get-tuple-element.238), channel_id=1, source_target_pairs={{0,4},{4,0},{8,12},{12,8},{1,5},{5,1},{9,13},{13,9},{2,6},{6,2},{1... | collective-permute-start | bytes 786440 | tf_op jit(solution)/shard_map/ppermute | solution.py:1315
  227.2 12.6 %collective-permute-start.15 = (bf16[256,512]{1,0:T(8,128)(2,1)S(1)}, bf16[256,512]{1,0:T(8,128)(2,1)S(1)}, u32[]{:S(2)}, u32[]{:S(2)}) collective-permute-start(bf16[256,512]{1,0:T(8,128)(2,1)S(1)} %get-tuple-element.239), channel_id=1, source_target_pairs={{0,8},{4,12},{8,0},{12,4},{1,9},{5,13},{9,1},{13,5},{2,10},{6,14},... | collective-permute-start | bytes 786440 | tf_op jit(solution)/shard_map/ppermute | solution.py:1315
  240.9 26.8 %collective-permute-start.22 = (bf16[416,512]{1,0:T(8,128)(2,1)S(1)}, bf16[416,512]{1,0:T(8,128)(2,1)S(1)}, u32[]{:S(2)}, u32[]{:S(2)}) collective-permute-start(bf16[416,512]{1,0:T(8,128)(2,1)S(1)} %pad_maximum_fusion.1), channel_id=1, source_target_pairs={{0,16},{16,0},{1,17},{17,1},{2,18},{18,2},{3,19},{19,3},{4,20},{20... | collective-permute-start | bytes 1277960 | tf_op jit(solution)/shard_map/ppermute | solution.py:1303
  249.7 25.6 %collective-permute-start.21 = (bf16[576,512]{1,0:T(8,128)(2,1)S(1)}, bf16[576,512]{1,0:T(8,128)(2,1)S(1)}, u32[]{:S(2)}, u32[]{:S(2)}) collective-permute-start(bf16[576,512]{1,0:T(8,128)(2,1)S(1)} %get-tuple-element.233), channel_id=1, source_target_pairs={{0,12},{4,8},{8,4},{12,0},{1,13},{5,9},{9,5},{13,1},{2,14},{6,10},... | collective-permute-start | bytes 1769480 | tf_op jit(solution)/shard_map/ppermute | solution.py:1315
  252.5 25.4 %collective-permute-start.20 = (bf16[576,512]{1,0:T(8,128)(2,1)S(1)}, bf16[576,512]{1,0:T(8,128)(2,1)S(1)}, u32[]{:S(2)}, u32[]{:S(2)}) collective-permute-start(bf16[576,512]{1,0:T(8,128)(2,1)S(1)} %get-tuple-element.234), channel_id=1, source_target_pairs={{0,4},{4,0},{8,12},{12,8},{1,5},{5,1},{9,13},{13,9},{2,6},{6,2},{1... | collective-permute-start | bytes 1769480 | tf_op jit(solution)/shard_map/ppermute | solution.py:1315
  252.5 36.0 %collective-permute-start.19 = (bf16[576,512]{1,0:T(8,128)(2,1)S(1)}, bf16[576,512]{1,0:T(8,128)(2,1)S(1)}, u32[]{:S(2)}, u32[]{:S(2)}) collective-permute-start(bf16[576,512]{1,0:T(8,128)(2,1)S(1)} %get-tuple-element.235), channel_id=1, source_target_pairs={{0,8},{4,12},{8,0},{12,4},{1,9},{5,13},{9,1},{13,5},{2,10},{6,14},... | collective-permute-start | bytes 1769480 | tf_op jit(solution)/shard_map/ppermute | solution.py:1315
  253.2 37.5 %collective-permute-start.23 = (bf16[2048,256]{1,0:T(8,128)(2,1)S(1)}, bf16[2048,256]{1,0:T(8,128)(2,1)S(1)}, u32[]{:S(2)}, u32[]{:S(2)}) collective-permute-start(bf16[2048,256]{1,0:T(8,128)(2,1)S(1)} %get-tuple-element.197), channel_id=1, source_target_pairs={{0,1},{1,0},{2,3},{3,2},{4,5},{5,4},{6,7},{7,6},{8,9},{9,8},{10,11... | collective-permute-start | bytes 3145736 | tf_op jit(solution)/shard_map/ppermute | solution.py:1303
  267.8 44.1 %collective-permute-start.31 = (bf16[416,512]{1,0:T(8,128)(2,1)S(1)}, bf16[416,512]{1,0:T(8,128)(2,1)S(1)}, u32[]{:S(2)}, u32[]{:S(2)}) collective-permute-start(bf16[416,512]{1,0:T(8,128)(2,1)S(1)} %add_convert_fusion.6), channel_id=1, source_target_pairs={{0,12},{4,8},{8,4},{12,0},{1,13},{5,9},{9,5},{13,1},{2,14},{6,10},... | collective-permute-start | bytes 1277960 | tf_op jit(solution)/shard_map/ppermute | solution.py:1315
  275.3 36.6 %collective-permute-start.30 = (bf16[416,512]{1,0:T(8,128)(2,1)S(1)}, bf16[416,512]{1,0:T(8,128)(2,1)S(1)}, u32[]{:S(2)}, u32[]{:S(2)}) collective-permute-start(bf16[416,512]{1,0:T(8,128)(2,1)S(1)} %add_convert_fusion.6), channel_id=1, source_target_pairs={{0,4},{4,0},{8,12},{12,8},{1,5},{5,1},{9,13},{13,9},{2,6},{6,2},{1... | collective-permute-start | bytes 1277960 | tf_op jit(solution)/shard_map/ppermute | solution.py:1315
  277.9 34.0 %collective-permute-start.29 = (bf16[416,512]{1,0:T(8,128)(2,1)S(1)}, bf16[416,512]{1,0:T(8,128)(2,1)S(1)}, u32[]{:S(2)}, u32[]{:S(2)}) collective-permute-start(bf16[416,512]{1,0:T(8,128)(2,1)S(1)} %add_convert_fusion.6), channel_id=1, source_target_pairs={{0,8},{4,12},{8,0},{12,4},{1,9},{5,13},{9,1},{13,5},{2,10},{6,14},... | collective-permute-start | bytes 1277960 | tf_op jit(solution)/shard_map/ppermute | solution.py:1315
  289.3 7.1 %collective-permute-start.24 = (bf16[320,512]{1,0:T(8,128)(2,1)S(1)}, bf16[320,512]{1,0:T(8,128)(2,1)S(1)}, u32[]{:S(2)}, u32[]{:S(2)}) collective-permute-start(bf16[320,512]{1,0:T(8,128)(2,1)S(1)} %fusion.1), channel_id=1, source_target_pairs={{0,1},{1,0},{2,3},{3,2},{4,5},{5,4},{6,7},{7,6},{8,9},{9,8},{10,11... | collective-permute-start | bytes 983048 | tf_op jit(solution)/shard_map/ppermute | solution.py:1303
  296.7 15.2 %collective-permute-start.25 = (bf16[320,512]{1,0:T(8,128)(2,1)S(1)}, bf16[320,512]{1,0:T(8,128)(2,1)S(1)}, u32[]{:S(2)}, u32[]{:S(2)}) collective-permute-start(bf16[320,512]{1,0:T(8,128)(2,1)S(1)} %pad_maximum_fusion.2), channel_id=1, source_target_pairs={{0,16},{16,0},{1,17},{17,1},{2,18},{18,2},{3,19},{19,3},{4,20},{20... | collective-permute-start | bytes 983048 | tf_op jit(solution)/shard_map/ppermute | solution.py:1303
  312.1 3.7 %collective-permute-start.32 = (bf16[1664,512]{1,0:T(8,128)(2,1)S(1)}, bf16[1664,512]{1,0:T(8,128)(2,1)S(1)}, u32[]{:S(2)}, u32[]{:S(2)}) collective-permute-start(bf16[1664,512]{1,0:T(8,128)(2,1)S(1)} %constant_dynamic-update-slice_fusion.mine), channel_id=1, source_target_pairs={{0,2},{2,0},{1,3},{3,1},{4,6},{6,4},{5,7},{7,5},{8,10},{10,8},{9,1... | collective-permute-start | bytes 5111816 | tf_op jit(solution)/shard_map/ppermute | solution.py:1303
  312.2 11.5 %collective-permute-start.28 = (bf16[320,512]{1,0:T(8,128)(2,1)S(1)}, bf16[320,512]{1,0:T(8,128)(2,1)S(1)}, u32[]{:S(2)}, u32[]{:S(2)}) collective-permute-start(bf16[320,512]{1,0:T(8,128)(2,1)S(1)} %add_convert_fusion.7), channel_id=1, source_target_pairs={{0,12},{4,8},{8,4},{12,0},{1,13},{5,9},{9,5},{13,1},{2,14},{6,10},... | collective-permute-start | bytes 983048 | tf_op jit(solution)/shard_map/ppermute | solution.py:1315
  312.2 17.1 %collective-permute-start.27 = (bf16[320,512]{1,0:T(8,128)(2,1)S(1)}, bf16[320,512]{1,0:T(8,128)(2,1)S(1)}, u32[]{:S(2)}, u32[]{:S(2)}) collective-permute-start(bf16[320,512]{1,0:T(8,128)(2,1)S(1)} %add_convert_fusion.7), channel_id=1, source_target_pairs={{0,4},{4,0},{8,12},{12,8},{1,5},{5,1},{9,13},{13,9},{2,6},{6,2},{1... | collective-permute-start | bytes 983048 | tf_op jit(solution)/shard_map/ppermute | solution.py:1315
  312.5 16.8 %collective-permute-start.26 = (bf16[320,512]{1,0:T(8,128)(2,1)S(1)}, bf16[320,512]{1,0:T(8,128)(2,1)S(1)}, u32[]{:S(2)}, u32[]{:S(2)}) collective-permute-start(bf16[320,512]{1,0:T(8,128)(2,1)S(1)} %add_convert_fusion.7), channel_id=1, source_target_pairs={{0,8},{4,12},{8,0},{12,4},{1,9},{5,13},{9,1},{13,5},{2,10},{6,14},... | collective-permute-start | bytes 983048 | tf_op jit(solution)/shard_map/ppermute | solution.py:1315
  329.4 3.1 collective-permute-start.33
  (27 other events, 173.1 us)

commit v6 on v5

--- a/solution.py
+++ b/solution.py
@@ -568,7 +568,7 @@
             for col in range(TILE):
                 value = slab(row * TILE + col, lanes)
                 before = (value - centre) * factor + offset
-                pad[row + 1, col + 1, :, lanes] = (before * sigmoid(before)).astype(BF16)
+                pad[row + 1, col + 1, :, lanes] = (before * jax.nn.sigmoid(before)).astype(BF16)
                 if copy is not None:
                     copy[row * TILE + col, :, lanes] = value.astype(BF16)
             return carry

time: 337 us -> 331 us (0.982); the launches traced: 336 us -> 326 us
  starting transfers between devices: 61 us -> 47 us
  waiting for transfers between devices: 61 us -> 65.1 us
    ppermute x15, starting transfers between devices: 31.4 us -> 20.8 us  [from_quad(): lax.ppermute(value, ('near', 'y'), [(at, at ^ bits) for at in range(4)])]
    ppermute x19, starting transfers between devices: 21.8 us -> 18.4 us  [swap(): return lax.ppermute(value, axis, [(0, 1), (1, 0)])]
  transfers between devices with their start and end apart: 36 -> 36, of which waited for: 13 -> 14; matrix products, arithmetic and copies ran while one was open for 3% -> 3% of each run, Pallas kernels for 38% -> 39%
where the time goes in v6:
time: 331 us; the launch traced here: 326 us
  Pallas kernels  191 us (58%)
  waiting for transfers between devices  65.1 us (20%)
  starting transfers between devices  47 us (14%)
  local copies, waits for them, and re-layouts  17.6 us (5%)
  other arithmetic  3.8 us (1%)
    pallas_call x1, Pallas kernels, attention(): call(functools.partial(attention_kernel, parts, outs, len(weight)), 'ssss...  43.2 us
    ppermute x19, waiting for transfers between devices, swap(): return lax.ppermute(value, axis, [(0, 1), (1, 0)])  41.8 us
    pallas_call x2, Pallas kernels, weight_grad(): call(functools.partial(weight_grad_kernel, paired, first, extra), 'svv' +...  29.5 us
    pallas_call x1, Pallas kernels, first(): call(functools.partial(first_kernel, len(parts), len(weight)), 'sss' + 'v...  24.2 us
    pallas_call x2, Pallas kernels, last(): call(functools.partial(last_kernel, whose, len(weight)), 'sssvvvvhhh' + '...  23.5 us
    ppermute x15, waiting for transfers between devices, from_quad(): lax.ppermute(value, ('near', 'y'), [(at, at ^ bits) for at in range(4)])  23.3 us
    pallas_call x1, Pallas kernels, second(): call(functools.partial(second_kernel, len(weight)), 'sssvvh' + 'h' * len(...  22.3 us
    ppermute x15, starting transfers between devices, from_quad(): lax.ppermute(value, ('near', 'y'), [(at, at ^ bits) for at in range(4)])  20.8 us
  transfers between devices with their start and end apart: 36, of which 14 were waited for; matrix products, arithmetic and copies ran while one was open for 3% of the time, Pallas kernels for 39%

profile of v6, /device:TPU:0, one launch (start us, length us, event | category | flops | bytes accessed | tf_op | source)
XLA Modules:
  0.0 325.5 jit_solution(15389719103539045303)
XLA Ops:
  1.7 3.0 collective-permute-start.1
  6.3 6.0 %pack_features.1 = (s32[64]{0:T(128)}, s32[64]{0:T(128)}, s32[16]{0:T(128)}, s32[16]{0:T(128)}, bf16[2048,256]{1,0:T(8,128)(2,1)}, /*index=5*/bf16[2048,256]{1,0:T(8,128)(2,1)}) custom-call(s32[3]{0:T(128)} %pad_add_fusion.position, s32[64,64]{1,0:T(8,128)} %bitcast.62, s32[5028]{0:T(1024)} %constant.33.clone.table, bf16[256,4096]{1,0:T(8,128)(2,1)} %bitcast.60), custom_call_target="tpu_custom_call" | custom-call | flops 4294967296 | bytes 6291456 | tf_op jit(solution)/shard_map/pack_features/pallas_call | solution.py:475
  12.4 2.1 collective-permute-start
  15.6 3.8 %all-to-all-start = ((bf16[4,9,32,512]{3,2,1,0:T(8,128)(2,1)}), bf16[4,9,32,512]{3,2,1,0:T(8,128)(2,1)S(1)}, u32[]{:S(2)}, u32[]{:S(2)}) async-start(bf16[4,9,32,512]{3,2,1,0:T(8,128)(2,1)} %broadcast_in_dim.8), calls=%async_computation | async-start | bytes 2359296 | tf_op jit(solution)/shard_map/all_to_all | solution.py:1307
  19.4 5.2 %pack_cotangent.1 = (bf16[2048,256]{1,0:T(8,128)(2,1)}, bf16[2048,256]{1,0:T(8,128)(2,1)}) custom-call(s32[3]{0:T(128)} %pad_add_fusion.position, s32[64]{0:T(128)} %get-tuple-element.123.slot_tile, bf16[256,4096]{1,0:T(8,128)(2,1)} %bitcast.61), custom_call_target="tpu_custom_call" | custom-call | flops 42949672960 | bytes 6291456 | tf_op jit(solution)/shard_map/pack_cotangent/pallas_call | solution.py:493
  25.9 14.6 %collective-permute-done.rest_1_ = bf16[2048,256]{1,0:T(8,128)(2,1)} collective-permute-done((bf16[2048,256]{1,0:T(8,128)(2,1)}, bf16[2048,256]{1,0:T(8,128)(2,1)}, u32[]{:S(2)}, u32[]{:S(2)}) %collective-permute-start) | collective-permute-done | bytes 1048608 | tf_op jit(solution)/shard_map/ppermute | solution.py:1303
  40.6 1.8 broadcast_in_dim.9
  42.4 4.1 %all-to-all-start.1 = ((bf16[8,9,32,512]{3,2,1,0:T(8,128)(2,1)}), bf16[8,9,32,512]{3,2,1,0:T(8,128)(2,1)S(1)}, u32[]{:S(2)}, u32[]{:S(2)}) async-start(bf16[8,9,32,512]{3,2,1,0:T(8,128)(2,1)} %broadcast_in_dim.9), calls=%async_computation.1 | async-start | bytes 4718592 | tf_op jit(solution)/shard_map/all_to_all | solution.py:1307
  48.1 1.6 stack.82.rest_2_
  49.7 1.6 collective-permute-start.2
  51.8 1.7 collective-permute-done.2.rest_3_
  54.1 24.2 %conv1_forward.1 = (f32[16,512]{1,0:T(8,128)}, bf16[2048,512]{1,0:T(8,128)(2,1)}, bf16[10,10,32,512]{3,2,1,0:T(8,128)(2,1)}, bf16[64,32,512]{2,1,0:T(8,128)(2,1)...) custom-call(s32[3]{0:T(128)} %pad_add_fusion.position, ...), custom_call_target="tpu_custom_call" | custom-call | flops 9663676416 | bytes 20971520 | tf_op jit(solution)/shard_map/conv1_forward/pallas_call | solution.py:644
  78.3 1.6 collective-permute-start.6
  79.9 1.4 copy-done
  81.3 22.3 %conv2_forward.1 = (bf16[2048,512]{1,0:T(8,128)(2,1)}, bf16[2048,512]{1,0:T(8,128)(2,1)}, f32[2,32,512]{2,1,0:T(8,128)}) custom-call(s32[3]{0:T(128)} %pad_add_fusion.position, s32[64]{0:T(128)} %get-tuple-element.123.slot_tile, s32[64]{0:T(128)} %get-tuple-element.124.slot_crop, f32[16,512]{1,0:T(8,128)} %get-tuple-element.131.par.rest_0_, ...), custom_call_target="tpu_custom_call" | custom-call | flops 9663676416 | bytes 16777216 | tf_op jit(solution)/shard_map/conv2_forward/pallas_call | solution.py:733
  103.7 43.2 %attention.1 = (bf16[2048,256]{1,0:T(8,128)(2,1)}, bf16[2048,256]{1,0:T(8,128)(2,1)}, bf16[1024,512]{1,0:T(8,128)(2,1)}, bf16[1024,512]{1,0:T(8,128)(2,1)}, f32[...) custom-call(s32[3]{0:T(128)} %pad_add_fusion.position, s32[64]{0:T(128)} %get-tuple-element.123.slot_tile, ...), custom_call_target="tpu_custom_call" | custom-call | flops 32212254720 | bytes 25165824 | tf_op jit(solution)/shard_map/attention/pallas_call | solution.py:1001
  146.9 1.9 copy-done.7
  148.8 1.2 copy-done.17
  151.3 16.0 %conv2_weight_grad.1 = (bf16[3328,512]{1,0:T(8,128)(2,1)S(1)}, bf16[3328,512]{1,0:T(8,128)(2,1)S(1)}) custom-call(s32[3]{0:T(128)S(1)} %copy-done.6, bf16[10,10,32,512]{3,2,1,0:T(8,128)(2,1)S(1)} %copy-done.12, bf16[10,10,32,512]{3,2,1,0:T(8,128)(2,1)S(1)} %copy-done.7, bf16[1024,512]{1,0:T(8,128)(2,1)S(1)} %copy-done.17, bf16[1024,512]{1,0:T(8,128)(2,1)S(1)} %copy-done.18), custom_call_target="tpu_custom_call" | custom-call | flops 9663676416 | bytes 12582912 | tf_op jit(solution)/shard_map/conv2_weight_grad/pallas_call | solution.py:1069
  168.1 19.2 %conv2_input_grad.1 = (bf16[10,10,32,512]{3,2,1,0:T(8,128)(2,1)S(1)}, f32[2,16,256]{2,1,0:T(8,128)S(1)}) custom-call(s32[3]{0:T(128)S(1)} %copy-done.6, s32[64]{0:T(128)S(1)} %copy-done.20, s32[64]{0:T(128)S(1)} %copy-done.21, f32[16,512]{1,0:T(8,128)S(1)} %copy-done.15, f32[2,32,512]{2,1,0:T(8,128)S(1)} %copy-done.19, ...), custom_call_target="tpu_custom_call" | custom-call | flops 9663676416 | bytes 16777216 | tf_op jit(solution)/shard_map/conv2_input_grad/pallas_call | solution.py:1182
  187.3 5.8 %collective-permute-done.8.rest_1_ = bf16[2048,256]{1,0:T(8,128)(2,1)S(1)} collective-permute-done((bf16[2048,256]{1,0:T(8,128)(2,1)S(1)}, bf16[2048,256]{1,0:T(8,128)(2,1)S(1)}, u32[]{:S(2)}, u32[]{:S(2)}) %collective-permute-start.8) | collective-permute-done | bytes 1048608 | tf_op jit(solution)/shard_map/ppermute | solution.py:1303
  194.7 2.6 collective-permute-start.13
  198.3 13.5 %conv1_weight_grad.1 = (bf16[2304,512]{1,0:T(8,128)(2,1)S(1)}, bf16[2304,512]{1,0:T(8,128)(2,1)S(1)}) custom-call(s32[3]{0:T(128)S(1)} %copy-done.6, bf16[10,10,32,512]{3,2,1,0:T(8,128)(2,1)S(1)} %copy-done.13, bf16[10,10,32,512]{3,2,1,0:T(8,128)(2,1)S(1)} %get-tuple-element.188.grad.rest_1_), custom_call_target="tpu_custom_call" | custom-call | flops 9663676416 | bytes 12582912 | tf_op jit(solution)/shard_map/conv1_weight_grad/pallas_call | solution.py:1069
  211.9 6.2 %collective-permute-done.10 = bf16[1024,512]{1,0:T(8,128)(2,1)S(1)} collective-permute-done((bf16[1024,512]{1,0:T(8,128)(2,1)S(1)}, bf16[1024,512]{1,0:T(8,128)(2,1)S(1)}, u32[]{:S(2)}, u32[]{:S(2)}) %collective-permute-start.10) | collective-permute-done | bytes 1048608 | tf_op jit(solution)/shard_map/ppermute | solution.py:1303
  219.4 2.2 collective-permute-start.17
  221.6 1.3 collective-permute-start.16
  223.0 11.8 %conv1_input_grad.2 = (bf16[2048,256]{1,0:T(8,128)(2,1)S(1)}, f32[16,256]{1,0:T(8,128)S(1)}) custom-call(s32[3]{0:T(128)S(1)} %copy-done.6, s32[64]{0:T(128)S(1)} %copy-done.20, s32[64]{0:T(128)S(1)} %copy-done.21, f32[16,512]{1,0:T(8,128)S(1)} %copy-done.15, f32[2,32,512]{2,1,0:T(8,128)S(1)} %copy-done.11, f32[2,16,256]{2,1,0:T(8,128)S(1)} %get-tuple-element.172.vecs2, ...), custom_call_target="tpu_custom_call" | custom-call | flops 4831838208 | bytes 10485760 | tf_op jit(solution)/shard_map/conv1_input_grad/pallas_call | solution.py:1265
  236.0 2.5 collective-permute-start.22
  239.3 3.0 collective-permute-start.21
  242.9 1.4 collective-permute-start.23
  244.3 11.7 %conv1_input_grad.3 = (f32[2048,256]{1,0:T(8,128)S(1)}, f32[16,256]{1,0:T(8,128)S(1)}) custom-call(s32[3]{0:T(128)S(1)} %copy-done.6, s32[64]{0:T(128)S(1)} %copy-done.20, s32[64]{0:T(128)S(1)} %copy-done.21, f32[16,512]{1,0:T(8,128)S(1)} %copy-done.15, f32[2,32,512]{2,1,0:T(8,128)S(1)} %copy-done.11, f32[2,16,256]{2,1,0:T(8,128)S(1)} %get-tuple-element.172.vecs2, ...), custom_call_target="tpu_custom_call" | custom-call | flops 4831838208 | bytes 10485760 | tf_op jit(solution)/shard_map/conv1_input_grad/pallas_call | solution.py:1265
  256.1 1.4 collective-permute-done.22
  257.6 1.5 collective-permute-start.31
  259.1 5.4 %collective-permute-done.21 = bf16[576,512]{1,0:T(8,128)(2,1)S(1)} collective-permute-done((bf16[576,512]{1,0:T(8,128)(2,1)S(1)}, bf16[576,512]{1,0:T(8,128)(2,1)S(1)}, u32[]{:S(2)}, u32[]{:S(2)}) %collective-permute-start.21) | collective-permute-done | bytes 589856 | tf_op jit(solution)/shard_map/ppermute | solution.py:1315
  264.5 1.4 collective-permute-start.30
  266.0 1.6 collective-permute-done.20
  267.6 3.6 %collective-permute-start.29 = (bf16[416,512]{1,0:T(8,128)(2,1)S(1)}, bf16[416,512]{1,0:T(8,128)(2,1)S(1)}, u32[]{:S(2)}, u32[]{:S(2)}) collective-permute-start(bf16[416,512]{1,0:T(8,128)(2,1)S(1)} %add_convert_fusion.6), channel_id=1, source_target_pairs={{0,8},{4,12},{8,0},{12,4},{1,9},{5,13},{9,1},{13,5},{2,10},{6,14},... | collective-permute-start | bytes 1277960 | tf_op jit(solution)/shard_map/ppermute | solution.py:1315
  271.2 5.9 %collective-permute-done.19 = bf16[576,512]{1,0:T(8,128)(2,1)S(1)} collective-permute-done((bf16[576,512]{1,0:T(8,128)(2,1)S(1)}, bf16[576,512]{1,0:T(8,128)(2,1)S(1)}, u32[]{:S(2)}, u32[]{:S(2)}) %collective-permute-start.19) | collective-permute-done | bytes 589856 | tf_op jit(solution)/shard_map/ppermute | solution.py:1315
  278.0 1.9 collective-permute-start.24
  279.9 4.5 %unpack_output.1 = bf16[256,4096]{1,0:T(8,128)(2,1)} custom-call(s32[3]{0:T(128)S(1)} %copy-done.6, s32[64]{0:T(128)S(1)} %copy-done.20, bf16[2048,256]{1,0:T(8,128)(2,1)S(1)} %copy-done.10, bf16[2048,256]{1,0:T(8,128)(2,1)S(1)} %collective-permute-done.8.rest_1_), custom_call_target="tpu_custom_call" | custom-call | flops 4294967296 | bytes 8388608 | tf_op jit(solution)/shard_map/unpack_output/pallas_call | solution.py:547
  286.1 6.2 %unpack_input_grad.1 = f32[256,4096]{1,0:T(8,128)} custom-call(s32[3]{0:T(128)S(1)} %copy-done.6, s32[64]{0:T(128)S(1)} %copy-done.20, f32[2048,256]{1,0:T(8,128)S(1)} %get-tuple-element.206.rest_0_, bf16[2048,256]{1,0:T(8,128)(2,1)S(1)} %collective-permute-done.23.rest_1_), custom_call_target="tpu_custom_call" | custom-call | flops 4294967296 | bytes 8388608 | tf_op jit(solution)/shard_map/unpack_input_grad/pallas_call | solution.py:547
  292.3 8.2 %collective-permute-done.25 = bf16[320,512]{1,0:T(8,128)(2,1)S(1)} collective-permute-done((bf16[320,512]{1,0:T(8,128)(2,1)S(1)}, bf16[320,512]{1,0:T(8,128)(2,1)S(1)}, u32[]{:S(2)}, u32[]{:S(2)}) %collective-permute-start.25) | collective-permute-done | bytes 327712 | tf_op jit(solution)/shard_map/ppermute | solution.py:1303
  302.7 1.9 collective-permute-start.26
  304.6 3.8 %conv2_grads.1 = (f32[256,512]{1,0:T(8,128)}, f32[256,512]{1,0:T(8,128)}, f32[256,512]{1,0:T(8,128)}, f32[256,512]{1,0:T(8,128)}, f32[9,256,512]{2,1,0:T(8,128)}) custom-call(s32[3]{0:T(128)S(1)} %copy-done.6, bf16[1664,512]{1,0:T(8,128)(2,1)S(1)} %constant_dynamic-update-slice_fusion.mine, bf16[1664,512]{1,0:T(8,128)(2,1)S(1)} %collective-permute-done.32.other), custom_call_target="tpu_custom_call" | custom-call | flops 4294967296 | bytes 6291456 | tf_op jit(solution)/shard_map/conv2_grads/pallas_call | solution.py:1423
  308.4 4.1 %collective-permute-done.28 = bf16[320,512]{1,0:T(8,128)(2,1)S(1)} collective-permute-done((bf16[320,512]{1,0:T(8,128)(2,1)S(1)}, bf16[320,512]{1,0:T(8,128)(2,1)S(1)}, u32[]{:S(2)}, u32[]{:S(2)}) %collective-permute-start.28) | collective-permute-done | bytes 327712 | tf_op jit(solution)/shard_map/ppermute | solution.py:1315
  312.5 6.1 %collective-permute-done.27 = bf16[320,512]{1,0:T(8,128)(2,1)S(1)} collective-permute-done((bf16[320,512]{1,0:T(8,128)(2,1)S(1)}, bf16[320,512]{1,0:T(8,128)(2,1)S(1)}, u32[]{:S(2)}, u32[]{:S(2)}) %collective-permute-start.27) | collective-permute-done | bytes 327712 | tf_op jit(solution)/shard_map/ppermute | solution.py:1315
  318.8 3.0 collective-permute-done.33.other
  321.9 3.0 conv1_grads.1
  (158 shorter events, 22.0 us)
Async XLA Ops:
  1.7 12.8 %collective-permute-start.1 = (bf16[9,32,512]{2,1,0:T(8,128)(2,1)S(1)}, bf16[9,32,512]{2,1,0:T(8,128)(2,1)S(1)}, u32[]{:S(2)}, u32[]{:S(2)}) collective-permute-start(bf16[9,32,512]{2,1,0:T(8,128)(2,1)S(1)} %constant_dynamic-slice_fusion.2), channel_id=1, source_target_pairs={{0,1},{1,0},{2,3},{3,2},{4,5},{5,4},{6,7},{7,6},{8,9},{9,8},{10,11... | collective-permute-start | bytes 884744 | tf_op jit(solution)/shard_map/ppermute | solution.py:1303
  5.7 20.0 %collective-permute-start.4 = (bf16[9,32,512]{2,1,0:T(8,128)(2,1)S(1)}, bf16[9,32,512]{2,1,0:T(8,128)(2,1)S(1)}, u32[]{:S(2)}, u32[]{:S(2)}) collective-permute-start(bf16[9,32,512]{2,1,0:T(8,128)(2,1)S(1)} %constant_dynamic-slice_fusion.1), channel_id=1, source_target_pairs={{0,1},{1,0},{2,3},{3,2},{4,5},{5,4},{6,7},{7,6},{8,9},{9,8},{10,11... | collective-permute-start | bytes 884744 | tf_op jit(solution)/shard_map/ppermute | solution.py:1303
  12.4 28.2 %collective-permute-start = (bf16[2048,256]{1,0:T(8,128)(2,1)}, bf16[2048,256]{1,0:T(8,128)(2,1)}, u32[]{:S(2)}, u32[]{:S(2)}) collective-permute-start(bf16[2048,256]{1,0:T(8,128)(2,1)} %get-tuple-element.128), channel_id=1, source_target_pairs={{0,1},{1,0},{2,3},{3,2},{4,5},{5,4},{6,7},{7,6},{8,9},{9,8},{10,11... | collective-permute-start | bytes 3145736 | tf_op jit(solution)/shard_map/ppermute | solution.py:1303
  15.6 25.0 %all-to-all-start = ((bf16[4,9,32,512]{3,2,1,0:T(8,128)(2,1)}), bf16[4,9,32,512]{3,2,1,0:T(8,128)(2,1)S(1)}, u32[]{:S(2)}, u32[]{:S(2)}) async-start(bf16[4,9,32,512]{3,2,1,0:T(8,128)(2,1)} %broadcast_in_dim.8), calls=%async_computation | async-start | bytes 2359296 | tf_op jit(solution)/shard_map/all_to_all | solution.py:1307
  42.4 37.6 %all-to-all-start.1 = ((bf16[8,9,32,512]{3,2,1,0:T(8,128)(2,1)}), bf16[8,9,32,512]{3,2,1,0:T(8,128)(2,1)S(1)}, u32[]{:S(2)}, u32[]{:S(2)}) async-start(bf16[8,9,32,512]{3,2,1,0:T(8,128)(2,1)} %broadcast_in_dim.9), calls=%async_computation.1 | async-start | bytes 4718592 | tf_op jit(solution)/shard_map/all_to_all | solution.py:1307
  46.4 7.1 %collective-permute-start.3 = (bf16[4,9,32,512]{3,2,1,0:T(8,128)(2,1)S(1)}, bf16[4,9,32,512]{3,2,1,0:T(8,128)(2,1)}, u32[]{:S(2)}, u32[]{:S(2)}) collective-permute-start(bf16[4,9,32,512]{3,2,1,0:T(8,128)(2,1)S(1)} %all-to-all-done.rest_5_.rest_4_), channel_id=1, source_target_pairs={{0,2},{2,0},{1,3},{3,1},{4,6},{6,4},{5,7},{7,5},{8,10},{10,8},{9,1... | collective-permute-start | bytes 3538952 | tf_op jit(solution)/shard_map/ppermute | solution.py:1303
  49.7 3.8 %collective-permute-start.2 = (f32[16,256]{1,0:T(8,128)S(1)}, f32[16,256]{1,0:T(8,128)S(1)}, u32[]{:S(2)}, u32[]{:S(2)}) collective-permute-start(f32[16,256]{1,0:T(8,128)S(1)} %stack.82.rest_2_), channel_id=1, source_target_pairs={{0,1},{1,0},{2,3},{3,2},{4,5},{5,4},{6,7},{7,6},{8,9},{9,8},{10,11... | collective-permute-start | bytes 49160 | tf_op jit(solution)/shard_map/ppermute | solution.py:1303
  51.2 27.0 %collective-permute-start.5 = (bf16[4,128,512]{2,1,0:T(8,128)(2,1)}, bf16[4,128,512]{2,1,0:T(8,128)(2,1)}, u32[]{:S(2)}, u32[]{:S(2)}) collective-permute-start(bf16[4,128,512]{2,1,0:T(8,128)(2,1)} %constant_dynamic-slice_fusion), channel_id=1, source_target_pairs={{0,1},{1,0},{2,3},{3,2},{4,5},{5,4},{6,7},{7,6},{8,9},{9,8},{10,11... | collective-permute-start | bytes 1572872 | tf_op jit(solution)/shard_map/ppermute | solution.py:1303
  54.1 24.2 %copy-start.32 = (bf16[2048,256]{1,0:T(8,128)(2,1)S(1)}, bf16[2048,256]{1,0:T(8,128)(2,1)}, u32[]{:S(2)}) copy-start(bf16[2048,256]{1,0:T(8,128)(2,1)} %get-tuple-element.141) | copy-start | bytes 3145732
  78.3 25.3 %collective-permute-start.6 = (bf16[2048,256]{1,0:T(8,128)(2,1)S(1)}, bf16[2048,256]{1,0:T(8,128)(2,1)}, u32[]{:S(2)}, u32[]{:S(2)}) collective-permute-start(bf16[2048,256]{1,0:T(8,128)(2,1)S(1)} %copy-done.32), channel_id=1, source_target_pairs={{0,1},{1,0},{2,3},{3,2},{4,5},{5,4},{6,7},{7,6},{8,9},{9,8},{10,11... | collective-permute-start | bytes 3145736 | tf_op jit(solution)/shard_map/ppermute | solution.py:1303
  79.9 23.7 %collective-permute-start.7 = (bf16[4,128,512]{2,1,0:T(8,128)(2,1)}, bf16[4,128,512]{2,1,0:T(8,128)(2,1)}, u32[]{:S(2)}, u32[]{:S(2)}) collective-permute-start(bf16[4,128,512]{2,1,0:T(8,128)(2,1)} %collective-permute-done.5.rest_7_), channel_id=1, source_target_pairs={{0,2},{2,0},{1,3},{3,1},{4,6},{6,4},{5,7},{7,5},{8,10},{10,8},{9,1... | collective-permute-start | bytes 1572872 | tf_op jit(solution)/shard_map/ppermute | solution.py:1303
  103.6 43.2 %copy-start.6 = (s32[3]{0:T(128)S(1)}, s32[3]{0:T(128)}, u32[]{:S(2)}) copy-start(s32[3]{0:T(128)} %pad_add_fusion.position) | copy-start | bytes 40
  103.6 43.2 %copy-start.12 = (bf16[10,10,32,512]{3,2,1,0:T(8,128)(2,1)S(1)}, bf16[10,10,32,512]{3,2,1,0:T(8,128)(2,1)}, u32[]{:S(2)}) copy-start(bf16[10,10,32,512]{3,2,1,0:T(8,128)(2,1)} %get-tuple-element.133.pad_hbm.active) | copy-start | bytes 9830404
  151.2 16.8 %copy-start.1 = (bf16[8,9,32,512]{3,2,1,0:T(8,128)(2,1)S(1)}, bf16[8,9,32,512]{3,2,1,0:T(8,128)(2,1)}, u32[]{:S(2)}) copy-start(bf16[8,9,32,512]{3,2,1,0:T(8,128)(2,1)} %copy-done) | copy-start | bytes 7077892
  151.2 16.8 %copy-start.4 = (bf16[9,256,512]{2,1,0:T(8,128)(2,1)S(1)}, bf16[9,256,512]{2,1,0:T(8,128)(2,1)}, u32[]{:S(2)}) copy-start(bf16[9,256,512]{2,1,0:T(8,128)(2,1)} %rest_0_.3) | copy-start | bytes 7077892
  151.2 16.8 %copy-start.14 = (bf16[64,32,512]{2,1,0:T(8,128)(2,1)S(1)}, bf16[64,32,512]{2,1,0:T(8,128)(2,1)}, u32[]{:S(2)}) copy-start(bf16[64,32,512]{2,1,0:T(8,128)(2,1)} %get-tuple-element.155.hidden_hbm) | copy-start | bytes 6291460
  151.3 16.8 %copy-start.15 = (f32[16,512]{1,0:T(8,128)S(1)}, f32[16,512]{1,0:T(8,128)}, u32[]{:S(2)}) copy-start(f32[16,512]{1,0:T(8,128)} %get-tuple-element.131.par.rest_0_) | copy-start | bytes 98308
  151.3 16.8 %copy-start.19 = (f32[2,32,512]{2,1,0:T(8,128)S(1)}, f32[2,32,512]{2,1,0:T(8,128)}, u32[]{:S(2)}) copy-start(f32[2,32,512]{2,1,0:T(8,128)} %get-tuple-element.149.stats2) | copy-start | bytes 393220
  167.3 25.7 %collective-permute-start.9 = (bf16[3328,512]{1,0:T(8,128)(2,1)S(1)}, bf16[3328,512]{1,0:T(8,128)(2,1)S(1)}, u32[]{:S(2)}, u32[]{:S(2)}) collective-permute-start(bf16[3328,512]{1,0:T(8,128)(2,1)S(1)} %get-tuple-element.153), channel_id=1, source_target_pairs={{0,2},{2,0},{1,3},{3,1},{4,6},{6,4},{5,7},{7,5},{8,10},{10,8},{9,1... | collective-permute-start | bytes 10223624 | tf_op jit(solution)/shard_map/ppermute | solution.py:1303
  167.9 25.1 %collective-permute-start.8 = (bf16[2048,256]{1,0:T(8,128)(2,1)S(1)}, bf16[2048,256]{1,0:T(8,128)(2,1)S(1)}, u32[]{:S(2)}, u32[]{:S(2)}) collective-permute-start(bf16[2048,256]{1,0:T(8,128)(2,1)S(1)} %copy-done.33), channel_id=1, source_target_pairs={{0,1},{1,0},{2,3},{3,2},{4,5},{5,4},{6,7},{7,6},{8,9},{9,8},{10,11... | collective-permute-start | bytes 3145736 | tf_op jit(solution)/shard_map/ppermute | solution.py:1303
  193.7 24.4 %collective-permute-start.10 = (bf16[1024,512]{1,0:T(8,128)(2,1)S(1)}, bf16[1024,512]{1,0:T(8,128)(2,1)S(1)}, u32[]{:S(2)}, u32[]{:S(2)}) collective-permute-start(bf16[1024,512]{1,0:T(8,128)(2,1)S(1)} %get-tuple-element.231), channel_id=1, source_target_pairs={{0,1},{1,0},{2,3},{3,2},{4,5},{5,4},{6,7},{7,6},{8,9},{9,8},{10,11... | collective-permute-start | bytes 3145736 | tf_op jit(solution)/shard_map/ppermute | solution.py:1303
  194.7 17.1 %collective-permute-start.13 = (bf16[320,512]{1,0:T(8,128)(2,1)S(1)}, bf16[320,512]{1,0:T(8,128)(2,1)S(1)}, u32[]{:S(2)}, u32[]{:S(2)}) collective-permute-start(bf16[320,512]{1,0:T(8,128)(2,1)S(1)} %get-tuple-element.227), channel_id=1, source_target_pairs={{0,12},{4,8},{8,4},{12,0},{1,13},{5,9},{9,5},{13,1},{2,14},{6,10},... | collective-permute-start | bytes 983048 | tf_op jit(solution)/shard_map/ppermute | solution.py:1315
  197.3 14.5 %collective-permute-start.12 = (bf16[320,512]{1,0:T(8,128)(2,1)S(1)}, bf16[320,512]{1,0:T(8,128)(2,1)S(1)}, u32[]{:S(2)}, u32[]{:S(2)}) collective-permute-start(bf16[320,512]{1,0:T(8,128)(2,1)S(1)} %get-tuple-element.229), channel_id=1, source_target_pairs={{0,4},{4,0},{8,12},{12,8},{1,5},{5,1},{9,13},{13,9},{2,6},{6,2},{1... | collective-permute-start | bytes 983048 | tf_op jit(solution)/shard_map/ppermute | solution.py:1315
  198.2 13.7 %collective-permute-start.11 = (bf16[320,512]{1,0:T(8,128)(2,1)S(1)}, bf16[320,512]{1,0:T(8,128)(2,1)S(1)}, u32[]{:S(2)}, u32[]{:S(2)}) collective-permute-start(bf16[320,512]{1,0:T(8,128)(2,1)S(1)} %get-tuple-element.230), channel_id=1, source_target_pairs={{0,8},{4,12},{8,0},{12,4},{1,9},{5,13},{9,1},{13,5},{2,10},{6,14},... | collective-permute-start | bytes 983048 | tf_op jit(solution)/shard_map/ppermute | solution.py:1315
  198.3 24.7 %copy-start.5 = (bf16[9,256,512]{2,1,0:T(8,128)(2,1)S(1)}, bf16[9,256,512]{2,1,0:T(8,128)(2,1)}, u32[]{:S(2)}) copy-start(bf16[9,256,512]{2,1,0:T(8,128)(2,1)} %rest_3_.3) | copy-start | bytes 7077892
  198.3 24.7 %copy-start.8 = (bf16[10,10,32,512]{3,2,1,0:T(8,128)(2,1)S(1)}, bf16[10,10,32,512]{3,2,1,0:T(8,128)(2,1)}, u32[]{:S(2)}) copy-start(bf16[10,10,32,512]{3,2,1,0:T(8,128)(2,1)} %get-tuple-element.154.grad.pad_hbm.rest_2_) | copy-start | bytes 9830404
  198.3 24.7 %copy-start.9 = (bf16[2048,512]{1,0:T(8,128)(2,1)S(1)}, bf16[2048,512]{1,0:T(8,128)(2,1)}, u32[]{:S(2)}) copy-start(bf16[2048,512]{1,0:T(8,128)(2,1)} %get-tuple-element.132.feats.rest_0_) | copy-start | bytes 6291460
  211.9 22.9 %copy-start.26 = (bf16[320,512]{1,0:T(8,128)(2,1)}, bf16[320,512]{1,0:T(8,128)(2,1)S(1)}, u32[]{:S(2)}) copy-start(bf16[320,512]{1,0:T(8,128)(2,1)S(1)} %collective-permute-done.11) | copy-start | bytes 983044
  218.4 20.1 %collective-permute-start.14 = (bf16[2304,512]{1,0:T(8,128)(2,1)S(1)}, bf16[2304,512]{1,0:T(8,128)(2,1)S(1)}, u32[]{:S(2)}, u32[]{:S(2)}) collective-permute-start(bf16[2304,512]{1,0:T(8,128)(2,1)S(1)} %get-tuple-element.170), channel_id=1, source_target_pairs={{0,2},{2,0},{1,3},{3,1},{4,6},{6,4},{5,7},{7,5},{8,10},{10,8},{9,1... | collective-permute-start | bytes 7077896 | tf_op jit(solution)/shard_map/ppermute | solution.py:1303
  218.5 16.4 %collective-permute-start.18 = (bf16[160,512]{1,0:T(8,128)(2,1)S(1)}, bf16[160,512]{1,0:T(8,128)(2,1)S(1)}, u32[]{:S(2)}, u32[]{:S(2)}) collective-permute-start(bf16[160,512]{1,0:T(8,128)(2,1)S(1)} %add_convert_fusion.19), channel_id=1, source_target_pairs={{0,1},{1,0},{2,3},{3,2},{4,5},{5,4},{6,7},{7,6},{8,9},{9,8},{10,11... | collective-permute-start | bytes 491528 | tf_op jit(solution)/shard_map/ppermute | solution.py:1303
  219.4 15.5 %collective-permute-start.17 = (bf16[256,512]{1,0:T(8,128)(2,1)S(1)}, bf16[256,512]{1,0:T(8,128)(2,1)S(1)}, u32[]{:S(2)}, u32[]{:S(2)}) collective-permute-start(bf16[256,512]{1,0:T(8,128)(2,1)S(1)} %get-tuple-element.237), channel_id=1, source_target_pairs={{0,12},{4,8},{8,4},{12,0},{1,13},{5,9},{9,5},{13,1},{2,14},{6,10},... | collective-permute-start | bytes 786440 | tf_op jit(solution)/shard_map/ppermute | solution.py:1315
  221.6 13.3 %collective-permute-start.16 = (bf16[256,512]{1,0:T(8,128)(2,1)S(1)}, bf16[256,512]{1,0:T(8,128)(2,1)S(1)}, u32[]{:S(2)}, u32[]{:S(2)}) collective-permute-start(bf16[256,512]{1,0:T(8,128)(2,1)S(1)} %get-tuple-element.238), channel_id=1, source_target_pairs={{0,4},{4,0},{8,12},{12,8},{1,5},{5,1},{9,13},{13,9},{2,6},{6,2},{1... | collective-permute-start | bytes 786440 | tf_op jit(solution)/shard_map/ppermute | solution.py:1315
  222.9 12.1 %collective-permute-start.15 = (bf16[256,512]{1,0:T(8,128)(2,1)S(1)}, bf16[256,512]{1,0:T(8,128)(2,1)S(1)}, u32[]{:S(2)}, u32[]{:S(2)}) collective-permute-start(bf16[256,512]{1,0:T(8,128)(2,1)S(1)} %get-tuple-element.239), channel_id=1, source_target_pairs={{0,8},{4,12},{8,0},{12,4},{1,9},{5,13},{9,1},{13,5},{2,10},{6,14},... | collective-permute-start | bytes 786440 | tf_op jit(solution)/shard_map/ppermute | solution.py:1315
  236.0 21.5 %collective-permute-start.22 = (bf16[416,512]{1,0:T(8,128)(2,1)S(1)}, bf16[416,512]{1,0:T(8,128)(2,1)S(1)}, u32[]{:S(2)}, u32[]{:S(2)}) collective-permute-start(bf16[416,512]{1,0:T(8,128)(2,1)S(1)} %pad_maximum_fusion.1), channel_id=1, source_target_pairs={{0,16},{16,0},{1,17},{17,1},{2,18},{18,2},{3,19},{19,3},{4,20},{20... | collective-permute-start | bytes 1277960 | tf_op jit(solution)/shard_map/ppermute | solution.py:1303
  239.3 25.2 %collective-permute-start.21 = (bf16[576,512]{1,0:T(8,128)(2,1)S(1)}, bf16[576,512]{1,0:T(8,128)(2,1)S(1)}, u32[]{:S(2)}, u32[]{:S(2)}) collective-permute-start(bf16[576,512]{1,0:T(8,128)(2,1)S(1)} %get-tuple-element.233), channel_id=1, source_target_pairs={{0,12},{4,8},{8,4},{12,0},{1,13},{5,9},{9,5},{13,1},{2,14},{6,10},... | collective-permute-start | bytes 1769480 | tf_op jit(solution)/shard_map/ppermute | solution.py:1315
  242.3 25.3 %collective-permute-start.20 = (bf16[576,512]{1,0:T(8,128)(2,1)S(1)}, bf16[576,512]{1,0:T(8,128)(2,1)S(1)}, u32[]{:S(2)}, u32[]{:S(2)}) collective-permute-start(bf16[576,512]{1,0:T(8,128)(2,1)S(1)} %get-tuple-element.234), channel_id=1, source_target_pairs={{0,4},{4,0},{8,12},{12,8},{1,5},{5,1},{9,13},{13,9},{2,6},{6,2},{1... | collective-permute-start | bytes 1769480 | tf_op jit(solution)/shard_map/ppermute | solution.py:1315
  242.9 34.3 %collective-permute-start.19 = (bf16[576,512]{1,0:T(8,128)(2,1)S(1)}, bf16[576,512]{1,0:T(8,128)(2,1)S(1)}, u32[]{:S(2)}, u32[]{:S(2)}) collective-permute-start(bf16[576,512]{1,0:T(8,128)(2,1)S(1)} %get-tuple-element.235), channel_id=1, source_target_pairs={{0,8},{4,12},{8,0},{12,4},{1,9},{5,13},{9,1},{13,5},{2,10},{6,14},... | collective-permute-start | bytes 1769480 | tf_op jit(solution)/shard_map/ppermute | solution.py:1315
  242.9 37.0 %collective-permute-start.23 = (bf16[2048,256]{1,0:T(8,128)(2,1)S(1)}, bf16[2048,256]{1,0:T(8,128)(2,1)S(1)}, u32[]{:S(2)}, u32[]{:S(2)}) collective-permute-start(bf16[2048,256]{1,0:T(8,128)(2,1)S(1)} %get-tuple-element.197), channel_id=1, source_target_pairs={{0,1},{1,0},{2,3},{3,2},{4,5},{5,4},{6,7},{7,6},{8,9},{9,8},{10,11... | collective-permute-start | bytes 3145736 | tf_op jit(solution)/shard_map/ppermute | solution.py:1303
  257.6 43.1 %collective-permute-start.31 = (bf16[416,512]{1,0:T(8,128)(2,1)S(1)}, bf16[416,512]{1,0:T(8,128)(2,1)S(1)}, u32[]{:S(2)}, u32[]{:S(2)}) collective-permute-start(bf16[416,512]{1,0:T(8,128)(2,1)S(1)} %add_convert_fusion.6), channel_id=1, source_target_pairs={{0,12},{4,8},{8,4},{12,0},{1,13},{5,9},{9,5},{13,1},{2,14},{6,10},... | collective-permute-start | bytes 1277960 | tf_op jit(solution)/shard_map/ppermute | solution.py:1315
  264.5 36.2 %collective-permute-start.30 = (bf16[416,512]{1,0:T(8,128)(2,1)S(1)}, bf16[416,512]{1,0:T(8,128)(2,1)S(1)}, u32[]{:S(2)}, u32[]{:S(2)}) collective-permute-start(bf16[416,512]{1,0:T(8,128)(2,1)S(1)} %add_convert_fusion.6), channel_id=1, source_target_pairs={{0,4},{4,0},{8,12},{12,8},{1,5},{5,1},{9,13},{13,9},{2,6},{6,2},{1... | collective-permute-start | bytes 1277960 | tf_op jit(solution)/shard_map/ppermute | solution.py:1315
  267.6 33.2 %collective-permute-start.29 = (bf16[416,512]{1,0:T(8,128)(2,1)S(1)}, bf16[416,512]{1,0:T(8,128)(2,1)S(1)}, u32[]{:S(2)}, u32[]{:S(2)}) collective-permute-start(bf16[416,512]{1,0:T(8,128)(2,1)S(1)} %add_convert_fusion.6), channel_id=1, source_target_pairs={{0,8},{4,12},{8,0},{12,4},{1,9},{5,13},{9,1},{13,5},{2,10},{6,14},... | collective-permute-start | bytes 1277960 | tf_op jit(solution)/shard_map/ppermute | solution.py:1315
  278.0 7.1 %collective-permute-start.24 = (bf16[320,512]{1,0:T(8,128)(2,1)S(1)}, bf16[320,512]{1,0:T(8,128)(2,1)S(1)}, u32[]{:S(2)}, u32[]{:S(2)}) collective-permute-start(bf16[320,512]{1,0:T(8,128)(2,1)S(1)} %fusion.1), channel_id=1, source_target_pairs={{0,1},{1,0},{2,3},{3,2},{4,5},{5,4},{6,7},{7,6},{8,9},{9,8},{10,11... | collective-permute-start | bytes 983048 | tf_op jit(solution)/shard_map/ppermute | solution.py:1303
  285.4 15.2 %collective-permute-start.25 = (bf16[320,512]{1,0:T(8,128)(2,1)S(1)}, bf16[320,512]{1,0:T(8,128)(2,1)S(1)}, u32[]{:S(2)}, u32[]{:S(2)}) collective-permute-start(bf16[320,512]{1,0:T(8,128)(2,1)S(1)} %pad_maximum_fusion.2), channel_id=1, source_target_pairs={{0,16},{16,0},{1,17},{17,1},{2,18},{18,2},{3,19},{19,3},{4,20},{20... | collective-permute-start | bytes 983048 | tf_op jit(solution)/shard_map/ppermute | solution.py:1303
  300.9 3.7 %collective-permute-start.32 = (bf16[1664,512]{1,0:T(8,128)(2,1)S(1)}, bf16[1664,512]{1,0:T(8,128)(2,1)S(1)}, u32[]{:S(2)}, u32[]{:S(2)}) collective-permute-start(bf16[1664,512]{1,0:T(8,128)(2,1)S(1)} %constant_dynamic-update-slice_fusion.mine), channel_id=1, source_target_pairs={{0,2},{2,0},{1,3},{3,1},{4,6},{6,4},{5,7},{7,5},{8,10},{10,8},{9,1... | collective-permute-start | bytes 5111816 | tf_op jit(solution)/shard_map/ppermute | solution.py:1303
  301.0 11.5 %collective-permute-start.28 = (bf16[320,512]{1,0:T(8,128)(2,1)S(1)}, bf16[320,512]{1,0:T(8,128)(2,1)S(1)}, u32[]{:S(2)}, u32[]{:S(2)}) collective-permute-start(bf16[320,512]{1,0:T(8,128)(2,1)S(1)} %add_convert_fusion.7), channel_id=1, source_target_pairs={{0,12},{4,8},{8,4},{12,0},{1,13},{5,9},{9,5},{13,1},{2,14},{6,10},... | collective-permute-start | bytes 983048 | tf_op jit(solution)/shard_map/ppermute | solution.py:1315
  301.8 16.8 %collective-permute-start.27 = (bf16[320,512]{1,0:T(8,128)(2,1)S(1)}, bf16[320,512]{1,0:T(8,128)(2,1)S(1)}, u32[]{:S(2)}, u32[]{:S(2)}) collective-permute-start(bf16[320,512]{1,0:T(8,128)(2,1)S(1)} %add_convert_fusion.7), channel_id=1, source_target_pairs={{0,4},{4,0},{8,12},{12,8},{1,5},{5,1},{9,13},{13,9},{2,6},{6,2},{1... | collective-permute-start | bytes 983048 | tf_op jit(solution)/shard_map/ppermute | solution.py:1315
  302.7 16.0 %collective-permute-start.26 = (bf16[320,512]{1,0:T(8,128)(2,1)S(1)}, bf16[320,512]{1,0:T(8,128)(2,1)S(1)}, u32[]{:S(2)}, u32[]{:S(2)}) collective-permute-start(bf16[320,512]{1,0:T(8,128)(2,1)S(1)} %add_convert_fusion.7), channel_id=1, source_target_pairs={{0,8},{4,12},{8,0},{12,4},{1,9},{5,13},{9,1},{13,5},{2,10},{6,14},... | collective-permute-start | bytes 983048 | tf_op jit(solution)/shard_map/ppermute | solution.py:1315
  318.8 3.1 collective-permute-start.33
  (27 other events, 168.9 us)
